TPU v7x, 32 devices: a whole 2x2x4 slice. The times are simulated.
32 devices in a mesh: dp: 32 (over z, y, x, core).
Axes of the slice: x: 2, y: 2, z: 4, core: 2. Of those that a mesh axis runs over, the one named last changes fastest.
Arguments:
- token_ids: int32 [128, 256], P('dp'), may hold values from 0 to 147
- durations: int32 [128, 256], P('dp'), may hold values from 0 to 993, as said below
- mel_frames: float32 [128, 1024, 80], P('dp'), may hold values from -6 to 6
- embedding: bfloat16 [148, 192], replicated, may hold values from -0.4375 to 0.4375
- w_qkv: bfloat16 [192, 576], replicated, may hold values from -0.4375 to 0.4375
- rel_key: bfloat16 [9, 96], replicated, may hold values from -0.625 to 0.625
- rel_value: bfloat16 [9, 96], replicated, may hold values from -0.625 to 0.625
- w_out: bfloat16 [192, 192], replicated, may hold values from -1.25 to 1.25
- attn_gain: float32 [192], replicated, may hold values from 0.5 to 1.5
- attn_shift: float32 [192], replicated, may hold values from -3 to 3
- w_ff1: bfloat16 [576, 768], replicated, may hold values from -0.25 to 0.25
- w_ff2: bfloat16 [2304, 192], replicated, may hold values from -0.125 to 0.125
- ffn_gain: float32 [192], replicated, may hold values from 0.5 to 1.5
- ffn_shift: float32 [192], replicated, may hold values from -3 to 3
- w_prior: bfloat16 [192, 160], replicated, may hold values from -0.21875 to 0.21875
- w_mix: float32 [4, 4], replicated, may hold values from -0.6 to 3, as said below
- w_start: bfloat16 [80, 192], replicated, may hold values from -0.625 to 0.625
- w_in: bfloat16 [4, 960, 384], replicated, may hold values from -0.1875 to 0.1875
- w_res: bfloat16 [3, 192, 384], replicated, may hold values from -0.4375 to 0.4375
- w_skip_last: bfloat16 [192, 192], replicated, may hold values from -0.4375 to 0.4375
- w_end: bfloat16 [192, 160], replicated, may hold values from -0.15625 to 0.15625
Outputs:
- loss: float32 [], replicated
- mel_grad: float32 [128, 1024, 80], P('dp')
- embedding_grad: float32 [148, 192], replicated
- w_qkv_grad: float32 [192, 576], replicated
- rel_key_grad: float32 [9, 96], replicated
- rel_value_grad: float32 [9, 96], replicated
- w_out_grad: float32 [192, 192], replicated
- attn_gain_grad: float32 [192], replicated
- attn_shift_grad: float32 [192], replicated
- w_ff1_grad: float32 [576, 768], replicated
- w_ff2_grad: float32 [2304, 192], replicated
- ffn_gain_grad: float32 [192], replicated
- ffn_shift_grad: float32 [192], replicated
- w_prior_grad: float32 [192, 160], replicated
- w_mix_grad: float32 [4, 4], replicated
- w_start_grad: float32 [80, 192], replicated
- w_in_grad: float32 [4, 960, 384], replicated
- w_res_grad: float32 [3, 192, 384], replicated
- w_skip_last_grad: float32 [192, 192], replicated
- w_end_grad: float32 [192, 160], replicated
Inputs may be any that keep to these rules, and one draw needn't show every extreme that they name: In each utterance the first L slots have positive durations and the rest zero, with 32 <= L <= 256; the durations sum to the utterance's frame count, between 256 and 1024; some utterance has L = 256, and another one has 1024 frames, L = 32 and a token of the largest duration. `w_mix`: each diagonal entry exceeds the sum of the magnitudes of the other entries of its row.
All inputs are finite; a program needn't handle non-finite values.
Results may differ from a plain program's by a relative error of at most 0.014.
Values sent between devices are 32-bit elements; how exact they have to be, the bound alone decides.
No kernel may reach another device: no remote copies, remote signals or barrier semaphores. Data moves between devices by JAX's collectives and lax.ppermute only.
A program may use at most 128 MiB of HBM per device.

v0:
```python
import math

import jax
import jax.numpy as jnp
from jax import lax
from jax.sharding import PartitionSpec as P

D = 192
HEADS = 2
HEAD = 96
FILTER = 768
MEL = 80
HID = 192
VOCAB = 148
KSIZE = 3
WKER = 5
WLAYERS = 4
WINDOW = 4


def matmul(first_op, second_op):
    return jnp.dot(first_op, second_op, preferred_element_type=jnp.float32)


def matmul_nt(first_op, second_op):
    return lax.dot_general(
        first_op, second_op, (((1,), (1,)), ((), ())), preferred_element_type=jnp.float32
    )


def inner_rows(first_op, second_op):
    return lax.dot_general(
        first_op, second_op, (((0,), (0,)), ((), ())), preferred_element_type=jnp.float32
    )


def unfold(inputs, kernel):
    half_width = kernel // 2
    padded = jnp.pad(inputs, ((half_width, half_width), (0, 0)))
    length = inputs.shape[0]
    return jnp.concatenate(
        [padded[offset_step : offset_step + length] for offset_step in range(kernel)], axis=1
    )


def fold(gradients, kernel, channels):
    half_width = kernel // 2
    length = gradients.shape[0]
    padded = jnp.pad(gradients, ((half_width, half_width), (0, 0)))
    running = jnp.zeros((length, channels), jnp.float32)
    for offset_step in range(kernel):
        begin = 2 * half_width - offset_step
        running = (
            running
            + padded[begin : begin + length, offset_step * channels : (offset_step + 1) * channels]
        )
    return running


def layer_norm(inputs, scale_vec, shift_vec):
    centered = inputs - jnp.mean(inputs, axis=1, keepdims=True)
    spread = jnp.mean(centered * centered, axis=1, keepdims=True)
    return centered * lax.rsqrt(spread + 1e-05) * scale_vec + shift_vec


def gate_units(pre_gate):
    return jnp.tanh(pre_gate[:, :HID]) * jax.nn.sigmoid(pre_gate[:, HID:])


def band_table(length):
    places = lax.iota(jnp.int32, length)
    offsets = places[None, :] - places[:, None]
    reach = lax.iota(jnp.int32, 2 * WINDOW + 1) - WINDOW
    return (offsets[None, :, :] == reach[:, None, None]).astype(jnp.float32)


def pair_up(frames):
    count_rows = frames.shape[0]
    width = frames.shape[1]
    return (
        frames.reshape(count_rows // 2, 2, width)
        .transpose(0, 2, 1)
        .reshape(count_rows // 2, 2 * width)
    )


def pair_open(pairs_in):
    count_rows = pairs_in.shape[0]
    width = pairs_in.shape[1]
    return (
        pairs_in.reshape(count_rows, width // 2, 2)
        .transpose(0, 2, 1)
        .reshape(2 * count_rows, width // 2)
    )


def to_groups(frames):
    count_rows = frames.shape[0]
    width = frames.shape[1]
    return (
        frames.reshape(count_rows, 2, width // 4, 2)
        .transpose(0, 2, 1, 3)
        .reshape(count_rows, width // 4, 4)
    )


def from_groups(grouped):
    count_rows = grouped.shape[0]
    groups = grouped.shape[1]
    return (
        grouped.reshape(count_rows, groups, 2, 2)
        .transpose(0, 2, 1, 3)
        .reshape(count_rows, 4 * groups)
    )


def invert_small(matrix):
    joined = jnp.concatenate([matrix, jnp.eye(4, dtype=jnp.float32)], axis=1)
    determinant = jnp.ones((), jnp.float32)
    for column in range(4):
        pivot_value = joined[column, column]
        determinant = determinant * pivot_value
        row_now = joined[column] / pivot_value
        joined = joined - joined[:, column : column + 1] * row_now[None, :]
        joined = joined.at[column].set(row_now)
    return (joined[:, 4:], determinant)


def one_hot_rows(token_rows):
    return token_rows[:, None] == lax.iota(jnp.int32, VOCAB)[None, :]


def encode(token_rows, durations_row, enc_w):
    (
        embedding,
        w_qkv,
        rel_key,
        rel_value,
        w_out,
        attn_gain,
        attn_shift,
        w_ff1,
        w_ff2,
        ffn_gain,
        ffn_shift,
        w_prior,
    ) = enc_w
    length = token_rows.shape[0]
    text_mask = (durations_row > 0).astype(jnp.float32)[:, None]
    embedded = (
        matmul(one_hot_rows(token_rows).astype(jnp.bfloat16), embedding) * math.sqrt(D) * text_mask
    )
    embed_low = embedded.astype(jnp.bfloat16)
    project = matmul(embed_low, w_qkv).astype(jnp.bfloat16)
    query_rows = project[:, :D].reshape(length, HEADS, HEAD)
    key_rows = project[:, D : 2 * D].reshape(length, HEADS, HEAD)
    value_rows = project[:, 2 * D :].reshape(length, HEADS, HEAD)
    band_mask = band_table(length)
    direct = jnp.einsum("ihd,jhd->hij", query_rows, key_rows, preferred_element_type=jnp.float32)
    near_terms = jnp.einsum("ihd,rd->hir", query_rows, rel_key, preferred_element_type=jnp.float32)
    near_full = jnp.einsum("hir,rij->hij", near_terms, band_mask, precision=lax.Precision.HIGHEST)
    key_bias = jnp.where(text_mask[:, 0] > 0, 0.0, -10000.0)
    scores = (direct + near_full) / math.sqrt(HEAD) + key_bias[None, None, :]
    attention = jax.nn.softmax(scores, axis=-1)
    attention_low = attention.astype(jnp.bfloat16)
    banded = jnp.einsum(
        "hij,rij->hir",
        attention_low.astype(jnp.float32),
        band_mask,
        precision=lax.Precision.HIGHEST,
    ).astype(jnp.bfloat16)
    attended = jnp.einsum(
        "hij,jhd->ihd", attention_low, value_rows, preferred_element_type=jnp.float32
    )
    attended = attended + jnp.einsum(
        "hir,rd->ihd", banded, rel_value, preferred_element_type=jnp.float32
    )
    attend_low = attended.reshape(length, D).astype(jnp.bfloat16)
    mixed_in = embedded + matmul(attend_low, w_out)
    normed = layer_norm(mixed_in, attn_gain, attn_shift)
    normed_low = (normed * text_mask).astype(jnp.bfloat16)
    filtered = matmul(unfold(normed_low, KSIZE), w_ff1)
    activ_low = (jax.nn.gelu(filtered) * text_mask).astype(jnp.bfloat16)
    summed = normed + matmul(unfold(activ_low, KSIZE), w_ff2) * text_mask
    encoded_low = (layer_norm(summed, ffn_gain, ffn_shift) * text_mask).astype(jnp.bfloat16)
    prior_rows = matmul(encoded_low, w_prior) * text_mask
    saved_state = (
        embed_low,
        query_rows,
        key_rows,
        value_rows,
        attention,
        attention_low,
        banded,
        attend_low,
        mixed_in,
        normed_low,
        filtered,
        activ_low,
        summed,
        encoded_low,
    )
    return (prior_rows, saved_state)


def encode_back(token_rows, durations_row, saved_state, prior_grad, enc_w):
    (
        embedding,
        w_qkv,
        rel_key,
        rel_value,
        w_out,
        attn_gain,
        attn_shift,
        w_ff1,
        w_ff2,
        ffn_gain,
        ffn_shift,
        w_prior,
    ) = enc_w
    (
        embed_low,
        query_rows,
        key_rows,
        value_rows,
        attention,
        attention_low,
        banded,
        attend_low,
        mixed_in,
        normed_low,
        filtered,
        activ_low,
        summed,
        encoded_low,
    ) = saved_state
    length = token_rows.shape[0]
    text_mask = (durations_row > 0).astype(jnp.float32)[:, None]
    band_mask = band_table(length)
    prior_low = (prior_grad * text_mask).astype(jnp.bfloat16)
    prior_wgrad = inner_rows(encoded_low, prior_low)
    encoded_grad = matmul_nt(prior_low, w_prior) * text_mask
    _, ffn_norm_back = jax.vjp(layer_norm, summed, ffn_gain, ffn_shift)
    summed_grad, ffn_gain_grad, ffn_shift_grad = ffn_norm_back(encoded_grad)
    second_low = (summed_grad * text_mask).astype(jnp.bfloat16)
    ff2_grad = inner_rows(unfold(activ_low, KSIZE), second_low)
    activ_grad = fold(matmul_nt(second_low, w_ff2), KSIZE, FILTER) * text_mask
    _, gelu_back = jax.vjp(jax.nn.gelu, filtered)
    first_low = gelu_back(activ_grad)[0].astype(jnp.bfloat16)
    ff1_grad = inner_rows(unfold(normed_low, KSIZE), first_low)
    normed_grad = summed_grad + fold(matmul_nt(first_low, w_ff1), KSIZE, D) * text_mask
    _, attn_norm_back = jax.vjp(layer_norm, mixed_in, attn_gain, attn_shift)
    mixed_grad, attn_gain_grad, attn_shift_grad = attn_norm_back(normed_grad)
    out_low = mixed_grad.astype(jnp.bfloat16)
    out_grad = inner_rows(attend_low, out_low)
    attention_weight_gradient = (
        matmul_nt(out_low, w_out).reshape(length, HEADS, HEAD).astype(jnp.bfloat16)
    )
    near_value = jnp.einsum(
        "ihd,rd->hir", attention_weight_gradient, rel_value, preferred_element_type=jnp.float32
    )
    weight_grad = jnp.einsum(
        "ihd,jhd->hij", attention_weight_gradient, value_rows, preferred_element_type=jnp.float32
    )
    weight_grad = weight_grad + jnp.einsum(
        "hir,rij->hij", near_value, band_mask, precision=lax.Precision.HIGHEST
    )
    value_grad = jnp.einsum(
        "hij,ihd->jhd", attention_low, attention_weight_gradient, preferred_element_type=jnp.float32
    )
    rel_value_grad = jnp.einsum(
        "hir,ihd->rd", banded, attention_weight_gradient, preferred_element_type=jnp.float32
    )
    score_grad = attention * (
        weight_grad - jnp.sum(attention * weight_grad, axis=-1, keepdims=True)
    )
    score_low = (score_grad / math.sqrt(HEAD)).astype(jnp.bfloat16)
    band_grad = jnp.einsum(
        "hij,rij->hir", score_low.astype(jnp.float32), band_mask, precision=lax.Precision.HIGHEST
    ).astype(jnp.bfloat16)
    query_grad = jnp.einsum("hij,jhd->ihd", score_low, key_rows, preferred_element_type=jnp.float32)
    query_grad = query_grad + jnp.einsum(
        "hir,rd->ihd", band_grad, rel_key, preferred_element_type=jnp.float32
    )
    key_grad = jnp.einsum("hij,ihd->jhd", score_low, query_rows, preferred_element_type=jnp.float32)
    rel_key_grad = jnp.einsum(
        "hir,ihd->rd", band_grad, query_rows, preferred_element_type=jnp.float32
    )
    project_low = jnp.concatenate(
        [query_grad.reshape(length, D), key_grad.reshape(length, D), value_grad.reshape(length, D)],
        axis=1,
    ).astype(jnp.bfloat16)
    qkv_grad = inner_rows(embed_low, project_low)
    embed_grad = (mixed_grad + matmul_nt(project_low, w_qkv)) * text_mask * math.sqrt(D)
    table_grad = lax.dot_general(
        one_hot_rows(token_rows).astype(jnp.float32),
        embed_grad,
        (((0,), (0,)), ((), ())),
        precision=lax.Precision.HIGHEST,
    )
    return (
        table_grad,
        qkv_grad,
        rel_key_grad,
        rel_value_grad,
        out_grad,
        attn_gain_grad,
        attn_shift_grad,
        ff1_grad,
        ff2_grad,
        ffn_gain_grad,
        ffn_shift_grad,
        prior_wgrad,
    )


def decode(pairs_in, durations_row, prior_rows, act_center, act_scale, dec_w, grad_unit):
    w_mix, w_start, w_in, w_res, w_skip_last, w_end = dec_w
    pair_total = pairs_in.shape[0]
    frame_total = 2 * pair_total
    end_pos = jnp.cumsum(durations_row)
    starts = end_pos - durations_row
    positions = lax.iota(jnp.int32, frame_total)
    pair_mask = (lax.iota(jnp.int32, pair_total) < end_pos[-1] // 2).astype(jnp.float32)[:, None]
    align_table = (
        (positions[:, None] >= starts[None, :]) & (positions[:, None] < end_pos[None, :])
    ).astype(jnp.float32)
    expanded = jnp.dot(align_table, prior_rows, precision=lax.Precision.HIGHEST)
    mean_rows = pair_up(expanded[:, :MEL])
    log_scales = pair_up(expanded[:, MEL:])
    normalized = (pairs_in - act_center) * act_scale * pair_mask
    grouped = to_groups(normalized)
    turned = from_groups(jnp.einsum("fgj,ij->fgi", grouped, w_mix, precision=lax.Precision.HIGHEST))
    passive = turned[:, :MEL]
    active = turned[:, MEL:]
    passive_low = passive.astype(jnp.bfloat16)
    hidden = matmul(passive_low, w_start) * pair_mask
    hidden_low = []
    gates_pre = []
    gated_low = []
    skipped = jnp.zeros((pair_total, HID), jnp.float32)
    for block_index in range(WLAYERS):
        hidden_low.append(hidden.astype(jnp.bfloat16))
        pre_gate = matmul(unfold(hidden_low[-1], WKER), w_in[block_index])
        gated_out = gate_units(pre_gate).astype(jnp.bfloat16)
        gates_pre.append(pre_gate)
        gated_low.append(gated_out)
        if block_index < WLAYERS - 1:
            both_parts = matmul(gated_out, w_res[block_index])
            hidden = (hidden + both_parts[:, :HID]) * pair_mask
            skipped = skipped + both_parts[:, HID:]
        else:
            skipped = skipped + matmul(gated_out, w_skip_last)
    output_low = (skipped * pair_mask).astype(jnp.bfloat16)
    coupled = matmul(output_low, w_end) * pair_mask
    shift_part = coupled[:, :MEL]
    log_part = coupled[:, MEL:]
    growth = jnp.exp(log_part)
    moved_half = (shift_part + growth * active) * pair_mask
    latent = jnp.concatenate([passive, moved_half], axis=1)
    inverse_var = jnp.exp(-2.0 * log_scales)
    latent_gap = latent - mean_rows
    neg_loglik = jnp.sum(pair_mask * (log_scales + 0.5 * inverse_var * latent_gap * latent_gap))
    neg_loglik = neg_loglik - jnp.sum(log_part * pair_mask)
    latent_grad = grad_unit * pair_mask * inverse_var * latent_gap
    frame_prior_grad = jnp.concatenate(
        [
            pair_open(-latent_grad),
            pair_open(grad_unit * pair_mask * (1.0 - inverse_var * latent_gap * latent_gap)),
        ],
        axis=1,
    )
    prior_grad = lax.dot_general(
        align_table, frame_prior_grad, (((0,), (0,)), ((), ())), precision=lax.Precision.HIGHEST
    )
    moved_grad = latent_grad[:, MEL:]
    coupled_low = jnp.concatenate(
        [moved_grad * pair_mask, (moved_grad * growth * active - grad_unit) * pair_mask], axis=1
    ).astype(jnp.bfloat16)
    active_grad = moved_grad * pair_mask * growth
    end_grad = inner_rows(output_low, coupled_low)
    skip_grad = matmul_nt(coupled_low, w_end) * pair_mask
    hidden_grad = jnp.zeros((pair_total, HID), jnp.float32)
    in_grads = [None] * WLAYERS
    res_grads = [None] * (WLAYERS - 1)
    last_grad = None
    for block_index in reversed(range(WLAYERS)):
        if block_index == WLAYERS - 1:
            part_low = skip_grad.astype(jnp.bfloat16)
            last_grad = inner_rows(gated_low[block_index], part_low)
            gated_grad = matmul_nt(part_low, w_skip_last)
        else:
            part_low = jnp.concatenate([hidden_grad * pair_mask, skip_grad], axis=1).astype(
                jnp.bfloat16
            )
            res_grads[block_index] = inner_rows(gated_low[block_index], part_low)
            gated_grad = matmul_nt(part_low, w_res[block_index])
            hidden_grad = hidden_grad * pair_mask
        _, gate_back = jax.vjp(gate_units, gates_pre[block_index])
        pre_low = gate_back(gated_grad)[0].astype(jnp.bfloat16)
        in_grads[block_index] = inner_rows(unfold(hidden_low[block_index], WKER), pre_low)
        hidden_grad = hidden_grad + fold(matmul_nt(pre_low, w_in[block_index]), WKER, HID)
    start_low = (hidden_grad * pair_mask).astype(jnp.bfloat16)
    start_grad = inner_rows(passive_low, start_low)
    passive_grad = latent_grad[:, :MEL] + matmul_nt(start_low, w_start)
    grouped_grad = to_groups(jnp.concatenate([passive_grad, active_grad], axis=1))
    mix_grad = jnp.einsum("fgi,fgj->ij", grouped_grad, grouped, precision=lax.Precision.HIGHEST)
    normal_grad = (
        from_groups(jnp.einsum("fgi,ij->fgj", grouped_grad, w_mix, precision=lax.Precision.HIGHEST))
        * pair_mask
    )
    dec_grads = (
        mix_grad,
        start_grad,
        jnp.stack(in_grads),
        jnp.stack(res_grads),
        last_grad,
        end_grad,
    )
    part_one = jnp.sum(normal_grad, axis=0)
    part_two = jnp.sum(normal_grad * normalized, axis=0)
    return (neg_loglik, prior_grad, dec_grads, normal_grad, part_one, part_two)


def on_device(
    token_ids,
    durations,
    mel_frames,
    embedding,
    w_qkv,
    rel_key,
    rel_value,
    w_out,
    attn_gain,
    attn_shift,
    w_ff1,
    w_ff2,
    ffn_gain,
    ffn_shift,
    w_prior,
    w_mix,
    w_start,
    w_in,
    w_res,
    w_skip_last,
    w_end,
):
    enc_w = (
        embedding,
        w_qkv,
        rel_key,
        rel_value,
        w_out,
        attn_gain,
        attn_shift,
        w_ff1,
        w_ff2,
        ffn_gain,
        ffn_shift,
        w_prior,
    )
    dec_w = (w_mix, w_start, w_in, w_res, w_skip_last, w_end)
    mel_pairs = jax.vmap(pair_up)(mel_frames)
    end_pos = jnp.cumsum(durations, axis=1)
    pair_lengths = end_pos[:, -1] // 2
    pair_mask = (lax.iota(jnp.int32, mel_pairs.shape[1])[None, :] < pair_lengths[:, None]).astype(
        jnp.float32
    )[:, :, None]
    local_count = jnp.sum(pair_lengths).astype(jnp.float32)
    first_sums, square_sums, pairs_total_count = lax.psum(
        (
            jnp.sum(mel_pairs * pair_mask, axis=(0, 1)),
            jnp.sum(mel_pairs * mel_pairs * pair_mask, axis=(0, 1)),
            local_count,
        ),
        "dp",
    )
    act_center = first_sums / pairs_total_count
    variance = square_sums / pairs_total_count - act_center * act_center
    log_act = -0.5 * jnp.log(variance + 1e-06)
    act_scale = jnp.exp(log_act)
    grad_unit = 1.0 / (2 * MEL * pairs_total_count)
    inverse_mix, mix_det = invert_small(w_mix)
    mix_extra = -(MEL // 2) * grad_unit * local_count * inverse_mix.T
    enc_zero = jax.tree.map(lambda array_in: jnp.zeros(array_in.shape, jnp.float32), enc_w)
    dec_zero = jax.tree.map(lambda array_in: jnp.zeros(array_in.shape, jnp.float32), dec_w)
    scalar_zero = jnp.zeros((), jnp.float32)
    channel_zero = jnp.zeros((2 * MEL,), jnp.float32)

    def item_step(carried, item_data):
        enc_acc, dec_acc, nll_acc, one_acc, two_acc = carried
        token_rows, durations_row, pairs_in = item_data
        prior_rows, saved_state = encode(token_rows, durations_row, enc_w)
        neg_loglik, prior_grad, dec_grads, normal_grad, part_one, part_two = decode(
            pairs_in, durations_row, prior_rows, act_center, act_scale, dec_w, grad_unit
        )
        enc_grads = encode_back(token_rows, durations_row, saved_state, prior_grad, enc_w)
        carried = (
            jax.tree.map(jnp.add, enc_acc, enc_grads),
            jax.tree.map(jnp.add, dec_acc, dec_grads),
            nll_acc + neg_loglik,
            one_acc + part_one,
            two_acc + part_two,
        )
        return (carried, normal_grad)

    carried, normal_grads = lax.scan(
        item_step,
        (enc_zero, dec_zero, scalar_zero, channel_zero, channel_zero),
        (token_ids, durations, mel_pairs),
    )
    enc_acc, dec_acc, nll_acc, one_acc, two_acc = carried
    sums_one = one_acc
    sums_two = two_acc
    sums_one, sums_two = lax.psum((sums_one, sums_two), "dp")
    log_grad = sums_two - grad_unit * pairs_total_count
    var_grad = -0.5 * log_grad / (variance + 1e-06)
    center_grad = -act_scale * sums_one - 2.0 * act_center * var_grad
    input_grad = pair_mask * (
        normal_grads * act_scale + (2.0 * mel_pairs * var_grad + center_grad) / pairs_total_count
    )
    mel_grad = jax.vmap(pair_open)(input_grad) * (2 * MEL * pairs_total_count)
    summed_all = lax.psum(
        (
            enc_acc[0],
            enc_acc[1],
            enc_acc[2],
            enc_acc[3],
            enc_acc[4],
            enc_acc[5],
            enc_acc[6],
            enc_acc[7],
            enc_acc[8],
            enc_acc[9],
            enc_acc[10],
            enc_acc[11],
            dec_acc[0] + mix_extra,
            dec_acc[1],
            dec_acc[2],
            dec_acc[3],
            dec_acc[4],
            dec_acc[5],
            nll_acc,
        ),
        "dp",
    )
    enc_total = summed_all[:12]
    dec_total = summed_all[12:18]
    nll_total = summed_all[18]
    loss_value = (
        nll_total
        - pairs_total_count * jnp.sum(log_act)
        - pairs_total_count * (MEL // 2) * jnp.log(mix_det)
    ) * grad_unit
    loss_value = loss_value + 0.5 * math.log(2.0 * math.pi)
    return (
        loss_value,
        mel_grad,
        enc_total[0],
        enc_total[1],
        enc_total[2],
        enc_total[3],
        enc_total[4],
        enc_total[5],
        enc_total[6],
        enc_total[7],
        enc_total[8],
        enc_total[9],
        enc_total[10],
        enc_total[11],
        dec_total[0],
        dec_total[1],
        dec_total[2],
        dec_total[3],
        dec_total[4],
        dec_total[5],
    )


def solution(mesh):
    placed = (
        P("dp", None),
        P("dp", None),
        P("dp", None, None),
        P(),
        P(),
        P(),
        P(),
        P(),
        P(),
        P(),
        P(),
        P(),
        P(),
        P(),
        P(),
        P(),
        P(),
        P(),
        P(),
        P(),
        P(),
    )
    return jax.shard_map(
        on_device,
        mesh=mesh,
        in_specs=placed,
        out_specs=(
            P(),
            P("dp", None, None),
            P(),
            P(),
            P(),
            P(),
            P(),
            P(),
            P(),
            P(),
            P(),
            P(),
            P(),
            P(),
            P(),
            P(),
            P(),
            P(),
            P(),
            P(),
        ),
        check_vma=False,
    )
```

profile of v0, /device:TPU:0, one launch (start us, length us, event | category | flops | bytes accessed | tf_op | source)
XLA Modules:
  0.0 855.6 jit_solution(6220911057161468836)
XLA Ops:
  13.2 2.2 copy.223
  15.4 4.2 multiply_reduce_fusion.10
  20.2 42.0 %all-reduce.21 = (f32[]{:T(128)}, f32[160]{0:T(256)S(1)}, f32[160]{0:T(256)S(1)}) all-reduce(f32[]{:T(128)S(6)} %convert_element_type.298, f32[160]{0:T(256)S(1)} %reduce_sum.304, f32[160]{0:T(256)S(1)} %reduce_sum.306), channel_id=1, replica_groups=mesh['dp'=32] {'dp'}, use_global_device_ids=true, to_apply=%region_5.6 | all-reduce | flops 321 | bytes 2568 | tf_op jit(solution)/shard_map/psum | solution.py:470
  64.8 527.9 %while.59 = (s32[]{:T(128)}, f32[148,192]{1,0:T(8,128)}, f32[192,576]{1,0:T(8,128)}, f32[9,96]{1,0:T(8,128)}, f32[9,96]{1,0:T(8,128)}, /*index=5*/f32[192,192]{1...) while((s32[]{:T(128)}, f32[148,192]{1,0:T(8,128)}, ...), condition=%wide.region_30.31_spmd.clone, body=%wide.region_8.30_spmd.clone.sunk | while | flops 8470547456 | bytes 389395104 | solution.py:507
  75.2 2.1 fusion.633
  82.6 2.3 dynamic-slice_reduce_fusion.2
  89.7 2.1 fusion.653
  104.1 2.8 multiply_convert_fusion.29
  114.4 2.8 negate_bitcast_fusion.2
  117.2 2.0 copy.301
  119.2 2.0 copy.308
  133.6 2.1 copy.302
  135.7 2.7 fusion.677
  160.5 3.0 multiply_reduce_fusion.21
  167.5 7.5 dynamic_update_slice.9
  181.9 2.1 fusion.683
  204.2 2.1 fusion.633
  211.5 2.3 dynamic-slice_reduce_fusion.2
  218.6 2.1 fusion.653
  232.8 2.8 multiply_convert_fusion.29
  243.1 2.8 negate_bitcast_fusion.2
  246.0 2.0 copy.301
  248.0 2.0 copy.308
  258.6 1.9 convolution_add_fusion.32
  263.4 2.1 copy.302
  265.5 2.7 fusion.677
  270.0 3.3 convolution_add_fusion.28
  283.8 2.3 maximum_add_fusion.5
  292.3 3.0 multiply_reduce_fusion.21
  299.3 7.7 dynamic_update_slice.9
  313.9 2.1 fusion.683
  335.9 2.1 fusion.633
  343.3 2.3 dynamic-slice_reduce_fusion.2
  350.4 2.1 fusion.653
  364.6 2.8 multiply_convert_fusion.29
  374.9 2.8 negate_bitcast_fusion.2
  377.7 2.0 copy.301
  379.8 2.0 copy.308
  395.2 2.1 copy.302
  397.3 2.7 fusion.677
  401.8 3.3 convolution_add_fusion.28
  415.8 2.3 maximum_add_fusion.5
  424.3 3.0 multiply_reduce_fusion.21
  431.2 7.5 dynamic_update_slice.9
  445.6 2.1 fusion.683
  467.7 2.1 fusion.633
  475.1 2.3 dynamic-slice_reduce_fusion.2
  482.2 2.1 fusion.653
  496.6 2.8 multiply_convert_fusion.29
  506.9 2.8 negate_bitcast_fusion.2
  509.7 2.0 copy.301
  511.7 2.0 copy.308
  527.2 2.1 copy.302
  529.3 2.7 fusion.677
  533.8 3.3 convolution_add_fusion.28
  547.5 2.3 maximum_add_fusion.5
  556.0 3.0 multiply_reduce_fusion.21
  563.0 7.5 dynamic_update_slice.9
  577.4 2.1 fusion.683
  600.4 44.0 %all-reduce.27 = (f32[]{:T(128)}, f32[160]{0:T(256)S(1)}, f32[160]{0:T(256)S(1)}, f32[9,96]{1,0:T(8,128)}, f32[9,96]{1,0:T(8,128)}, /*index=5*/f32[192]{0:T(256)...) all-reduce(f32[]{:T(128)} %get-tuple-element.2086, ...), channel_id=1, replica_groups=mesh['dp'=32] {'dp'}, use_global_device_ids=true, to_apply=%region_31.32 | all-reduce | flops 18193 | bytes 145544 | tf_op jit(solution)/shard_map/psum | solution.py:523
  650.3 3.4 multiply_multiply_fusion.10
  656.7 175.5 %all-reduce.26.cloned.1.call-done = (f32[148,192]{1,0:T(8,128)}, f32[192,576]{1,0:T(8,128)}, f32[192,192]{1,0:T(8,128)}, f32[576,768]{1,0:T(8,128)}, f32[2304,19...) async-done(((f32[148,192]{1,0:T(8,128)}, f32[192,576]{1,0:T(8,128)}, ...) | async-done | bytes 11418640 | tf_op jit(solution)/shard_map/psum | solution.py:523
  837.4 2.9 copy.430
  842.3 2.6 copy.433
  (1943 shorter events, 372.2 us)
Async XLA Ops:
  7.2 825.0 %all-reduce.26.cloned.1.call-start = ((), (), s32[]{:S(2)}) async-start(), calls=%async_computation | async-start | bytes 23379968 | tf_op jit(solution)/shard_map/psum | solution.py:523
  15.4 49.4 %copy-start.94 = (bf16[9,96]{1,0:T(8,128)(2,1)S(1)}, bf16[9,96]{1,0:T(8,128)(2,1)}, u32[]{:S(2)}) copy-start(bf16[9,96]{1,0:T(8,128)(2,1)} %param.36) | copy-start | bytes 5188
  15.4 49.4 %copy-start.96 = (bf16[9,96]{1,0:T(8,128)(2,1)S(1)}, bf16[9,96]{1,0:T(8,128)(2,1)}, u32[]{:S(2)}) copy-start(bf16[9,96]{1,0:T(8,128)(2,1)} %param.37) | copy-start | bytes 5188
  15.4 49.4 %copy-start.114 = (f32[192]{0:T(256)S(1)}, f32[192]{0:T(256)}, u32[]{:S(2)}) copy-start(f32[192]{0:T(256)} %param.39) | copy-start | bytes 2308
  65.1 7.1 copy-start.131
  65.1 13.1 %copy-start.160 = (s32[9]{0:T(128)}, s32[9]{0:T(128)S(1)}, u32[]{:S(2)}) copy-start(s32[9]{0:T(128)S(1)} %iota_add_fusion.2) | copy-start | bytes 112 | tf_op jit(solution)/shard_map/while
  65.8 11.5 %copy-start.108 = (s32[1,256]{1,0:T(1,128)}, s32[1,256]{1,0:T(1,128)S(1)}, u32[]{:S(2)}) copy-start(s32[1,256]{1,0:T(1,128)S(1)} %constant_dynamic-slice_fusion.4) | copy-start | bytes 3076 | tf_op jit(solution)/shard_map/while
  72.2 12.8 %copy-start.83 = (f32[2,40,2]{2,0,1:T(2,128)}, f32[2,40,2]{2,0,1:T(2,128)S(1)}, u32[]{:S(2)}) copy-start(f32[2,40,2]{2,0,1:T(2,128)S(1)} %copy.297) | copy-start | bytes 1924 | tf_op jit(solution)/shard_map/while
  80.9 26.2 %copy-start.98 = (f32[256]{0:T(256)}, f32[256]{0:T(256)S(1)}, u32[]{:S(2)}) copy-start(f32[256]{0:T(256)S(1)} %fusion.639) | copy-start | bytes 3076 | tf_op jit(solution)/shard_map/while
  81.7 22.3 %copy-start.42 = (bf16[256,192]{0,1:T(8,128)(2,1)}, bf16[256,192]{0,1:T(8,128)(2,1)S(1)}, u32[]{:S(2)}) copy-start(bf16[256,192]{0,1:T(8,128)(2,1)S(1)} %multiply_convert_fusion.28) | copy-start | bytes 294916 | tf_op jit(solution)/shard_map/while
  114.4 8.7 %copy-start.18 = (f32[512,80]{0,1:T(8,128)S(1)}, f32[512,80]{0,1:T(8,128)}, u32[]{:S(2)}) copy-start(f32[512,80]{0,1:T(8,128)} %copy-done.17) | copy-start | bytes 491524 | tf_op jit(solution)/shard_map/while
  114.4 8.7 %copy-start.20 = (f32[512,80]{0,1:T(8,128)S(1)}, f32[512,80]{0,1:T(8,128)}, u32[]{:S(2)}) copy-start(f32[512,80]{0,1:T(8,128)} %copy-done.19) | copy-start | bytes 491524 | tf_op jit(solution)/shard_map/while
  164.0 11.0 %copy-start.41 = (bf16[2304,192]{0,1:T(8,128)(2,1)S(1)}, bf16[2304,192]{0,1:T(8,128)(2,1)}, u32[]{:S(2)}) copy-start(bf16[2304,192]{0,1:T(8,128)(2,1)} %get-tuple-element.1892) | copy-start | bytes 2654212 | tf_op jit(solution)/shard_map/while
  165.6 9.9 %copy-start.127 = (f32[4,4]{1,0:T(4,128)}, f32[4,4]{1,0:T(4,128)S(1)}, u32[]{:S(2)}) copy-start(f32[4,4]{1,0:T(4,128)S(1)} %fusion.704) | copy-start | bytes 196 | tf_op jit(solution)/shard_map/while
  165.8 9.2 %copy-start.139 = (f32[160]{0:T(256)}, f32[160]{0:T(256)S(1)}, u32[]{:S(2)}) copy-start(f32[160]{0:T(256)S(1)} %get-tuple-element.1878) | copy-start | bytes 1924 | tf_op jit(solution)/shard_map/while
  165.8 9.7 %copy-start.136 = (f32[160]{0:T(256)}, f32[160]{0:T(256)S(1)}, u32[]{:S(2)}) copy-start(f32[160]{0:T(256)S(1)} %get-tuple-element.1879) | copy-start | bytes 1924 | tf_op jit(solution)/shard_map/while
  194.0 7.1 copy-start.131
  194.1 13.1 %copy-start.160 = (s32[9]{0:T(128)}, s32[9]{0:T(128)S(1)}, u32[]{:S(2)}) copy-start(s32[9]{0:T(128)S(1)} %iota_add_fusion.2) | copy-start | bytes 112 | tf_op jit(solution)/shard_map/while
  194.8 11.5 %copy-start.108 = (s32[1,256]{1,0:T(1,128)}, s32[1,256]{1,0:T(1,128)S(1)}, u32[]{:S(2)}) copy-start(s32[1,256]{1,0:T(1,128)S(1)} %constant_dynamic-slice_fusion.4) | copy-start | bytes 3076 | tf_op jit(solution)/shard_map/while
  201.2 12.8 %copy-start.83 = (f32[2,40,2]{2,0,1:T(2,128)}, f32[2,40,2]{2,0,1:T(2,128)S(1)}, u32[]{:S(2)}) copy-start(f32[2,40,2]{2,0,1:T(2,128)S(1)} %copy.297) | copy-start | bytes 1924 | tf_op jit(solution)/shard_map/while
  209.9 25.9 %copy-start.98 = (f32[256]{0:T(256)}, f32[256]{0:T(256)S(1)}, u32[]{:S(2)}) copy-start(f32[256]{0:T(256)S(1)} %fusion.639) | copy-start | bytes 3076 | tf_op jit(solution)/shard_map/while
  210.7 22.1 %copy-start.42 = (bf16[256,192]{0,1:T(8,128)(2,1)}, bf16[256,192]{0,1:T(8,128)(2,1)S(1)}, u32[]{:S(2)}) copy-start(bf16[256,192]{0,1:T(8,128)(2,1)S(1)} %multiply_convert_fusion.28) | copy-start | bytes 294916 | tf_op jit(solution)/shard_map/while
  243.1 8.7 %copy-start.18 = (f32[512,80]{0,1:T(8,128)S(1)}, f32[512,80]{0,1:T(8,128)}, u32[]{:S(2)}) copy-start(f32[512,80]{0,1:T(8,128)} %copy-done.17) | copy-start | bytes 491524 | tf_op jit(solution)/shard_map/while
  243.1 8.7 %copy-start.20 = (f32[512,80]{0,1:T(8,128)S(1)}, f32[512,80]{0,1:T(8,128)}, u32[]{:S(2)}) copy-start(f32[512,80]{0,1:T(8,128)} %copy-done.19) | copy-start | bytes 491524 | tf_op jit(solution)/shard_map/while
  253.0 7.6 copy-start.52
  295.8 11.2 %copy-start.41 = (bf16[2304,192]{0,1:T(8,128)(2,1)S(1)}, bf16[2304,192]{0,1:T(8,128)(2,1)}, u32[]{:S(2)}) copy-start(bf16[2304,192]{0,1:T(8,128)(2,1)} %get-tuple-element.1892) | copy-start | bytes 2654212 | tf_op jit(solution)/shard_map/while
  297.4 10.1 %copy-start.127 = (f32[4,4]{1,0:T(4,128)}, f32[4,4]{1,0:T(4,128)S(1)}, u32[]{:S(2)}) copy-start(f32[4,4]{1,0:T(4,128)S(1)} %fusion.704) | copy-start | bytes 196 | tf_op jit(solution)/shard_map/while
  297.6 9.4 %copy-start.139 = (f32[160]{0:T(256)}, f32[160]{0:T(256)S(1)}, u32[]{:S(2)}) copy-start(f32[160]{0:T(256)S(1)} %get-tuple-element.1878) | copy-start | bytes 1924 | tf_op jit(solution)/shard_map/while
  297.6 9.9 %copy-start.136 = (f32[160]{0:T(256)}, f32[160]{0:T(256)S(1)}, u32[]{:S(2)}) copy-start(f32[160]{0:T(256)S(1)} %get-tuple-element.1879) | copy-start | bytes 1924 | tf_op jit(solution)/shard_map/while
  325.8 7.1 copy-start.131
  325.8 13.1 %copy-start.160 = (s32[9]{0:T(128)}, s32[9]{0:T(128)S(1)}, u32[]{:S(2)}) copy-start(s32[9]{0:T(128)S(1)} %iota_add_fusion.2) | copy-start | bytes 112 | tf_op jit(solution)/shard_map/while
  326.5 11.5 %copy-start.108 = (s32[1,256]{1,0:T(1,128)}, s32[1,256]{1,0:T(1,128)S(1)}, u32[]{:S(2)}) copy-start(s32[1,256]{1,0:T(1,128)S(1)} %constant_dynamic-slice_fusion.4) | copy-start | bytes 3076 | tf_op jit(solution)/shard_map/while
  332.9 12.8 %copy-start.83 = (f32[2,40,2]{2,0,1:T(2,128)}, f32[2,40,2]{2,0,1:T(2,128)S(1)}, u32[]{:S(2)}) copy-start(f32[2,40,2]{2,0,1:T(2,128)S(1)} %copy.297) | copy-start | bytes 1924 | tf_op jit(solution)/shard_map/while
  341.6 26.0 %copy-start.98 = (f32[256]{0:T(256)}, f32[256]{0:T(256)S(1)}, u32[]{:S(2)}) copy-start(f32[256]{0:T(256)S(1)} %fusion.639) | copy-start | bytes 3076 | tf_op jit(solution)/shard_map/while
  342.5 22.1 %copy-start.42 = (bf16[256,192]{0,1:T(8,128)(2,1)}, bf16[256,192]{0,1:T(8,128)(2,1)S(1)}, u32[]{:S(2)}) copy-start(bf16[256,192]{0,1:T(8,128)(2,1)S(1)} %multiply_convert_fusion.28) | copy-start | bytes 294916 | tf_op jit(solution)/shard_map/while
  374.9 8.7 %copy-start.18 = (f32[512,80]{0,1:T(8,128)S(1)}, f32[512,80]{0,1:T(8,128)}, u32[]{:S(2)}) copy-start(f32[512,80]{0,1:T(8,128)} %copy-done.17) | copy-start | bytes 491524 | tf_op jit(solution)/shard_map/while
  374.9 8.7 %copy-start.20 = (f32[512,80]{0,1:T(8,128)S(1)}, f32[512,80]{0,1:T(8,128)}, u32[]{:S(2)}) copy-start(f32[512,80]{0,1:T(8,128)} %copy-done.19) | copy-start | bytes 491524 | tf_op jit(solution)/shard_map/while
  384.7 7.6 copy-start.52
  427.8 11.0 %copy-start.41 = (bf16[2304,192]{0,1:T(8,128)(2,1)S(1)}, bf16[2304,192]{0,1:T(8,128)(2,1)}, u32[]{:S(2)}) copy-start(bf16[2304,192]{0,1:T(8,128)(2,1)} %get-tuple-element.1892) | copy-start | bytes 2654212 | tf_op jit(solution)/shard_map/while
  429.4 9.9 %copy-start.127 = (f32[4,4]{1,0:T(4,128)}, f32[4,4]{1,0:T(4,128)S(1)}, u32[]{:S(2)}) copy-start(f32[4,4]{1,0:T(4,128)S(1)} %fusion.704) | copy-start | bytes 196 | tf_op jit(solution)/shard_map/while
  429.6 9.1 %copy-start.139 = (f32[160]{0:T(256)}, f32[160]{0:T(256)S(1)}, u32[]{:S(2)}) copy-start(f32[160]{0:T(256)S(1)} %get-tuple-element.1878) | copy-start | bytes 1924 | tf_op jit(solution)/shard_map/while
  429.6 9.7 %copy-start.136 = (f32[160]{0:T(256)}, f32[160]{0:T(256)S(1)}, u32[]{:S(2)}) copy-start(f32[160]{0:T(256)S(1)} %get-tuple-element.1879) | copy-start | bytes 1924 | tf_op jit(solution)/shard_map/while
  457.6 7.1 copy-start.131
  457.6 13.1 %copy-start.160 = (s32[9]{0:T(128)}, s32[9]{0:T(128)S(1)}, u32[]{:S(2)}) copy-start(s32[9]{0:T(128)S(1)} %iota_add_fusion.2) | copy-start | bytes 112 | tf_op jit(solution)/shard_map/while
  458.3 11.5 %copy-start.108 = (s32[1,256]{1,0:T(1,128)}, s32[1,256]{1,0:T(1,128)S(1)}, u32[]{:S(2)}) copy-start(s32[1,256]{1,0:T(1,128)S(1)} %constant_dynamic-slice_fusion.4) | copy-start | bytes 3076 | tf_op jit(solution)/shard_map/while
  464.7 12.8 %copy-start.83 = (f32[2,40,2]{2,0,1:T(2,128)}, f32[2,40,2]{2,0,1:T(2,128)S(1)}, u32[]{:S(2)}) copy-start(f32[2,40,2]{2,0,1:T(2,128)S(1)} %copy.297) | copy-start | bytes 1924 | tf_op jit(solution)/shard_map/while
  473.4 26.2 %copy-start.98 = (f32[256]{0:T(256)}, f32[256]{0:T(256)S(1)}, u32[]{:S(2)}) copy-start(f32[256]{0:T(256)S(1)} %fusion.639) | copy-start | bytes 3076 | tf_op jit(solution)/shard_map/while
  474.2 22.3 %copy-start.42 = (bf16[256,192]{0,1:T(8,128)(2,1)}, bf16[256,192]{0,1:T(8,128)(2,1)S(1)}, u32[]{:S(2)}) copy-start(bf16[256,192]{0,1:T(8,128)(2,1)S(1)} %multiply_convert_fusion.28) | copy-start | bytes 294916 | tf_op jit(solution)/shard_map/while
  506.9 8.7 %copy-start.18 = (f32[512,80]{0,1:T(8,128)S(1)}, f32[512,80]{0,1:T(8,128)}, u32[]{:S(2)}) copy-start(f32[512,80]{0,1:T(8,128)} %copy-done.17) | copy-start | bytes 491524 | tf_op jit(solution)/shard_map/while
  506.9 8.7 %copy-start.20 = (f32[512,80]{0,1:T(8,128)S(1)}, f32[512,80]{0,1:T(8,128)}, u32[]{:S(2)}) copy-start(f32[512,80]{0,1:T(8,128)} %copy-done.19) | copy-start | bytes 491524 | tf_op jit(solution)/shard_map/while
  516.7 7.6 copy-start.52
  559.5 11.0 %copy-start.41 = (bf16[2304,192]{0,1:T(8,128)(2,1)S(1)}, bf16[2304,192]{0,1:T(8,128)(2,1)}, u32[]{:S(2)}) copy-start(bf16[2304,192]{0,1:T(8,128)(2,1)} %get-tuple-element.1892) | copy-start | bytes 2654212 | tf_op jit(solution)/shard_map/while
  561.2 9.9 %copy-start.127 = (f32[4,4]{1,0:T(4,128)}, f32[4,4]{1,0:T(4,128)S(1)}, u32[]{:S(2)}) copy-start(f32[4,4]{1,0:T(4,128)S(1)} %fusion.704) | copy-start | bytes 196 | tf_op jit(solution)/shard_map/while
  561.4 9.2 %copy-start.139 = (f32[160]{0:T(256)}, f32[160]{0:T(256)S(1)}, u32[]{:S(2)}) copy-start(f32[160]{0:T(256)S(1)} %get-tuple-element.1878) | copy-start | bytes 1924 | tf_op jit(solution)/shard_map/while
  561.4 9.7 %copy-start.136 = (f32[160]{0:T(256)}, f32[160]{0:T(256)S(1)}, u32[]{:S(2)}) copy-start(f32[160]{0:T(256)S(1)} %get-tuple-element.1879) | copy-start | bytes 1924 | tf_op jit(solution)/shard_map/while
  593.3 7.1 copy-start.105
  593.3 7.1 copy-start.137
  593.3 7.1 copy-start.140
  593.3 7.1 copy-start.143
  593.4 56.9 %copy-start.157 = (f32[160]{0:T(256)S(1)}, f32[160]{0:T(256)}, u32[]{:S(2)}) copy-start(f32[160]{0:T(256)} %copy-done.156) | copy-start | bytes 1924
  593.4 56.9 %copy-start.134 = (f32[160]{0:T(256)S(1)}, f32[160]{0:T(256)}, u32[]{:S(2)}) copy-start(f32[160]{0:T(256)} %copy-done.133) | copy-start | bytes 1924
  593.4 57.0 %copy-start.62 = (f32[4,512,160]{1,0,2:T(4,128)S(1)}, f32[4,512,160]{1,0,2:T(4,128)}, u32[]{:S(2)}) copy-start(f32[4,512,160]{1,0,2:T(4,128)} %get-tuple-element.2105) | copy-start | bytes 3932164
  593.4 57.0 %copy-start.130 = (f32[4,512]{1,0:T(4,128)S(1)}, f32[4,512]{1,0:T(4,128)}, u32[]{:S(2)}) copy-start(f32[4,512]{1,0:T(4,128)} %copy-done.129) | copy-start | bytes 24580
  833.8 7.8 copy-start.121
  (509 other events, 1278.6 us)
Sparse Core Ops, SparseCore 0:
  593.5 238.6 all-reduce.25
where the time goes:
time: 865 us; the launch traced here: 856 us
  matrix products  239 us (28%)
  local copies, waits for them, and re-layouts  223 us (26%)
  waiting for transfers between devices  176 us (20%)
  blocking collectives  86 us (10%)
  other arithmetic  78.6 us (9%)
  loops' own time  30 us (3%)
  between operations  23.5 us (3%)
    psum x1, waiting for transfers between devices, on_device(): lax.psum((enc_acc[0], enc_acc[1], enc_acc[2], enc_acc[3], enc_acc[4], enc...  175 us
    while x1156, local copies, waits for them, and re-layouts  60.8 us
    dot_general x64, matrix products, matmul(): return jnp.dot(first_op, second_op, preferred_element_type=jnp.float32)  59.9 us
    dot_general x60, matrix products, inner_rows(): lax.dot_general(first_op, second_op, (((0,), (0,)), ((), ())), preferred_...  51.7 us
    psum x1, blocking collectives, on_device(): lax.psum((enc_acc[0], enc_acc[1], enc_acc[2], enc_acc[3], enc_acc[4], enc...  44 us
    dot_general x60, matrix products, matmul_nt(): lax.dot_general(first_op, second_op, (((1,), (1,)), ((), ())), preferred_...  43.8 us
    psum x1, blocking collectives, on_device(): lax.psum((jnp.sum(mel_pairs * pair_mask, axis=(0, 1)), jnp.sum(mel_pairs...  42 us
    dynamic_update_slice x8, local copies, waits for them, and re-layouts, on_device(): lax.scan(item_step, (enc_zero, dec_zero, scalar_zero, channel_zero, chann...  31.6 us
  transfers between devices with their start and end apart: 1, of which 1 were waited for; matrix products, arithmetic and copies ran while one was open for 1% of the time, Pallas kernels for 0%

commit v1 on v0

v1 whole, which is shorter than its diff:
```python
import functools
import math

import jax
import jax.numpy as jnp
from jax import lax
from jax.experimental import pallas as pl
from jax.experimental.pallas import tpu as pltpu
from jax.sharding import PartitionSpec as P

D = 192
HEADS = 2
HEAD = 96
LANES = 128
FILTER = 768
MEL = 80
HID = 192
VOCAB = 148
KSIZE = 3
WKER = 5
WLAYERS = 4
WINDOW = 4
PERIOD = 16

F32 = jnp.float32
BF16 = jnp.bfloat16
HIGH = lax.Precision.HIGHEST
VMEM_BYTES = 58 * 1024 * 1024


def contract(first_op, second_op, dims, precision=None):
    return lax.dot_general(
        first_op, second_op, (dims, ((), ())), preferred_element_type=F32, precision=precision
    )


def dot_nn(first_op, second_op, precision=None):
    return contract(first_op, second_op, ((1,), (0,)), precision)


def dot_nt(first_op, second_op, precision=None):
    return contract(first_op, second_op, ((1,), (1,)), precision)


def dot_tn(first_op, second_op, precision=None):
    return contract(first_op, second_op, ((0,), (0,)), precision)


def halves(values):
    high = values.astype(BF16)
    low = (values - high.astype(F32)).astype(BF16)
    return high, low


def iota(shape, axis):
    return lax.broadcasted_iota(jnp.int32, shape, axis)


def rows_of(length):
    return iota((length, 1), 0)


def full_spec(array):
    rank = len(array.shape)
    return pl.BlockSpec(array.shape, lambda *_: (0,) * rank)


def item_spec(array):
    rank = len(array.shape)
    return pl.BlockSpec((1,) + array.shape[1:], lambda b: (b,) + (0,) * (rank - 1))


def layer_spec(array, layer):
    rank = len(array.shape)
    return pl.BlockSpec((1, 1) + array.shape[2:], lambda b: (layer, b) + (0,) * (rank - 2))


def weight_spec(array, layer):
    rank = len(array.shape)
    return pl.BlockSpec((1,) + array.shape[1:], lambda b: (layer,) + (0,) * (rank - 1))


def shape_of(shape, dtype=F32):
    return jax.ShapeDtypeStruct(shape, dtype)


def run(body, grid, ins, in_specs, outs, out_specs, scratch=(), flops=0, name=None):
    return pl.pallas_call(
        body,
        grid=grid,
        in_specs=in_specs,
        out_specs=out_specs,
        out_shape=outs,
        scratch_shapes=list(scratch),
        compiler_params=pltpu.CompilerParams(vmem_limit_bytes=VMEM_BYTES),
        cost_estimate=pl.CostEstimate(flops=flops, bytes_accessed=1 << 20, transcendentals=0),
        name=name,
    )(*ins)


def pair_rows(durations_row):
    return jnp.sum(durations_row, axis=1, keepdims=True) >> 1


def stats_body(mel_ref, dur_ref, out_ref):
    items, frames, _ = mel_ref.shape
    pairs = frames // 2
    pad = jnp.zeros((1, LANES - MEL), F32)
    count = jnp.zeros((1, 1), F32)
    sums = [jnp.zeros((1, MEL), F32) for _ in range(4)]
    for item in range(items):
        pair_count = pair_rows(dur_ref[item : item + 1, :])
        count = count + pair_count.astype(F32)
        inside = rows_of(pairs) < pair_count
        for side in range(2):
            values = jnp.where(inside, mel_ref[item, pl.ds(side, pairs, stride=2), :], 0.0)
            sums[side] = sums[side] + jnp.sum(values, axis=0, keepdims=True)
            sums[2 + side] = sums[2 + side] + jnp.sum(values * values, axis=0, keepdims=True)
    out_ref[...] = jnp.zeros_like(out_ref)
    for place in range(4):
        out_ref[place : place + 1, :] = jnp.concatenate([sums[place], pad], axis=1)
    out_ref[4:5, :] = jnp.broadcast_to(count, (1, LANES))


def read_stats(stats):
    total = stats[4:5, 0:1]
    sums = jnp.concatenate([stats[0:1], stats[1:2]], axis=1)
    squares = jnp.concatenate([stats[2:3], stats[3:4]], axis=1)
    center = sums / total
    variance = squares / total - center * center
    log_act = -0.5 * jnp.log(variance + 1e-06)
    return total, center, variance, log_act, jnp.exp(log_act)


def mix_places():
    row = rows_of(2 * LANES)
    col = iota((1, 2 * LANES), 1)
    row_lane = row & (LANES - 1)
    col_lane = col & (LANES - 1)
    upper = (row_lane >= MEL // 2).astype(jnp.int32)
    row_group = row_lane - upper * (MEL // 2)
    row_member = 2 * upper + (row >> 7)
    col_group = col_lane >> 1
    col_member = 2 * (col >> 7) + (col_lane & 1)
    match = (row_group == col_group) & (row_lane < MEL) & (col_lane < MEL)
    return row_member, col_member, match


def weights_body(
    mix_ref,
    qkv_ref,
    relk_ref,
    relv_ref,
    out_ref,
    prior_ref,
    start_ref,
    end_ref,
    mixm_ref,
    small_ref,
    qkv_pad_ref,
    relk_pad_ref,
    relv_pad_ref,
    out_pad_ref,
    wide_ref,
    prior_pad_ref,
    start_pad_ref,
    end_pad_ref,
):
    row_member, col_member, match = mix_places()
    table = jnp.zeros((2 * LANES, 2 * LANES), F32)
    for i in range(4):
        column = jnp.zeros((2 * LANES, 1), F32)
        for j in range(4):
            column = jnp.where(row_member == j, mix_ref[i, j], column)
        table = jnp.where(col_member == i, column, table)
    mixm_ref[...] = jnp.where(match, table, 0.0)

    ri = iota((8, LANES), 0)
    ci = iota((8, LANES), 1)
    joined = jnp.where((ci == ri + 4) & (ri < 4), 1.0, 0.0).astype(F32)
    for i in range(4):
        for j in range(4):
            joined = jnp.where((ri == i) & (ci == j), mix_ref[i, j], joined)
    determinant = jnp.ones((1, 1), F32)
    for column in range(4):
        pivot = joined[column : column + 1, column : column + 1]
        determinant = determinant * pivot
        row_now = joined[column : column + 1, :] / pivot
        joined = joined - joined[:, column : column + 1] * row_now
        joined = jnp.where(ri == column, row_now, joined)
    small_ref[...] = jnp.where(ri == 4, determinant, joined)

    def select(source, target_shape_rows, wanted):
        return jnp.where(rows_of(target_shape_rows) == wanted, 1.0, 0.0).astype(BF16)

    place = iota((1, 6 * LANES), 1)
    lane = place & (LANES - 1)
    wanted = jnp.where(lane < HEAD, (place >> 7) * HEAD + lane, -1)
    qkv_pad_ref[...] = dot_nn(qkv_ref[...], select(None, 3 * D, wanted)).astype(BF16)

    place = iota((1, 2 * LANES), 1)
    lane = place & (LANES - 1)
    wanted = jnp.where(lane < HEAD, (place >> 7) * HEAD + lane, -1)
    out_pad_ref[...] = dot_tn(select(None, D, wanted), out_ref[...]).astype(BF16)

    wanted = iota((1, LANES), 1) & (PERIOD - 1)
    repeat = select(None, 2 * WINDOW + 1, wanted)
    pad = jnp.zeros((LANES, LANES - HEAD), F32)
    relk_pad_ref[...] = jnp.concatenate([dot_tn(repeat, relk_ref[...]), pad], axis=1).astype(BF16)
    relv_pad_ref[...] = jnp.concatenate([dot_tn(repeat, relv_ref[...]), pad], axis=1).astype(BF16)

    place = iota((1, 8 * LANES), 1)
    lane = place & (LANES - 1)
    group = (place >> 7) & 3
    fits = (lane < MEL) & ((lane & 1) == (place >> 9))
    wanted = jnp.where(fits, (group >> 1) * MEL + (group & 1) * (MEL // 2) + (lane >> 1), -1)
    wide = select(None, 2 * MEL, wanted)
    wide_ref[...] = wide
    prior_pad_ref[...] = dot_nn(prior_ref[...], wide).astype(BF16)

    wanted = iota((1, LANES), 1)
    start_pad_ref[...] = dot_tn(select(None, MEL, wanted), start_ref[...]).astype(BF16)
    place = iota((1, 2 * LANES), 1)
    lane = place & (LANES - 1)
    wanted = jnp.where(lane < MEL, (place >> 7) * MEL + lane, -1)
    end_pad_ref[...] = dot_nn(end_ref[...], select(None, 2 * MEL, wanted)).astype(BF16)


def text_rows(dur_ref):
    item = pl.program_id(0)
    return dur_ref[pl.ds(item, 1), :]


def text_inside(durations_row, length):
    tokens = jnp.sum((durations_row > 0).astype(jnp.int32), axis=1, keepdims=True)
    return rows_of(length) < tokens


def norm_parts(inputs):
    centered = inputs - jnp.mean(inputs, axis=1, keepdims=True)
    spread = jnp.mean(centered * centered, axis=1, keepdims=True)
    inverse = lax.rsqrt(spread + 1e-05)
    return centered * inverse, inverse


def norm_back(inputs, gain, gradient):
    unit, inverse = norm_parts(inputs)
    gain_grad = jnp.sum(gradient * unit, axis=0, keepdims=True)
    shift_grad = jnp.sum(gradient, axis=0, keepdims=True)
    scaled = gradient * gain
    mean_one = jnp.mean(scaled, axis=1, keepdims=True)
    mean_two = jnp.mean(scaled * unit, axis=1, keepdims=True)
    return inverse * (scaled - mean_one - unit * mean_two), gain_grad, shift_grad


def band_of(length):
    offset = iota((length, length), 1) - iota((length, length), 0)
    return (offset <= WINDOW) & (offset >= -WINDOW)


def turn_rows(values, left):
    length = values.shape[0]
    step = rows_of(length) & (PERIOD - 1)
    first = WINDOW if left else LANES - WINDOW
    values = pltpu.roll(values, first, 1)
    for bit in (1, 2, 4, 8):
        moved = pltpu.roll(values, (LANES - bit) if left else bit, 1)
        values = jnp.where((step & bit) != 0, moved, values)
    return values


def band_gather(weights_low, band, folding):
    kept = jnp.where(band, weights_low, jnp.zeros_like(weights_low))
    return turn_rows(dot_nn(kept, folding), True).astype(BF16)


def band_spread(near, band):
    turned = turn_rows(near, False)
    count = band.shape[1] // LANES
    return jnp.where(band, jnp.concatenate([turned] * count, axis=1), 0.0)


def folding_of(length):
    same = (iota((length, LANES), 0) & (PERIOD - 1)) == (iota((length, LANES), 1) & (PERIOD - 1))
    return jnp.where(same, 1.0, 0.0).astype(BF16)


def one_turn(rel_pad):
    return jnp.where(rows_of(LANES) < PERIOD, rel_pad, jnp.zeros_like(rel_pad))


def attention_body(
    tok_ref,
    dur_ref,
    emb_ref,
    qkv_ref,
    relk_ref,
    relv_ref,
    out_ref,
    gain_ref,
    shift_ref,
    emb_low_ref,
    proj_ref,
    att_ref,
    banded_ref,
    attend_ref,
    mixed_ref,
    normed_ref,
):
    item = pl.program_id(0)
    tokens = tok_ref[pl.ds(item, 1), :]
    durations = text_rows(dur_ref)
    length = tokens.shape[1]
    inside = text_inside(durations, length)
    hot = jnp.where(iota((VOCAB, length), 0) == tokens, 1.0, 0.0).astype(BF16)
    embedded = jnp.where(inside, dot_tn(hot, emb_ref[...]) * math.sqrt(D), 0.0)
    emb_low = embedded.astype(BF16)
    emb_low_ref[0] = emb_low
    proj = dot_nn(emb_low, qkv_ref[...]).astype(BF16)
    proj_ref[0] = proj
    key_bias = jnp.where(durations > 0, 0.0, -10000.0)
    band = band_of(length)
    folding = folding_of(length)
    relv = one_turn(relv_ref[...])
    parts = []
    for head in range(HEADS):
        query = proj[:, head * LANES : (head + 1) * LANES]
        key = proj[:, (HEADS + head) * LANES : (HEADS + head + 1) * LANES]
        value = proj[:, (2 * HEADS + head) * LANES : (2 * HEADS + head + 1) * LANES]
        near = band_spread(dot_nt(query, relk_ref[...]), band)
        scores = (dot_nt(query, key) + near) / math.sqrt(HEAD) + key_bias
        raised = jnp.exp(scores - jnp.max(scores, axis=1, keepdims=True))
        attention = raised / jnp.sum(raised, axis=1, keepdims=True)
        att_ref[0, head] = attention
        low = attention.astype(BF16)
        banded = band_gather(low, band, folding)
        banded_ref[0, head] = banded
        parts.append(dot_nn(low, value) + dot_nn(banded, relv))
    attend = jnp.concatenate(parts, axis=1).astype(BF16)
    attend_ref[0] = attend
    mixed = embedded + dot_nn(attend, out_ref[...])
    mixed_ref[0] = mixed
    unit, _ = norm_parts(mixed)
    normed_ref[0] = unit * gain_ref[...] + shift_ref[...]


def shifted(values, offset):
    if offset == 0:
        return values
    length = values.shape[0]
    moved = pltpu.roll(values, (-offset) % length, 0)
    place = rows_of(length)
    keep = (place < length - offset) if offset > 0 else (place >= -offset)
    return jnp.where(keep, moved, 0.0)


def unfold(values, kernel, reverse=False):
    half = kernel // 2
    steps = [step - half for step in range(kernel)]
    if reverse:
        steps = [-step for step in steps]
    return jnp.concatenate([shifted(values, step).astype(BF16) for step in steps], axis=1)


GELU_A = math.sqrt(2.0 / math.pi)
GELU_B = 0.044715


def gelu_tanh(values):
    return jnp.tanh(GELU_A * (values + GELU_B * values * values * values))


def feed_body(
    dur_ref,
    normed_ref,
    ff1_ref,
    ff2_ref,
    gain_ref,
    shift_ref,
    prior_ref,
    filt_ref,
    activ_ref,
    summed_ref,
    enc_ref,
    high_ref,
    low_ref,
):
    durations = text_rows(dur_ref)
    normed = normed_ref[0]
    length = normed.shape[0]
    inside = text_inside(durations, length)
    filtered = dot_nn(unfold(jnp.where(inside, normed, 0.0), KSIZE), ff1_ref[...])
    filt_ref[0] = filtered
    activ = jnp.where(inside, 0.5 * filtered * (1.0 + gelu_tanh(filtered)), 0.0)
    activ_ref[0] = activ.astype(BF16)
    summed = normed + jnp.where(inside, dot_nn(unfold(activ, KSIZE), ff2_ref[...]), 0.0)
    summed_ref[0] = summed
    unit, _ = norm_parts(summed)
    encoded = jnp.where(inside, unit * gain_ref[...] + shift_ref[...], 0.0).astype(BF16)
    enc_ref[0] = encoded
    prior = dot_nn(encoded, prior_ref[...])
    high, low = halves(prior)
    wide = prior.shape[1] // 2
    high_ref[0, :length] = high[:, :wide]
    high_ref[0, length:] = high[:, wide:]
    low_ref[0, :length] = low[:, :wide]
    low_ref[0, length:] = low[:, wide:]


def accumulate(ref, values, first):
    @pl.when(first)
    def _():
        ref[...] = values

    @pl.when(jnp.logical_not(first))
    def _():
        ref[...] = ref[...] + values


def align_of(durations_row, pairs):
    length = durations_row.shape[1]
    upper = jnp.where(iota((length, length), 0) <= iota((length, length), 1), 1.0, 0.0).astype(F32)
    wide = jnp.broadcast_to(durations_row.astype(F32), (8, length))
    ends = dot_nn(wide, upper, HIGH)[0:1].astype(jnp.int32)
    starts = ends - durations_row
    frame = 2 * rows_of(pairs)
    even = (frame >= starts) & (frame < ends)
    odd = (frame + 1 >= starts) & (frame + 1 < ends)
    both = jnp.concatenate([jnp.where(even, 1.0, 0.0), jnp.where(odd, 1.0, 0.0)], axis=1)
    return both.astype(BF16)


def feed_back_body(
    dur_ref,
    flow_ref,
    wide_ref,
    enc_ref,
    summed_ref,
    filt_ref,
    activ_ref,
    normed_ref,
    ff1_ref,
    ff2_ref,
    gain_ref,
    prior_ref,
    ngrad_ref,
    prior_out_ref,
    ff1_out_ref,
    ff2_out_ref,
    gain_out_ref,
    shift_out_ref,
):
    first = pl.program_id(0) == 0
    durations = text_rows(dur_ref)
    length = durations.shape[1]
    inside = text_inside(durations, length)
    flow = flow_ref[0]
    align = align_of(durations, flow.shape[0])
    flow_high, flow_low = halves(flow)
    spread = dot_tn(align, flow_high) + dot_tn(align, flow_low)
    half = wide_ref.shape[1] // 2
    grad = jnp.zeros((length, 2 * MEL), F32)
    for side in range(2):
        part_high, part_low = halves(spread[side * length : (side + 1) * length])
        chosen = wide_ref[:, side * half : (side + 1) * half]
        grad = grad + dot_nt(part_high, chosen) + dot_nt(part_low, chosen)
    prior_low = jnp.where(inside, grad, 0.0).astype(BF16)
    accumulate(prior_out_ref, dot_tn(enc_ref[0], prior_low), first)
    enc_grad = jnp.where(inside, dot_nt(prior_low, prior_ref[...]), 0.0)
    summed_grad, gain_grad, shift_grad = norm_back(summed_ref[0], gain_ref[...], enc_grad)
    accumulate(gain_out_ref, gain_grad, first)
    accumulate(shift_out_ref, shift_grad, first)
    second = jnp.where(inside, summed_grad, 0.0)
    activ = activ_ref[0]
    activ_grad = jnp.zeros((length, FILTER), F32)
    for step in range(KSIZE):
        moved = shifted(second, KSIZE // 2 - step).astype(BF16)
        rows = slice(step * FILTER, (step + 1) * FILTER)
        activ_grad = activ_grad + dot_nt(moved, ff2_ref[rows, :])
        accumulate(ff2_out_ref.at[rows, :], dot_tn(activ, moved), first)
    filtered = filt_ref[0]
    tanh = gelu_tanh(filtered)
    slope = 0.5 * (1.0 + tanh) + 0.5 * filtered * (1.0 - tanh * tanh) * GELU_A * (
        1.0 + 3.0 * GELU_B * filtered * filtered
    )
    first_grad = jnp.where(inside, activ_grad * slope, 0.0)
    normed_low = jnp.where(inside, normed_ref[0], 0.0).astype(BF16)
    back = jnp.zeros((length, D), F32)
    for step in range(KSIZE):
        moved = shifted(first_grad, KSIZE // 2 - step).astype(BF16)
        rows = slice(step * D, (step + 1) * D)
        back = back + dot_nt(moved, ff1_ref[rows, :])
        accumulate(ff1_out_ref.at[rows, :], dot_tn(normed_low, moved), first)
    ngrad_ref[0] = summed_grad + jnp.where(inside, back, 0.0)


def attention_back_body(
    tok_ref,
    dur_ref,
    ngrad_ref,
    mixed_ref,
    attend_ref,
    att_ref,
    banded_ref,
    proj_ref,
    emb_low_ref,
    qkv_ref,
    relk_ref,
    relv_ref,
    out_ref,
    gain_ref,
    table_ref,
    qkv_out_ref,
    relk_out_ref,
    relv_out_ref,
    out_out_ref,
    gain_out_ref,
    shift_out_ref,
    qkv_acc,
    out_acc,
    relk_acc,
    relv_acc,
):
    item = pl.program_id(0)
    first = item == 0
    last = item == pl.num_programs(0) - 1
    tokens = tok_ref[pl.ds(item, 1), :]
    durations = text_rows(dur_ref)
    length = tokens.shape[1]
    inside = text_inside(durations, length)
    mixed_grad, gain_grad, shift_grad = norm_back(mixed_ref[0], gain_ref[...], ngrad_ref[0])
    accumulate(gain_out_ref, gain_grad, first)
    accumulate(shift_out_ref, shift_grad, first)
    out_low = mixed_grad.astype(BF16)
    accumulate(out_acc, dot_tn(attend_ref[0], out_low), first)
    weight = dot_nt(out_low, out_ref[...]).astype(BF16)
    band = band_of(length)
    folding = folding_of(length)
    relk = one_turn(relk_ref[...])
    proj = proj_ref[0]
    queries, keys, values = [], [], []
    relk_sum = jnp.zeros((LANES, LANES), F32)
    relv_sum = jnp.zeros((LANES, LANES), F32)
    for head in range(HEADS):
        query = proj[:, head * LANES : (head + 1) * LANES]
        key = proj[:, (HEADS + head) * LANES : (HEADS + head + 1) * LANES]
        value = proj[:, (2 * HEADS + head) * LANES : (2 * HEADS + head + 1) * LANES]
        mine = weight[:, head * LANES : (head + 1) * LANES]
        near = band_spread(dot_nt(mine, relv_ref[...]), band)
        grad = dot_nt(mine, value) + near
        attention = att_ref[0, head]
        values.append(dot_tn(attention.astype(BF16), mine))
        relv_sum = relv_sum + dot_tn(banded_ref[0, head], mine)
        score = attention * (grad - jnp.sum(attention * grad, axis=1, keepdims=True))
        score_low = (score / math.sqrt(HEAD)).astype(BF16)
        band_grad = band_gather(score_low, band, folding)
        queries.append(dot_nn(score_low, key) + dot_nn(band_grad, relk))
        keys.append(dot_tn(score_low, query))
        relk_sum = relk_sum + dot_tn(band_grad, query)
    accumulate(relk_acc, relk_sum, first)
    accumulate(relv_acc, relv_sum, first)
    proj_low = jnp.concatenate(queries + keys + values, axis=1).astype(BF16)
    accumulate(qkv_acc, dot_tn(emb_low_ref[0], proj_low), first)
    back = mixed_grad + dot_nt(proj_low, qkv_ref[...])
    embed_grad = jnp.where(inside, back, 0.0) * math.sqrt(D)
    hot = jnp.where(iota((VOCAB, length), 0) == tokens, 1.0, 0.0).astype(BF16)
    high, low = halves(embed_grad)
    accumulate(table_ref, dot_nn(hot, high) + dot_nn(hot, low), first)

    @pl.when(last)
    def _():
        for part in range(3 * HEADS):
            qkv_out_ref[:, part * HEAD : (part + 1) * HEAD] = qkv_acc[
                :, part * LANES : part * LANES + HEAD
            ]
        for head in range(HEADS):
            out_out_ref[head * HEAD : (head + 1) * HEAD, :] = out_acc[
                head * LANES : head * LANES + HEAD, :
            ]
        relk_out_ref[...] = relk_acc[: 2 * WINDOW + 1, :HEAD]
        relv_out_ref[...] = relv_acc[: 2 * WINDOW + 1, :HEAD]


def split_pairs(mel_ref, pairs):
    pad = jnp.zeros((pairs, LANES - MEL), F32)
    even = mel_ref[0, pl.ds(0, pairs, stride=2), :]
    odd = mel_ref[0, pl.ds(1, pairs, stride=2), :]
    return jnp.concatenate([even, pad, odd, pad], axis=1)


def gates_of(pre):
    return jnp.tanh(pre[:, :HID]), 1.0 / (1.0 + jnp.exp(-pre[:, HID:]))


def flow_body(
    mel_ref,
    dur_ref,
    high_ref,
    low_ref,
    stats_ref,
    mixm_ref,
    start_ref,
    win_ref,
    wres_ref,
    wlast_ref,
    wend_ref,
    normal_ref,
    passive_ref,
    hidden_ref,
    pre_ref,
    skip_ref,
    active_ref,
    lgrad_ref,
    flow_ref,
    nll_ref,
    end_out_ref,
    end_acc,
):
    first = pl.program_id(0) == 0
    last = pl.program_id(0) == pl.num_programs(0) - 1
    pairs = mel_ref.shape[1] // 2
    durations = text_rows(dur_ref)
    inside = rows_of(pairs) < pair_rows(durations)
    total, center, _, _, scale = read_stats(stats_ref[...])
    unit = 1.0 / (2 * MEL * total)
    normalized = jnp.where(inside, (split_pairs(mel_ref, pairs) - center) * scale, 0.0)
    normal_ref[0] = normalized
    turned = dot_nn(normalized, mixm_ref[...], HIGH)
    passive = turned[:, :LANES]
    active = turned[:, LANES:]
    passive_low = passive.astype(BF16)
    passive_ref[0] = passive_low
    hidden = jnp.where(inside, dot_nn(passive_low, start_ref[...]), 0.0)
    skipped = jnp.zeros((pairs, HID), F32)
    for layer in range(WLAYERS):
        hidden_ref[layer, 0] = hidden.astype(BF16)
        pre = dot_nn(unfold(hidden, WKER), win_ref[layer])
        pre_ref[layer, 0] = pre
        tanh, gate = gates_of(pre)
        gated = (tanh * gate).astype(BF16)
        if layer < WLAYERS - 1:
            both = dot_nn(gated, wres_ref[layer])
            hidden = jnp.where(inside, hidden + both[:, :HID], 0.0)
            skipped = skipped + both[:, HID:]
        else:
            skipped = skipped + dot_nn(gated, wlast_ref[...])
    output_low = jnp.where(inside, skipped, 0.0).astype(BF16)
    coupled = jnp.where(inside, dot_nn(output_low, wend_ref[...]), 0.0)
    shift_part = coupled[:, :LANES]
    log_part = coupled[:, LANES:]
    growth = jnp.exp(log_part)
    moved = jnp.where(inside, shift_part + growth * active, 0.0)
    align = align_of(durations, pairs)
    prior = dot_nn(align, high_ref[0]) + dot_nn(align, low_ref[0])
    latent = jnp.concatenate([passive, moved], axis=1)
    gap = latent - prior[:, : 2 * LANES]
    log_scales = prior[:, 2 * LANES :]
    inverse = jnp.exp(-2.0 * log_scales)
    scaled = inverse * gap
    square = scaled * gap
    terms = jnp.where(inside, log_scales + 0.5 * square, 0.0)
    sums = jnp.sum(terms, axis=0, keepdims=True)
    sums = sums[:, :LANES] + sums[:, LANES:] - jnp.sum(log_part, axis=0, keepdims=True)
    accumulate(nll_ref, jnp.broadcast_to(sums, (8, LANES)), first)
    latent_grad = jnp.where(inside, unit * scaled, 0.0)
    scale_grad = jnp.where(inside, unit * (1.0 - square), 0.0)
    flow_ref[0] = jnp.concatenate([-latent_grad, scale_grad], axis=1)
    lgrad_ref[0] = latent_grad[:, :LANES]
    moved_grad = latent_grad[:, LANES:]
    active_grad = moved_grad * growth
    active_ref[0] = active_grad
    log_grad = jnp.where(inside, active_grad * active - unit, 0.0)
    coupled_low = jnp.concatenate([moved_grad, log_grad], axis=1).astype(BF16)
    accumulate(end_acc, dot_tn(output_low, coupled_low), first)
    skip_grad = jnp.where(inside, dot_nt(coupled_low, wend_ref[...]), 0.0)
    skip_ref[0] = skip_grad.astype(BF16)

    @pl.when(last)
    def _():
        end_out_ref[:, :MEL] = end_acc[:, :MEL]
        end_out_ref[:, MEL:] = end_acc[:, LANES : LANES + MEL]


def layer_body(layer, dur_ref, *refs):
    top = layer == WLAYERS - 1
    if top:
        skip_ref, pre_ref, hidden_ref, win_ref, wres_ref, out_grad_ref, win_out, wres_out, wide = refs
    else:
        (
            skip_ref,
            pre_ref,
            hidden_ref,
            win_ref,
            wres_ref,
            hgrad_ref,
            out_grad_ref,
            win_out,
            wres_out,
            wide,
        ) = refs
    first = pl.program_id(0) == 0

    @pl.when(first)
    def _():
        for step in range(WKER):
            wide[:, step * 2 * HID : (step + 1) * 2 * HID] = win_ref[
                0, step * HID : (step + 1) * HID, :
            ]

    pairs = pre_ref.shape[2]
    inside = rows_of(pairs) < pair_rows(text_rows(dur_ref))
    tanh, gate = gates_of(pre_ref[0, 0])
    gated = (tanh * gate).astype(BF16)
    skip_low = skip_ref[0]
    if top:
        gated_grad = dot_nt(skip_low, wres_ref[...])
        accumulate(wres_out, dot_tn(gated, skip_low), first)
        kept = None
    else:
        kept = jnp.where(inside, hgrad_ref[0], 0.0)
        part = jnp.concatenate([kept, skip_low.astype(F32)], axis=1).astype(BF16)
        gated_grad = dot_nt(part, wres_ref[0])
        accumulate(wres_out, dot_tn(gated, part), first)
    tanh_grad = gated_grad * gate * (1.0 - tanh * tanh)
    gate_grad = gated_grad * tanh * gate * (1.0 - gate)
    pre_grad = jnp.concatenate([tanh_grad, gate_grad], axis=1)
    spread = unfold(pre_grad, WKER, reverse=True)
    sums = dot_tn(hidden_ref[0, 0], spread)
    for step in range(WKER):
        accumulate(
            win_out.at[step * HID : (step + 1) * HID, :],
            sums[:, step * 2 * HID : (step + 1) * 2 * HID],
            first,
        )
    back = dot_nt(spread, wide[...])
    out_grad_ref[0] = back if top else kept + back


def mix_body(
    dur_ref,
    hgrad_ref,
    passive_ref,
    lgrad_ref,
    active_ref,
    normal_ref,
    start_ref,
    mixm_ref,
    ngrad_ref,
    start_out_ref,
    sums_ref,
    mix_out_ref,
    start_acc,
    mix_acc,
):
    first = pl.program_id(0) == 0
    last = pl.program_id(0) == pl.num_programs(0) - 1
    pairs = hgrad_ref.shape[1]
    inside = rows_of(pairs) < pair_rows(text_rows(dur_ref))
    start_low = jnp.where(inside, hgrad_ref[0], 0.0).astype(BF16)
    accumulate(start_acc, dot_tn(passive_ref[0], start_low), first)
    passive_grad = lgrad_ref[0] + dot_nt(start_low, start_ref[...])
    turned_grad = jnp.concatenate([passive_grad, active_ref[0]], axis=1)
    normalized = normal_ref[0]
    accumulate(mix_acc, dot_tn(normalized, turned_grad, HIGH), first)
    normal_grad = jnp.where(inside, dot_nt(turned_grad, mixm_ref[...], HIGH), 0.0)
    ngrad_ref[0] = normal_grad
    one = jnp.sum(normal_grad, axis=0, keepdims=True)
    two = jnp.sum(normal_grad * normalized, axis=0, keepdims=True)
    rows = [one[:, :LANES], one[:, LANES:], two[:, :LANES], two[:, LANES:]]
    rows.append(jnp.zeros((4, LANES), F32))
    accumulate(sums_ref, jnp.concatenate(rows, axis=0), first)

    @pl.when(last)
    def _():
        start_out_ref[...] = start_acc[:MEL, :]
        row_member, col_member, match = mix_places()
        kept = jnp.where(match, mix_acc[...], 0.0)
        ri = iota((8, LANES), 0)
        ci = iota((8, LANES), 1)
        mixed = jnp.zeros((8, LANES), F32)
        for i in range(4):
            column = jnp.sum(jnp.where(col_member == i, kept, 0.0), axis=1, keepdims=True)
            for j in range(4):
                entry = jnp.sum(
                    jnp.where(row_member == j, column, 0.0), axis=0, keepdims=True
                )
                mixed = jnp.where((ri == i) & (ci == j), entry, mixed)
        mix_out_ref[...] = mixed


def frames_body(mel_ref, dur_ref, ngrad_ref, stats_ref, sums_ref, out_ref):
    pairs = mel_ref.shape[1] // 2
    inside = rows_of(pairs) < pair_rows(text_rows(dur_ref))
    total, center, variance, _, scale = read_stats(stats_ref[...])
    unit = 1.0 / (2 * MEL * total)
    sums = sums_ref[...]
    one = jnp.concatenate([sums[0:1], sums[1:2]], axis=1)
    two = jnp.concatenate([sums[2:3], sums[3:4]], axis=1)
    log_grad = two - unit * total
    var_grad = -0.5 * log_grad / (variance + 1e-06)
    center_grad = -scale * one - 2.0 * center * var_grad
    values = split_pairs(mel_ref, pairs)
    grads = ngrad_ref[0] * scale + (2.0 * values * var_grad + center_grad) / total
    grads = jnp.where(inside, grads, 0.0) * (2 * MEL * total)
    out_ref[0, pl.ds(0, pairs, stride=2), :] = grads[:, :MEL]
    out_ref[0, pl.ds(1, pairs, stride=2), :] = grads[:, LANES : LANES + MEL]


def small_sum(values, devices):
    bit = 1
    while bit < devices:
        values = values + lax.ppermute(values, "dp", [(i, i ^ bit) for i in range(devices)])
        bit *= 2
    return values


def big_sum(arrays, devices):
    return lax.psum(arrays, "dp")


def on_device(
    devices,
    token_ids,
    durations,
    mel_frames,
    embedding,
    w_qkv,
    rel_key,
    rel_value,
    w_out,
    attn_gain,
    attn_shift,
    w_ff1,
    w_ff2,
    ffn_gain,
    ffn_shift,
    w_prior,
    w_mix,
    w_start,
    w_in,
    w_res,
    w_skip_last,
    w_end,
):
    items, length = token_ids.shape
    frames = mel_frames.shape[1]
    pairs = frames // 2
    grid = (items,)
    vmem = pl.BlockSpec(memory_space=pltpu.VMEM)
    smem = pl.BlockSpec(memory_space=pltpu.SMEM)
    gain_one = attn_gain.reshape(1, D)
    shift_one = attn_shift.reshape(1, D)
    gain_two = ffn_gain.reshape(1, D)
    shift_two = ffn_shift.reshape(1, D)

    stats = run(
        stats_body, (), [mel_frames, durations], [vmem] * 2, shape_of((8, LANES)), vmem, name="stats"
    )
    stats = small_sum(stats, devices)

    prepared = [
        shape_of((2 * LANES, 2 * LANES)),
        shape_of((8, LANES)),
        shape_of((D, 6 * LANES), BF16),
        shape_of((LANES, LANES), BF16),
        shape_of((LANES, LANES), BF16),
        shape_of((2 * LANES, D), BF16),
        shape_of((2 * MEL, 8 * LANES), BF16),
        shape_of((D, 8 * LANES), BF16),
        shape_of((LANES, HID), BF16),
        shape_of((HID, 2 * LANES), BF16),
    ]
    mixm, small, qkv_pad, relk_pad, relv_pad, out_pad, wide, prior_pad, start_pad, end_pad = run(
        weights_body,
        (),
        [w_mix, w_qkv, rel_key, rel_value, w_out, w_prior, w_start, w_end],
        [smem] + [vmem] * 7,
        prepared,
        [vmem] * len(prepared),
        name="weights",
    )

    ins = [
        token_ids,
        durations,
        embedding,
        qkv_pad,
        relk_pad,
        relv_pad,
        out_pad,
        gain_one,
        shift_one,
    ]
    outs = [
        shape_of((items, length, D), BF16),
        shape_of((items, length, 6 * LANES), BF16),
        shape_of((items, HEADS, length, length)),
        shape_of((items, HEADS, length, LANES), BF16),
        shape_of((items, length, 2 * LANES), BF16),
        shape_of((items, length, D)),
        shape_of((items, length, D)),
    ]
    emb_low, proj, attention, banded, attend, mixed, normed = run(
        attention_body,
        grid,
        ins,
        [full_spec(a) for a in ins],
        outs,
        [item_spec(a) for a in outs],
        name="attention",
    )

    ins = [durations, normed, w_ff1, w_ff2, gain_two, shift_two, prior_pad]
    outs = [
        shape_of((items, length, FILTER)),
        shape_of((items, length, FILTER), BF16),
        shape_of((items, length, D)),
        shape_of((items, length, D), BF16),
        shape_of((items, 2 * length, 4 * LANES), BF16),
        shape_of((items, 2 * length, 4 * LANES), BF16),
    ]
    filtered, activ, summed, encoded, prior_high, prior_low = run(
        feed_body,
        grid,
        ins,
        [full_spec(durations), item_spec(normed)] + [full_spec(a) for a in ins[2:]],
        outs,
        [item_spec(a) for a in outs],
        name="feed",
    )

    ins = [
        mel_frames,
        durations,
        prior_high,
        prior_low,
        stats,
        mixm,
        start_pad,
        w_in,
        w_res,
        w_skip_last,
        end_pad,
    ]
    outs = [
        shape_of((items, pairs, 2 * LANES)),
        shape_of((items, pairs, LANES), BF16),
        shape_of((WLAYERS, items, pairs, HID), BF16),
        shape_of((WLAYERS, items, pairs, 2 * HID)),
        shape_of((items, pairs, HID), BF16),
        shape_of((items, pairs, LANES)),
        shape_of((items, pairs, LANES)),
        shape_of((items, pairs, 4 * LANES)),
        shape_of((8, LANES)),
        shape_of((HID, 2 * MEL)),
    ]
    stacked = [
        pl.BlockSpec((WLAYERS, 1) + a.shape[2:], lambda b: (0, b, 0, 0)) for a in outs[2:4]
    ]
    out_specs = (
        [item_spec(a) for a in outs[:2]]
        + stacked
        + [item_spec(a) for a in outs[4:8]]
        + [full_spec(a) for a in outs[8:]]
    )
    (
        normalized,
        passive,
        hidden,
        pre,
        skip,
        active_grad,
        latent_grad,
        flow,
        nll,
        end_grad,
    ) = run(
        flow_body,
        grid,
        ins,
        [item_spec(mel_frames), full_spec(durations), item_spec(prior_high), item_spec(prior_low)]
        + [full_spec(a) for a in ins[4:]],
        outs,
        out_specs,
        [pltpu.VMEM((HID, 2 * LANES), F32)],
        name="flow",
    )

    in_grads = [None] * WLAYERS
    res_grads = [None] * WLAYERS
    hgrad = None
    for layer in reversed(range(WLAYERS)):
        top = layer == WLAYERS - 1
        ins = [durations, skip, pre, hidden, w_in, w_skip_last if top else w_res]
        in_specs = [
            full_spec(durations),
            item_spec(skip),
            layer_spec(pre, layer),
            layer_spec(hidden, layer),
            weight_spec(w_in, layer),
            full_spec(w_skip_last) if top else weight_spec(w_res, layer),
        ]
        if not top:
            ins.append(hgrad)
            in_specs.append(item_spec(hgrad))
        outs = [
            shape_of((items, pairs, HID)),
            shape_of((WKER * HID, 2 * HID)),
            shape_of((HID, HID if top else 2 * HID)),
        ]
        hgrad, in_grads[layer], res_grads[layer] = run(
            functools.partial(layer_body, layer),
            grid,
            ins,
            in_specs,
            outs,
            [item_spec(outs[0]), full_spec(outs[1]), full_spec(outs[2])],
            [pltpu.VMEM((HID, WKER * 2 * HID), BF16)],
            name="layer" + str(layer),
        )

    ins = [durations, hgrad, passive, latent_grad, active_grad, normalized, start_pad, mixm]
    outs = [
        shape_of((items, pairs, 2 * LANES)),
        shape_of((MEL, HID)),
        shape_of((8, LANES)),
        shape_of((8, LANES)),
    ]
    normal_grad, start_grad, sums, mix_grad = run(
        mix_body,
        grid,
        ins,
        [full_spec(durations)] + [item_spec(a) for a in ins[1:6]] + [full_spec(a) for a in ins[6:]],
        outs,
        [item_spec(outs[0])] + [full_spec(a) for a in outs[1:]],
        [pltpu.VMEM((LANES, HID), F32), pltpu.VMEM((2 * LANES, 2 * LANES), F32)],
        name="mix",
    )
    sums = jnp.concatenate([sums[:4], nll[:4]], axis=0)
    sums = small_sum(sums, devices)

    ins = [durations, flow, wide, encoded, summed, filtered, activ, normed, w_ff1, w_ff2, gain_two, w_prior]
    outs = [
        shape_of((items, length, D)),
        shape_of((D, 2 * MEL)),
        shape_of((KSIZE * D, FILTER)),
        shape_of((KSIZE * FILTER, D)),
        shape_of((1, D)),
        shape_of((1, D)),
    ]
    kinds = [full_spec, item_spec, full_spec] + [item_spec] * 5 + [full_spec] * 4
    ngrad, prior_grad, ff1_grad, ff2_grad, gain_two_grad, shift_two_grad = run(
        feed_back_body,
        grid,
        ins,
        [kind(a) for kind, a in zip(kinds, ins)],
        outs,
        [item_spec(outs[0])] + [full_spec(a) for a in outs[1:]],
        name="feed_back",
    )

    ins = [
        token_ids,
        durations,
        ngrad,
        mixed,
        attend,
        attention,
        banded,
        proj,
        emb_low,
        qkv_pad,
        relk_pad,
        relv_pad,
        out_pad,
        gain_one,
    ]
    kinds = [full_spec] * 2 + [item_spec] * 7 + [full_spec] * 5
    outs = [
        shape_of((VOCAB, D)),
        shape_of((D, 3 * D)),
        shape_of((2 * WINDOW + 1, HEAD)),
        shape_of((2 * WINDOW + 1, HEAD)),
        shape_of((D, D)),
        shape_of((1, D)),
        shape_of((1, D)),
    ]
    table_grad, qkv_grad, relk_grad, relv_grad, out_grad, gain_one_grad, shift_one_grad = run(
        attention_back_body,
        grid,
        ins,
        [kind(a) for kind, a in zip(kinds, ins)],
        outs,
        [full_spec(a) for a in outs],
        [
            pltpu.VMEM((D, 6 * LANES), F32),
            pltpu.VMEM((2 * LANES, D), F32),
            pltpu.VMEM((LANES, LANES), F32),
            pltpu.VMEM((LANES, LANES), F32),
        ],
        name="attention_back",
    )

    ins = [mel_frames, durations, normal_grad, stats, sums]
    kinds = [item_spec, full_spec, item_spec, full_spec, full_spec]
    mel_grad = run(
        frames_body,
        grid,
        ins,
        [kind(a) for kind, a in zip(kinds, ins)],
        shape_of(mel_frames.shape),
        item_spec(mel_frames),
        name="frames",
    )

    total = stats[4, 0]
    unit = 1.0 / (2 * MEL * total)
    variance = stats[2:4, :MEL] / total - (stats[0:2, :MEL] / total) ** 2
    log_act = -0.5 * jnp.log(variance + 1e-06)
    loss = (
        jnp.sum(sums[4])
        - total * jnp.sum(log_act)
        - total * (MEL // 2) * jnp.log(small[4, 0])
    ) * unit + 0.5 * math.log(2.0 * math.pi)

    grads = big_sum(
        (
            table_grad,
            qkv_grad,
            relk_grad,
            relv_grad,
            out_grad,
            gain_one_grad.reshape(D),
            shift_one_grad.reshape(D),
            ff1_grad,
            ff2_grad,
            gain_two_grad.reshape(D),
            shift_two_grad.reshape(D),
            prior_grad,
            mix_grad[:4, :4],
            start_grad,
            jnp.stack(in_grads),
            jnp.stack(res_grads[:-1]),
            res_grads[-1],
            end_grad,
        ),
        devices,
    )
    grads = list(grads)
    grads[12] = grads[12] - (MEL // 2) * unit * total * small[:4, 4:8].T
    return (loss, mel_grad, *grads)


def solution(mesh):
    devices = mesh.shape["dp"]
    placed = (P("dp", None), P("dp", None), P("dp", None, None)) + (P(),) * 18
    return jax.shard_map(
        functools.partial(on_device, devices),
        mesh=mesh,
        in_specs=placed,
        out_specs=(P(), P("dp", None, None)) + (P(),) * 18,
        check_vma=False,
    )
```

time: 865 us -> 627 us (0.72)
  matrix products: 239 us -> 0 us
  local copies, waits for them, and re-layouts: 223 us -> 30.8 us
  Pallas kernels: 0 us -> 190 us
  waiting for transfers between devices: 176 us -> 360 us
  blocking collectives: 86 us -> 0 us
  other arithmetic: 78.6 us -> 9.49 us
  loops' own time: 30 us -> 0 us
  starting transfers between devices: 0.04 us -> 15.4 us
    dot_general x268 -> x0, matrix products: 238 us -> none  [the longest x64 59.9 us: matmul(): return jnp.dot(first_op, second_op, preferred_element_type=jnp.float32)]
    pallas_call x0 -> x13, Pallas kernels: none -> 190 us  [run(): pl.pallas_call(body, grid=grid, in_specs=in_specs, out_specs=out_specs, o...]
    psum x1 -> x2, waiting for transfers between devices: 175 us -> 349 us  [big_sum(): return lax.psum(arrays, 'dp')]
    psum x2 -> x0, blocking collectives: 86 us -> none  [the longest x1 44 us: on_device(): lax.psum((enc_acc[0], enc_acc[1], enc_acc[2], enc_acc[3], enc_acc[4], enc...]
    while x1156 -> x0, local copies, waits for them, and re-layouts: 60.8 us -> none
    dynamic_update_slice x8 -> x0, local copies, waits for them, and re-layouts: 31.6 us -> none  [on_device(): lax.scan(item_step, (enc_zero, dec_zero, scalar_zero, channel_zero, chann...]
    another operation x1 -> x0, loops' own time: 30 us -> none  [on_device(): lax.scan(item_step, (enc_zero, dec_zero, scalar_zero, channel_zero, chann...]
    transpose x25 -> x0, local copies, waits for them, and re-layouts: 23.8 us -> none  [the longest x8 16.3 us: pair_open(): return pairs_in.reshape(count_rows, width // 2, 2).transpose(0, 2, 1).res...]
  transfers between devices with their start and end apart: 1 -> 12, of which waited for: 1 -> 10; matrix products, arithmetic and copies ran while one was open for 1% -> 2% of each run, Pallas kernels for 0% -> 5%
where the time goes in v1:
time: 627 us; the launch traced here: 626 us
  waiting for transfers between devices  360 us (57%)
  Pallas kernels  190 us (30%)
  local copies, waits for them, and re-layouts  30.8 us (5%)
  between operations  20.1 us (3%)
  starting transfers between devices  15.4 us (2%)
  other arithmetic  9.49 us (2%)
    psum x2, waiting for transfers between devices, big_sum(): return lax.psum(arrays, 'dp')  349 us
    pallas_call x13, Pallas kernels, run(): pl.pallas_call(body, grid=grid, in_specs=in_specs, out_specs=out_specs, o...  190 us
    unnamed x80, local copies, waits for them, and re-layouts  28.4 us
    ppermute x10, starting transfers between devices, small_sum(): lax.ppermute(values, 'dp', [(i, i ^ bit) for i in range(devices)])  15.3 us
  transfers between devices with their start and end apart: 12, of which 10 were waited for; matrix products, arithmetic and copies ran while one was open for 2% of the time, Pallas kernels for 5%

profile of v1, /device:TPU:0, one launch (start us, length us, event | category | flops | bytes accessed | tf_op | source)
XLA Modules:
  0.0 626.2 jit_solution(15219077048069915890)
XLA Ops:
  7.3 2.8 copy.45.mel_ref
  10.1 3.0 stats.1
  13.0 0.5 collective-permute-start
  13.5 1.0 collective-permute-done
  14.5 0.7 add.75
  15.2 2.8 collective-permute-start.1
  18.1 1.6 collective-permute-done.1
  19.6 2.1 collective-permute-start.2
  21.7 1.6 collective-permute-done.2
  23.3 2.1 collective-permute-start.3
  25.4 1.6 collective-permute-done.3
  26.9 3.0 collective-permute-start.4
  30.0 0.7 copy.41.prior_ref
  30.7 0.7 copy.42.end_ref
  31.5 1.4 copy.43.ff2_ref
  32.9 3.0 weights.1
  35.8 14.7 %attention.1 = (bf16[4,256,192]{2,1,0:T(8,128)(2,1)}, bf16[4,256,768]{2,1,0:T(8,128)(2,1)}, f32[4,2,256,256]{3,2,1,0:T(8,128)}, bf16[4,2,256,128]{3,2,1,0:T(8,12...) custom-call(s32[4,256]{1,0:T(4,128)} %tok_ref.3, s32[4,256]{1,0:T(4,128)} %dur_ref.23, ...), custom_call_target="tpu_custom_call" | custom-call | bytes 1048576 | tf_op jit(solution)/shard_map/attention/pallas_call | solution.py:88
  50.6 10.7 %feed.1 = (f32[4,256,768]{2,1,0:T(8,128)}, bf16[4,256,768]{2,1,0:T(8,128)(2,1)}, f32[4,256,192]{2,1,0:T(8,128)}, bf16[4,256,192]{2,1,0:T(8,128)(2,1)}, bf16[4,51...) custom-call(s32[4,256]{1,0:T(4,128)} %dur_ref.23, f32[4,256,192]{2,1,0:T(8,128)} %get-tuple-element.86.normed_ref, ...), custom_call_target="tpu_custom_call" | custom-call | bytes 1048576 | tf_op jit(solution)/shard_map/feed/pallas_call | solution.py:88
  61.3 0.6 add.79.stats_ref
  61.9 36.3 %flow.1 = (f32[4,512,256]{2,1,0:T(8,128)}, bf16[4,512,128]{2,1,0:T(8,128)(2,1)}, bf16[4,4,512,192]{3,2,1,0:T(8,128)(2,1)}, f32[4,4,512,384]{3,2,1,0:T(8,128)}, b...) custom-call(f32[4,1024,80]{2,1,0:T(8,128)} %copy.45.mel_ref, ...), custom_call_target="tpu_custom_call" | custom-call | bytes 1048576 | tf_op jit(solution)/shard_map/flow/pallas_call | solution.py:88
  98.2 12.1 %layer3.1 = (f32[4,512,192]{2,1,0:T(8,128)}, f32[960,384]{1,0:T(8,128)}, f32[192,192]{1,0:T(8,128)}) custom-call(s32[4,256]{1,0:T(4,128)} %dur_ref.23, bf16[4,512,192]{2,1,0:T(8,128)(2,1)} %get-tuple-element.93.refs_0_, f32[4,4,512,384]{3,2,1,0:T(8,128)} %get-tuple-element.94.refs_1_, bf16[4,4,512,192]{3,2,1,0:T(8,128)(2,1)} %get-tuple-element.95.refs_2_, ...), custom_call_target="tpu_custom_call" | custom-call | bytes 1048576 | tf_op jit(solution)/shard_map/layer3/pallas_call | solution.py:88
  110.3 14.5 %layer2.1 = (f32[4,512,192]{2,1,0:T(8,128)}, f32[960,384]{1,0:T(8,128)}, f32[192,384]{1,0:T(8,128)}) custom-call(s32[4,256]{1,0:T(4,128)} %dur_ref.23, bf16[4,512,192]{2,1,0:T(8,128)(2,1)} %get-tuple-element.93.refs_0_, f32[4,4,512,384]{3,2,1,0:T(8,128)} %get-tuple-element.94.refs_1_, bf16[4,4,512,192]{3,2,1,0:T(8,128)(2,1)} %get-tuple-element.95.refs_2_, ...), custom_call_target="tpu_custom_call" | custom-call | bytes 1048576 | tf_op jit(solution)/shard_map/layer2/pallas_call | solution.py:88
  124.8 14.7 %layer1.1 = (f32[4,512,192]{2,1,0:T(8,128)}, f32[960,384]{1,0:T(8,128)}, f32[192,384]{1,0:T(8,128)}) custom-call(s32[4,256]{1,0:T(4,128)} %dur_ref.23, bf16[4,512,192]{2,1,0:T(8,128)(2,1)} %get-tuple-element.93.refs_0_, f32[4,4,512,384]{3,2,1,0:T(8,128)} %get-tuple-element.94.refs_1_, bf16[4,4,512,192]{3,2,1,0:T(8,128)(2,1)} %get-tuple-element.95.refs_2_, ...), custom_call_target="tpu_custom_call" | custom-call | bytes 1048576 | tf_op jit(solution)/shard_map/layer1/pallas_call | solution.py:88
  139.5 14.5 %layer0.1 = (f32[4,512,192]{2,1,0:T(8,128)}, f32[960,384]{1,0:T(8,128)}, f32[192,384]{1,0:T(8,128)}) custom-call(s32[4,256]{1,0:T(4,128)} %dur_ref.23, bf16[4,512,192]{2,1,0:T(8,128)(2,1)} %get-tuple-element.93.refs_0_, f32[4,4,512,384]{3,2,1,0:T(8,128)} %get-tuple-element.94.refs_1_, bf16[4,4,512,192]{3,2,1,0:T(8,128)(2,1)} %get-tuple-element.95.refs_2_, ...), custom_call_target="tpu_custom_call" | custom-call | bytes 1048576 | tf_op jit(solution)/shard_map/layer0/pallas_call | solution.py:88
  154.0 13.1 %mix.1 = (f32[4,512,256]{2,1,0:T(8,128)}, f32[80,192]{1,0:T(8,128)}, f32[8,128]{1,0:T(8,128)}, f32[8,128]{1,0:T(8,128)}) custom-call(s32[4,256]{1,0:T(4,128)} %dur_ref.23, f32[4,512,192]{2,1,0:T(8,128)} %get-tuple-element.99.hgrad_ref, bf16[4,512,128]{2,1,0:T(8,128)(2,1)} %get-tuple-element.100.passive_ref, f32[4,512,128]{2,1,0:T(8,128)} %get-tuple-element.101.lgrad_ref, ...), custom_call_target="tpu_custom_call" | custom-call | bytes 1048576 | tf_op jit(solution)/shard_map/mix/pallas_call | solution.py:88
  167.2 1.3 slice.34
  168.5 2.8 pad_maximum_fusion
  171.2 28.3 %feed_back.1 = (f32[4,256,192]{2,1,0:T(8,128)}, f32[192,160]{1,0:T(8,128)}, f32[576,768]{1,0:T(8,128)}, f32[2304,192]{1,0:T(8,128)}, f32[1,192]{1,0:T(1,128)}, /*index=5*/f32[1,192]{1,0:T(1,128)}) custom-call(s32[4,256]{1,0:T(4,128)} %dur_ref.23, f32[4,512,512]{2,1,0:T(8,128)} %get-tuple-element.108.flow_ref, bf16[160,1024]{1,0:T(8,128)(2,1)} %get-tuple-element.109.wide_ref, ...), custom_call_target="tpu_custom_call" | custom-call | bytes 1048576 | tf_op jit(solution)/shard_map/feed_back/pallas_call | solution.py:88
  199.6 20.7 %attention_back.1 = (f32[148,192]{1,0:T(8,128)}, f32[192,576]{1,0:T(8,128)}, f32[9,96]{1,0:T(8,128)}, f32[9,96]{1,0:T(8,128)}, f32[192,192]{1,0:T(8,128)}, /*index=5*/f32[1,192]{1,0:T(1,128)}, f32[1,192]{1,0:T(1,128)}) custom-call(s32[4,256]{1,0:T(4,128)} %tok_ref.3, s32[4,256]{1,0:T(4,128)} %dur_ref.23, f32[4,256,192]{2,1,0:T(8,128)} %get-tuple-element.114.ngrad_ref, ...), custom_call_target="tpu_custom_call" | custom-call | bytes 1048576 | tf_op jit(solution)/shard_map/attention_back/pallas_call | solution.py:88
  220.4 1.0 pad_maximum_fusion.1
  221.4 0.6 copy-done.24
  222.1 1.2 collective-permute-done.5
  223.3 1.6 collective-permute-start.6
  224.8 2.1 collective-permute-done.6
  227.0 1.5 collective-permute-start.7
  228.5 2.1 collective-permute-done.7
  230.6 1.6 collective-permute-start.8
  232.2 0.5 slice.33
  233.5 0.5 slice.30
  234.3 1.3 multiply_reduce_fusion
  238.9 0.6 add.84.sums_ref
  239.5 4.8 frames.1
  244.3 2.7 copy.50
  247.0 1.3 slice_reduce_fusion
  248.9 94.8 %all-reduce.5.cloned.1.call-done = (f32[9,96]{1,0:T(8,128)}, f32[9,96]{1,0:T(8,128)}, f32[192]{0:T(256)}, f32[192]{0:T(256)}, f32[192]{0:T(256)}, /*index=5*/f32[192]{0:T(256)}, f32[4,4]{1,0:T(4,128)}, f32[80,192]{1,0:T(8,128)}) async-done(((f32[9,96]{1,0:T(8,128)}, f32[9,96]{1,0:T(8,128)}, f32[192]{0:T(256)}, f32[192]{0:T(256)}, f32[192]{0:T(256)}, /*index=5*/f32[192]{0:T(256)}, f32[4,4]{1,0:T(4,128)}, ...) | async-done | bytes 71504 | tf_op jit(solution)/shard_map/psum | solution.py:818
  343.7 1.3 fusion.1
  345.0 253.9 %all-reduce.7.cloned.1.call-done = (f32[148,192]{1,0:T(8,128)}, f32[192,576]{1,0:T(8,128)}, f32[192,192]{1,0:T(8,128)}, f32[576,768]{1,0:T(8,128)}, f32[2304,192...) async-done(((f32[148,192]{1,0:T(8,128)}, f32[192,576]{1,0:T(8,128)}, ...) | async-done | bytes 11418640 | tf_op jit(solution)/shard_map/psum | solution.py:818
  598.9 3.0 copy.51
  601.9 0.8 copy.52
  602.7 0.8 copy.53
  603.5 0.7 copy.72
  604.1 0.8 copy.73
  604.9 0.6 copy.74
  605.5 0.6 copy.75
  606.1 0.7 copy.76
  606.8 0.6 copy.77
  607.4 0.6 copy.78
  607.9 1.2 copy.79
  609.1 0.6 copy.80
  609.7 0.6 copy.81
  610.3 0.6 copy.82
  610.9 5.7 copy.83
  616.6 0.9 copy.84
  617.6 0.7 copy.85
  (77 shorter events, 0.8 us)
Async XLA Ops:
  7.2 22.8 %copy-start.16 = (bf16[192,160]{0,1:T(8,128)(2,1)S(1)}, bf16[192,160]{0,1:T(8,128)(2,1)}, u32[]{:S(2)}) copy-start(bf16[192,160]{0,1:T(8,128)(2,1)} %param.35) | copy-start | bytes 184324
  7.2 23.5 %copy-start.17 = (bf16[192,160]{0,1:T(8,128)(2,1)S(1)}, bf16[192,160]{0,1:T(8,128)(2,1)}, u32[]{:S(2)}) copy-start(bf16[192,160]{0,1:T(8,128)(2,1)} %param.41) | copy-start | bytes 184324
  7.2 336.5 %all-reduce.5.cloned.1.call-start = ((), (), s32[]{:S(2)}) async-start(), calls=%async_computation | async-start | bytes 208896 | tf_op jit(solution)/shard_map/psum | solution.py:818
  10.1 21.4 %copy-start.6 = (bf16[2304,192]{0,1:T(8,128)(2,1)S(1)}, bf16[2304,192]{0,1:T(8,128)(2,1)}, u32[]{:S(2)}) copy-start(bf16[2304,192]{0,1:T(8,128)(2,1)} %param.32) | copy-start | bytes 2654212
  13.0 1.5 collective-permute-start
  15.2 4.4 collective-permute-start.1
  19.6 3.6 collective-permute-start.2
  23.3 3.7 collective-permute-start.3
  26.9 34.3 %collective-permute-start.4 = (f32[8,128]{1,0:T(8,128)S(1)}, f32[8,128]{1,0:T(8,128)S(1)}, u32[]{:S(2)}, u32[]{:S(2)}) collective-permute-start(f32[8,128]{1,0:T(8,128)S(1)} %add.78), channel_id=1, source_target_pairs={{0,16},{1,17},{2,18},{3,19},{4,20},{5,21},{6,22},{7,23},{8,24},{9,... | collective-permute-start | bytes 12296 | tf_op jit(solution)/shard_map/ppermute | solution.py:812
  154.0 14.4 %copy-start.1 = (f32[960,384]{1,0:T(8,128)S(1)}, f32[960,384]{1,0:T(8,128)}, u32[]{:S(2)}) copy-start(f32[960,384]{1,0:T(8,128)} %get-tuple-element.138) | copy-start | bytes 4423684
  154.0 14.4 %copy-start.2 = (f32[960,384]{1,0:T(8,128)S(1)}, f32[960,384]{1,0:T(8,128)}, u32[]{:S(2)}) copy-start(f32[960,384]{1,0:T(8,128)} %get-tuple-element.137) | copy-start | bytes 4423684
  154.0 14.4 %copy-start.3 = (f32[960,384]{1,0:T(8,128)S(1)}, f32[960,384]{1,0:T(8,128)}, u32[]{:S(2)}) copy-start(f32[960,384]{1,0:T(8,128)} %get-tuple-element.136) | copy-start | bytes 4423684
  154.0 14.4 %copy-start.4 = (f32[960,384]{1,0:T(8,128)S(1)}, f32[960,384]{1,0:T(8,128)}, u32[]{:S(2)}) copy-start(f32[960,384]{1,0:T(8,128)} %get-tuple-element.135) | copy-start | bytes 4423684
  199.5 20.8 %copy-start.8 = (f32[192,384]{1,0:T(8,128)S(1)}, f32[192,384]{1,0:T(8,128)}, u32[]{:S(2)}) copy-start(f32[192,384]{1,0:T(8,128)} %get-tuple-element.141) | copy-start | bytes 884740
  199.6 20.8 %copy-start.9 = (f32[192,384]{1,0:T(8,128)S(1)}, f32[192,384]{1,0:T(8,128)}, u32[]{:S(2)}) copy-start(f32[192,384]{1,0:T(8,128)} %get-tuple-element.140) | copy-start | bytes 884740
  199.6 20.8 %copy-start.10 = (f32[192,384]{1,0:T(8,128)S(1)}, f32[192,384]{1,0:T(8,128)}, u32[]{:S(2)}) copy-start(f32[192,384]{1,0:T(8,128)} %get-tuple-element.139) | copy-start | bytes 884740
  220.3 378.6 %all-reduce.7.cloned.1.call-start = ((), (), s32[]{:S(2)}) async-start(), calls=%async_computation.1 | async-start | bytes 24690688 | tf_op jit(solution)/shard_map/psum | solution.py:818
  221.3 0.7 copy-start.24
  221.3 0.7 copy-start.23
  221.3 10.8 %copy-start.22 = (f32[8,128]{1,0:T(8,128)S(1)}, f32[8,128]{1,0:T(8,128)}, u32[]{:S(2)}) copy-start(f32[8,128]{1,0:T(8,128)} %get-tuple-element.106) | copy-start | bytes 12292
  221.4 12.1 %copy-start.19 = (f32[8,128]{1,0:T(8,128)S(1)}, f32[8,128]{1,0:T(8,128)}, u32[]{:S(2)}) copy-start(f32[8,128]{1,0:T(8,128)} %add.79.stats_ref) | copy-start | bytes 12292
  222.0 1.2 collective-permute-start.5
  223.3 3.7 collective-permute-start.6
  227.0 3.6 collective-permute-start.7
  230.6 3.6 collective-permute-start.8
  234.2 4.7 collective-permute-start.9
  598.9 3.0 copy-start.14
  598.9 3.8 copy-start.13
  598.9 4.6 copy-start.15
  598.9 5.3 copy-start.7
  598.9 6.0 copy-start.21
  598.9 6.7 %copy-start.20 = (f32[9,96]{1,0:T(8,128)S(1)}, f32[9,96]{1,0:T(8,128)}, u32[]{:S(2)}) copy-start(f32[9,96]{1,0:T(8,128)} %get-tuple-element.187) | copy-start | bytes 10372
  598.9 7.2 %copy-start.12 = (f32[192,192]{1,0:T(8,128)S(1)}, f32[192,192]{1,0:T(8,128)}, u32[]{:S(2)}) copy-start(f32[192,192]{1,0:T(8,128)} %get-tuple-element.188) | copy-start | bytes 442372
  601.9 4.9 copy-start.28
  601.9 5.5 copy-start.27
  601.9 6.0 copy-start
  604.9 4.2 copy-start.26
  604.9 4.8 copy-start.25
  604.9 5.4 copy-start.18
  610.9 5.7 copy-start.5
  610.9 6.6 %copy-start.11 = (f32[192,192]{1,0:T(8,128)S(1)}, f32[192,192]{1,0:T(8,128)}, u32[]{:S(2)}) copy-start(f32[192,192]{1,0:T(8,128)} %get-tuple-element.200) | copy-start | bytes 442372
Sparse Core Ops, SparseCore 0:
  220.4 123.2 all-reduce.4
  353.0 245.7 all-reduce.6

commit v2 on v1

v2 whole, which is shorter than its diff:
```python
import functools
import math

import jax
import jax.numpy as jnp
from jax import lax
from jax.experimental import pallas as pl
from jax.experimental.pallas import tpu as pltpu
from jax.sharding import PartitionSpec as P

D = 192
HEADS = 2
HEAD = 96
LANES = 128
FILTER = 768
MEL = 80
HID = 192
VOCAB = 148
KSIZE = 3
WKER = 5
WLAYERS = 4
WINDOW = 4
PERIOD = 16

F32 = jnp.float32
BF16 = jnp.bfloat16
HIGH = lax.Precision.HIGHEST
VMEM_BYTES = 58 * 1024 * 1024
WIDE = 384
UNIT = 1152
REST = 768
TAIL = 384
COST = 0.1e9
ROW_TABLE = 2 * D
ROW_PRIOR = ROW_TABLE + MEL
ROW_NORM = ROW_PRIOR + MEL
ROW_REL = ROW_NORM + 8


def contract(first_op, second_op, dims, precision=None):
    return lax.dot_general(
        first_op, second_op, (dims, ((), ())), preferred_element_type=F32, precision=precision
    )


def dot_nn(first_op, second_op, precision=None):
    return contract(first_op, second_op, ((1,), (0,)), precision)


def dot_nt(first_op, second_op, precision=None):
    return contract(first_op, second_op, ((1,), (1,)), precision)


def dot_tn(first_op, second_op, precision=None):
    return contract(first_op, second_op, ((0,), (0,)), precision)


def halves(values):
    high = values.astype(BF16)
    low = (values - high.astype(F32)).astype(BF16)
    return high, low


def iota(shape, axis):
    return lax.broadcasted_iota(jnp.int32, shape, axis)


def rows_of(length):
    return iota((length, 1), 0)


def full_spec(array):
    rank = len(array.shape)
    return pl.BlockSpec(array.shape, lambda *_: (0,) * rank)


def item_spec(array):
    rank = len(array.shape)
    return pl.BlockSpec((1,) + array.shape[1:], lambda b: (b,) + (0,) * (rank - 1))


def layer_spec(array, layer):
    rank = len(array.shape)
    return pl.BlockSpec((1, 1) + array.shape[2:], lambda b: (layer, b) + (0,) * (rank - 2))


def weight_spec(array, layer):
    rank = len(array.shape)
    return pl.BlockSpec((1,) + array.shape[1:], lambda b: (layer,) + (0,) * (rank - 1))


def shape_of(shape, dtype=F32):
    return jax.ShapeDtypeStruct(shape, dtype)


def run(body, grid, ins, in_specs, outs, out_specs, scratch=(), micros=5, after=(), aliases=None, name=None):
    count, extra = len(ins), len(after)

    def wrapped(*refs):
        body(*refs[:count], *refs[count + extra :])

    return pl.pallas_call(
        wrapped,
        grid=grid,
        in_specs=list(in_specs) + [pl.BlockSpec(memory_space=pl.ANY)] * extra,
        out_specs=out_specs,
        out_shape=outs,
        scratch_shapes=list(scratch),
        compiler_params=pltpu.CompilerParams(vmem_limit_bytes=VMEM_BYTES),
        cost_estimate=pl.CostEstimate(
            flops=int(micros * COST), bytes_accessed=1 << 10, transcendentals=0
        ),
        input_output_aliases=aliases or {},
        name=name,
    )(*ins, *after)


def pair_rows(durations_row):
    return jnp.sum(durations_row, axis=1, keepdims=True) >> 1


def stats_body(mel_ref, dur_ref, out_ref):
    items, _, frames = mel_ref.shape
    lane = iota((1, frames), 1)
    count = jnp.zeros((1, 1), F32)
    sums = jnp.zeros((MEL, LANES), F32)
    squares = jnp.zeros((MEL, LANES), F32)
    for item in range(items):
        pair_count = pair_rows(dur_ref[item : item + 1, :])
        count = count + pair_count.astype(F32)
        values = jnp.where(lane < 2 * pair_count, mel_ref[item], 0.0)
        for part in range(frames // LANES):
            piece = values[:, part * LANES : (part + 1) * LANES]
            sums = sums + piece
            squares = squares + piece * piece
    place = iota((MEL, LANES), 1)
    table = jnp.zeros((MEL, LANES), F32)
    for side in range(2):
        chosen = (place & 1) == side
        for spot, held in ((side, sums), (2 + side, squares)):
            column = jnp.sum(jnp.where(chosen, held, 0.0), axis=1, keepdims=True)
            table = jnp.where(place == spot, column, table)
    table = jnp.concatenate([table, jnp.zeros((LANES - MEL, LANES), F32)], axis=0)
    rows = table.T[0:8]
    out_ref[...] = jnp.where(iota((8, LANES), 0) == 4, count, rows)


def read_stats(stats):
    total = stats[4:5, 0:1]
    sums = jnp.concatenate([stats[0:1], stats[1:2]], axis=1)
    squares = jnp.concatenate([stats[2:3], stats[3:4]], axis=1)
    center = sums / total
    variance = squares / total - center * center
    log_act = -0.5 * jnp.log(variance + 1e-06)
    return total, center, variance, log_act, jnp.exp(log_act)


def mix_places():
    row = rows_of(2 * LANES)
    col = iota((1, 2 * LANES), 1)
    row_lane = row & (LANES - 1)
    col_lane = col & (LANES - 1)
    upper = (row_lane >= MEL // 2).astype(jnp.int32)
    row_group = row_lane - upper * (MEL // 2)
    row_member = 2 * upper + (row >> 7)
    col_group = col_lane >> 1
    col_member = 2 * (col >> 7) + (col_lane & 1)
    match = (row_group == col_group) & (row_lane < MEL) & (col_lane < MEL)
    return row_member, col_member, match


def weights_body(
    mix_ref,
    qkv_ref,
    relk_ref,
    relv_ref,
    out_ref,
    prior_ref,
    start_ref,
    end_ref,
    res_ref,
    last_ref,
    mixm_ref,
    small_ref,
    qkv_pad_ref,
    relk_pad_ref,
    relv_pad_ref,
    out_pad_ref,
    wide_ref,
    prior_pad_ref,
    start_pad_ref,
    end_pad_ref,
    res_four_ref,
):
    row_member, col_member, match = mix_places()
    table = jnp.zeros((2 * LANES, 2 * LANES), F32)
    for i in range(4):
        column = jnp.zeros((2 * LANES, 1), F32)
        for j in range(4):
            column = jnp.where(row_member == j, mix_ref[i, j], column)
        table = jnp.where(col_member == i, column, table)
    mixm_ref[...] = jnp.where(match, table, 0.0)
    res_four_ref[: WLAYERS - 1] = res_ref[...]
    res_four_ref[WLAYERS - 1] = jnp.concatenate(
        [jnp.zeros((HID, HID), F32), last_ref[...].astype(F32)], axis=1
    ).astype(BF16)

    ri = iota((8, LANES), 0)
    ci = iota((8, LANES), 1)
    joined = jnp.where((ci == ri + 4) & (ri < 4), 1.0, 0.0).astype(F32)
    for i in range(4):
        for j in range(4):
            joined = jnp.where((ri == i) & (ci == j), mix_ref[i, j], joined)
    determinant = jnp.ones((1, 1), F32)
    for column in range(4):
        pivot = joined[column : column + 1, column : column + 1]
        determinant = determinant * pivot
        row_now = joined[column : column + 1, :] / pivot
        joined = joined - joined[:, column : column + 1] * row_now
        joined = jnp.where(ri == column, row_now, joined)
    turned = jnp.zeros((8, LANES), F32)
    for i in range(4):
        for j in range(4):
            turned = jnp.where((ri == j) & (ci == i), joined[i : i + 1, 4 + j : 5 + j], turned)
    small_ref[...] = jnp.where(ri == 4, determinant, turned)

    def select(count, wanted):
        return jnp.where(rows_of(count) == wanted, 1.0, 0.0).astype(BF16)

    place = iota((1, 6 * LANES), 1)
    lane = place & (LANES - 1)
    wanted = jnp.where(lane < HEAD, (place >> 7) * HEAD + lane, -1)
    qkv_pad_ref[...] = dot_nn(qkv_ref[...], select(3 * D, wanted)).astype(BF16)

    place = iota((1, 2 * LANES), 1)
    lane = place & (LANES - 1)
    wanted = jnp.where(lane < HEAD, (place >> 7) * HEAD + lane, -1)
    out_pad_ref[...] = dot_tn(select(D, wanted), out_ref[...]).astype(BF16)

    wanted = iota((1, LANES), 1) & (PERIOD - 1)
    repeat = select(2 * WINDOW + 1, wanted)
    pad = jnp.zeros((LANES, LANES - HEAD), F32)
    relk_pad_ref[...] = jnp.concatenate([dot_tn(repeat, relk_ref[...]), pad], axis=1).astype(BF16)
    relv_pad_ref[...] = jnp.concatenate([dot_tn(repeat, relv_ref[...]), pad], axis=1).astype(BF16)

    place = iota((1, 8 * LANES), 1)
    lane = place & (LANES - 1)
    group = (place >> 7) & 3
    fits = (lane < MEL) & ((lane & 1) == (place >> 9))
    wanted = jnp.where(fits, (group >> 1) * MEL + (group & 1) * (MEL // 2) + (lane >> 1), -1)
    wide = select(2 * MEL, wanted)
    wide_ref[...] = wide
    prior_pad_ref[...] = dot_tn(prior_ref[...], wide).astype(BF16)

    wanted = iota((1, LANES), 1)
    start_pad_ref[...] = dot_tn(select(MEL, wanted), start_ref[...]).astype(BF16)
    place = iota((1, 2 * LANES), 1)
    lane = place & (LANES - 1)
    wanted = jnp.where(lane < MEL, (place >> 7) * MEL + lane, -1)
    end_pad_ref[...] = dot_tn(end_ref[...], select(2 * MEL, wanted)).astype(BF16)


def text_rows(dur_ref):
    item = pl.program_id(0)
    return dur_ref[pl.ds(item, 1), :]


def text_inside(durations_row, length):
    tokens = jnp.sum((durations_row > 0).astype(jnp.int32), axis=1, keepdims=True)
    return rows_of(length) < tokens


def norm_parts(inputs):
    centered = inputs - jnp.mean(inputs, axis=1, keepdims=True)
    spread = jnp.mean(centered * centered, axis=1, keepdims=True)
    inverse = lax.rsqrt(spread + 1e-05)
    return centered * inverse, inverse


def norm_back(inputs, gain, gradient):
    unit, inverse = norm_parts(inputs)
    gain_grad = jnp.sum(gradient * unit, axis=0, keepdims=True)
    shift_grad = jnp.sum(gradient, axis=0, keepdims=True)
    scaled = gradient * gain
    mean_one = jnp.mean(scaled, axis=1, keepdims=True)
    mean_two = jnp.mean(scaled * unit, axis=1, keepdims=True)
    return inverse * (scaled - mean_one - unit * mean_two), gain_grad, shift_grad


def band_of(length):
    offset = iota((length, length), 1) - iota((length, length), 0)
    return (offset <= WINDOW) & (offset >= -WINDOW)


def turn_rows(values, left):
    length = values.shape[0]
    step = rows_of(length) & (PERIOD - 1)
    first = WINDOW if left else LANES - WINDOW
    values = pltpu.roll(values, first, 1)
    for bit in (1, 2, 4, 8):
        moved = pltpu.roll(values, (LANES - bit) if left else bit, 1)
        values = jnp.where((step & bit) != 0, moved, values)
    return values


def band_gather(weights_low, band, folding):
    kept = jnp.where(band, weights_low, jnp.zeros_like(weights_low))
    return turn_rows(dot_nn(kept, folding), True).astype(BF16)


def band_spread(near, band):
    turned = turn_rows(near, False)
    count = band.shape[1] // LANES
    return jnp.where(band, jnp.concatenate([turned] * count, axis=1), 0.0)


def folding_of(length):
    same = (iota((length, LANES), 0) & (PERIOD - 1)) == (iota((length, LANES), 1) & (PERIOD - 1))
    return jnp.where(same, 1.0, 0.0).astype(BF16)


def one_turn(rel_pad):
    return jnp.where(rows_of(LANES) < PERIOD, rel_pad, jnp.zeros_like(rel_pad))


def attention_body(
    tok_ref,
    dur_ref,
    emb_ref,
    qkv_ref,
    relk_ref,
    relv_ref,
    out_ref,
    gain_ref,
    shift_ref,
    emb_low_ref,
    proj_ref,
    att_ref,
    banded_ref,
    attend_ref,
    mixed_ref,
    normed_ref,
):
    item = pl.program_id(0)
    tokens = tok_ref[pl.ds(item, 1), :]
    durations = text_rows(dur_ref)
    length = tokens.shape[1]
    inside = text_inside(durations, length)
    hot = jnp.where(iota((VOCAB, length), 0) == tokens, 1.0, 0.0).astype(BF16)
    embedded = jnp.where(inside, dot_tn(hot, emb_ref[...]) * math.sqrt(D), 0.0)
    emb_low = embedded.astype(BF16)
    emb_low_ref[0] = emb_low
    proj = dot_nn(emb_low, qkv_ref[...]).astype(BF16)
    proj_ref[0] = proj
    key_bias = jnp.where(durations > 0, 0.0, -10000.0)
    band = band_of(length)
    folding = folding_of(length)
    relv = one_turn(relv_ref[...])
    parts = []
    for head in range(HEADS):
        query = proj[:, head * LANES : (head + 1) * LANES]
        key = proj[:, (HEADS + head) * LANES : (HEADS + head + 1) * LANES]
        value = proj[:, (2 * HEADS + head) * LANES : (2 * HEADS + head + 1) * LANES]
        near = band_spread(dot_nt(query, relk_ref[...]), band)
        scores = (dot_nt(query, key) + near) / math.sqrt(HEAD) + key_bias
        raised = jnp.exp(scores - jnp.max(scores, axis=1, keepdims=True))
        attention = raised / jnp.sum(raised, axis=1, keepdims=True)
        att_ref[0, head] = attention
        low = attention.astype(BF16)
        banded = band_gather(low, band, folding)
        banded_ref[0, head] = banded
        parts.append(dot_nn(low, value) + dot_nn(banded, relv))
    attend = jnp.concatenate(parts, axis=1).astype(BF16)
    attend_ref[0] = attend
    mixed = embedded + dot_nn(attend, out_ref[...])
    mixed_ref[0] = mixed
    unit, _ = norm_parts(mixed)
    normed_ref[0] = unit * gain_ref[...] + shift_ref[...]


def shifted(values, offset):
    if offset == 0:
        return values
    length = values.shape[0]
    moved = pltpu.roll(values, (-offset) % length, 0)
    place = rows_of(length)
    keep = (place < length - offset) if offset > 0 else (place >= -offset)
    return jnp.where(keep, moved, 0.0)


def unfold(values, kernel, reverse=False):
    half = kernel // 2
    steps = [step - half for step in range(kernel)]
    if reverse:
        steps = [-step for step in steps]
    return jnp.concatenate([shifted(values, step).astype(BF16) for step in steps], axis=1)


GELU_A = math.sqrt(2.0 / math.pi)
GELU_B = 0.044715


def gelu_tanh(values):
    return jnp.tanh(GELU_A * (values + GELU_B * values * values * values))


def feed_body(
    dur_ref,
    normed_ref,
    ff1_ref,
    ff2_ref,
    gain_ref,
    shift_ref,
    prior_ref,
    filt_ref,
    activ_ref,
    summed_ref,
    enc_ref,
    expand_ref,
    expand_low_ref,
):
    durations = text_rows(dur_ref)
    normed = normed_ref[0]
    length = normed.shape[0]
    inside = text_inside(durations, length)
    filtered = dot_nn(unfold(jnp.where(inside, normed, 0.0), KSIZE), ff1_ref[...])
    filt_ref[0] = filtered
    activ = jnp.where(inside, 0.5 * filtered * (1.0 + gelu_tanh(filtered)), 0.0)
    activ_ref[0] = activ.astype(BF16)
    summed = normed + jnp.where(inside, dot_nt(unfold(activ, KSIZE), ff2_ref[...]), 0.0)
    summed_ref[0] = summed
    unit, _ = norm_parts(summed)
    encoded = jnp.where(inside, unit * gain_ref[...] + shift_ref[...], 0.0).astype(BF16)
    enc_ref[0] = encoded
    prior = dot_nn(encoded, prior_ref[...])
    wide = prior.shape[1] // 2
    high, low = halves(prior)
    expand_ref[0, :length] = high[:, :wide]
    expand_ref[0, length:] = high[:, wide:]
    expand_low_ref[0, :length] = low[:, :wide]
    expand_low_ref[0, length:] = low[:, wide:]


def accumulate(ref, values, first):
    @pl.when(first)
    def _():
        ref[...] = values

    @pl.when(jnp.logical_not(first))
    def _():
        ref[...] = ref[...] + values


def align_of(durations_row, pairs):
    length = durations_row.shape[1]
    upper = jnp.where(iota((length, length), 0) <= iota((length, length), 1), 1.0, 0.0).astype(F32)
    wide = jnp.broadcast_to(durations_row.astype(F32), (8, length))
    ends = dot_nn(wide, upper, HIGH)[0:1].astype(jnp.int32)
    starts = ends - durations_row
    frame = 2 * rows_of(pairs)
    even = (frame >= starts) & (frame < ends)
    odd = (frame + 1 >= starts) & (frame + 1 < ends)
    both = jnp.concatenate([jnp.where(even, 1.0, 0.0), jnp.where(odd, 1.0, 0.0)], axis=1)
    return both.astype(BF16)


def feed_back_body(
    dur_ref,
    flow_ref,
    wide_ref,
    enc_ref,
    summed_ref,
    filt_ref,
    activ_ref,
    normed_ref,
    ff1_ref,
    ff2_ref,
    gain_ref,
    prior_ref,
    place_ref,
    ngrad_ref,
    prior_out_ref,
    gain_out_ref,
    shift_out_ref,
    one_kept_ref,
    one_sent_ref,
    two_kept_ref,
    two_sent_ref,
    out_ref,
):
    first = pl.program_id(0) == 0
    durations = text_rows(dur_ref)
    length = durations.shape[1]
    inside = text_inside(durations, length)
    flow = flow_ref[0]
    align = align_of(durations, flow.shape[0])
    spread = dot_tn(align, flow)
    half = wide_ref.shape[1] // 2
    grad = jnp.zeros((length, 2 * MEL), F32)
    for side in range(2):
        part_high, part_low = halves(spread[side * length : (side + 1) * length])
        chosen = wide_ref[:, side * half : (side + 1) * half]
        grad = grad + dot_nt(part_high, chosen) + dot_nt(part_low, chosen)
    prior_low = jnp.where(inside, grad, 0.0).astype(BF16)
    accumulate(prior_out_ref, dot_tn(prior_low, enc_ref[0]), first)
    enc_grad = jnp.where(inside, dot_nn(prior_low, prior_ref[...]), 0.0)
    summed_grad, gain_grad, shift_grad = norm_back(summed_ref[0], gain_ref[...], enc_grad)
    accumulate(gain_out_ref, gain_grad, first)
    accumulate(shift_out_ref, shift_grad, first)
    second = jnp.where(inside, summed_grad, 0.0)
    activ = activ_ref[0]
    activ_grad = jnp.zeros((length, FILTER), F32)
    for step in range(KSIZE):
        moved = shifted(second, KSIZE // 2 - step).astype(BF16)
        columns = slice(step * FILTER, (step + 1) * FILTER)
        activ_grad = activ_grad + dot_nn(moved, ff2_ref[:, columns])
        sums = dot_tn(moved, activ)
        for part in range(2):
            begin = UNIT + (2 * step + part) * D
            accumulate(
                out_ref.at[begin : begin + D, :], sums[:, part * WIDE : (part + 1) * WIDE], first
            )
    filtered = filt_ref[0]
    tanh = gelu_tanh(filtered)
    slope = 0.5 * (1.0 + tanh) + 0.5 * filtered * (1.0 - tanh * tanh) * GELU_A * (
        1.0 + 3.0 * GELU_B * filtered * filtered
    )
    first_grad = jnp.where(inside, activ_grad * slope, 0.0)
    normed_low = jnp.where(inside, normed_ref[0], 0.0).astype(BF16)
    back = jnp.zeros((length, D), F32)
    for step in range(KSIZE):
        moved = shifted(first_grad, KSIZE // 2 - step).astype(BF16)
        rows = slice(step * D, (step + 1) * D)
        back = back + dot_nt(moved, ff1_ref[rows, :])
        sums = dot_tn(normed_low, moved)
        for part in range(2):
            begin = part * KSIZE * D + step * D
            accumulate(
                out_ref.at[begin : begin + D, :], sums[:, part * WIDE : (part + 1) * WIDE], first
            )
    ngrad_ref[0] = summed_grad + jnp.where(inside, back, 0.0)

    @pl.when(pl.program_id(0) == pl.num_programs(0) - 1)
    def _():
        give_halves(place_ref, out_ref.at[:UNIT, :], one_kept_ref, one_sent_ref)
        give_halves(place_ref, out_ref.at[UNIT:, :], two_kept_ref, two_sent_ref)


def attention_back_body(
    tok_ref,
    dur_ref,
    ngrad_ref,
    mixed_ref,
    attend_ref,
    att_ref,
    banded_ref,
    proj_ref,
    emb_low_ref,
    qkv_ref,
    relk_ref,
    relv_ref,
    out_ref,
    gain_ref,
    prior_ref,
    gain_two_ref,
    shift_two_ref,
    place_ref,
    kept_ref,
    sent_ref,
    rest_ref,
    table_acc,
    qkv_acc,
    out_acc,
    relk_acc,
    relv_acc,
    gain_acc,
    shift_acc,
):
    item = pl.program_id(0)
    first = item == 0
    last = item == pl.num_programs(0) - 1
    tokens = tok_ref[pl.ds(item, 1), :]
    durations = text_rows(dur_ref)
    length = tokens.shape[1]
    inside = text_inside(durations, length)
    mixed_grad, gain_grad, shift_grad = norm_back(mixed_ref[0], gain_ref[...], ngrad_ref[0])
    accumulate(gain_acc, gain_grad, first)
    accumulate(shift_acc, shift_grad, first)
    out_low = mixed_grad.astype(BF16)
    accumulate(out_acc, dot_tn(attend_ref[0], out_low), first)
    weight = dot_nt(out_low, out_ref[...]).astype(BF16)
    band = band_of(length)
    folding = folding_of(length)
    relk = one_turn(relk_ref[...])
    proj = proj_ref[0]
    queries, keys, values = [], [], []
    relk_sum = jnp.zeros((LANES, LANES), F32)
    relv_sum = jnp.zeros((LANES, LANES), F32)
    for head in range(HEADS):
        query = proj[:, head * LANES : (head + 1) * LANES]
        key = proj[:, (HEADS + head) * LANES : (HEADS + head + 1) * LANES]
        value = proj[:, (2 * HEADS + head) * LANES : (2 * HEADS + head + 1) * LANES]
        mine = weight[:, head * LANES : (head + 1) * LANES]
        near = band_spread(dot_nt(mine, relv_ref[...]), band)
        grad = dot_nt(mine, value) + near
        attention = att_ref[0, head]
        values.append(dot_tn(attention.astype(BF16), mine))
        relv_sum = relv_sum + dot_tn(banded_ref[0, head], mine)
        score = attention * (grad - jnp.sum(attention * grad, axis=1, keepdims=True))
        score_low = (score / math.sqrt(HEAD)).astype(BF16)
        band_grad = band_gather(score_low, band, folding)
        queries.append(dot_nn(score_low, key) + dot_nn(band_grad, relk))
        keys.append(dot_tn(score_low, query))
        relk_sum = relk_sum + dot_tn(band_grad, query)
    accumulate(relk_acc, relk_sum, first)
    accumulate(relv_acc, relv_sum, first)
    proj_low = jnp.concatenate(queries + keys + values, axis=1).astype(BF16)
    accumulate(qkv_acc, dot_tn(emb_low_ref[0], proj_low), first)
    back = mixed_grad + dot_nt(proj_low, qkv_ref[...])
    embed_grad = jnp.where(inside, back, 0.0) * math.sqrt(D)
    hot = jnp.where(iota((VOCAB, length), 0) == tokens, 1.0, 0.0).astype(BF16)
    high, low = halves(embed_grad)
    accumulate(table_acc, dot_nn(hot, high) + dot_nn(hot, low), first)

    @pl.when(last)
    def _():
        def beside(left, right):
            return jnp.concatenate([left, right], axis=1)

        rest_ref[...] = jnp.zeros_like(rest_ref)
        packed = [qkv_acc[:, part * LANES : part * LANES + HEAD] for part in range(3 * HEADS)]
        half = D // 2
        rest_ref[:D, :] = jnp.concatenate(packed[:4], axis=1)
        rest_ref[D : D + half, :] = jnp.concatenate(
            [packed[4][:half], packed[5][:half], packed[4][half:], packed[5][half:]], axis=1
        )
        rest_ref[D + half : 2 * D, :] = beside(
            out_acc[:HEAD, :], out_acc[LANES : LANES + HEAD, :]
        )
        rest_ref[ROW_TABLE : ROW_TABLE + MEL, :D] = table_acc[:MEL, :]
        rest_ref[ROW_TABLE : ROW_TABLE + VOCAB - MEL, D:] = table_acc[MEL:, :]
        rest_ref[ROW_PRIOR : ROW_PRIOR + MEL, :] = beside(prior_ref[:MEL, :], prior_ref[MEL:, :])
        rest_ref[ROW_NORM : ROW_NORM + 1, :] = beside(gain_acc[...], shift_acc[...])
        rest_ref[ROW_NORM + 1 : ROW_NORM + 2, :] = beside(gain_two_ref[...], shift_two_ref[...])
        rest_ref[ROW_REL : ROW_REL + PERIOD, :LANES] = relk_acc[:PERIOD, :]
        rest_ref[ROW_REL : ROW_REL + PERIOD, LANES : 2 * LANES] = relv_acc[:PERIOD, :]
        give_halves(place_ref, rest_ref, kept_ref, sent_ref)


def split_pairs(mel_ref, rows_ref):
    frames = mel_ref.shape[2]
    pairs = frames // 2
    rows_ref[:, :MEL] = mel_ref[0].T
    pad = jnp.zeros((pairs, LANES - MEL), F32)
    even = rows_ref[pl.ds(0, pairs, stride=2), :][:, :MEL]
    odd = rows_ref[pl.ds(1, pairs, stride=2), :][:, :MEL]
    return jnp.concatenate([even, pad, odd, pad], axis=1)


def gates_of(pre):
    return jnp.tanh(pre[:, :HID]), 1.0 / (1.0 + jnp.exp(-pre[:, HID:]))


def give_halves(place_ref, acc_ref, kept_ref, sent_ref):
    half = kept_ref.shape[0]
    mine = pl.multiple_of((place_ref[0] & 1) * half, 8)
    other = pl.multiple_of(half - mine, 8)
    kept_ref[...] = acc_ref[pl.ds(mine, half), :]
    sent_ref[...] = acc_ref[pl.ds(other, half), :]


def dot_three(values, table, back=False):
    high, low = halves(values)
    table_high, table_low = halves(table)
    left = jnp.concatenate([high, low, high], axis=1)
    if back:
        return dot_nt(left, jnp.concatenate([table_high, table_high, table_low], axis=1))
    return dot_nn(left, jnp.concatenate([table_high, table_high, table_low], axis=0))


def shifted_rows(values, offset, period):
    if offset == 0:
        return values
    length = values.shape[0]
    moved = pltpu.roll(values, (-offset) % length, 0)
    place = rows_of(length) & (period - 1)
    keep = (place < period - offset) if offset > 0 else (place >= -offset)
    return jnp.where(keep, moved, 0.0)


def unfold_rows(values, kernel, period, reverse=False):
    half = kernel // 2
    steps = [step - half for step in range(kernel)]
    if reverse:
        steps = [-step for step in steps]
    return jnp.concatenate(
        [shifted_rows(values, step, period).astype(BF16) for step in steps], axis=1
    )


STEP_POST = WLAYERS + 1
STEPS = 2 * WLAYERS + 2


def decoder_body(
    mel_ref,
    dur_ref,
    expand_ref,
    expand_low_ref,
    stats_ref,
    mixm_ref,
    start_ref,
    win_ref,
    wres_ref,
    wend_ref,
    place_ref,
    units_ref,
    kept_ref,
    sent_ref,
    tail_kept_ref,
    tail_sent_ref,
    flow_ref,
    ngrad_ref,
    sums_ref,
    normal,
    passive_low,
    hidden_low,
    pre,
    hidden,
    skip,
    active,
    skip_low,
    passive_grad,
    gated,
    part,
    spread,
    wide,
    unit,
    rows,
    end_acc,
    tail,
):
    step = pl.program_id(0)
    items, _, frames = mel_ref.shape
    pairs = frames // 2
    both = 2 if items % 2 == 0 else 1
    blocks = items // both
    block_rows = both * pairs
    conv = WKER * HID

    def inside_item(item):
        return rows_of(pairs) < pair_rows(dur_ref[item : item + 1, :])

    def inside_block(block):
        return jnp.concatenate([inside_item(block * both + i) for i in range(both)], axis=0)

    def span(block):
        return slice(block * block_rows, (block + 1) * block_rows)

    def item_span(item):
        return slice(item * pairs, (item + 1) * pairs)

    @pl.when(step == 0)
    def _():
        _, center, _, _, scale = read_stats(stats_ref[...])
        for item in range(items):
            here = item_span(item)
            inside = inside_item(item)
            rows[:, :MEL] = mel_ref[item].T
            pad = jnp.zeros((pairs, LANES - MEL), F32)
            even = rows[pl.ds(0, pairs, stride=2), :][:, :MEL]
            odd = rows[pl.ds(1, pairs, stride=2), :][:, :MEL]
            values = jnp.concatenate([even, pad, odd, pad], axis=1)
            normalized = jnp.where(inside, (values - center) * scale, 0.0)
            normal[here, :] = normalized
            turned = dot_three(normalized, mixm_ref[...])
            passive = turned[:, :LANES]
            passive_grad[here, :] = passive
            active[here, :] = turned[:, LANES:]
            low = passive.astype(BF16)
            passive_low[here, :] = low
            hidden[here, :] = jnp.where(inside, dot_nn(low, start_ref[...]), 0.0)
            skip[here, :] = jnp.zeros((pairs, HID), F32)

    @pl.when((step >= 1) & (step <= WLAYERS))
    def _():
        layer = step - 1
        for block in range(blocks):
            here = span(block)
            inside = inside_block(block)
            state = hidden[here, :]
            hidden_low[layer, here, :] = state.astype(BF16)
            pre_gate = dot_nn(unfold_rows(state, WKER, pairs), win_ref[0])
            pre[layer, here, :] = pre_gate.astype(BF16)
            tanh, gate = gates_of(pre_gate)
            sums = dot_nn((tanh * gate).astype(BF16), wres_ref[layer])
            hidden[here, :] = jnp.where(inside, state + sums[:, :HID], 0.0)
            skip[here, :] = skip[here, :] + sums[:, HID:]

    @pl.when(step == STEP_POST)
    def _():
        total, _, _, _, _ = read_stats(stats_ref[...])
        unit_grad = 1.0 / (2 * MEL * total)
        end_sum = jnp.zeros(end_acc.shape, F32)
        nll = jnp.zeros((1, LANES), F32)
        for item in range(items):
            here = item_span(item)
            inside = inside_item(item)
            output_low = jnp.where(inside, skip[here, :], 0.0).astype(BF16)
            coupled = jnp.where(inside, dot_nn(output_low, wend_ref[...]), 0.0)
            shift_part = coupled[:, :LANES]
            log_part = coupled[:, LANES:]
            growth = jnp.exp(log_part)
            moving = active[here, :]
            moved = jnp.where(inside, shift_part + growth * moving, 0.0)
            align = align_of(dur_ref[item : item + 1, :], pairs)
            prior = dot_nn(align, expand_ref[item]) + dot_nn(align, expand_low_ref[item])
            latent = jnp.concatenate([passive_grad[here, :], moved], axis=1)
            gap = latent - prior[:, : 2 * LANES]
            log_scales = prior[:, 2 * LANES :]
            scaled = jnp.exp(-2.0 * log_scales) * gap
            square = scaled * gap
            terms = jnp.where(inside, log_scales + 0.5 * square, 0.0)
            sums = jnp.sum(terms, axis=0, keepdims=True)
            nll = nll + sums[:, :LANES] + sums[:, LANES:]
            nll = nll - jnp.sum(log_part, axis=0, keepdims=True)
            latent_grad = jnp.where(inside, unit_grad * scaled, 0.0)
            scale_grad = jnp.where(inside, unit_grad * (1.0 - square), 0.0)
            flow_ref[item] = jnp.concatenate([-latent_grad, scale_grad], axis=1).astype(BF16)
            passive_grad[here, :] = latent_grad[:, :LANES]
            moved_grad = latent_grad[:, LANES:]
            active_grad = moved_grad * growth
            log_grad = jnp.where(inside, active_grad * moving - unit_grad, 0.0)
            active[here, :] = active_grad
            coupled_low = jnp.concatenate([moved_grad, log_grad], axis=1).astype(BF16)
            end_sum = end_sum + dot_tn(coupled_low, output_low)
            skip_grad = jnp.where(inside, dot_nt(coupled_low, wend_ref[...]), 0.0)
            skip_low[here, :] = skip_grad.astype(BF16)
            hidden[here, :] = jnp.zeros((pairs, HID), F32)
        end_acc[...] = end_sum
        sums_ref[...] = jnp.where(iota((8, LANES), 0) == 4, nll, 0.0)

    @pl.when(step > STEP_POST)
    def _():
        layer = STEPS - 1 - step
        for tap in range(WKER):
            wide[:, tap * 2 * HID : (tap + 1) * 2 * HID] = win_ref[
                0, tap * HID : (tap + 1) * HID, :
            ]
        for block in range(blocks):
            here = span(block)
            tanh, gate = gates_of(pre[layer, here, :].astype(F32))
            gated[here, :] = (tanh * gate).astype(BF16)
            kept = hidden[here, :]
            both_low = jnp.concatenate([kept, skip_low[here, :].astype(F32)], axis=1).astype(BF16)
            part[here, :] = both_low
            gated_grad = dot_nt(both_low, wres_ref[layer])
            tanh_grad = gated_grad * gate * (1.0 - tanh * tanh)
            gate_grad = gated_grad * tanh * gate * (1.0 - gate)
            pre_grad = jnp.concatenate([tanh_grad, gate_grad], axis=1)
            taps = unfold_rows(pre_grad, WKER, pairs, reverse=True)
            spread[here, :] = taps
            back = kept + dot_nt(taps, wide[...])
            hidden[here, :] = jnp.where(inside_block(block), back, 0.0)
        sums = dot_tn(hidden_low[layer], spread[...])
        for tap in range(WKER):
            unit[tap * HID : (tap + 1) * HID, :] = sums[:, tap * 2 * HID : (tap + 1) * 2 * HID]
        unit[conv:, :] = dot_tn(gated[...], part[...])

        @pl.when(layer == WLAYERS - 1)
        def _():
            unit[conv : conv + MEL, :HID] = end_acc[:MEL, :]
            unit[conv + MEL : conv + 2 * MEL, :HID] = end_acc[LANES : LANES + MEL, :]

        @pl.when(layer > 0)
        def _():
            units_ref[...] = unit[...]

        @pl.when(layer == 0)
        def _():
            give_halves(place_ref, unit, kept_ref, sent_ref)

    @pl.when(step == STEPS - 1)
    def _():
        start_sum = jnp.zeros((LANES, HID), F32)
        mix_sum = jnp.zeros((2 * LANES, 2 * LANES), F32)
        one = jnp.zeros((1, 2 * LANES), F32)
        two = jnp.zeros((1, 2 * LANES), F32)
        for item in range(items):
            here = item_span(item)
            start_low = hidden[here, :].astype(BF16)
            start_sum = start_sum + dot_tn(passive_low[here, :], start_low)
            turned_passive = passive_grad[here, :] + dot_nt(start_low, start_ref[...])
            turned_grad = jnp.concatenate([turned_passive, active[here, :]], axis=1)
            normalized = normal[here, :]
            mix_sum = mix_sum + dot_tn(normalized.astype(BF16), turned_grad.astype(BF16))
            normal_grad = dot_three(turned_grad, mixm_ref[...], back=True)
            normal_grad = jnp.where(inside_item(item), normal_grad, 0.0)
            ngrad_ref[item] = normal_grad
            one = one + jnp.sum(normal_grad, axis=0, keepdims=True)
            two = two + jnp.sum(normal_grad * normalized, axis=0, keepdims=True)
        sums_ref[0:1, :] = one[:, :LANES]
        sums_ref[1:2, :] = one[:, LANES:]
        sums_ref[2:3, :] = two[:, :LANES]
        sums_ref[3:4, :] = two[:, LANES:]
        half = MEL // 2
        tail[...] = jnp.zeros_like(tail)
        tail[:half, :] = jnp.concatenate([start_sum[:half, :], start_sum[half:MEL, :]], axis=1)
        row_member, col_member, match = mix_places()
        kept = jnp.where(match, mix_sum, 0.0)
        ri = iota((8, LANES), 0)
        ci = iota((8, LANES), 1)
        mixed = jnp.zeros((8, LANES), F32)
        for i in range(4):
            column = jnp.sum(jnp.where(col_member == i, kept, 0.0), axis=1, keepdims=True)
            for j in range(4):
                entry = jnp.sum(jnp.where(row_member == j, column, 0.0), axis=0, keepdims=True)
                mixed = jnp.where((ri == i) & (ci == j), entry, mixed)
        tail[half : half + 8, :LANES] = mixed
        give_halves(place_ref, tail, tail_kept_ref, tail_sent_ref)


def frames_body(
    mel_ref, dur_ref, ngrad_ref, stats_ref, sums_ref, small_ref, out_ref, loss_ref, rows_ref
):
    pairs = mel_ref.shape[2] // 2
    inside = rows_of(pairs) < pair_rows(text_rows(dur_ref))
    total, center, variance, log_act, scale = read_stats(stats_ref[...])
    unit = 1.0 / (2 * MEL * total)
    sums = sums_ref[...]
    spot = iota((1, 2 * LANES), 1) & (LANES - 1)
    log_sum = jnp.sum(jnp.where(spot < MEL, log_act, 0.0), axis=1, keepdims=True)
    nll = jnp.sum(sums[4:5], axis=1, keepdims=True)
    log_det = jnp.log(small_ref[4:5, 0:1])
    loss = (nll - total * log_sum - total * (MEL // 2) * log_det) * unit
    loss_ref[...] = loss + 0.5 * math.log(2.0 * math.pi)
    one = jnp.concatenate([sums[0:1], sums[1:2]], axis=1)
    two = jnp.concatenate([sums[2:3], sums[3:4]], axis=1)
    log_grad = two - unit * total
    var_grad = -0.5 * log_grad / (variance + 1e-06)
    center_grad = -scale * one - 2.0 * center * var_grad
    values = split_pairs(mel_ref, rows_ref)
    grads = ngrad_ref[0] * scale + (2.0 * values * var_grad + center_grad) / total
    grads = jnp.where(inside, grads, 0.0) * (2 * MEL * total)
    rows_ref[pl.ds(0, pairs, stride=2), :] = grads[:, :LANES]
    rows_ref[pl.ds(1, pairs, stride=2), :] = grads[:, LANES:]
    out_ref[0] = rows_ref[...].T[:MEL, :]


def small_sum(values, devices):
    bit = 1
    while bit < devices:
        values = values + lax.ppermute(values, "dp", [(i, i ^ bit) for i in range(devices)])
        bit *= 2
    return values


def swap(values, bit, devices):
    return lax.ppermute(values, "dp", [(i, i ^ bit) for i in range(devices)])


def swap_half(unit, devices):
    kept, sent = unit
    return kept, swap(sent, 1, devices)


def digits(devices):
    found = []
    shift = 1
    while (1 << shift) < devices:
        radix = 4 if (1 << (shift + 2)) <= devices else 2
        found.append((shift, radix))
        shift += 2 if radix == 4 else 1
    return found


def whole_vmem(count):
    return [pl.BlockSpec(memory_space=pltpu.VMEM)] * count


def call_whole(body, place, ins, outs, scratch, after, micros, name):
    return run(
        body,
        (),
        [place, *ins],
        [pl.BlockSpec(memory_space=pltpu.SMEM)] + whole_vmem(len(ins)),
        outs,
        whole_vmem(len(outs)),
        scratch,
        micros=micros,
        after=after,
        name=name,
    )


def hop_out(jobs, place, after=()):
    ins = []
    outs = []
    scratch = []
    plans = []
    for units, shift, radix in jobs:
        plan = []
        begin = 0
        for unit in units:
            row = unit[0].shape[0] // radix
            plan.append((len(ins), len(unit), row, begin))
            ins += unit
            begin += row
        plans.append((plan, len(outs), shift, radix))
        outs += [shape_of((begin, WIDE))] * radix
        scratch.append(pltpu.VMEM((radix, begin, WIDE), F32))
    n_in, n_out = len(ins), len(outs)

    def body(place_ref, *refs):
        out_refs = refs[n_in : n_in + n_out]
        tables = refs[n_in + n_out :]
        for (plan, at, shift, radix), table in zip(plans, tables):
            digit = (place_ref[0] >> shift) & (radix - 1)
            for first, count, row, begin in plan:
                for part in range(radix):
                    span = slice(part * row, (part + 1) * row)
                    value = refs[first][span, :]
                    for extra in range(1, count):
                        value = value + refs[first + extra][span, :]
                    table[part, begin : begin + row, :] = value
            for step in range(radix):
                out_refs[at + step][...] = table[digit ^ step]

    found = call_whole(body, place, ins, outs, scratch, after, 3, "hop_out")
    return [found[at : at + radix] for _, at, _, radix in plans]


def hop_in(jobs, place, after=()):
    ins = []
    outs = []
    plans = []
    for parts, shift in jobs:
        plans.append((len(ins), len(parts), shift))
        ins += parts
        outs.append(shape_of((len(parts), *parts[0].shape)))
    n_in = len(ins)

    def body(place_ref, *refs):
        for (first, radix, shift), out in zip(plans, refs[n_in:]):
            digit = (place_ref[0] >> shift) & (radix - 1)
            for step in range(radix):
                out[digit ^ step] = refs[first + step][...]

    return call_whole(body, place, ins, outs, (), after, 2, "hop_in")


def add_parts(jobs, place, after=()):
    ins = [part for parts in jobs for part in parts]
    outs = [shape_of(parts[0].shape) for parts in jobs]
    n_in = len(ins)

    def body(place_ref, *refs):
        at = 0
        for parts, out in zip(jobs, refs[n_in:]):
            value = refs[at][...]
            for extra in range(at + 1, at + len(parts)):
                value = value + refs[extra][...]
            out[...] = value
            at += len(parts)

    return call_whole(body, place, ins, outs, (), after, 1, "add_parts")


def send_parts(parts, shift, devices):
    return [parts[0]] + [
        swap(part, step << shift, devices) for step, part in enumerate(parts) if step > 0
    ]


def sum_chunks(chunks, place, devices, after):
    steps = digits(devices)
    orders = [steps[i:] + steps[:i] for i in range(len(chunks))]
    state = chunks
    for level in range(len(steps)):
        jobs = [(units, *order[level]) for units, order in zip(state, orders)]
        parts = hop_out(jobs, place, after if level == 0 else ())
        state = [
            [send_parts(part, order[level][0], devices)] for part, order in zip(parts, orders)
        ]
    return add_parts([units[0] for units in state], place), orders


def gather_chunks(state, orders, place, devices, meanwhile):
    for level in reversed(range(len(orders[0]))):
        jobs = []
        for part, order in zip(state, orders):
            shift, radix = order[level]
            jobs.append((send_parts([part] * radix, shift, devices), shift))
        if level == 0:
            after = meanwhile(state)
        state = hop_in(jobs, place, after if level == 0 else ())
    state = [part.reshape(part.shape[0], -1, WIDE) for part in state]
    return state, [swap(part, 1, devices) for part in state]


def rebuild(bit, mine_ref, other_ref, begin, rows, table):
    radix = mine_ref.shape[0]
    part = rows // 2 // radix
    for core in range(2):
        for digit in range(radix):
            mine = mine_ref[digit, begin : begin + part, :]
            other = other_ref[digit, begin : begin + part, :]
            at = core * (rows // 2) + digit * part
            table[at : at + part, :] = jnp.where(bit == core, mine, other)
    return begin + part


def unpack_units_body(units_ref, in_ref, res_ref, last_ref, end_ref, sems):
    conv = WKER * HID
    copies = []
    for layer in range(1, WLAYERS):
        begin = (WLAYERS - 1 - layer) * UNIT
        copies.append((units_ref.at[pl.ds(begin, conv), :], in_ref.at[layer]))
        if layer < WLAYERS - 1:
            copies.append((units_ref.at[pl.ds(begin + conv, HID), :], res_ref.at[layer]))
    copies = [
        pltpu.make_async_copy(source, target, sems.at[i])
        for i, (source, target) in enumerate(copies)
    ]
    for copy in copies:
        copy.start()
    last_ref[...] = units_ref[conv:UNIT, HID:]
    end_ref[...] = units_ref[conv : conv + 2 * MEL, :HID]
    for copy in copies:
        copy.wait()


def unpack_units(units, after):
    vmem = pl.BlockSpec(memory_space=pltpu.VMEM)
    anywhere = pl.BlockSpec(memory_space=pl.ANY)
    outs = [
        shape_of((WLAYERS, WKER * HID, 2 * HID)),
        shape_of((WLAYERS - 1, HID, 2 * HID)),
        shape_of((HID, HID)),
        shape_of((2 * MEL, HID)),
    ]
    return run(
        unpack_units_body,
        (),
        [units],
        [vmem],
        outs,
        [anywhere] * 2 + [vmem] * 2,
        [pltpu.SemaphoreType.DMA((2 * WLAYERS - 3,))],
        micros=5,
        after=after,
        name="unpack_units",
    )


def unpack_body(
    place_ref,
    mine_ref,
    other_ref,
    mine_low_ref,
    other_low_ref,
    small_ref,
    in_given,
    res_given,
    one_ref,
    two_ref,
    table_ref,
    qkv_ref,
    out_ref,
    relk_ref,
    relv_ref,
    norms_ref,
    prior_ref,
    start_ref,
    mix_ref,
    in_ref,
    res_ref,
    first,
    second,
    rest,
    unit,
    tail,
    sems,
):
    bit = place_ref[0] & 1
    conv = WKER * HID
    begin = rebuild(bit, mine_low_ref, other_low_ref, 0, UNIT, unit)
    copies = [
        pltpu.make_async_copy(unit.at[pl.ds(0, conv), :], in_ref.at[0], sems.at[0]),
        pltpu.make_async_copy(unit.at[pl.ds(conv, HID), :], res_ref.at[0], sems.at[1]),
    ]
    for copy in copies:
        copy.start()
    rebuild(bit, mine_low_ref, other_low_ref, begin, TAIL, tail)
    half = MEL // 2
    start_ref[:half, :] = tail[:half, :HID]
    start_ref[half:, :] = tail[:half, HID:]
    mix_ref[...] = tail[half : half + 8, :LANES] - small_ref[...] / 4.0
    begin = rebuild(bit, mine_ref, other_ref, 0, UNIT, first)
    for part in range(2):
        one_ref[:, part * WIDE : (part + 1) * WIDE] = first[
            part * KSIZE * D : (part + 1) * KSIZE * D, :
        ]
    begin = rebuild(bit, mine_ref, other_ref, begin, UNIT, second)
    for part in range(2 * KSIZE):
        two_ref[:, part * WIDE : (part + 1) * WIDE] = second[part * D : (part + 1) * D, :]
    rebuild(bit, mine_ref, other_ref, begin, REST, rest)
    half = D // 2
    qkv_ref[:, :WIDE] = rest[:D, :]
    qkv_ref[:half, WIDE:] = rest[D : D + half, :D]
    qkv_ref[half:, WIDE:] = rest[D : D + half, D:]
    out_ref[:half, :] = rest[D + half : 2 * D, :D]
    out_ref[half:, :] = rest[D + half : 2 * D, D:]
    table_ref[:MEL, :] = rest[ROW_TABLE : ROW_TABLE + MEL, :D]
    table_ref[MEL:, :] = rest[ROW_TABLE : ROW_TABLE + VOCAB - MEL, D:]
    prior_ref[:MEL, :] = rest[ROW_PRIOR : ROW_PRIOR + MEL, :D]
    prior_ref[MEL:, :] = rest[ROW_PRIOR : ROW_PRIOR + MEL, D:]
    relk_ref[...] = rest[ROW_REL : ROW_REL + 2 * WINDOW + 1, :HEAD]
    relv_ref[...] = rest[ROW_REL : ROW_REL + 2 * WINDOW + 1, LANES : LANES + HEAD]
    norms_ref[...] = jnp.concatenate(
        [rest[ROW_NORM : ROW_NORM + 2, :D], rest[ROW_NORM : ROW_NORM + 2, D:]], axis=0
    )
    for copy in copies:
        copy.wait()


def unpack(upper, lower, place, inverse, in_grad, res_grad):
    vmem = pl.BlockSpec(memory_space=pltpu.VMEM)
    anywhere = pl.BlockSpec(memory_space=pl.ANY)
    reach = 2 * WINDOW + 1
    outs = [
        shape_of((KSIZE * D, FILTER)),
        shape_of((D, KSIZE * FILTER)),
        shape_of((VOCAB, D)),
        shape_of((D, 3 * D)),
        shape_of((D, D)),
        shape_of((reach, HEAD)),
        shape_of((reach, HEAD)),
        shape_of((4, D)),
        shape_of((2 * MEL, D)),
        shape_of((MEL, HID)),
        shape_of((8, LANES)),
        shape_of(in_grad.shape),
        shape_of(res_grad.shape),
    ]
    return run(
        unpack_body,
        (),
        [place, *upper, *lower, inverse, in_grad, res_grad],
        [pl.BlockSpec(memory_space=pltpu.SMEM)] + [vmem] * 5 + [anywhere] * 2,
        outs,
        [vmem] * (len(outs) - 2) + [anywhere] * 2,
        [
            pltpu.VMEM((UNIT, WIDE), F32),
            pltpu.VMEM((UNIT, WIDE), F32),
            pltpu.VMEM((REST, WIDE), F32),
            pltpu.VMEM((UNIT, WIDE), F32),
            pltpu.VMEM((TAIL, WIDE), F32),
            pltpu.SemaphoreType.DMA((2,)),
        ],
        micros=5,
        aliases={6: 11, 7: 12},
        name="unpack",
    )


def on_device(
    devices,
    token_ids,
    durations,
    mel_frames,
    embedding,
    w_qkv,
    rel_key,
    rel_value,
    w_out,
    attn_gain,
    attn_shift,
    w_ff1,
    w_ff2,
    ffn_gain,
    ffn_shift,
    w_prior,
    w_mix,
    w_start,
    w_in,
    w_res,
    w_skip_last,
    w_end,
):
    items, length = token_ids.shape
    frames = mel_frames.shape[1]
    mel_frames = mel_frames.transpose(0, 2, 1)
    ff2_t = w_ff2.T
    prior_t = w_prior.T
    end_t = w_end.T
    pairs = frames // 2
    grid = (items,)
    place = lax.axis_index("dp").reshape(1).astype(jnp.int32)

    def halves_of(rows):
        return [shape_of((rows // 2, WIDE))] * 2

    vmem = pl.BlockSpec(memory_space=pltpu.VMEM)
    smem = pl.BlockSpec(memory_space=pltpu.SMEM)
    gain_one = attn_gain.reshape(1, D)
    shift_one = attn_shift.reshape(1, D)
    gain_two = ffn_gain.reshape(1, D)
    shift_two = ffn_shift.reshape(1, D)

    stats = run(
        stats_body, (), [mel_frames, durations], [vmem] * 2, shape_of((8, LANES)), vmem, name="stats"
    )
    stats = small_sum(stats, devices)

    prepared = [
        shape_of((2 * LANES, 2 * LANES)),
        shape_of((8, LANES)),
        shape_of((D, 6 * LANES), BF16),
        shape_of((LANES, LANES), BF16),
        shape_of((LANES, LANES), BF16),
        shape_of((2 * LANES, D), BF16),
        shape_of((2 * MEL, 8 * LANES), BF16),
        shape_of((D, 8 * LANES), BF16),
        shape_of((LANES, HID), BF16),
        shape_of((HID, 2 * LANES), BF16),
        shape_of((WLAYERS, HID, 2 * HID), BF16),
    ]
    (
        mixm,
        small,
        qkv_pad,
        relk_pad,
        relv_pad,
        out_pad,
        wide,
        prior_pad,
        start_pad,
        end_pad,
        res_four,
    ) = run(
        weights_body,
        (),
        [w_mix, w_qkv, rel_key, rel_value, w_out, prior_t, w_start, end_t, w_res, w_skip_last],
        [smem] + [vmem] * 9,
        prepared,
        [vmem] * len(prepared),
        name="weights",
    )

    ins = [
        token_ids,
        durations,
        embedding,
        qkv_pad,
        relk_pad,
        relv_pad,
        out_pad,
        gain_one,
        shift_one,
    ]
    outs = [
        shape_of((items, length, D), BF16),
        shape_of((items, length, 6 * LANES), BF16),
        shape_of((items, HEADS, length, length)),
        shape_of((items, HEADS, length, LANES), BF16),
        shape_of((items, length, 2 * LANES), BF16),
        shape_of((items, length, D)),
        shape_of((items, length, D)),
    ]
    emb_low, proj, attention, banded, attend, mixed, normed = run(
        attention_body,
        grid,
        ins,
        [full_spec(a) for a in ins],
        outs,
        [item_spec(a) for a in outs],
        micros=14,
        name="attention",
    )

    ins = [durations, normed, w_ff1, ff2_t, gain_two, shift_two, prior_pad]
    outs = [
        shape_of((items, length, FILTER)),
        shape_of((items, length, FILTER), BF16),
        shape_of((items, length, D)),
        shape_of((items, length, D), BF16),
        shape_of((items, 2 * length, 4 * LANES), BF16),
        shape_of((items, 2 * length, 4 * LANES), BF16),
    ]
    filtered, activ, summed, encoded, expand, expand_low = run(
        feed_body,
        grid,
        ins,
        [full_spec(durations), item_spec(normed)] + [full_spec(a) for a in ins[2:]],
        outs,
        [item_spec(a) for a in outs],
        micros=10,
        name="feed",
    )

    ins = [mel_frames, durations, expand, expand_low, stats, mixm, start_pad, w_in, res_four, end_pad, place]
    kinds = [full_spec] * 10
    in_specs = [kind(a) for kind, a in zip(kinds, ins)] + [smem]
    in_specs[7] = pl.BlockSpec(
        (1,) + w_in.shape[1:],
        lambda s: (jnp.where(s <= STEP_POST, jnp.clip(s - 1, 0, WLAYERS - 1), STEPS - 1 - s), 0, 0),
    )
    outs = [
        shape_of(((WLAYERS - 1) * UNIT, WIDE)),
        *halves_of(UNIT),
        *halves_of(TAIL),
        shape_of((items, pairs, 4 * LANES), BF16),
        shape_of((items, pairs, 2 * LANES)),
        shape_of((8, LANES)),
    ]
    out_specs = [full_spec(a) for a in outs]
    out_specs[0] = pl.BlockSpec(
        (UNIT, WIDE), lambda s: (jnp.clip(s - STEP_POST - 1, 0, WLAYERS - 2), 0)
    )
    count = items * pairs
    units, kept, sent, tail_kept, tail_sent, flow, normal_grad, sums = run(
        decoder_body,
        (STEPS,),
        ins,
        in_specs,
        outs,
        out_specs,
        [
            pltpu.VMEM((count, 2 * LANES), F32),
            pltpu.VMEM((count, LANES), BF16),
            pltpu.VMEM((WLAYERS, count, HID), BF16),
            pltpu.VMEM((WLAYERS, count, 2 * HID), BF16),
            pltpu.VMEM((count, HID), F32),
            pltpu.VMEM((count, HID), F32),
            pltpu.VMEM((count, LANES), F32),
            pltpu.VMEM((count, HID), BF16),
            pltpu.VMEM((count, LANES), F32),
            pltpu.VMEM((count, HID), BF16),
            pltpu.VMEM((count, 2 * HID), BF16),
            pltpu.VMEM((count, WKER * 2 * HID), BF16),
            pltpu.VMEM((HID, WKER * 2 * HID), BF16),
            pltpu.VMEM((UNIT, WIDE), F32),
            pltpu.VMEM((frames, LANES), F32),
            pltpu.VMEM((2 * LANES, HID), F32),
            pltpu.VMEM((TAIL, WIDE), F32),
        ],
        micros=80,
        name="decoder",
    )
    units = lax.psum(units, "dp")
    first_unit = swap_half((kept, sent), devices)
    last_unit = swap_half((tail_kept, tail_sent), devices)
    sums = sums + swap(sums, 1, devices)
    sum_steps = digits(devices)

    ins = [durations, flow, wide, encoded, summed, filtered, activ, normed, w_ff1, ff2_t, gain_two, prior_t]
    outs = [
        shape_of((items, length, D)),
        shape_of((2 * MEL, D)),
        shape_of((1, D)),
        shape_of((1, D)),
        *halves_of(UNIT),
        *halves_of(UNIT),
    ]
    kinds = [full_spec, item_spec, full_spec] + [item_spec] * 5 + [full_spec] * 4
    ngrad, prior_grad, gain_two_grad, shift_two_grad, *feed_units = run(
        feed_back_body,
        grid,
        ins + [place],
        [kind(a) for kind, a in zip(kinds, ins)] + [smem],
        outs,
        [item_spec(outs[0])] + [full_spec(a) for a in outs[1:]],
        [pltpu.VMEM((2 * UNIT, WIDE), F32)],
        after=(sums,),
        micros=28,
        name="feed_back",
    )

    shift, radix = sum_steps[0]
    sums = sum(send_parts([sums] * radix, shift, devices))
    feed_sums = sums
    ins = [
        token_ids,
        durations,
        ngrad,
        mixed,
        attend,
        attention,
        banded,
        proj,
        emb_low,
        qkv_pad,
        relk_pad,
        relv_pad,
        out_pad,
        gain_one,
        prior_grad,
        gain_two_grad,
        shift_two_grad,
    ]
    kinds = [full_spec] * 2 + [item_spec] * 7 + [full_spec] * 8
    rest = run(
        attention_back_body,
        grid,
        ins + [place],
        [kind(a) for kind, a in zip(kinds, ins)] + [smem],
        halves_of(REST),
        [full_spec(a) for a in halves_of(REST)],
        [
            pltpu.VMEM((REST, WIDE), F32),
            pltpu.VMEM((VOCAB, D), F32),
            pltpu.VMEM((D, 6 * LANES), F32),
            pltpu.VMEM((2 * LANES, D), F32),
            pltpu.VMEM((LANES, LANES), F32),
            pltpu.VMEM((LANES, LANES), F32),
            pltpu.VMEM((1, D), F32),
            pltpu.VMEM((1, D), F32),
        ],
        after=(feed_sums,),
        micros=20,
        name="attention_back",
    )

    for shift, radix in sum_steps[1:]:
        sums = sum(send_parts([sums] * radix, shift, devices))
    feed_units = [swap_half(feed_units[:2], devices), swap_half(feed_units[2:], devices)]
    rest = swap_half(rest, devices)
    state, orders = sum_chunks(
        [[*feed_units, rest], [first_unit, last_unit]], place, devices, (sums,)
    )

    ins = [mel_frames, durations, normal_grad, stats, sums, small]
    kinds = [item_spec, full_spec, item_spec, full_spec, full_spec, full_spec]
    mel_grad, loss = run(
        frames_body,
        grid,
        ins,
        [kind(a) for kind, a in zip(kinds, ins)],
        [shape_of(mel_frames.shape), shape_of((1, 1))],
        [item_spec(mel_frames), pl.BlockSpec((1, 1), lambda b: (0, 0))],
        [pltpu.VMEM((frames, LANES), F32)],
        after=(state[0],),
        name="frames",
    )

    kept_grads = []

    def meanwhile(state):
        kept_grads.extend(unpack_units(units, (mel_grad, state[0])))
        return (kept_grads[2],)

    state, other = gather_chunks(state, orders, place, devices, meanwhile)
    in_grad, res_grad, last_grad, end_grad = kept_grads
    (
        ff1_grad,
        ff2_grad,
        table_grad,
        qkv_grad,
        out_grad,
        relk_grad,
        relv_grad,
        norm_grads,
        prior_grad,
        start_grad,
        mix_grad,
        in_grad,
        res_grad,
    ) = unpack((state[0], other[0]), (state[1], other[1]), place, small, in_grad, res_grad)

    return (
        loss.reshape(()),
        mel_grad.transpose(0, 2, 1),
        table_grad,
        qkv_grad,
        relk_grad,
        relv_grad,
        out_grad,
        norm_grads[0],
        norm_grads[2],
        ff1_grad,
        ff2_grad.T,
        norm_grads[1],
        norm_grads[3],
        prior_grad.T,
        mix_grad[:4, :4],
        start_grad,
        in_grad,
        res_grad,
        last_grad,
        end_grad.T,
    )


def solution(mesh):
    devices = mesh.shape["dp"]
    placed = (P("dp", None), P("dp", None), P("dp", None, None)) + (P(),) * 18
    return jax.shard_map(
        functools.partial(on_device, devices),
        mesh=mesh,
        in_specs=placed,
        out_specs=(P(), P("dp", None, None)) + (P(),) * 18,
        check_vma=False,
    )
```

time: 627 us -> 345 us (0.55)
  waiting for transfers between devices: 360 us -> 82.6 us
  starting transfers between devices: 15.4 us -> 52.7 us
  local copies, waits for them, and re-layouts: 30.8 us -> 9.87 us
  Pallas kernels: 190 us -> 183 us
  other arithmetic: 9.49 us -> 3.19 us
    psum x2 -> x1, waiting for transfers between devices: 349 us -> 0.01 us  [on_device(): units = lax.psum(units, 'dp')]
    ppermute x0 -> x38, waiting for transfers between devices: none -> 80 us  [swap(): return lax.ppermute(values, 'dp', [(i, i ^ bit) for i in range(devices)])]
    ppermute x0 -> x38, starting transfers between devices: none -> 43 us  [swap(): return lax.ppermute(values, 'dp', [(i, i ^ bit) for i in range(devices)])]
    unnamed x80 -> x70, local copies, waits for them, and re-layouts: 28.4 us -> 7.2 us
    ppermute x10 -> x5, waiting for transfers between devices: 11.4 us -> 2.63 us  [small_sum(): lax.ppermute(values, 'dp', [(i, i ^ bit) for i in range(devices)])]
    pallas_call x13 -> x15, Pallas kernels: 190 us -> 183 us  [run(): pl.pallas_call(wrapped, grid=grid, in_specs=list(in_specs) + [pl.BlockSpe...]
    ppermute x10 -> x5, starting transfers between devices: 15.3 us -> 9.63 us  [small_sum(): lax.ppermute(values, 'dp', [(i, i ^ bit) for i in range(devices)])]
  transfers between devices with their start and end apart: 12 -> 44, of which waited for: 10 -> 20; matrix products, arithmetic and copies ran while one was open for 2% -> 1% of each run, Pallas kernels for 5% -> 29%
where the time goes in v2:
time: 345 us; the launch traced here: 346 us
  Pallas kernels  183 us (53%)
  waiting for transfers between devices  82.6 us (24%)
  starting transfers between devices  52.7 us (15%)
  between operations  14.9 us (4%)
  local copies, waits for them, and re-layouts  9.87 us (3%)
    pallas_call x15, Pallas kernels, run(): pl.pallas_call(wrapped, grid=grid, in_specs=list(in_specs) + [pl.BlockSpe...  183 us
    ppermute x38, waiting for transfers between devices, swap(): return lax.ppermute(values, 'dp', [(i, i ^ bit) for i in range(devices)])  80 us
    ppermute x38, starting transfers between devices, swap(): return lax.ppermute(values, 'dp', [(i, i ^ bit) for i in range(devices)])  43 us
    ppermute x5, starting transfers between devices, small_sum(): lax.ppermute(values, 'dp', [(i, i ^ bit) for i in range(devices)])  9.63 us
    unnamed x70, local copies, waits for them, and re-layouts  7.2 us
  transfers between devices with their start and end apart: 44, of which 20 were waited for; matrix products, arithmetic and copies ran while one was open for 1% of the time, Pallas kernels for 29%

profile of v2, /device:TPU:0, one launch (start us, length us, event | category | flops | bytes accessed | tf_op | source)
XLA Modules:
  0.0 345.8 jit_solution(6217124635641225268)
XLA Ops:
  7.2 2.4 stats.1
  10.1 1.0 collective-permute-done
  11.8 2.8 collective-permute-start.1
  14.6 1.6 collective-permute-done.1
  16.2 2.1 collective-permute-start.2
  18.2 3.4 weights.1
  21.6 1.6 collective-permute-start.3
  23.3 14.7 %attention.1 = (bf16[4,256,192]{2,1,0:T(8,128)(2,1)}, bf16[4,256,768]{2,1,0:T(8,128)(2,1)}, f32[4,2,256,256]{3,2,1,0:T(8,128)}, bf16[4,2,256,128]{3,2,1,0:T(8,12...) custom-call(s32[4,256]{1,0:T(4,128)} %refs_0_.9, s32[4,256]{1,0:T(4,128)} %refs_1_.11, ...), custom_call_target="tpu_custom_call" | custom-call | flops 1400000000 | bytes 1024 | tf_op jit(solution)/shard_map/attention/pallas_call | solution.py:102
  37.9 2.7 collective-permute-start.4
  40.6 10.7 %feed.1 = (f32[4,256,768]{2,1,0:T(8,128)}, bf16[4,256,768]{2,1,0:T(8,128)(2,1)}, f32[4,256,192]{2,1,0:T(8,128)}, bf16[4,256,192]{2,1,0:T(8,128)(2,1)}, bf16[4,51...) custom-call(s32[4,256]{1,0:T(4,128)} %refs_1_.11, f32[4,256,192]{2,1,0:T(8,128)} %get-tuple-element.107.refs_1_.refs_7_, ...), custom_call_target="tpu_custom_call" | custom-call | flops 1000000000 | bytes 1024 | tf_op jit(solution)/shard_map/feed/pallas_call | solution.py:102
  51.9 70.5 %decoder.1 = (f32[3456,384]{1,0:T(8,128)}, f32[576,384]{1,0:T(8,128)}, f32[576,384]{1,0:T(8,128)}, f32[192,384]{1,0:T(8,128)}, f32[192,384]{1,0:T(8,128)}, /*ind...) custom-call(f32[4,80,1024]{2,1,0:T(8,128)} %bitcast.23, s32[4,256]{1,0:T(4,128)} %refs_1_.11, ...), custom_call_target="tpu_custom_call" | custom-call | flops 8000000000 | bytes 1024 | tf_op jit(solution)/shard_map/decoder/pallas_call | solution.py:102
  123.8 1.6 collective-permute-start.6
  125.9 1.5 collective-permute-start.8
  127.4 25.8 %feed_back.1 = (f32[4,256,192]{2,1,0:T(8,128)}, f32[160,192]{1,0:T(8,128)}, f32[1,192]{1,0:T(1,128)}, f32[1,192]{1,0:T(1,128)}, f32[576,384]{1,0:T(8,128)}, /*in...) custom-call(s32[4,256]{1,0:T(4,128)} %refs_1_.11, bf16[4,512,512]{2,1,0:T(8,128)(2,1)} %get-tuple-element.118.refs_1_, ...), custom_call_target="tpu_custom_call" | custom-call | flops 2800000000 | bytes 1024 | tf_op jit(solution)/shard_map/feed_back/pallas_call | solution.py:102
  153.8 1.3 add_add_fusion.1.refs_18_
  155.1 21.3 %attention_back.1 = (f32[384,384]{1,0:T(8,128)}, f32[384,384]{1,0:T(8,128)}) custom-call(s32[4,256]{1,0:T(4,128)} %refs_0_.9, s32[4,256]{1,0:T(4,128)} %refs_1_.11, f32[4,256,192]{2,1,0:T(8,128)} %get-tuple-element.128.refs_2_, f32[4,256,192]{2,1,0:T(8,128)} %get-tuple-element.129.refs_3_, bf16[4,256,256]{2,1,0:T(8,128)(2,1)} %get-tuple-element.130.refs_4_, ...), custom_call_target="tpu_custom_call" | custom-call | flops 2000000000 | bytes 1024 | tf_op jit(solution)/shard_map/attention_back/pallas_call | solution.py:102
  176.5 1.1 collective-permute-start.10
  177.6 3.5 %collective-permute-done.10 = f32[8,128]{1,0:T(8,128)S(1)} collective-permute-done((f32[8,128]{1,0:T(8,128)S(1)}, f32[8,128]{1,0:T(8,128)S(1)}, u32[]{:S(2)}, u32[]{:S(2)}) %collective-permute-start.10) | collective-permute-done | bytes 4128 | tf_op jit(solution)/shard_map/ppermute | solution.py:959
  181.9 4.5 %collective-permute-done.11 = f32[8,128]{1,0:T(8,128)S(1)} collective-permute-done((f32[8,128]{1,0:T(8,128)S(1)}, f32[8,128]{1,0:T(8,128)S(1)}, u32[]{:S(2)}, u32[]{:S(2)}) %collective-permute-start.11) | collective-permute-done | bytes 4128 | tf_op jit(solution)/shard_map/ppermute | solution.py:959
  186.5 3.6 %collective-permute-done.9 = f32[8,128]{1,0:T(8,128)S(1)} collective-permute-done((f32[8,128]{1,0:T(8,128)S(1)}, f32[8,128]{1,0:T(8,128)S(1)}, u32[]{:S(2)}, u32[]{:S(2)}) %collective-permute-start.9) | collective-permute-done | bytes 4128 | tf_op jit(solution)/shard_map/ppermute | solution.py:959
  190.7 1.0 collective-permute-done.16.refs_10_
  193.5 5.1 %hop_out.2 = (f32[384,384]{1,0:T(8,128)}, f32[384,384]{1,0:T(8,128)}, f32[384,384]{1,0:T(8,128)}, f32[384,384]{1,0:T(8,128)}, f32[192,384]{1,0:T(8,128)}, /*inde...) custom-call(s32[1]{0:T(128)} %bitcast.8.refs_10_.refs_12_.refs_17_.refs_0_, ...), custom_call_target="tpu_custom_call" | custom-call | flops 300000000 | bytes 1024 | tf_op jit(solution)/shard_map/hop_out/pallas_call | solution.py:102
  198.5 1.5 collective-permute-start.17
  200.7 1.4 collective-permute-start.19
  202.1 1.4 collective-permute-start.21
  203.4 8.6 %collective-permute-done.20.refs_6_ = f32[192,384]{1,0:T(8,128)S(1)} collective-permute-done((f32[192,384]{1,0:T(8,128)}, f32[192,384]{1,0:T(8,128)S(1)}, u32[]{:S(2)}, u32[]{:S(2)}) %collective-permute-start.20) | collective-permute-done | bytes 294944 | tf_op jit(solution)/shard_map/ppermute | solution.py:959
  212.1 3.3 collective-permute-start.22
  215.4 12.2 %collective-permute-done.21.refs_7_ = f32[192,384]{1,0:T(8,128)S(1)} collective-permute-done((f32[192,384]{1,0:T(8,128)}, f32[192,384]{1,0:T(8,128)S(1)}, u32[]{:S(2)}, u32[]{:S(2)}) %collective-permute-start.21) | collective-permute-done | bytes 294944 | tf_op jit(solution)/shard_map/ppermute | solution.py:959
  227.7 1.7 collective-permute-done.18.refs_3_
  230.4 3.1 hop_out.3
  233.5 0.9 collective-permute-start.26
  234.5 4.5 %collective-permute-start.23 = (f32[96,384]{1,0:T(8,128)}, f32[96,384]{1,0:T(8,128)S(1)}, u32[]{:S(2)}, u32[]{:S(2)}) collective-permute-start(f32[96,384]{1,0:T(8,128)} %get-tuple-element.153), channel_id=1, source_target_pairs={{0,8},{1,9},{2,10},{3,11},{4,12},{5,13},{6,14},{7,15},{8,0},{9,1},... | collective-permute-start | bytes 442376 | tf_op jit(solution)/shard_map/ppermute | solution.py:959
  239.0 2.4 collective-permute-start.25
  241.4 0.9 collective-permute-start.27
  242.3 1.1 collective-permute-start.28
  243.4 2.5 collective-permute-done.27.refs_7_
  246.0 1.8 collective-permute-done.28.refs_8_
  247.8 5.7 %collective-permute-done.24.refs_3_ = f32[96,384]{1,0:T(8,128)S(1)} collective-permute-done((f32[96,384]{1,0:T(8,128)}, f32[96,384]{1,0:T(8,128)S(1)}, u32[]{:S(2)}, u32[]{:S(2)}) %collective-permute-start.24) | collective-permute-done | bytes 147488 | tf_op jit(solution)/shard_map/ppermute | solution.py:959
  254.2 2.0 add_parts.1
  256.2 1.0 collective-permute-start.32
  257.2 2.3 collective-permute-start.29
  259.5 2.4 collective-permute-start.31
  261.9 1.1 collective-permute-start.33
  263.0 1.4 collective-permute-start.34
  264.4 2.1 collective-permute-done.33.refs_7_
  266.5 2.0 collective-permute-done.34.refs_8_
  269.3 4.4 %collective-permute-done.30.refs_3_ = f32[96,384]{1,0:T(8,128)S(1)} collective-permute-done((f32[96,384]{1,0:T(8,128)}, f32[96,384]{1,0:T(8,128)S(1)}, u32[]{:S(2)}, u32[]{:S(2)}) %collective-permute-start.30) | collective-permute-done | bytes 147488 | tf_op jit(solution)/shard_map/ppermute | solution.py:959
  273.8 6.4 %collective-permute-done.31.refs_4_ = f32[96,384]{1,0:T(8,128)S(1)} collective-permute-done((f32[96,384]{1,0:T(8,128)}, f32[96,384]{1,0:T(8,128)S(1)}, u32[]{:S(2)}, u32[]{:S(2)}) %collective-permute-start.31) | collective-permute-done | bytes 147488 | tf_op jit(solution)/shard_map/ppermute | solution.py:959
  280.9 2.2 hop_in.2
  283.1 2.2 collective-permute-start.38
  285.3 1.1 collective-permute-start.35
  286.4 1.1 collective-permute-start.36
  287.5 1.3 collective-permute-start.37
  288.8 1.3 collective-permute-start.39
  290.1 12.2 %collective-permute-done.38.refs_6_ = f32[4,48,384]{2,1,0:T(8,128)S(1)} collective-permute-done((f32[4,48,384]{2,1,0:T(8,128)}, f32[4,48,384]{2,1,0:T(8,128)S(1)}, u32[]{:S(2)}, u32[]{:S(2)}) %collective-permute-start.38) | collective-permute-done | bytes 294944 | tf_op jit(solution)/shard_map/ppermute | solution.py:959
  302.2 2.4 collective-permute-start.40
  304.7 5.0 %frames.1 = (f32[4,80,1024]{2,1,0:T(8,128)}, f32[1,1]{1,0:T(1,128)}) custom-call(f32[4,80,1024]{2,1,0:T(8,128)} %bitcast.24, s32[4,256]{1,0:T(4,128)} %refs_1_.11, f32[4,512,256]{2,1,0:T(8,128)} %get-tuple-element.115.refs_2_, f32[8,128]{1,0:T(8,128)} %add.42.refs_4_.refs_3_, f32[8,128]{1,0:T(8,128)} %add_add_fusion.refs_11_.refs_4_, ...), custom_call_target="tpu_custom_call" | custom-call | flops 500000000 | bytes 1024 | tf_op jit(solution)/shard_map/frames/pallas_call | solution.py:102
  309.6 5.6 %unpack_units.1 = (f32[4,960,384]{2,1,0:T(8,128)}, f32[3,192,384]{2,1,0:T(8,128)}, f32[192,192]{1,0:T(8,128)}, f32[160,192]{1,0:T(8,128)}) custom-call(f32[3456,384]{1,0:T(8,128)} %all-reduce.2.cloned.1.call-done.refs_0_, f32[4,80,1024]{2,1,0:T(8,128)} %get-tuple-element.162.refs_1_, f32[4,96,384]{2,1,0:T(8,128)} %get-tuple-element.164.refs_2_.refs_1_), custom_call_target="tpu_custom_call" | custom-call | flops 500000000 | bytes 1024 | tf_op jit(solution)/shard_map/unpack_units/pallas_call | solution.py:102
  316.6 3.9 %hop_in.3 = (f32[4,4,96,384]{3,2,1,0:T(8,128)}, f32[4,4,48,384]{3,2,1,0:T(8,128)}) custom-call(s32[1]{0:T(128)} %bitcast.8.refs_10_.refs_12_.refs_17_.refs_0_, f32[4,96,384]{2,1,0:T(8,128)} %get-tuple-element.164.refs_2_.refs_1_, f32[4,96,384]{2,1,0:T(8,128)} %copy-done.6, f32[4,96,384]{2,1,0:T(8,128)} %copy-done.7, f32[4,96,384]{2,1,0:T(8,128)} %copy-done.8, ...), custom_call_target="tpu_custom_call" | custom-call | flops 200000000 | bytes 1024 | tf_op jit(solution)/shard_map/hop_in/pallas_call | solution.py:102
  321.1 5.9 %collective-permute-done.42.refs_4_ = f32[4,192,384]{2,1,0:T(8,128)S(1)} collective-permute-done((f32[4,192,384]{2,1,0:T(8,128)}, f32[4,192,384]{2,1,0:T(8,128)S(1)}, u32[]{:S(2)}, u32[]{:S(2)}) %collective-permute-start.42) | collective-permute-done | bytes 1179680 | tf_op jit(solution)/shard_map/ppermute | solution.py:959
  327.0 1.0 copy-done.1
  328.8 7.1 %unpack.1 = (f32[576,768]{1,0:T(8,128)}, f32[192,2304]{1,0:T(8,128)}, f32[148,192]{1,0:T(8,128)}, f32[192,576]{1,0:T(8,128)}, f32[192,192]{1,0:T(8,128)}, /*inde...) custom-call(s32[1]{0:T(128)} %bitcast.8.refs_10_.refs_12_.refs_17_.r, ...), custom_call_target="tpu_custom_call", output_to_operand_aliasing={{11}: (6, {}), {12}: (7, {})} | custom-call | flops 500000000 | bytes 1024 | tf_op jit(solution)/shard_map/unpack/pallas_call | solution.py:102
  335.9 1.4 fusion
  337.3 1.3 slice.19
  (120 shorter events, 14.1 us)
Async XLA Ops:
  7.2 302.4 %all-reduce.2.cloned.1.call-start = ((), (), s32[]{:S(2)}) async-start(), calls=%async_computation | async-start | bytes 10616832 | tf_op jit(solution)/shard_map/psum | solution.py:1451
  9.6 1.5 collective-permute-start
  11.8 4.4 %collective-permute-start.1 = (f32[8,128]{1,0:T(8,128)S(1)}, f32[8,128]{1,0:T(8,128)S(1)}, u32[]{:S(2)}, u32[]{:S(2)}) collective-permute-start(f32[8,128]{1,0:T(8,128)S(1)} %add.38), channel_id=1, source_target_pairs={{0,2},{1,3},{2,0},{3,1},{4,6},{5,7},{6,4},{7,5},{8,10},{9,11},{10,... | collective-permute-start | bytes 12296 | tf_op jit(solution)/shard_map/ppermute | solution.py:953
  16.2 5.4 %collective-permute-start.2 = (f32[8,128]{1,0:T(8,128)S(1)}, f32[8,128]{1,0:T(8,128)S(1)}, u32[]{:S(2)}, u32[]{:S(2)}) collective-permute-start(f32[8,128]{1,0:T(8,128)S(1)} %add.39), channel_id=1, source_target_pairs={{0,4},{1,5},{2,6},{3,7},{4,0},{5,1},{6,2},{7,3},{8,12},{9,13},{10,... | collective-permute-start | bytes 12296 | tf_op jit(solution)/shard_map/ppermute | solution.py:953
  21.6 16.3 %collective-permute-start.3 = (f32[8,128]{1,0:T(8,128)S(1)}, f32[8,128]{1,0:T(8,128)S(1)}, u32[]{:S(2)}, u32[]{:S(2)}) collective-permute-start(f32[8,128]{1,0:T(8,128)S(1)} %add.40), channel_id=1, source_target_pairs={{0,8},{1,9},{2,10},{3,11},{4,12},{5,13},{6,14},{7,15},{8,0},{9,1},... | collective-permute-start | bytes 12296 | tf_op jit(solution)/shard_map/ppermute | solution.py:953
  37.9 13.3 %collective-permute-start.4 = (f32[8,128]{1,0:T(8,128)S(1)}, f32[8,128]{1,0:T(8,128)S(1)}, u32[]{:S(2)}, u32[]{:S(2)}) collective-permute-start(f32[8,128]{1,0:T(8,128)S(1)} %add.41), channel_id=1, source_target_pairs={{0,16},{1,17},{2,18},{3,19},{4,20},{5,21},{6,22},{7,23},{8,24},{9,... | collective-permute-start | bytes 12296 | tf_op jit(solution)/shard_map/ppermute | solution.py:953
  122.4 1.4 collective-permute-start.5
  122.5 69.2 %collective-permute-start.15 = (f32[576,384]{1,0:T(8,128)}, f32[576,384]{1,0:T(8,128)S(1)}, u32[]{:S(2)}, u32[]{:S(2)}) collective-permute-start(f32[576,384]{1,0:T(8,128)} %get-tuple-element.141), channel_id=1, source_target_pairs={{0,1},{1,0},{2,3},{3,2},{4,5},{5,4},{6,7},{7,6},{8,9},{9,8},{10,11... | collective-permute-start | bytes 2654216 | tf_op jit(solution)/shard_map/ppermute | solution.py:959
  123.8 3.6 %copy-start.32 = (f32[8,128]{1,0:T(8,128)}, f32[8,128]{1,0:T(8,128)S(1)}, u32[]{:S(2)}) copy-start(f32[8,128]{1,0:T(8,128)S(1)} %add.43.refs_13_) | copy-start | bytes 12292
  123.8 29.4 %collective-permute-start.6 = (f32[8,128]{1,0:T(8,128)S(1)}, f32[8,128]{1,0:T(8,128)S(1)}, u32[]{:S(2)}, u32[]{:S(2)}) collective-permute-start(f32[8,128]{1,0:T(8,128)S(1)} %add.43.refs_13_), channel_id=1, source_target_pairs={{0,2},{1,3},{2,0},{3,1},{4,6},{5,7},{6,4},{7,5},{8,10},{9,11},{10,... | collective-permute-start | bytes 12296 | tf_op jit(solution)/shard_map/ppermute | solution.py:959
  125.4 28.4 %collective-permute-start.7 = (f32[8,128]{1,0:T(8,128)S(1)}, f32[8,128]{1,0:T(8,128)S(1)}, u32[]{:S(2)}, u32[]{:S(2)}) collective-permute-start(f32[8,128]{1,0:T(8,128)S(1)} %add.43.refs_13_), channel_id=1, source_target_pairs={{0,4},{1,5},{2,6},{3,7},{4,0},{5,1},{6,2},{7,3},{8,12},{9,13},{10,... | collective-permute-start | bytes 12296 | tf_op jit(solution)/shard_map/ppermute | solution.py:959
  125.9 27.9 %collective-permute-start.8 = (f32[8,128]{1,0:T(8,128)S(1)}, f32[8,128]{1,0:T(8,128)S(1)}, u32[]{:S(2)}, u32[]{:S(2)}) collective-permute-start(f32[8,128]{1,0:T(8,128)S(1)} %add.43.refs_13_), channel_id=1, source_target_pairs={{0,6},{1,7},{2,4},{3,5},{4,2},{5,3},{6,0},{7,1},{8,14},{9,15},{10,... | collective-permute-start | bytes 12296 | tf_op jit(solution)/shard_map/ppermute | solution.py:959
  153.2 38.5 %collective-permute-start.12 = (f32[576,384]{1,0:T(8,128)}, f32[576,384]{1,0:T(8,128)S(1)}, u32[]{:S(2)}, u32[]{:S(2)}) collective-permute-start(f32[576,384]{1,0:T(8,128)} %get-tuple-element.125), channel_id=1, source_target_pairs={{0,1},{1,0},{2,3},{3,2},{4,5},{5,4},{6,7},{7,6},{8,9},{9,8},{10,11... | collective-permute-start | bytes 2654216 | tf_op jit(solution)/shard_map/ppermute | solution.py:959
  153.3 38.4 %collective-permute-start.13 = (f32[576,384]{1,0:T(8,128)}, f32[576,384]{1,0:T(8,128)S(1)}, u32[]{:S(2)}, u32[]{:S(2)}) collective-permute-start(f32[576,384]{1,0:T(8,128)} %get-tuple-element.127), channel_id=1, source_target_pairs={{0,1},{1,0},{2,3},{3,2},{4,5},{5,4},{6,7},{7,6},{8,9},{9,8},{10,11... | collective-permute-start | bytes 2654216 | tf_op jit(solution)/shard_map/ppermute | solution.py:959
  155.1 21.4 %copy-start.31 = (f32[8,128]{1,0:T(8,128)S(1)}, f32[8,128]{1,0:T(8,128)}, u32[]{:S(2)}) copy-start(f32[8,128]{1,0:T(8,128)} %add_add_fusion.1.refs_18_) | copy-start | bytes 12292
  155.1 35.0 %copy-start.34 = (f32[192,384]{1,0:T(8,128)S(1)}, f32[192,384]{1,0:T(8,128)}, u32[]{:S(2)}) copy-start(f32[192,384]{1,0:T(8,128)} %get-tuple-element.143) | copy-start | bytes 884740
  176.4 15.3 %collective-permute-start.14 = (f32[384,384]{1,0:T(8,128)}, f32[384,384]{1,0:T(8,128)S(1)}, u32[]{:S(2)}, u32[]{:S(2)}) collective-permute-start(f32[384,384]{1,0:T(8,128)} %get-tuple-element.139), channel_id=1, source_target_pairs={{0,1},{1,0},{2,3},{3,2},{4,5},{5,4},{6,7},{7,6},{8,9},{9,8},{10,11... | collective-permute-start | bytes 1769480 | tf_op jit(solution)/shard_map/ppermute | solution.py:959
  176.5 4.6 %collective-permute-start.10 = (f32[8,128]{1,0:T(8,128)S(1)}, f32[8,128]{1,0:T(8,128)S(1)}, u32[]{:S(2)}, u32[]{:S(2)}) collective-permute-start(f32[8,128]{1,0:T(8,128)S(1)} %copy-done.31), channel_id=1, source_target_pairs={{0,16},{1,17},{2,18},{3,19},{4,20},{5,21},{6,22},{7,23},{8,24},{9,... | collective-permute-start | bytes 12296 | tf_op jit(solution)/shard_map/ppermute | solution.py:959
  181.1 5.4 %collective-permute-start.11 = (f32[8,128]{1,0:T(8,128)S(1)}, f32[8,128]{1,0:T(8,128)S(1)}, u32[]{:S(2)}, u32[]{:S(2)}) collective-permute-start(f32[8,128]{1,0:T(8,128)S(1)} %copy-done.31), channel_id=1, source_target_pairs={{0,24},{1,25},{2,26},{3,27},{4,28},{5,29},{6,30},{7,31},{8,16},{9,... | collective-permute-start | bytes 12296 | tf_op jit(solution)/shard_map/ppermute | solution.py:959
  186.5 3.6 %collective-permute-start.9 = (f32[8,128]{1,0:T(8,128)S(1)}, f32[8,128]{1,0:T(8,128)S(1)}, u32[]{:S(2)}, u32[]{:S(2)}) collective-permute-start(f32[8,128]{1,0:T(8,128)S(1)} %copy-done.31), channel_id=1, source_target_pairs={{0,8},{1,9},{2,10},{3,11},{4,12},{5,13},{6,14},{7,15},{8,0},{9,1},... | collective-permute-start | bytes 12296 | tf_op jit(solution)/shard_map/ppermute | solution.py:959
  190.1 1.6 collective-permute-start.16
  191.7 1.5 copy-start.3
  191.7 1.7 copy-start.4
  198.5 13.6 %collective-permute-start.20 = (f32[192,384]{1,0:T(8,128)}, f32[192,384]{1,0:T(8,128)S(1)}, u32[]{:S(2)}, u32[]{:S(2)}) collective-permute-start(f32[192,384]{1,0:T(8,128)} %get-tuple-element.149), channel_id=1, source_target_pairs={{0,8},{1,9},{2,10},{3,11},{4,12},{5,13},{6,14},{7,15},{8,0},{9,1},... | collective-permute-start | bytes 884744 | tf_op jit(solution)/shard_map/ppermute | solution.py:959
  198.5 29.1 %collective-permute-start.17 = (f32[384,384]{1,0:T(8,128)}, f32[384,384]{1,0:T(8,128)S(1)}, u32[]{:S(2)}, u32[]{:S(2)}) collective-permute-start(f32[384,384]{1,0:T(8,128)} %get-tuple-element.145), channel_id=1, source_target_pairs={{0,2},{1,3},{2,0},{3,1},{4,6},{5,7},{6,4},{7,5},{8,10},{9,11},{10,... | collective-permute-start | bytes 1769480 | tf_op jit(solution)/shard_map/ppermute | solution.py:959
  200.1 29.3 %collective-permute-start.18 = (f32[384,384]{1,0:T(8,128)}, f32[384,384]{1,0:T(8,128)S(1)}, u32[]{:S(2)}, u32[]{:S(2)}) collective-permute-start(f32[384,384]{1,0:T(8,128)} %get-tuple-element.146), channel_id=1, source_target_pairs={{0,4},{1,5},{2,6},{3,7},{4,0},{5,1},{6,2},{7,3},{8,12},{9,13},{10,... | collective-permute-start | bytes 1769480 | tf_op jit(solution)/shard_map/ppermute | solution.py:959
  200.7 28.7 %collective-permute-start.19 = (f32[384,384]{1,0:T(8,128)}, f32[384,384]{1,0:T(8,128)S(1)}, u32[]{:S(2)}, u32[]{:S(2)}) collective-permute-start(f32[384,384]{1,0:T(8,128)} %get-tuple-element.147), channel_id=1, source_target_pairs={{0,6},{1,7},{2,4},{3,5},{4,2},{5,3},{6,0},{7,1},{8,14},{9,15},{10,... | collective-permute-start | bytes 1769480 | tf_op jit(solution)/shard_map/ppermute | solution.py:959
  202.1 25.6 %collective-permute-start.21 = (f32[192,384]{1,0:T(8,128)}, f32[192,384]{1,0:T(8,128)S(1)}, u32[]{:S(2)}, u32[]{:S(2)}) collective-permute-start(f32[192,384]{1,0:T(8,128)} %get-tuple-element.150), channel_id=1, source_target_pairs={{0,16},{1,17},{2,18},{3,19},{4,20},{5,21},{6,22},{7,23},{8,24},{9,... | collective-permute-start | bytes 884744 | tf_op jit(solution)/shard_map/ppermute | solution.py:959
  212.1 17.3 %copy-start.13 = (f32[192,384]{1,0:T(8,128)}, f32[192,384]{1,0:T(8,128)S(1)}, u32[]{:S(2)}) copy-start(f32[192,384]{1,0:T(8,128)S(1)} %collective-permute-done.20.refs_6_) | copy-start | bytes 884740
  212.1 15.6 %collective-permute-start.22 = (f32[192,384]{1,0:T(8,128)}, f32[192,384]{1,0:T(8,128)S(1)}, u32[]{:S(2)}, u32[]{:S(2)}) collective-permute-start(f32[192,384]{1,0:T(8,128)} %get-tuple-element.151), channel_id=1, source_target_pairs={{0,24},{1,25},{2,26},{3,27},{4,28},{5,29},{6,30},{7,31},{8,16},{9,... | collective-permute-start | bytes 884744 | tf_op jit(solution)/shard_map/ppermute | solution.py:959
  227.6 1.8 copy-start.14
  227.6 1.8 copy-start.15
  227.7 1.8 copy-start.9
  233.5 8.8 %collective-permute-start.26 = (f32[48,384]{1,0:T(8,128)}, f32[48,384]{1,0:T(8,128)S(1)}, u32[]{:S(2)}, u32[]{:S(2)}) collective-permute-start(f32[48,384]{1,0:T(8,128)} %get-tuple-element.157), channel_id=1, source_target_pairs={{0,2},{1,3},{2,0},{3,1},{4,6},{5,7},{6,4},{7,5},{8,10},{9,11},{10,... | collective-permute-start | bytes 221192 | tf_op jit(solution)/shard_map/ppermute | solution.py:959
  234.5 13.3 %collective-permute-start.23 = (f32[96,384]{1,0:T(8,128)}, f32[96,384]{1,0:T(8,128)S(1)}, u32[]{:S(2)}, u32[]{:S(2)}) collective-permute-start(f32[96,384]{1,0:T(8,128)} %get-tuple-element.153), channel_id=1, source_target_pairs={{0,8},{1,9},{2,10},{3,11},{4,12},{5,13},{6,14},{7,15},{8,0},{9,1},... | collective-permute-start | bytes 442376 | tf_op jit(solution)/shard_map/ppermute | solution.py:959
  239.0 14.4 %collective-permute-start.24 = (f32[96,384]{1,0:T(8,128)}, f32[96,384]{1,0:T(8,128)S(1)}, u32[]{:S(2)}, u32[]{:S(2)}) collective-permute-start(f32[96,384]{1,0:T(8,128)} %get-tuple-element.154), channel_id=1, source_target_pairs={{0,16},{1,17},{2,18},{3,19},{4,20},{5,21},{6,22},{7,23},{8,24},{9,... | collective-permute-start | bytes 442376 | tf_op jit(solution)/shard_map/ppermute | solution.py:959
  239.0 14.4 %collective-permute-start.25 = (f32[96,384]{1,0:T(8,128)}, f32[96,384]{1,0:T(8,128)S(1)}, u32[]{:S(2)}, u32[]{:S(2)}) collective-permute-start(f32[96,384]{1,0:T(8,128)} %get-tuple-element.155), channel_id=1, source_target_pairs={{0,24},{1,25},{2,26},{3,27},{4,28},{5,29},{6,30},{7,31},{8,16},{9,... | collective-permute-start | bytes 442376 | tf_op jit(solution)/shard_map/ppermute | solution.py:959
  241.4 4.6 %collective-permute-start.27 = (f32[48,384]{1,0:T(8,128)}, f32[48,384]{1,0:T(8,128)S(1)}, u32[]{:S(2)}, u32[]{:S(2)}) collective-permute-start(f32[48,384]{1,0:T(8,128)} %get-tuple-element.158), channel_id=1, source_target_pairs={{0,4},{1,5},{2,6},{3,7},{4,0},{5,1},{6,2},{7,3},{8,12},{9,13},{10,... | collective-permute-start | bytes 221192 | tf_op jit(solution)/shard_map/ppermute | solution.py:959
  242.3 11.1 %copy-start.25 = (f32[48,384]{1,0:T(8,128)}, f32[48,384]{1,0:T(8,128)S(1)}, u32[]{:S(2)}) copy-start(f32[48,384]{1,0:T(8,128)S(1)} %collective-permute-done.26.refs_6_) | copy-start | bytes 221188
  242.3 5.5 %collective-permute-start.28 = (f32[48,384]{1,0:T(8,128)}, f32[48,384]{1,0:T(8,128)S(1)}, u32[]{:S(2)}, u32[]{:S(2)}) collective-permute-start(f32[48,384]{1,0:T(8,128)} %get-tuple-element.159), channel_id=1, source_target_pairs={{0,6},{1,7},{2,4},{3,5},{4,2},{5,3},{6,0},{7,1},{8,14},{9,15},{10,... | collective-permute-start | bytes 221192 | tf_op jit(solution)/shard_map/ppermute | solution.py:959
  246.0 7.5 %copy-start.27 = (f32[48,384]{1,0:T(8,128)}, f32[48,384]{1,0:T(8,128)S(1)}, u32[]{:S(2)}) copy-start(f32[48,384]{1,0:T(8,128)S(1)} %collective-permute-done.27.refs_7_) | copy-start | bytes 221188
  247.8 5.7 %copy-start.28 = (f32[48,384]{1,0:T(8,128)}, f32[48,384]{1,0:T(8,128)S(1)}, u32[]{:S(2)}) copy-start(f32[48,384]{1,0:T(8,128)S(1)} %collective-permute-done.28.refs_8_) | copy-start | bytes 221188
  247.8 5.7 %copy-start.19 = (f32[96,384]{1,0:T(8,128)}, f32[96,384]{1,0:T(8,128)S(1)}, u32[]{:S(2)}) copy-start(f32[96,384]{1,0:T(8,128)S(1)} %collective-permute-done.23.refs_2_) | copy-start | bytes 442372
  256.2 6.8 %collective-permute-start.32 = (f32[48,384]{1,0:T(8,128)}, f32[48,384]{1,0:T(8,128)S(1)}, u32[]{:S(2)}, u32[]{:S(2)}) collective-permute-start(f32[48,384]{1,0:T(8,128)} %get-tuple-element.163.refs_5_), channel_id=1, source_target_pairs={{0,2},{1,3},{2,0},{3,1},{4,6},{5,7},{6,4},{7,5},{8,10},{9,11},{10,... | collective-permute-start | bytes 221192 | tf_op jit(solution)/shard_map/ppermute | solution.py:959
  257.2 12.1 %collective-permute-start.29 = (f32[96,384]{1,0:T(8,128)}, f32[96,384]{1,0:T(8,128)S(1)}, u32[]{:S(2)}, u32[]{:S(2)}) collective-permute-start(f32[96,384]{1,0:T(8,128)} %get-tuple-element.160.refs_6_.refs_1_), channel_id=1, source_target_pairs={{0,8},{1,9},{2,10},{3,11},{4,12},{5,13},{6,14},{7,15},{8,0},{9,1},... | collective-permute-start | bytes 442376 | tf_op jit(solution)/shard_map/ppermute | solution.py:959
  259.5 14.2 %collective-permute-start.30 = (f32[96,384]{1,0:T(8,128)}, f32[96,384]{1,0:T(8,128)S(1)}, u32[]{:S(2)}, u32[]{:S(2)}) collective-permute-start(f32[96,384]{1,0:T(8,128)} %get-tuple-element.160.refs_6_.refs_1_), channel_id=1, source_target_pairs={{0,16},{1,17},{2,18},{3,19},{4,20},{5,21},{6,22},{7,23},{8,24},{9,... | collective-permute-start | bytes 442376 | tf_op jit(solution)/shard_map/ppermute | solution.py:959
  259.5 20.6 %collective-permute-start.31 = (f32[96,384]{1,0:T(8,128)}, f32[96,384]{1,0:T(8,128)S(1)}, u32[]{:S(2)}, u32[]{:S(2)}) collective-permute-start(f32[96,384]{1,0:T(8,128)} %get-tuple-element.160.refs_6_.refs_1_), channel_id=1, source_target_pairs={{0,24},{1,25},{2,26},{3,27},{4,28},{5,29},{6,30},{7,31},{8,16},{9,... | collective-permute-start | bytes 442376 | tf_op jit(solution)/shard_map/ppermute | solution.py:959
  261.9 4.6 %collective-permute-start.33 = (f32[48,384]{1,0:T(8,128)}, f32[48,384]{1,0:T(8,128)S(1)}, u32[]{:S(2)}, u32[]{:S(2)}) collective-permute-start(f32[48,384]{1,0:T(8,128)} %get-tuple-element.163.refs_5_), channel_id=1, source_target_pairs={{0,4},{1,5},{2,6},{3,7},{4,0},{5,1},{6,2},{7,3},{8,12},{9,13},{10,... | collective-permute-start | bytes 221192 | tf_op jit(solution)/shard_map/ppermute | solution.py:959
  263.0 17.2 %copy-start.26 = (f32[48,384]{1,0:T(8,128)}, f32[48,384]{1,0:T(8,128)S(1)}, u32[]{:S(2)}) copy-start(f32[48,384]{1,0:T(8,128)S(1)} %collective-permute-done.32.refs_6_) | copy-start | bytes 221188
  263.0 5.6 %collective-permute-start.34 = (f32[48,384]{1,0:T(8,128)}, f32[48,384]{1,0:T(8,128)S(1)}, u32[]{:S(2)}, u32[]{:S(2)}) collective-permute-start(f32[48,384]{1,0:T(8,128)} %get-tuple-element.163.refs_5_), channel_id=1, source_target_pairs={{0,6},{1,7},{2,4},{3,5},{4,2},{5,3},{6,0},{7,1},{8,14},{9,15},{10,... | collective-permute-start | bytes 221192 | tf_op jit(solution)/shard_map/ppermute | solution.py:959
  266.5 13.6 %copy-start.29 = (f32[48,384]{1,0:T(8,128)}, f32[48,384]{1,0:T(8,128)S(1)}, u32[]{:S(2)}) copy-start(f32[48,384]{1,0:T(8,128)S(1)} %collective-permute-done.33.refs_7_) | copy-start | bytes 221188
  268.5 11.6 %copy-start.30 = (f32[48,384]{1,0:T(8,128)}, f32[48,384]{1,0:T(8,128)S(1)}, u32[]{:S(2)}) copy-start(f32[48,384]{1,0:T(8,128)S(1)} %collective-permute-done.34.refs_8_) | copy-start | bytes 221188
  269.3 10.8 %copy-start.22 = (f32[96,384]{1,0:T(8,128)}, f32[96,384]{1,0:T(8,128)S(1)}, u32[]{:S(2)}) copy-start(f32[96,384]{1,0:T(8,128)S(1)} %collective-permute-done.29.refs_2_) | copy-start | bytes 442372
  273.8 6.4 %copy-start.23 = (f32[96,384]{1,0:T(8,128)}, f32[96,384]{1,0:T(8,128)S(1)}, u32[]{:S(2)}) copy-start(f32[96,384]{1,0:T(8,128)S(1)} %collective-permute-done.30.refs_3_) | copy-start | bytes 442372
  283.1 19.1 %collective-permute-start.38 = (f32[4,48,384]{2,1,0:T(8,128)}, f32[4,48,384]{2,1,0:T(8,128)S(1)}, u32[]{:S(2)}, u32[]{:S(2)}) collective-permute-start(f32[4,48,384]{2,1,0:T(8,128)} %get-tuple-element.165.refs_5_), channel_id=1, source_target_pairs={{0,8},{1,9},{2,10},{3,11},{4,12},{5,13},{6,14},{7,15},{8,0},{9,1},... | collective-permute-start | bytes 884744 | tf_op jit(solution)/shard_map/ppermute | solution.py:959
  285.3 29.9 %collective-permute-start.35 = (f32[4,96,384]{2,1,0:T(8,128)}, f32[4,96,384]{2,1,0:T(8,128)S(1)}, u32[]{:S(2)}, u32[]{:S(2)}) collective-permute-start(f32[4,96,384]{2,1,0:T(8,128)} %get-tuple-element.164.refs_2_.refs_1_), channel_id=1, source_target_pairs={{0,2},{1,3},{2,0},{3,1},{4,6},{5,7},{6,4},{7,5},{8,10},{9,11},{10,... | collective-permute-start | bytes 1769480 | tf_op jit(solution)/shard_map/ppermute | solution.py:959
  286.4 28.9 %collective-permute-start.36 = (f32[4,96,384]{2,1,0:T(8,128)}, f32[4,96,384]{2,1,0:T(8,128)S(1)}, u32[]{:S(2)}, u32[]{:S(2)}) collective-permute-start(f32[4,96,384]{2,1,0:T(8,128)} %get-tuple-element.164.refs_2_.refs_1_), channel_id=1, source_target_pairs={{0,4},{1,5},{2,6},{3,7},{4,0},{5,1},{6,2},{7,3},{8,12},{9,13},{10,... | collective-permute-start | bytes 1769480 | tf_op jit(solution)/shard_map/ppermute | solution.py:959
  287.5 27.8 %collective-permute-start.37 = (f32[4,96,384]{2,1,0:T(8,128)}, f32[4,96,384]{2,1,0:T(8,128)S(1)}, u32[]{:S(2)}, u32[]{:S(2)}) collective-permute-start(f32[4,96,384]{2,1,0:T(8,128)} %get-tuple-element.164.refs_2_.refs_1_), channel_id=1, source_target_pairs={{0,6},{1,7},{2,4},{3,5},{4,2},{5,3},{6,0},{7,1},{8,14},{9,15},{10,... | collective-permute-start | bytes 1769480 | tf_op jit(solution)/shard_map/ppermute | solution.py:959
  288.8 26.4 %collective-permute-start.39 = (f32[4,48,384]{2,1,0:T(8,128)}, f32[4,48,384]{2,1,0:T(8,128)S(1)}, u32[]{:S(2)}, u32[]{:S(2)}) collective-permute-start(f32[4,48,384]{2,1,0:T(8,128)} %get-tuple-element.165.refs_5_), channel_id=1, source_target_pairs={{0,16},{1,17},{2,18},{3,19},{4,20},{5,21},{6,22},{7,23},{8,24},{9,... | collective-permute-start | bytes 884744 | tf_op jit(solution)/shard_map/ppermute | solution.py:959
  302.2 13.0 %copy-start.16 = (f32[4,48,384]{2,1,0:T(8,128)}, f32[4,48,384]{2,1,0:T(8,128)S(1)}, u32[]{:S(2)}) copy-start(f32[4,48,384]{2,1,0:T(8,128)S(1)} %collective-permute-done.38.refs_6_) | copy-start | bytes 884740
  302.2 13.0 %collective-permute-start.40 = (f32[4,48,384]{2,1,0:T(8,128)}, f32[4,48,384]{2,1,0:T(8,128)S(1)}, u32[]{:S(2)}, u32[]{:S(2)}) collective-permute-start(f32[4,48,384]{2,1,0:T(8,128)} %get-tuple-element.165.refs_5_), channel_id=1, source_target_pairs={{0,24},{1,25},{2,26},{3,27},{4,28},{5,29},{6,30},{7,31},{8,16},{9,... | collective-permute-start | bytes 884744 | tf_op jit(solution)/shard_map/ppermute | solution.py:959
  320.5 6.4 %collective-permute-start.41 = (f32[4,384,384]{2,1,0:T(8,128)}, f32[4,384,384]{2,1,0:T(8,128)S(1)}, u32[]{:S(2)}, u32[]{:S(2)}) collective-permute-start(f32[4,384,384]{2,1,0:T(8,128)} %bitcast.20), channel_id=1, source_target_pairs={{0,1},{1,0},{2,3},{3,2},{4,5},{5,4},{6,7},{7,6},{8,9},{9,8},{10,11... | collective-permute-start | bytes 7077896 | tf_op jit(solution)/shard_map/ppermute | solution.py:959
  320.5 6.4 %collective-permute-start.42 = (f32[4,192,384]{2,1,0:T(8,128)}, f32[4,192,384]{2,1,0:T(8,128)S(1)}, u32[]{:S(2)}, u32[]{:S(2)}) collective-permute-start(f32[4,192,384]{2,1,0:T(8,128)} %bitcast.26), channel_id=1, source_target_pairs={{0,1},{1,0},{2,3},{3,2},{4,5},{5,4},{6,7},{7,6},{8,9},{9,8},{10,11... | collective-permute-start | bytes 3538952 | tf_op jit(solution)/shard_map/ppermute | solution.py:959
  327.0 1.8 copy-start
  (15 other events, 13.6 us)
Sparse Core Ops, SparseCore 0:
  123.1 180.4 all-reduce.1

commit v3 on v2

v3 whole, which is shorter than its diff:
```python
import functools
import math

import jax
import jax.numpy as jnp
from jax import lax
from jax.experimental import pallas as pl
from jax.experimental.pallas import tpu as pltpu
from jax.sharding import PartitionSpec as P

D = 192
HEADS = 2
HEAD = 96
LANES = 128
FILTER = 768
MEL = 80
HID = 192
VOCAB = 148
KSIZE = 3
WKER = 5
WLAYERS = 4
WINDOW = 4
PERIOD = 16

F32 = jnp.float32
BF16 = jnp.bfloat16
HIGH = lax.Precision.HIGHEST
VMEM_BYTES = 58 * 1024 * 1024
WIDE = 384
UNIT = 1152
REST = 640
TAIL = 128
COST = 1.15e9
ROW_TABLE = 2 * D
ROW_PRIOR = ROW_TABLE + MEL
ROW_NORM = ROW_PRIOR + MEL
ROW_REL = ROW_NORM + 8


def contract(first_op, second_op, dims, precision=None):
    return lax.dot_general(
        first_op, second_op, (dims, ((), ())), preferred_element_type=F32, precision=precision
    )


def dot_nn(first_op, second_op, precision=None):
    return contract(first_op, second_op, ((1,), (0,)), precision)


def dot_nt(first_op, second_op, precision=None):
    return contract(first_op, second_op, ((1,), (1,)), precision)


def dot_tn(first_op, second_op, precision=None):
    return contract(first_op, second_op, ((0,), (0,)), precision)


def halves(values):
    high = values.astype(BF16)
    low = (values - high.astype(F32)).astype(BF16)
    return high, low


def iota(shape, axis):
    return lax.broadcasted_iota(jnp.int32, shape, axis)


def rows_of(length):
    return iota((length, 1), 0)


def full_spec(array):
    rank = len(array.shape)
    return pl.BlockSpec(array.shape, lambda *_: (0,) * rank)


def item_spec(array):
    rank = len(array.shape)
    return pl.BlockSpec((1,) + array.shape[1:], lambda b: (b,) + (0,) * (rank - 1))


def layer_spec(array, layer):
    rank = len(array.shape)
    return pl.BlockSpec((1, 1) + array.shape[2:], lambda b: (layer, b) + (0,) * (rank - 2))


def weight_spec(array, layer):
    rank = len(array.shape)
    return pl.BlockSpec((1,) + array.shape[1:], lambda b: (layer,) + (0,) * (rank - 1))


def shape_of(shape, dtype=F32):
    return jax.ShapeDtypeStruct(shape, dtype)


def run(body, grid, ins, in_specs, outs, out_specs, scratch=(), micros=5, after=(), aliases=None, name=None):
    count, extra = len(ins), len(after)

    def wrapped(*refs):
        body(*refs[:count], *refs[count + extra :])

    return pl.pallas_call(
        wrapped,
        grid=grid,
        in_specs=list(in_specs) + [pl.BlockSpec(memory_space=pl.ANY)] * extra,
        out_specs=out_specs,
        out_shape=outs,
        scratch_shapes=list(scratch),
        compiler_params=pltpu.CompilerParams(vmem_limit_bytes=VMEM_BYTES),
        cost_estimate=pl.CostEstimate(
            flops=int(micros * COST), bytes_accessed=1 << 20, transcendentals=0
        ),
        input_output_aliases=aliases or {},
        name=name,
    )(*ins, *after)


def pair_rows(durations_row):
    return jnp.sum(durations_row, axis=1, keepdims=True) >> 1


def stats_body(mel_ref, dur_ref, out_ref):
    items, _, frames = mel_ref.shape
    lane = iota((1, frames), 1)
    count = jnp.zeros((1, 1), F32)
    sums = jnp.zeros((MEL, LANES), F32)
    squares = jnp.zeros((MEL, LANES), F32)
    for item in range(items):
        pair_count = pair_rows(dur_ref[item : item + 1, :])
        count = count + pair_count.astype(F32)
        values = jnp.where(lane < 2 * pair_count, mel_ref[item], 0.0)
        for part in range(frames // LANES):
            piece = values[:, part * LANES : (part + 1) * LANES]
            sums = sums + piece
            squares = squares + piece * piece
    place = iota((MEL, LANES), 1)
    table = jnp.zeros((MEL, LANES), F32)
    for side in range(2):
        chosen = (place & 1) == side
        for spot, held in ((side, sums), (2 + side, squares)):
            column = jnp.sum(jnp.where(chosen, held, 0.0), axis=1, keepdims=True)
            table = jnp.where(place == spot, column, table)
    table = jnp.concatenate([table, jnp.zeros((LANES - MEL, LANES), F32)], axis=0)
    rows = table.T[0:8]
    out_ref[...] = jnp.where(iota((8, LANES), 0) == 4, count, rows)


def read_stats(stats):
    total = stats[4:5, 0:1]
    sums = jnp.concatenate([stats[0:1], stats[1:2]], axis=1)
    squares = jnp.concatenate([stats[2:3], stats[3:4]], axis=1)
    center = sums / total
    variance = squares / total - center * center
    log_act = -0.5 * jnp.log(variance + 1e-06)
    return total, center, variance, log_act, jnp.exp(log_act)


def mix_places():
    row = rows_of(2 * LANES)
    col = iota((1, 2 * LANES), 1)
    row_lane = row & (LANES - 1)
    col_lane = col & (LANES - 1)
    upper = (row_lane >= MEL // 2).astype(jnp.int32)
    row_group = row_lane - upper * (MEL // 2)
    row_member = 2 * upper + (row >> 7)
    col_group = col_lane >> 1
    col_member = 2 * (col >> 7) + (col_lane & 1)
    match = (row_group == col_group) & (row_lane < MEL) & (col_lane < MEL)
    return row_member, col_member, match


def weights_body(
    mix_ref,
    qkv_ref,
    relk_ref,
    relv_ref,
    out_ref,
    prior_ref,
    start_ref,
    end_ref,
    res_ref,
    last_ref,
    mixm_ref,
    small_ref,
    qkv_pad_ref,
    relk_pad_ref,
    relv_pad_ref,
    out_pad_ref,
    wide_ref,
    prior_pad_ref,
    start_pad_ref,
    end_pad_ref,
    res_four_ref,
):
    row_member, col_member, match = mix_places()
    table = jnp.zeros((2 * LANES, 2 * LANES), F32)
    for i in range(4):
        column = jnp.zeros((2 * LANES, 1), F32)
        for j in range(4):
            column = jnp.where(row_member == j, mix_ref[i, j], column)
        table = jnp.where(col_member == i, column, table)
    mixm_ref[...] = jnp.where(match, table, 0.0)
    res_four_ref[: WLAYERS - 1] = res_ref[...]
    res_four_ref[WLAYERS - 1] = jnp.concatenate(
        [jnp.zeros((HID, HID), F32), last_ref[...].astype(F32)], axis=1
    ).astype(BF16)

    ri = iota((8, LANES), 0)
    ci = iota((8, LANES), 1)
    joined = jnp.where((ci == ri + 4) & (ri < 4), 1.0, 0.0).astype(F32)
    for i in range(4):
        for j in range(4):
            joined = jnp.where((ri == i) & (ci == j), mix_ref[i, j], joined)
    determinant = jnp.ones((1, 1), F32)
    for column in range(4):
        pivot = joined[column : column + 1, column : column + 1]
        determinant = determinant * pivot
        row_now = joined[column : column + 1, :] / pivot
        joined = joined - joined[:, column : column + 1] * row_now
        joined = jnp.where(ri == column, row_now, joined)
    turned = jnp.zeros((8, LANES), F32)
    for i in range(4):
        for j in range(4):
            turned = jnp.where((ri == j) & (ci == i), joined[i : i + 1, 4 + j : 5 + j], turned)
    small_ref[...] = jnp.where(ri == 4, determinant, turned)

    def select(count, wanted):
        return jnp.where(rows_of(count) == wanted, 1.0, 0.0).astype(BF16)

    place = iota((1, 6 * LANES), 1)
    lane = place & (LANES - 1)
    wanted = jnp.where(lane < HEAD, (place >> 7) * HEAD + lane, -1)
    qkv_pad_ref[...] = dot_nn(qkv_ref[...], select(3 * D, wanted)).astype(BF16)

    place = iota((1, 2 * LANES), 1)
    lane = place & (LANES - 1)
    wanted = jnp.where(lane < HEAD, (place >> 7) * HEAD + lane, -1)
    out_pad_ref[...] = dot_tn(select(D, wanted), out_ref[...]).astype(BF16)

    wanted = iota((1, LANES), 1) & (PERIOD - 1)
    repeat = select(2 * WINDOW + 1, wanted)
    pad = jnp.zeros((LANES, LANES - HEAD), F32)
    relk_pad_ref[...] = jnp.concatenate([dot_tn(repeat, relk_ref[...]), pad], axis=1).astype(BF16)
    relv_pad_ref[...] = jnp.concatenate([dot_tn(repeat, relv_ref[...]), pad], axis=1).astype(BF16)

    place = iota((1, 8 * LANES), 1)
    lane = place & (LANES - 1)
    group = (place >> 7) & 3
    fits = (lane < MEL) & ((lane & 1) == (place >> 9))
    wanted = jnp.where(fits, (group >> 1) * MEL + (group & 1) * (MEL // 2) + (lane >> 1), -1)
    wide = select(2 * MEL, wanted)
    wide_ref[...] = wide
    prior_pad_ref[...] = dot_tn(prior_ref[...], wide).astype(BF16)

    wanted = iota((1, LANES), 1)
    start_pad_ref[...] = dot_tn(select(MEL, wanted), start_ref[...]).astype(BF16)
    place = iota((1, 2 * LANES), 1)
    lane = place & (LANES - 1)
    wanted = jnp.where(lane < MEL, (place >> 7) * MEL + lane, -1)
    end_pad_ref[...] = dot_tn(end_ref[...], select(2 * MEL, wanted)).astype(BF16)


def text_rows(dur_ref):
    item = pl.program_id(0)
    return dur_ref[pl.ds(item, 1), :]


def text_inside(durations_row, length):
    tokens = jnp.sum((durations_row > 0).astype(jnp.int32), axis=1, keepdims=True)
    return rows_of(length) < tokens


def norm_parts(inputs):
    centered = inputs - jnp.mean(inputs, axis=1, keepdims=True)
    spread = jnp.mean(centered * centered, axis=1, keepdims=True)
    inverse = lax.rsqrt(spread + 1e-05)
    return centered * inverse, inverse


def norm_back(inputs, gain, gradient):
    unit, inverse = norm_parts(inputs)
    gain_grad = jnp.sum(gradient * unit, axis=0, keepdims=True)
    shift_grad = jnp.sum(gradient, axis=0, keepdims=True)
    scaled = gradient * gain
    mean_one = jnp.mean(scaled, axis=1, keepdims=True)
    mean_two = jnp.mean(scaled * unit, axis=1, keepdims=True)
    return inverse * (scaled - mean_one - unit * mean_two), gain_grad, shift_grad


def band_of(length):
    offset = iota((length, length), 1) - iota((length, length), 0)
    return (offset <= WINDOW) & (offset >= -WINDOW)


def turn_rows(values, left):
    pieces = []
    for block in range(values.shape[0] // 8):
        if left:
            first, stride = (WINDOW + 8 * (block & 1), PERIOD - 1)
        else:
            first, stride = (PERIOD - WINDOW + 8 * (block & 1), 1)
        piece = values[block * 8 : (block + 1) * 8]
        pieces.append(pltpu.roll(piece, first, 1, stride=stride, stride_axis=0))
    return jnp.concatenate(pieces, axis=0)


def band_gather(weights_low, band, folding):
    kept = jnp.where(band, weights_low, jnp.zeros_like(weights_low))
    return turn_rows(dot_nn(kept, folding), True).astype(BF16)


def band_spread(near, band):
    turned = turn_rows(near, False)
    count = band.shape[1] // LANES
    return jnp.where(band, jnp.concatenate([turned] * count, axis=1), 0.0)


def folding_of(length):
    same = (iota((length, LANES), 0) & (PERIOD - 1)) == (iota((length, LANES), 1) & (PERIOD - 1))
    return jnp.where(same, 1.0, 0.0).astype(BF16)


def one_turn(rel_pad):
    return jnp.where(rows_of(LANES) < PERIOD, rel_pad, jnp.zeros_like(rel_pad))


def shifted_rows(values, offset, period):
    if offset == 0:
        return values
    length = values.shape[0]
    moved = pltpu.roll(values, (-offset) % length, 0)
    place = rows_of(length) & (period - 1)
    keep = (place < period - offset) if offset > 0 else (place >= -offset)
    return jnp.where(keep, moved, 0.0)


def unfold_rows(values, kernel, period, reverse=False):
    half = kernel // 2
    steps = [step - half for step in range(kernel)]
    if reverse:
        steps = [-step for step in steps]
    return jnp.concatenate(
        [shifted_rows(values, step, period).astype(BF16) for step in steps], axis=1
    )


GELU_A = math.sqrt(2.0 / math.pi)
GELU_B = 0.044715


def gelu_tanh(values):
    return jnp.tanh(GELU_A * (values + GELU_B * values * values * values))


def text_blocks(dur_ref, items):
    item = pl.program_id(0) * items
    rows = [dur_ref[pl.ds(item + i, 1), :] for i in range(items)]
    inside = [text_inside(row, row.shape[1]) for row in rows]
    return rows, jnp.concatenate(inside, axis=0)


def token_table(tok_ref, item):
    tokens = tok_ref[pl.ds(item, 1), :]
    return jnp.where(iota((VOCAB, tokens.shape[1]), 0) == tokens, 1.0, 0.0).astype(BF16)


def encoder_body(
    tok_ref,
    dur_ref,
    emb_ref,
    qkv_ref,
    relk_ref,
    relv_ref,
    out_ref,
    gain_ref,
    shift_ref,
    ff1_ref,
    ff2_ref,
    gain_two_ref,
    shift_two_ref,
    prior_ref,
    emb_low_ref,
    proj_ref,
    att_ref,
    banded_ref,
    attend_ref,
    mixed_ref,
    normed_low_ref,
    filt_ref,
    activ_ref,
    summed_ref,
    enc_ref,
    expand_ref,
    expand_low_ref,
):
    group, length, _ = emb_low_ref.shape
    first = pl.program_id(0) * group
    durations, inside = text_blocks(dur_ref, group)

    def rows(item):
        return slice(item * length, (item + 1) * length)

    def keep(ref, values):
        for item in range(group):
            ref[item] = values[rows(item)]

    looked = [dot_tn(token_table(tok_ref, first + i), emb_ref[...]) for i in range(group)]
    embedded = jnp.where(inside, jnp.concatenate(looked, axis=0) * math.sqrt(D), 0.0)
    emb_low = embedded.astype(BF16)
    keep(emb_low_ref, emb_low)
    proj = dot_nn(emb_low, qkv_ref[...]).astype(BF16)
    keep(proj_ref, proj)
    band = band_of(length)
    folding = folding_of(length)
    relv = one_turn(relv_ref[...])
    attended = []
    for item in range(group):
        key_bias = jnp.where(durations[item] > 0, 0.0, -10000.0)
        parts = []
        for head in range(HEADS):
            query, key, value = [
                proj[rows(item), part * LANES : (part + 1) * LANES]
                for part in (head, HEADS + head, 2 * HEADS + head)
            ]
            near = band_spread(dot_nt(query, relk_ref[...]), band)
            scores = (dot_nt(query, key) + near) * (1.0 / math.sqrt(HEAD)) + key_bias
            raised = jnp.exp(scores - jnp.max(scores, axis=1, keepdims=True))
            attention = raised * (1.0 / jnp.sum(raised, axis=1, keepdims=True))
            low = attention.astype(BF16)
            att_ref[item, head] = low
            banded = band_gather(low, band, folding)
            banded_ref[item, head] = banded
            parts.append(dot_nn(low, value) + dot_nn(banded, relv))
        attended.append(jnp.concatenate(parts, axis=1))
    attend = jnp.concatenate(attended, axis=0).astype(BF16)
    keep(attend_ref, attend)
    mixed = embedded + dot_nn(attend, out_ref[...])
    keep(mixed_ref, mixed)
    unit, _ = norm_parts(mixed)
    normed = unit * gain_ref[...] + shift_ref[...]
    masked = jnp.where(inside, normed, 0.0)
    keep(normed_low_ref, masked.astype(BF16))
    filtered = dot_nn(unfold_rows(masked, KSIZE, length), ff1_ref[...])
    keep(filt_ref, filtered.astype(BF16))
    activ = jnp.where(inside, 0.5 * filtered * (1.0 + gelu_tanh(filtered)), 0.0)
    keep(activ_ref, activ.astype(BF16))
    second = dot_nt(unfold_rows(activ, KSIZE, length), ff2_ref[...])
    summed = normed + jnp.where(inside, second, 0.0)
    keep(summed_ref, summed)
    unit, _ = norm_parts(summed)
    encoded = jnp.where(inside, unit * gain_two_ref[...] + shift_two_ref[...], 0.0).astype(BF16)
    keep(enc_ref, encoded)
    prior = dot_nn(encoded, prior_ref[...])
    high, low = halves(prior)
    wide = prior.shape[1] // 2
    for item in range(group):
        for side in range(2):
            spot = slice(side * length, (side + 1) * length)
            columns = slice(side * wide, (side + 1) * wide)
            expand_ref[item, spot] = high[rows(item), columns]
            expand_low_ref[item, spot] = low[rows(item), columns]


def accumulate(ref, values, first):
    @pl.when(first)
    def _():
        ref[...] = values

    @pl.when(jnp.logical_not(first))
    def _():
        ref[...] = ref[...] + values


def align_of(durations_row, pairs):
    length = durations_row.shape[1]
    upper = jnp.where(iota((length, length), 0) <= iota((length, length), 1), 1.0, 0.0).astype(F32)
    wide = jnp.broadcast_to(durations_row.astype(F32), (8, length))
    ends = dot_nn(wide, upper, HIGH)[0:1].astype(jnp.int32)
    starts = ends - durations_row
    frame = 2 * rows_of(pairs)
    even = (frame >= starts) & (frame < ends)
    odd = (frame + 1 >= starts) & (frame + 1 < ends)
    both = jnp.concatenate([jnp.where(even, 1.0, 0.0), jnp.where(odd, 1.0, 0.0)], axis=1)
    return both.astype(BF16)


def encoder_back_body(
    tok_ref,
    dur_ref,
    flow_ref,
    enc_ref,
    summed_ref,
    filt_ref,
    activ_ref,
    normed_low_ref,
    mixed_ref,
    attend_ref,
    att_ref,
    banded_ref,
    proj_ref,
    emb_low_ref,
    wide_ref,
    ff1_ref,
    ff2_ref,
    gain_two_ref,
    prior_ref,
    qkv_ref,
    relk_ref,
    relv_ref,
    out_ref,
    gain_ref,
    place_ref,
    kept_ref,
    sent_ref,
    one_acc,
    two_acc,
    rest_acc,
    table_acc,
    qkv_acc,
    out_acc,
    relk_acc,
    relv_acc,
    prior_acc,
    norm_acc,
    sems,
):
    group, length, _ = emb_low_ref.shape
    step = pl.program_id(0)
    first = step == 0
    last = step == pl.num_programs(0) - 1
    durations, inside = text_blocks(dur_ref, group)
    mine = place_ref[0] & 1
    deals = []
    begin = 0
    for source in (one_acc, two_acc, rest_acc):
        half = source.shape[0] // 2
        for side, target in ((mine, kept_ref), (1 - mine, sent_ref)):
            deals.append(
                pltpu.make_async_copy(
                    source.at[pl.ds(pl.multiple_of(side * half, 8), half), :],
                    target.at[pl.ds(begin, half), :],
                    sems.at[len(deals)],
                )
            )
        begin += half
    everything = (one_acc, two_acc, table_acc, qkv_acc, out_acc, relk_acc, relv_acc, prior_acc, norm_acc)

    @pl.when(first)
    def _():
        for ref in everything:
            ref[...] = jnp.zeros_like(ref)

    def rows(item):
        return slice(item * length, (item + 1) * length)

    def whole(ref):
        return jnp.concatenate([ref[i] for i in range(group)], axis=0)

    def norm_sums(at, gain_grad, shift_grad):
        norm_acc[at : at + 1, :] = norm_acc[at : at + 1, :] + gain_grad
        norm_acc[at + 1 : at + 2, :] = norm_acc[at + 1 : at + 2, :] + shift_grad

    half = wide_ref.shape[1] // 2
    gathered = []
    for item in range(group):
        align = align_of(durations[item], flow_ref.shape[1])
        spread = dot_tn(align, flow_ref[item])
        pieces = []
        for side in range(2):
            pieces += halves(spread[side * length : (side + 1) * length])
        gathered.append(jnp.concatenate(pieces, axis=1))
    chosen = jnp.concatenate(
        [wide_ref[:, side * half : (side + 1) * half] for side in (0, 0, 1, 1)], axis=1
    )
    grad = dot_nt(jnp.concatenate(gathered, axis=0), chosen)
    prior_low = jnp.where(inside, grad, 0.0).astype(BF16)
    prior_acc[...] = prior_acc[...] + dot_tn(prior_low, whole(enc_ref))
    enc_grad = jnp.where(inside, dot_nn(prior_low, prior_ref[...]), 0.0)
    summed_grad, gain_grad, shift_grad = norm_back(whole(summed_ref), gain_two_ref[...], enc_grad)
    norm_sums(2, gain_grad, shift_grad)
    second = jnp.where(inside, summed_grad, 0.0)
    taps = unfold_rows(second, KSIZE, length, reverse=True)
    sums = dot_tn(taps, whole(activ_ref))
    for tap in range(KSIZE):
        for part in range(2):
            begin = (2 * tap + part) * D
            two_acc[begin : begin + D, :] = (
                two_acc[begin : begin + D, :]
                + sums[tap * D : (tap + 1) * D, part * WIDE : (part + 1) * WIDE]
            )
    activ_grad = dot_nn(
        taps,
        jnp.concatenate(
            [ff2_ref[:, tap * FILTER : (tap + 1) * FILTER] for tap in range(KSIZE)], axis=0
        ),
    )
    filtered = whole(filt_ref).astype(F32)
    tanh = gelu_tanh(filtered)
    slope = 0.5 * (1.0 + tanh) + 0.5 * filtered * (1.0 - tanh * tanh) * GELU_A * (
        1.0 + 3.0 * GELU_B * filtered * filtered
    )
    first_grad = jnp.where(inside, activ_grad * slope, 0.0)
    taps = unfold_rows(first_grad, KSIZE, length, reverse=True)
    sums = dot_tn(whole(normed_low_ref), taps)
    for tap in range(KSIZE):
        for part in range(2):
            begin = part * KSIZE * D + tap * D
            column = tap * FILTER + part * WIDE
            one_acc[begin : begin + D, :] = (
                one_acc[begin : begin + D, :] + sums[:, column : column + WIDE]
            )
    back = dot_nt(
        taps,
        jnp.concatenate([ff1_ref[tap * D : (tap + 1) * D, :] for tap in range(KSIZE)], axis=1),
    )

    @pl.when(last)
    def _():
        for copy in deals[:4]:
            copy.start()

    normed_grad = summed_grad + jnp.where(inside, back, 0.0)
    mixed_grad, gain_grad, shift_grad = norm_back(whole(mixed_ref), gain_ref[...], normed_grad)
    norm_sums(0, gain_grad, shift_grad)
    out_low = mixed_grad.astype(BF16)
    out_acc[...] = out_acc[...] + dot_tn(whole(attend_ref), out_low)
    weight = dot_nt(out_low, out_ref[...]).astype(BF16)
    band = band_of(length)
    folding = folding_of(length)
    relk = one_turn(relk_ref[...])
    projected = []
    relk_sum = relk_acc[...]
    relv_sum = relv_acc[...]
    for item in range(group):
        queries, keys, values = [], [], []
        for head in range(HEADS):
            query, key, value = [
                proj_ref[item, :, part * LANES : (part + 1) * LANES]
                for part in (head, HEADS + head, 2 * HEADS + head)
            ]
            mine = weight[rows(item), head * LANES : (head + 1) * LANES]
            near = band_spread(dot_nt(mine, relv_ref[...]), band)
            grad = dot_nt(mine, value) + near
            low = att_ref[item, head]
            attention = low.astype(F32)
            values.append(dot_tn(low, mine))
            relv_sum = relv_sum + dot_tn(banded_ref[item, head], mine)
            score = attention * (grad - jnp.sum(attention * grad, axis=1, keepdims=True))
            score_low = (score * (1.0 / math.sqrt(HEAD))).astype(BF16)
            band_grad = band_gather(score_low, band, folding)
            queries.append(dot_nn(score_low, key) + dot_nn(band_grad, relk))
            keys.append(dot_tn(score_low, query))
            relk_sum = relk_sum + dot_tn(band_grad, query)
        projected.append(jnp.concatenate(queries + keys + values, axis=1))
    relk_acc[...] = relk_sum
    relv_acc[...] = relv_sum
    proj_low = jnp.concatenate(projected, axis=0).astype(BF16)
    qkv_acc[...] = qkv_acc[...] + dot_tn(whole(emb_low_ref), proj_low)
    embed_grad = jnp.where(inside, mixed_grad + dot_nt(proj_low, qkv_ref[...]), 0.0) * math.sqrt(D)
    hot = jnp.concatenate(
        [token_table(tok_ref, step * group + item) for item in range(group)], axis=1
    )
    high, low = halves(embed_grad)
    table_acc[...] = table_acc[...] + dot_nn(
        jnp.concatenate([hot, hot], axis=1), jnp.concatenate([high, low], axis=0)
    )

    @pl.when(last)
    def _():
        def beside(left, right):
            return jnp.concatenate([left, right], axis=1)

        rest_acc[...] = jnp.zeros_like(rest_acc)
        packed = [qkv_acc[:, part * LANES : part * LANES + HEAD] for part in range(3 * HEADS)]
        side = D // 2
        rest_acc[:D, :] = jnp.concatenate(packed[:4], axis=1)
        rest_acc[D : D + side, :] = jnp.concatenate(
            [packed[4][:side], packed[5][:side], packed[4][side:], packed[5][side:]], axis=1
        )
        rest_acc[D + side : 2 * D, :] = beside(out_acc[:HEAD, :], out_acc[LANES : LANES + HEAD, :])
        rest_acc[ROW_TABLE : ROW_TABLE + MEL, :D] = table_acc[:MEL, :]
        rest_acc[ROW_TABLE : ROW_TABLE + VOCAB - MEL, D:] = table_acc[MEL:, :]
        rest_acc[ROW_PRIOR : ROW_PRIOR + MEL, :] = beside(prior_acc[:MEL, :], prior_acc[MEL:, :])
        rest_acc[ROW_NORM : ROW_NORM + 1, :] = beside(norm_acc[0:1, :], norm_acc[1:2, :])
        rest_acc[ROW_NORM + 1 : ROW_NORM + 2, :] = beside(norm_acc[2:3, :], norm_acc[3:4, :])
        rest_acc[ROW_REL : ROW_REL + PERIOD, :LANES] = relk_acc[:PERIOD, :]
        rest_acc[ROW_REL : ROW_REL + PERIOD, LANES : 2 * LANES] = relv_acc[:PERIOD, :]
        for copy in deals[4:]:
            copy.start()
        for copy in deals:
            copy.wait()


def split_pairs(mel_ref, rows_ref):
    frames = mel_ref.shape[2]
    pairs = frames // 2
    rows_ref[:, :MEL] = mel_ref[0].T
    pad = jnp.zeros((pairs, LANES - MEL), F32)
    even = rows_ref[pl.ds(0, pairs, stride=2), :][:, :MEL]
    odd = rows_ref[pl.ds(1, pairs, stride=2), :][:, :MEL]
    return jnp.concatenate([even, pad, odd, pad], axis=1)


def gates_of(pre):
    return jnp.tanh(pre[:, :HID]), 1.0 / (1.0 + jnp.exp(-pre[:, HID:]))


def dot_three(values, table, back=False):
    high, low = halves(values)
    table_high, table_low = halves(table)
    left = jnp.concatenate([high, low, high], axis=1)
    if back:
        return dot_nt(left, jnp.concatenate([table_high, table_high, table_low], axis=1))
    return dot_nn(left, jnp.concatenate([table_high, table_high, table_low], axis=0))


STEP_POST = WLAYERS + 1
STEPS = 2 * WLAYERS + 2


def decoder_body(
    mel_ref,
    dur_ref,
    expand_ref,
    expand_low_ref,
    stats_ref,
    mixm_ref,
    start_ref,
    win_ref,
    wres_ref,
    wend_ref,
    place_ref,
    kept_ref,
    sent_ref,
    last_kept_ref,
    last_sent_ref,
    flow_ref,
    ngrad_ref,
    normal,
    passive_low,
    hidden_low,
    pre,
    hidden,
    skip,
    active,
    skip_low,
    passive_grad,
    gated,
    part,
    spread,
    wide,
    unit,
    rows,
    end_acc,
    start_acc,
    mix_acc,
    tail,
    high,
    low,
    flow,
    sums,
    sems,
):
    step = pl.program_id(0)
    items, _, frames = mel_ref.shape
    pairs = frames // 2
    conv = WKER * HID
    fetch = [
        pltpu.make_async_copy(expand_ref, high, sems.at[0]),
        pltpu.make_async_copy(expand_low_ref, low, sems.at[1]),
    ]
    write = pltpu.make_async_copy(flow, flow_ref, sems.at[2])
    mine = place_ref[0] & 1

    def deal(source, rows_each, targets, begin, first_sem):
        return [
            pltpu.make_async_copy(
                source.at[pl.ds(pl.multiple_of(side * rows_each, 8), rows_each), :],
                target.at[pl.ds(begin, rows_each), :],
                sems.at[first_sem + i],
            )
            for i, (side, target) in enumerate(((mine, targets[0]), (1 - mine, targets[1])))
        ]

    half = UNIT // 2
    deals = [deal(unit.at[0], half, (last_kept_ref, last_sent_ref), 0, 3)]
    for above in range(1, WLAYERS):
        begin = (WLAYERS - 1 - above) * half
        deals.append(deal(unit.at[above & 1], half, (kept_ref, sent_ref), begin, 3 + 2 * above))
    last_deal = deal(
        tail, TAIL // 2, (kept_ref, sent_ref), (WLAYERS - 1) * half, 3 + 2 * WLAYERS
    )

    def inside_item(item):
        return rows_of(pairs) < pair_rows(dur_ref[pl.ds(item, 1), :])

    def span(item):
        return pl.ds(pl.multiple_of(item * pairs, pairs), pairs)

    def each(body, count=items):
        def one(item, carry):
            body(item)
            return carry

        lax.fori_loop(0, count, one, 0)

    both = 2 if items % 2 == 0 else 1
    blocks = items // both
    block_rows = both * pairs

    def block_span(block):
        return pl.ds(pl.multiple_of(block * block_rows, block_rows), block_rows)

    def inside_block(block):
        return jnp.concatenate([inside_item(block * both + i) for i in range(both)], axis=0)

    @pl.when(step == 0)
    def _():
        for copy in fetch:
            copy.start()
        _, center, _, _, scale = read_stats(stats_ref[...])

        def one(item):
            inside = inside_item(item)
            rows[:, :MEL] = mel_ref[item].T
            pad = jnp.zeros((pairs, LANES - MEL), F32)
            even = rows[pl.ds(0, pairs, stride=2), :][:, :MEL]
            odd = rows[pl.ds(1, pairs, stride=2), :][:, :MEL]
            values = jnp.concatenate([even, pad, odd, pad], axis=1)
            normalized = jnp.where(inside, (values - center) * scale, 0.0)
            normal[item] = normalized
            turned = dot_three(normalized, mixm_ref[...])
            passive = turned[:, :LANES]
            passive_grad[item] = passive
            active[item] = turned[:, LANES:]
            low_now = passive.astype(BF16)
            passive_low[item] = low_now
            hidden[span(item), :] = jnp.where(inside, dot_nn(low_now, start_ref[...]), 0.0)
            skip[span(item), :] = jnp.zeros((pairs, HID), F32)

        each(one)

    @pl.when((step >= 1) & (step <= WLAYERS))
    def _():
        layer = step - 1

        def one(block):
            here = block_span(block)
            state = hidden[here, :]
            hidden_low[layer, here, :] = state.astype(BF16)
            pre_gate = dot_nn(unfold_rows(state, WKER, pairs), win_ref[0])
            pre[layer, here, :] = pre_gate.astype(BF16)
            tanh, gate = gates_of(pre_gate)
            sums = dot_nn((tanh * gate).astype(BF16), wres_ref[layer])
            hidden[here, :] = jnp.where(inside_block(block), state + sums[:, :HID], 0.0)
            skip[here, :] = skip[here, :] + sums[:, HID:]

        each(one, blocks)

    @pl.when(step == STEP_POST)
    def _():
        for copy in fetch:
            copy.wait()
        total, _, _, _, _ = read_stats(stats_ref[...])
        unit_grad = 1.0 / (2 * MEL * total)
        end_acc[...] = jnp.zeros_like(end_acc)
        sums[...] = jnp.zeros_like(sums)

        def one(item):
            inside = inside_item(item)
            output_low = jnp.where(inside, skip[span(item), :], 0.0).astype(BF16)
            coupled = jnp.where(inside, dot_nn(output_low, wend_ref[...]), 0.0)
            shift_part = coupled[:, :LANES]
            log_part = coupled[:, LANES:]
            growth = jnp.exp(log_part)
            moving = active[item]
            moved = jnp.where(inside, shift_part + growth * moving, 0.0)
            align = align_of(dur_ref[pl.ds(item, 1), :], pairs)
            prior = dot_nn(align, high[item]) + dot_nn(align, low[item])
            latent = jnp.concatenate([passive_grad[item], moved], axis=1)
            gap = latent - prior[:, : 2 * LANES]
            log_scales = prior[:, 2 * LANES :]
            scaled = jnp.exp(-2.0 * log_scales) * gap
            square = scaled * gap
            terms = jnp.where(inside, log_scales + 0.5 * square, 0.0)
            term = jnp.sum(terms, axis=0, keepdims=True)
            nll = term[:, :LANES] + term[:, LANES:] - jnp.sum(log_part, axis=0, keepdims=True)
            sums[4:5, :] = sums[4:5, :] + nll
            latent_grad = jnp.where(inside, unit_grad * scaled, 0.0)
            scale_grad = jnp.where(inside, unit_grad * (1.0 - square), 0.0)
            flow[item] = jnp.concatenate([-latent_grad, scale_grad], axis=1).astype(BF16)
            passive_grad[item] = latent_grad[:, :LANES]
            moved_grad = latent_grad[:, LANES:]
            active_grad = moved_grad * growth
            log_grad = jnp.where(inside, active_grad * moving - unit_grad, 0.0)
            active[item] = active_grad
            coupled_low = jnp.concatenate([moved_grad, log_grad], axis=1).astype(BF16)
            end_acc[...] = end_acc[...] + dot_tn(coupled_low, output_low)
            skip_grad = jnp.where(inside, dot_nt(coupled_low, wend_ref[...]), 0.0)
            skip_low[span(item), :] = skip_grad.astype(BF16)
            hidden[span(item), :] = jnp.zeros((pairs, HID), F32)

        each(one)
        write.start()

    @pl.when(step > STEP_POST)
    def _():
        layer = STEPS - 1 - step
        for tap in range(WKER):
            wide[:, tap * 2 * HID : (tap + 1) * 2 * HID] = win_ref[
                0, tap * HID : (tap + 1) * HID, :
            ]

        def one(block):
            here = block_span(block)
            tanh, gate = gates_of(pre[layer, here, :].astype(F32))
            gated[here, :] = (tanh * gate).astype(BF16)
            kept = hidden[here, :]
            left = jnp.concatenate([kept, skip_low[here, :].astype(F32)], axis=1).astype(BF16)
            part[here, :] = left
            gated_grad = dot_nt(left, wres_ref[layer])
            tanh_grad = gated_grad * gate * (1.0 - tanh * tanh)
            gate_grad = gated_grad * tanh * gate * (1.0 - gate)
            pre_grad = jnp.concatenate([tanh_grad, gate_grad], axis=1)
            taps = unfold_rows(pre_grad, WKER, pairs, reverse=True)
            spread[here, :] = taps
            back = kept + dot_nt(taps, wide[...])
            hidden[here, :] = jnp.where(inside_block(block), back, 0.0)

        each(one, blocks)
        for later in range(WLAYERS - 2):

            @pl.when(layer == later)
            def _(later=later):
                for copy in deals[later + 2]:
                    copy.wait()

        parity = layer & 1
        found = dot_tn(hidden_low[layer], spread[...])
        for tap in range(WKER):
            unit[parity, tap * HID : (tap + 1) * HID, :] = found[
                :, tap * 2 * HID : (tap + 1) * 2 * HID
            ]
        unit[parity, conv:, :] = dot_tn(gated[...], part[...])

        @pl.when(layer == WLAYERS - 1)
        def _():
            side = (WLAYERS - 1) & 1
            unit[side, conv : conv + MEL, :HID] = end_acc[:MEL, :]
            unit[side, conv + MEL : conv + 2 * MEL, :HID] = end_acc[LANES : LANES + MEL, :]

        for now in range(WLAYERS):

            @pl.when(layer == now)
            def _(now=now):
                for copy in deals[now]:
                    copy.start()

    @pl.when(step == STEPS - 1)
    def _():
        start_acc[...] = jnp.zeros_like(start_acc)
        mix_acc[...] = jnp.zeros_like(mix_acc)

        def one(item):
            start_low = hidden[span(item), :].astype(BF16)
            start_acc[...] = start_acc[...] + dot_tn(passive_low[item], start_low)
            turned_passive = passive_grad[item] + dot_nt(start_low, start_ref[...])
            turned_grad = jnp.concatenate([turned_passive, active[item]], axis=1)
            normalized = normal[item]
            mix_acc[...] = mix_acc[...] + dot_tn(
                normalized.astype(BF16), turned_grad.astype(BF16)
            )
            normal_grad = dot_three(turned_grad, mixm_ref[...], back=True)
            normal_grad = jnp.where(inside_item(item), normal_grad, 0.0)
            ngrad_ref[item] = normal_grad
            one_sum = jnp.sum(normal_grad, axis=0, keepdims=True)
            two_sum = jnp.sum(normal_grad * normalized, axis=0, keepdims=True)
            for at, found in ((0, one_sum), (2, two_sum)):
                sums[at : at + 1, :] = sums[at : at + 1, :] + found[:, :LANES]
                sums[at + 1 : at + 2, :] = sums[at + 1 : at + 2, :] + found[:, LANES:]

        each(one)
        tail[...] = jnp.zeros_like(tail)
        cut = MEL // 2
        tail[:cut, :] = jnp.concatenate([start_acc[:cut, :], start_acc[cut:MEL, :]], axis=1)
        row_member, col_member, match = mix_places()
        kept = jnp.where(match, mix_acc[...], 0.0)
        ri = iota((8, LANES), 0)
        ci = iota((8, LANES), 1)
        mixed = jnp.zeros((8, LANES), F32)
        for i in range(4):
            column = jnp.sum(jnp.where(col_member == i, kept, 0.0), axis=1, keepdims=True)
            for j in range(4):
                entry = jnp.sum(jnp.where(row_member == j, column, 0.0), axis=0, keepdims=True)
                mixed = jnp.where((ri == i) & (ci == j), entry, mixed)
        tail[cut : cut + 8, :LANES] = mixed
        tail[cut : cut + 8, LANES : 2 * LANES] = sums[...]
        for copy in last_deal:
            copy.start()
        for copy in (*last_deal, *deals[0], *deals[1], write):
            copy.wait()


def frames_body(
    mel_ref, dur_ref, ngrad_ref, stats_ref, sums_ref, small_ref, out_ref, loss_ref, rows_ref
):
    pairs = mel_ref.shape[2] // 2
    inside = rows_of(pairs) < pair_rows(text_rows(dur_ref))
    total, center, variance, log_act, scale = read_stats(stats_ref[...])
    unit = 1.0 / (2 * MEL * total)
    sums = sums_ref[...]
    spot = iota((1, 2 * LANES), 1) & (LANES - 1)
    log_sum = jnp.sum(jnp.where(spot < MEL, log_act, 0.0), axis=1, keepdims=True)
    nll = jnp.sum(sums[4:5], axis=1, keepdims=True)
    log_det = jnp.log(small_ref[4:5, 0:1])
    loss = (nll - total * log_sum - total * (MEL // 2) * log_det) * unit
    loss_ref[...] = loss + 0.5 * math.log(2.0 * math.pi)
    one = jnp.concatenate([sums[0:1], sums[1:2]], axis=1)
    two = jnp.concatenate([sums[2:3], sums[3:4]], axis=1)
    log_grad = two - unit * total
    var_grad = -0.5 * log_grad / (variance + 1e-06)
    center_grad = -scale * one - 2.0 * center * var_grad
    values = split_pairs(mel_ref, rows_ref)
    grads = ngrad_ref[0] * scale + (2.0 * values * var_grad + center_grad) / total
    grads = jnp.where(inside, grads, 0.0) * (2 * MEL * total)
    rows_ref[pl.ds(0, pairs, stride=2), :] = grads[:, :LANES]
    rows_ref[pl.ds(1, pairs, stride=2), :] = grads[:, LANES:]
    out_ref[0] = rows_ref[...].T[:MEL, :]


def swap(values, bit, devices):
    return lax.ppermute(values, "dp", [(i, i ^ bit) for i in range(devices)])


def swap_half(unit, devices):
    kept, sent = unit
    return kept, swap(sent, 1, devices)


def digits(devices, shift=1):
    found = []
    while (1 << shift) < devices:
        radix = 4 if (1 << (shift + 2)) <= devices else 2
        found.append((shift, radix))
        shift += 2 if radix == 4 else 1
    return found


def whole_vmem(count):
    return [pl.BlockSpec(memory_space=pltpu.VMEM)] * count


def call_whole(body, place, ins, outs, scratch, after, micros, name):
    return run(
        body,
        (),
        [place, *ins],
        [pl.BlockSpec(memory_space=pltpu.SMEM)] + whole_vmem(len(ins)),
        outs,
        whole_vmem(len(outs)),
        scratch,
        micros=micros,
        after=after,
        name=name,
    )


def hop_out(jobs, place, after=()):
    ins = []
    outs = []
    scratch = []
    plans = []
    for units, shift, radix in jobs:
        plan = []
        begin = 0
        for unit in units:
            row = unit[0].shape[0] // radix
            plan.append((len(ins), len(unit), row, begin))
            ins += unit
            begin += row
        plans.append((plan, len(outs), shift, radix))
        outs += [shape_of((begin, WIDE))] * radix
        aligned = all(row % 8 == 0 for _, _, row, _ in plan)
        scratch.append(pltpu.VMEM((1, 8, LANES) if aligned else (radix, begin, WIDE), F32))
    n_in, n_out = len(ins), len(outs)

    def body(place_ref, *refs):
        out_refs = refs[n_in : n_in + n_out]
        tables = refs[n_in + n_out :]
        for (plan, at, shift, radix), table in zip(plans, tables):
            digit = (place_ref[0] >> shift) & (radix - 1)
            if all(row % 8 == 0 for _, _, row, _ in plan):
                for step in range(radix):
                    for first, count, row, begin in plan:
                        span = pl.ds(pl.multiple_of((digit ^ step) * row, 8), row)
                        value = refs[first][span, :]
                        for extra in range(1, count):
                            value = value + refs[first + extra][span, :]
                        out_refs[at + step][begin : begin + row, :] = value
                continue
            for first, count, row, begin in plan:
                for part in range(radix):
                    span = slice(part * row, (part + 1) * row)
                    value = refs[first][span, :]
                    for extra in range(1, count):
                        value = value + refs[first + extra][span, :]
                    table[part, begin : begin + row, :] = value
            for step in range(radix):
                out_refs[at + step][...] = table[digit ^ step]

    found = call_whole(body, place, ins, outs, scratch, after, 3, "hop_out")
    return [found[at : at + radix] for _, at, _, radix in plans]


def hop_in(jobs, place, after=()):
    ins = []
    outs = []
    plans = []
    for parts, shift in jobs:
        plans.append((len(ins), len(parts), shift))
        ins += parts
        outs.append(shape_of((len(parts), *parts[0].shape)))
    n_in = len(ins)

    def body(place_ref, *refs):
        for (first, radix, shift), out in zip(plans, refs[n_in:]):
            digit = (place_ref[0] >> shift) & (radix - 1)
            for step in range(radix):
                out[digit ^ step] = refs[first + step][...]

    return call_whole(body, place, ins, outs, (), after, 2, "hop_in")


def add_parts(jobs, place, after=()):
    ins = [part for parts in jobs for part in parts]
    outs = [shape_of(parts[0].shape) for parts in jobs]
    n_in = len(ins)

    def body(place_ref, *refs):
        at = 0
        for parts, out in zip(jobs, refs[n_in:]):
            value = refs[at][...]
            for extra in range(at + 1, at + len(parts)):
                value = value + refs[extra][...]
            out[...] = value
            at += len(parts)

    return call_whole(body, place, ins, outs, (), after, 1, "add_parts")


def send_parts(parts, shift, devices):
    return [parts[0]] + [
        swap(part, step << shift, devices) for step, part in enumerate(parts) if step > 0
    ]


def spread_level(units, level, place, devices, after=()):
    shift, radix = digits(devices)[level]
    parts = hop_out([(units, shift, radix)], place, after)[0]
    return send_parts(parts, shift, devices)


def gather_level(part, level, place, devices, after=()):
    shift, radix = digits(devices)[level]
    return hop_in([(send_parts([part] * radix, shift, devices), shift)], place, after)[0]


def last_level(part, devices):
    shift, radix = digits(devices)[0]
    return send_parts([part.reshape(-1, WIDE)] * radix, shift, devices)


def table_parts(place_ref, shift, radix, mine_refs, other_refs, table):
    digit = (place_ref[0] >> shift) & (radix - 1)
    core = place_ref[0] & 1
    for step in range(radix):
        table[core, digit ^ step] = mine_refs[step][...]
        table[1 - core, digit ^ step] = other_refs[step][...]


def segments(begin, count, rows):
    found = []
    at = begin
    while at < begin + count:
        part, row = divmod(at, rows)
        size = min(rows - row, begin + count - at)
        found.append((part, row, size, at - begin))
        at += size
    return found


def unpack_upper_body(
    shift,
    radix,
    place_ref,
    small_ref,
    *refs,
):
    mine, other = refs[:radix], refs[radix : 2 * radix]
    in_ref, res_ref, last_ref, end_ref, start_ref, mix_ref, sums_ref, table, tail, sems = refs[2 * radix :]
    table_parts(place_ref, shift, radix, mine, other, table)
    rows = table.shape[2]
    conv = WKER * HID
    half = UNIT // 2
    copies = []

    def move(core, begin, count, target, at):
        for part, row, size, place in segments(begin, count, rows):
            copies.append(
                pltpu.make_async_copy(
                    table.at[core, part, pl.ds(row, size), :],
                    target.at[pl.ds(at + place, size), :],
                    sems.at[len(copies)],
                )
            )

    for layer in range(1, WLAYERS):
        begin = (WLAYERS - 1 - layer) * half
        move(0, begin, half, in_ref.at[layer], 0)
        move(1, begin, conv - half, in_ref.at[layer], half)
        if layer < WLAYERS - 1:
            move(1, begin + conv - half, HID, res_ref.at[layer], 0)
    for copy in copies:
        copy.start()
    for part, row, size, at in segments(conv - half, HID, rows):
        values = table[1, part, row : row + size, :]
        last_ref[at : at + size, :] = values[:, HID:]
        end_ref[at : at + size, :] = values[:, :HID]
    for core in range(2):
        for part, row, size, at in segments((WLAYERS - 1) * half, TAIL // 2, rows):
            begin = core * (TAIL // 2) + at
            tail[begin : begin + size, :] = table[core, part, row : row + size, :]
    cut = MEL // 2
    start_ref[:cut, :] = tail[:cut, :HID]
    start_ref[cut:, :] = tail[:cut, HID:]
    mix_ref[...] = tail[cut : cut + 8, :LANES] - small_ref[...] / 4.0
    sums_ref[...] = tail[cut : cut + 8, LANES : 2 * LANES]
    for copy in copies:
        copy.wait()


def unpack_upper(parts, other, place, small, devices, after):
    shift, radix = digits(devices)[0]
    vmem = pl.BlockSpec(memory_space=pltpu.VMEM)
    anywhere = pl.BlockSpec(memory_space=pl.ANY)
    outs = [
        shape_of((WLAYERS, WKER * HID, 2 * HID)),
        shape_of((WLAYERS - 1, HID, 2 * HID)),
        shape_of((HID, HID)),
        shape_of((HID, HID)),
        shape_of((MEL, HID)),
        shape_of((8, LANES)),
        shape_of((8, LANES)),
    ]
    return run(
        functools.partial(unpack_upper_body, shift, radix),
        (),
        [place, small, *parts, *other],
        [pl.BlockSpec(memory_space=pltpu.SMEM)] + [vmem] * (1 + 2 * radix),
        outs,
        [anywhere] * 2 + [vmem] * 5,
        [
            pltpu.VMEM((2, radix, *parts[0].shape), F32),
            pltpu.VMEM((TAIL, WIDE), F32),
            pltpu.SemaphoreType.DMA((40,)),
        ],
        micros=5,
        after=after,
        name="unpack_upper",
    )


def unpack_lower_body(shift, radix, place_ref, in_given, res_given, *refs):
    mine, other = refs[:radix], refs[radix : 2 * radix]
    (
        in_ref,
        res_ref,
        one_ref,
        two_ref,
        table_ref,
        qkv_ref,
        out_ref,
        relk_ref,
        relv_ref,
        prior_ref,
        *norm_refs,
        table,
        rest,
        sems,
    ) = refs[2 * radix :]
    table_parts(place_ref, shift, radix, mine, other, table)
    conv = WKER * HID
    half = UNIT // 2
    quarter = half // radix
    copies = []
    for core in range(2):
        for digit in range(radix):
            at = core * half + digit * quarter
            pieces = [(0, max(0, min(quarter, conv - at)), in_ref, at)]
            pieces.append((pieces[0][1], quarter - pieces[0][1], res_ref, at + pieces[0][1] - conv))
            for row, size, target, to in pieces:
                if size:
                    copies.append(
                        pltpu.make_async_copy(
                            table.at[core, digit, pl.ds(row, size), :],
                            target.at[0, pl.ds(to, size), :],
                            sems.at[len(copies)],
                        )
                    )
    for copy in copies:
        copy.start()
    rows = table.shape[2] - quarter

    def read(core, begin, count):
        return [
            (table[core, part, quarter + row : quarter + row + size, :], at)
            for part, row, size, at in segments(begin, count, rows)
        ]

    for core in range(2):
        for values, at in read(core, 0, half):
            one_ref[at : at + values.shape[0], core * WIDE : (core + 1) * WIDE] = values
        for third in range(KSIZE):
            block = core * KSIZE + third
            for values, at in read(core, half + third * D, D):
                two_ref[at : at + values.shape[0], block * WIDE : (block + 1) * WIDE] = values
        for values, at in read(core, 2 * half, REST // 2):
            begin = core * (REST // 2) + at
            rest[begin : begin + values.shape[0], :] = values
    side = D // 2
    qkv_ref[:, :WIDE] = rest[:D, :]
    qkv_ref[:side, WIDE:] = rest[D : D + side, :D]
    qkv_ref[side:, WIDE:] = rest[D : D + side, D:]
    out_ref[:side, :] = rest[D + side : 2 * D, :D]
    out_ref[side:, :] = rest[D + side : 2 * D, D:]
    table_ref[:MEL, :] = rest[ROW_TABLE : ROW_TABLE + MEL, :D]
    table_ref[MEL:, :] = rest[ROW_TABLE : ROW_TABLE + VOCAB - MEL, D:]
    prior_ref[:MEL, :] = rest[ROW_PRIOR : ROW_PRIOR + MEL, :D]
    prior_ref[MEL:, :] = rest[ROW_PRIOR : ROW_PRIOR + MEL, D:]
    relk_ref[...] = rest[ROW_REL : ROW_REL + 2 * WINDOW + 1, :HEAD]
    relv_ref[...] = rest[ROW_REL : ROW_REL + 2 * WINDOW + 1, LANES : LANES + HEAD]
    for i, ref in enumerate(norm_refs):
        row = rest[ROW_NORM + (i >> 1) : ROW_NORM + (i >> 1) + 1, :]
        ref[...] = row[:, (i & 1) * D : (i & 1) * D + D].reshape(D)
    for copy in copies:
        copy.wait()


def unpack_lower(parts, other, place, in_grad, res_grad, devices):
    shift, radix = digits(devices)[0]
    vmem = pl.BlockSpec(memory_space=pltpu.VMEM)
    anywhere = pl.BlockSpec(memory_space=pl.ANY)
    reach = 2 * WINDOW + 1
    outs = [
        shape_of(in_grad.shape),
        shape_of(res_grad.shape),
        shape_of((KSIZE * D, FILTER)),
        shape_of((D, KSIZE * FILTER)),
        shape_of((VOCAB, D)),
        shape_of((D, 3 * D)),
        shape_of((D, D)),
        shape_of((reach, HEAD)),
        shape_of((reach, HEAD)),
        shape_of((2 * MEL, D)),
        *[shape_of((D,))] * 4,
    ]
    return run(
        functools.partial(unpack_lower_body, shift, radix),
        (),
        [place, in_grad, res_grad, *parts, *other],
        [pl.BlockSpec(memory_space=pltpu.SMEM)] + [anywhere] * 2 + [vmem] * (2 * radix),
        outs,
        [anywhere] * 2 + [vmem] * (len(outs) - 2),
        [
            pltpu.VMEM((2, radix, *parts[0].shape), F32),
            pltpu.VMEM((REST, WIDE), F32),
            pltpu.SemaphoreType.DMA((2 * radix + 2,)),
        ],
        micros=5,
        aliases={1: 0, 2: 1},
        name="unpack_lower",
    )


def on_device(
    devices,
    token_ids,
    durations,
    mel_frames,
    embedding,
    w_qkv,
    rel_key,
    rel_value,
    w_out,
    attn_gain,
    attn_shift,
    w_ff1,
    w_ff2,
    ffn_gain,
    ffn_shift,
    w_prior,
    w_mix,
    w_start,
    w_in,
    w_res,
    w_skip_last,
    w_end,
):
    items, length = token_ids.shape
    frames = mel_frames.shape[1]
    mel_frames = mel_frames.transpose(0, 2, 1)
    ff2_t = w_ff2.T
    prior_t = w_prior.T
    end_t = w_end.T
    pairs = frames // 2
    grid = (items,)
    place = lax.axis_index("dp").reshape(1).astype(jnp.int32)

    def halves_of(rows):
        return [shape_of((rows // 2, WIDE))] * 2

    vmem = pl.BlockSpec(memory_space=pltpu.VMEM)
    smem = pl.BlockSpec(memory_space=pltpu.SMEM)
    gain_one = attn_gain.reshape(1, D)
    shift_one = attn_shift.reshape(1, D)
    gain_two = ffn_gain.reshape(1, D)
    shift_two = ffn_shift.reshape(1, D)

    stats = run(
        stats_body, (), [mel_frames, durations], [vmem] * 2, shape_of((8, LANES)), vmem, name="stats"
    )
    stats_steps = digits(devices, 0)
    shift, radix = stats_steps[0]
    local_stats = stats
    stats = sum(send_parts([stats] * radix, shift, devices))

    prepared = [
        shape_of((2 * LANES, 2 * LANES)),
        shape_of((8, LANES)),
        shape_of((D, 6 * LANES), BF16),
        shape_of((LANES, LANES), BF16),
        shape_of((LANES, LANES), BF16),
        shape_of((2 * LANES, D), BF16),
        shape_of((2 * MEL, 8 * LANES), BF16),
        shape_of((D, 8 * LANES), BF16),
        shape_of((LANES, HID), BF16),
        shape_of((HID, 2 * LANES), BF16),
        shape_of((WLAYERS, HID, 2 * HID), BF16),
    ]
    (
        mixm,
        small,
        qkv_pad,
        relk_pad,
        relv_pad,
        out_pad,
        wide,
        prior_pad,
        start_pad,
        end_pad,
        res_four,
    ) = run(
        weights_body,
        (),
        [w_mix, w_qkv, rel_key, rel_value, w_out, prior_t, w_start, end_t, w_res, w_skip_last],
        [smem] + [vmem] * 9,
        prepared,
        [vmem] * len(prepared),
        after=(local_stats,),
        name="weights",
    )

    group = 2 if items % 2 == 0 else 1

    def group_spec(array):
        rank = len(array.shape)
        return pl.BlockSpec((group,) + array.shape[1:], lambda b: (b,) + (0,) * (rank - 1))

    ins = [
        token_ids,
        durations,
        embedding,
        qkv_pad,
        relk_pad,
        relv_pad,
        out_pad,
        gain_one,
        shift_one,
        w_ff1,
        ff2_t,
        gain_two,
        shift_two,
        prior_pad,
    ]
    outs = [
        shape_of((items, length, D), BF16),
        shape_of((items, length, 6 * LANES), BF16),
        shape_of((items, HEADS, length, length), BF16),
        shape_of((items, HEADS, length, LANES), BF16),
        shape_of((items, length, 2 * LANES), BF16),
        shape_of((items, length, D)),
        shape_of((items, length, D), BF16),
        shape_of((items, length, FILTER), BF16),
        shape_of((items, length, FILTER), BF16),
        shape_of((items, length, D)),
        shape_of((items, length, D), BF16),
        shape_of((items, 2 * length, 4 * LANES), BF16),
        shape_of((items, 2 * length, 4 * LANES), BF16),
    ]
    (
        emb_low,
        proj,
        attention,
        banded,
        attend,
        mixed,
        normed_low,
        filtered,
        activ,
        summed,
        encoded,
        expand,
        expand_low,
    ) = run(
        encoder_body,
        (items // group,),
        ins,
        [full_spec(a) for a in ins],
        outs,
        [group_spec(a) for a in outs],
        micros=20,
        after=(stats,),
        name="encoder",
    )
    for shift, radix in stats_steps[1:]:
        stats = sum(send_parts([stats] * radix, shift, devices))

    ins = [mel_frames, durations, expand, expand_low, stats, mixm, start_pad, w_in, res_four, end_pad, place]
    kinds = [full_spec] * 10
    in_specs = [kind(a) for kind, a in zip(kinds, ins)] + [smem]
    in_specs[2] = in_specs[3] = pl.BlockSpec(memory_space=pl.ANY)
    in_specs[7] = pl.BlockSpec(
        (1,) + w_in.shape[1:],
        lambda s: (jnp.where(s <= STEP_POST, jnp.clip(s - 1, 0, WLAYERS - 1), STEPS - 1 - s), 0, 0),
    )
    dealt = ((WLAYERS - 1) * UNIT + TAIL) // 2
    outs = [
        *[shape_of((dealt, WIDE))] * 2,
        *halves_of(UNIT),
        shape_of((items, pairs, 4 * LANES), BF16),
        shape_of((items, pairs, 2 * LANES)),
    ]
    out_specs = [pl.BlockSpec(memory_space=pl.ANY)] * 5 + [full_spec(outs[5])]
    count = items * pairs
    kept, sent, last_kept, last_sent, flow, normal_grad = run(
        decoder_body,
        (STEPS,),
        ins,
        in_specs,
        outs,
        out_specs,
        [
            pltpu.VMEM((items, pairs, 2 * LANES), F32),
            pltpu.VMEM((items, pairs, LANES), BF16),
            pltpu.VMEM((WLAYERS, count, HID), BF16),
            pltpu.VMEM((WLAYERS, count, 2 * HID), BF16),
            pltpu.VMEM((count, HID), F32),
            pltpu.VMEM((count, HID), F32),
            pltpu.VMEM((items, pairs, LANES), F32),
            pltpu.VMEM((count, HID), BF16),
            pltpu.VMEM((items, pairs, LANES), F32),
            pltpu.VMEM((count, HID), BF16),
            pltpu.VMEM((count, 2 * HID), BF16),
            pltpu.VMEM((count, WKER * 2 * HID), BF16),
            pltpu.VMEM((HID, WKER * 2 * HID), BF16),
            pltpu.VMEM((2, UNIT, WIDE), F32),
            pltpu.VMEM((frames, LANES), F32),
            pltpu.VMEM((2 * LANES, HID), F32),
            pltpu.VMEM((LANES, HID), F32),
            pltpu.VMEM((2 * LANES, 2 * LANES), F32),
            pltpu.VMEM((TAIL, WIDE), F32),
            pltpu.VMEM(expand.shape, BF16),
            pltpu.VMEM(expand.shape, BF16),
            pltpu.VMEM((items, pairs, 4 * LANES), BF16),
            pltpu.VMEM((8, LANES), F32),
            pltpu.SemaphoreType.DMA((5 + 2 * WLAYERS,)),
        ],
        micros=80,
        name="decoder",
    )
    recv = swap(sent, 1, devices)
    upper = spread_level([[kept, recv]], 0, place, devices)
    last_recv = swap(last_sent, 1, devices)

    ins = [
        token_ids,
        durations,
        flow,
        encoded,
        summed,
        filtered,
        activ,
        normed_low,
        mixed,
        attend,
        attention,
        banded,
        proj,
        emb_low,
        wide,
        w_ff1,
        ff2_t,
        gain_two,
        prior_t,
        qkv_pad,
        relk_pad,
        relv_pad,
        out_pad,
        gain_one,
        place,
    ]
    kinds = [full_spec] * 2 + [group_spec] * 12 + [full_spec] * 10
    outs = halves_of(2 * UNIT + REST)
    fed_kept, fed_sent = run(
        encoder_back_body,
        (items // group,),
        ins,
        [kind(a) for kind, a in zip(kinds, ins)] + [smem],
        outs,
        [pl.BlockSpec(memory_space=pl.ANY)] * 2,
        [
            pltpu.VMEM((UNIT, WIDE), F32),
            pltpu.VMEM((UNIT, WIDE), F32),
            pltpu.VMEM((REST, WIDE), F32),
            pltpu.VMEM((VOCAB, D), F32),
            pltpu.VMEM((D, 6 * LANES), F32),
            pltpu.VMEM((2 * LANES, D), F32),
            pltpu.VMEM((LANES, LANES), F32),
            pltpu.VMEM((LANES, LANES), F32),
            pltpu.VMEM((2 * MEL, D), F32),
            pltpu.VMEM((8, D), F32),
            pltpu.SemaphoreType.DMA((6,)),
        ],
        after=(upper[0],),
        micros=30,
        name="encoder_back",
    )
    levels = len(digits(devices))
    upper, fed_sent, fed_kept = lax.optimization_barrier((upper, fed_sent, fed_kept))
    fed_recv = swap(fed_sent, 1, devices)
    for level in range(1, levels):
        upper = spread_level([upper], level, place, devices, (fed_kept,))
    units = [[last_kept, last_recv], [fed_kept, fed_recv]]
    lower = spread_level(units, 0, place, devices, (upper[0],))
    upper = add_parts([upper], place, (lower[0],))[0]
    for level in reversed(range(1, levels)):
        upper = gather_level(upper, level, place, devices, (upper,))
    upper_parts = last_level(upper, devices)
    for level in range(1, levels):
        lower = spread_level([lower], level, place, devices, (upper,))
    lower = add_parts([lower], place)[0]
    for level in reversed(range(1, levels)):
        lower = gather_level(lower, level, place, devices)
    upper_parts, lower = lax.optimization_barrier((upper_parts, lower))
    upper_other = [swap(part, 1, devices) for part in upper_parts]
    lower, upper_other = lax.optimization_barrier((lower, upper_other))
    lower_parts = last_level(lower, devices)
    in_grad, res_grad, last_grad, end_grad, start_grad, mix_grad, sums = unpack_upper(
        upper_parts, upper_other, place, small, devices, ()
    )
    ins = [mel_frames, durations, normal_grad, stats, sums, small]
    kinds = [item_spec, full_spec, item_spec, full_spec, full_spec, full_spec]
    mel_grad, loss = run(
        frames_body,
        grid,
        ins,
        [kind(a) for kind, a in zip(kinds, ins)],
        [shape_of(mel_frames.shape), shape_of((1, 1))],
        [item_spec(mel_frames), pl.BlockSpec((1, 1), lambda b: (0, 0))],
        [pltpu.VMEM((frames, LANES), F32)],
        name="frames",
    )

    lower_parts = [lax.optimization_barrier((part, mel_grad))[0] for part in lower_parts]
    lower_other = [swap(part, 1, devices) for part in lower_parts]
    (
        in_grad,
        res_grad,
        ff1_grad,
        ff2_grad,
        table_grad,
        qkv_grad,
        out_grad,
        relk_grad,
        relv_grad,
        prior_grad,
        *norm_grads,
    ) = unpack_lower(lower_parts, lower_other, place, in_grad, res_grad, devices)

    return (
        loss.reshape(()),
        mel_grad.transpose(0, 2, 1),
        table_grad,
        qkv_grad,
        relk_grad,
        relv_grad,
        out_grad,
        norm_grads[0],
        norm_grads[1],
        ff1_grad,
        ff2_grad.T,
        norm_grads[2],
        norm_grads[3],
        prior_grad.T,
        mix_grad[:4, :4],
        start_grad,
        in_grad,
        res_grad,
        last_grad,
        end_grad[: 2 * MEL].T,
    )


def solution(mesh):
    devices = mesh.shape["dp"]
    placed = (P("dp", None), P("dp", None), P("dp", None, None)) + (P(),) * 18
    return jax.shard_map(
        functools.partial(on_device, devices),
        mesh=mesh,
        in_specs=placed,
        out_specs=(P(), P("dp", None, None)) + (P(),) * 18,
        check_vma=False,
    )
```

time: 345 us -> 298 us (0.86)
  Pallas kernels: 183 us -> 152 us
  between operations: 14.9 us -> 1.15 us
  waiting for transfers between devices: 82.6 us -> 74.6 us
  starting transfers between devices: 52.7 us -> 57.9 us
    pallas_call x15 -> x16, Pallas kernels: 183 us -> 152 us  [run(): pl.pallas_call(wrapped, grid=grid, in_specs=list(in_specs) + [pl.BlockSpe...]
    ppermute x38 -> x42, starting transfers between devices: 43 us -> 57.9 us  [swap(): return lax.ppermute(values, 'dp', [(i, i ^ bit) for i in range(devices)])]
    ppermute x5 -> x0, starting transfers between devices: 9.63 us -> none  [small_sum(): lax.ppermute(values, 'dp', [(i, i ^ bit) for i in range(devices)])]
    ppermute x38 -> x42, waiting for transfers between devices: 80 us -> 74.6 us  [swap(): return lax.ppermute(values, 'dp', [(i, i ^ bit) for i in range(devices)])]
    unnamed x70 -> x82, local copies, waits for them, and re-layouts: 7.2 us -> 9.88 us
  transfers between devices with their start and end apart: 44 -> 42, of which waited for: 20 -> 23; matrix products, arithmetic and copies ran while one was open for 1% -> 0% of each run, Pallas kernels for 29% -> 25%
where the time goes in v3:
time: 298 us
  Pallas kernels  152 us (51%)
  waiting for transfers between devices  74.6 us (25%)
  starting transfers between devices  57.9 us (19%)
  local copies, waits for them, and re-layouts  11.1 us (4%)
    pallas_call x16, Pallas kernels, run(): pl.pallas_call(wrapped, grid=grid, in_specs=list(in_specs) + [pl.BlockSpe...  152 us
    ppermute x42, waiting for transfers between devices, swap(): return lax.ppermute(values, 'dp', [(i, i ^ bit) for i in range(devices)])  74.6 us
    ppermute x42, starting transfers between devices, swap(): return lax.ppermute(values, 'dp', [(i, i ^ bit) for i in range(devices)])  57.9 us
    unnamed x82, local copies, waits for them, and re-layouts  9.88 us
  transfers between devices with their start and end apart: 42, of which 23 were waited for; matrix products, arithmetic and copies ran while one was open for 0% of the time, Pallas kernels for 25%

profile of v3, /device:TPU:0, one launch (start us, length us, event | category | flops | bytes accessed | tf_op | source)
XLA Modules:
  0.0 297.9 jit_solution(6345043606640980802)
XLA Ops:
  0.7 2.4 stats.1.refs_10_
  3.0 2.4 collective-permute-start.2
  6.1 0.9 collective-permute-done.2
  6.9 2.3 collective-permute-done.1
  9.9 2.5 collective-permute-start.5
  13.4 3.4 %weights.1 = (f32[256,256]{1,0:T(8,128)}, f32[8,128]{1,0:T(8,128)}, bf16[192,768]{1,0:T(8,128)(2,1)}, bf16[128,128]{1,0:T(8,128)(2,1)}, bf16[128,128]{1,0:T(8,12...) custom-call(f32[4,4]{1,0:T(4,128)} %refs_0_.3, ...), custom_call_target="tpu_custom_call" | custom-call | flops 5750000128 | bytes 1048576 | tf_op jit(solution)/shard_map/weights/pallas_call | solution.py:102
  16.9 2.7 collective-permute-start.6
  19.5 16.4 %encoder.1 = (bf16[4,256,192]{2,1,0:T(8,128)(2,1)}, bf16[4,256,768]{2,1,0:T(8,128)(2,1)}, bf16[4,2,256,256]{3,2,1,0:T(8,128)(2,1)}, bf16[4,2,256,128]{3,2,1,0:T(...) custom-call(s32[4,256]{1,0:T(4,128)} %refs_0_.5, ...), custom_call_target="tpu_custom_call" | custom-call | flops 23000000512 | bytes 1048576 | tf_op jit(solution)/shard_map/encoder/pallas_call | solution.py:102
  36.5 60.2 %decoder.1 = (f32[1792,384]{1,0:T(8,128)}, f32[1792,384]{1,0:T(8,128)}, f32[576,384]{1,0:T(8,128)}, f32[576,384]{1,0:T(8,128)}, bf16[4,512,512]{2,1,0:T(8,128)(2,1)}, /*index=5*/f32[4,512,256]{2,1,0:T(8,128)}) custom-call(f32[4,80,1024]{2,1,0:T(8,128)} %bitcast.18, s32[4,256]{1,0:T(4,128)} %refs_1_.11, bf16[4,512,512]{2,1,0:T(8,128)(2,1)} %get-tuple-element.116.refs_2_, ...), custom_call_target="tpu_custom_call" | custom-call | flops 92000002048 | bytes 1048576 | tf_op jit(solution)/shard_map/decoder/pallas_call | solution.py:102
  96.8 5.3 %collective-permute-done.7.refs_2_ = f32[1792,384]{1,0:T(8,128)S(1)} collective-permute-done((f32[1792,384]{1,0:T(8,128)}, f32[1792,384]{1,0:T(8,128)S(1)}, u32[]{:S(2)}, u32[]{:S(2)}) %collective-permute-start.7) | collective-permute-done | bytes 2752544 | tf_op jit(solution)/shard_map/ppermute | solution.py:1032
  102.1 1.5 copy-done.3
  103.6 4.5 %hop_out.4 = (f32[448,384]{1,0:T(8,128)}, f32[448,384]{1,0:T(8,128)}, f32[448,384]{1,0:T(8,128)}, f32[448,384]{1,0:T(8,128)}) custom-call(s32[1]{0:T(128)} %bitcast.8.refs_10_.refs_0_.refs_24_, f32[1792,384]{1,0:T(8,128)} %get-tuple-element.124.refs_1_, f32[1792,384]{1,0:T(8,128)} %copy-done.3), custom_call_target="tpu_custom_call" | custom-call | flops 3449999872 | bytes 1048576 | tf_op jit(solution)/shard_map/hop_out/pallas_call | solution.py:102
  108.7 1.5 collective-permute-start.9
  110.2 1.4 collective-permute-start.10
  111.6 28.6 %encoder_back.1 = (f32[1472,384]{1,0:T(8,128)}, f32[1472,384]{1,0:T(8,128)}) custom-call(s32[4,256]{1,0:T(4,128)} %refs_0_.5, s32[4,256]{1,0:T(4,128)} %refs_1_.11, bf16[4,512,512]{2,1,0:T(8,128)(2,1)} %get-tuple-element.130.refs_2_, bf16[4,256,192]{2,1,0:T(8,128)(2,1)} %get-tuple-element.131.refs_3_, f32[4,256,192]{2,1,0:T(8,128)} %get-tuple-element.132.refs_4_, ...), custom_call_target="tpu_custom_call" | custom-call | flops 34500001792 | bytes 1048576 | tf_op jit(solution)/shard_map/encoder_back/pallas_call | solution.py:102
  140.2 1.3 collective-permute-done.10.refs_4_
  142.3 2.7 hop_out.5
  145.0 1.6 collective-permute-start.11
  146.9 2.5 collective-permute-start.13
  149.4 0.9 copy-done.6
  151.0 4.8 %hop_out.6 = (f32[512,384]{1,0:T(8,128)}, f32[512,384]{1,0:T(8,128)}, f32[512,384]{1,0:T(8,128)}, f32[512,384]{1,0:T(8,128)}) custom-call(s32[1]{0:T(128)} %bitcast.8.refs_10_.refs_0_.refs_24_, f32[576,384]{1,0:T(8,128)} %get-tuple-element.154.refs_1_, f32[576,384]{1,0:T(8,128)} %copy-done.6, f32[1472,384]{1,0:T(8,128)} %get-tuple-element.149.refs_5_.refs_3_, ...), custom_call_target="tpu_custom_call" | custom-call | flops 3449999872 | bytes 1048576 | tf_op jit(solution)/shard_map/hop_out/pallas_call | solution.py:102
  155.9 1.0 collective-permute-start.22
  156.9 1.5 collective-permute-start.23
  158.4 1.0 collective-permute-start.24
  159.4 2.3 collective-permute-done.12.refs_3_
  162.3 1.9 add_parts.2.refs_1_.refs_5_
  165.0 4.1 %collective-permute-start.17 = (f32[112,384]{1,0:T(8,128)}, f32[112,384]{1,0:T(8,128)S(1)}, u32[]{:S(2)}, u32[]{:S(2)}) collective-permute-start(f32[112,384]{1,0:T(8,128)} %add_parts.2.refs_1_.refs_5_), channel_id=1, source_target_pairs={{0,16},{1,17},{2,18},{3,19},{4,20},{5,21},{6,22},{7,23},{8,24},{9,... | collective-permute-start | bytes 516104 | tf_op jit(solution)/shard_map/ppermute | solution.py:1032
  169.0 4.3 %collective-permute-done.18.refs_4_ = f32[112,384]{1,0:T(8,128)S(1)} collective-permute-done((f32[112,384]{1,0:T(8,128)}, f32[112,384]{1,0:T(8,128)S(1)}, u32[]{:S(2)}, u32[]{:S(2)}) %collective-permute-start.18) | collective-permute-done | bytes 172064 | tf_op jit(solution)/shard_map/ppermute | solution.py:1032
  173.3 6.4 %collective-permute-start.16 = (f32[112,384]{1,0:T(8,128)}, f32[112,384]{1,0:T(8,128)S(1)}, u32[]{:S(2)}, u32[]{:S(2)}) collective-permute-start(f32[112,384]{1,0:T(8,128)} %add_parts.2.refs_1_.refs_5_), channel_id=1, source_target_pairs={{0,8},{1,9},{2,10},{3,11},{4,12},{5,13},{6,14},{7,15},{8,0},{9,1},... | collective-permute-start | bytes 516104 | tf_op jit(solution)/shard_map/ppermute | solution.py:1032
  179.7 2.4 collective-permute-done.17.refs_3_
  182.1 3.6 %collective-permute-done.16.refs_2_ = f32[112,384]{1,0:T(8,128)S(1)} collective-permute-done((f32[112,384]{1,0:T(8,128)}, f32[112,384]{1,0:T(8,128)S(1)}, u32[]{:S(2)}, u32[]{:S(2)}) %collective-permute-start.16) | collective-permute-done | bytes 172064 | tf_op jit(solution)/shard_map/ppermute | solution.py:1032
  186.4 2.0 hop_in.2.refs_5_
  188.4 3.4 %collective-permute-done.23.refs_3_ = f32[512,384]{1,0:T(8,128)S(1)} collective-permute-done((f32[512,384]{1,0:T(8,128)}, f32[512,384]{1,0:T(8,128)S(1)}, u32[]{:S(2)}, u32[]{:S(2)}) %collective-permute-start.23) | collective-permute-done | bytes 786464 | tf_op jit(solution)/shard_map/ppermute | solution.py:1032
  191.9 0.9 copy-done.12
  192.7 0.9 copy-done.13
  193.6 2.9 hop_out.7
  197.2 1.2 collective-permute-start.26
  198.4 2.5 collective-permute-start.27
  200.9 1.6 collective-permute-start.21
  202.7 3.5 %collective-permute-done.25.refs_2_ = f32[128,384]{1,0:T(8,128)S(1)} collective-permute-done((f32[128,384]{1,0:T(8,128)}, f32[128,384]{1,0:T(8,128)S(1)}, u32[]{:S(2)}, u32[]{:S(2)}) %collective-permute-start.25) | collective-permute-done | bytes 196640 | tf_op jit(solution)/shard_map/ppermute | solution.py:1032
  206.2 5.8 %collective-permute-done.26.refs_3_ = f32[128,384]{1,0:T(8,128)S(1)} collective-permute-done((f32[128,384]{1,0:T(8,128)}, f32[128,384]{1,0:T(8,128)S(1)}, u32[]{:S(2)}, u32[]{:S(2)}) %collective-permute-start.26) | collective-permute-done | bytes 196640 | tf_op jit(solution)/shard_map/ppermute | solution.py:1032
  212.7 1.9 add_parts.3.refs_1_
  214.6 1.6 collective-permute-start.30
  216.2 4.8 %collective-permute-start.29 = (f32[128,384]{1,0:T(8,128)}, f32[128,384]{1,0:T(8,128)S(1)}, u32[]{:S(2)}, u32[]{:S(2)}) collective-permute-start(f32[128,384]{1,0:T(8,128)} %add_parts.3.refs_1_), channel_id=1, source_target_pairs={{0,16},{1,17},{2,18},{3,19},{4,20},{5,21},{6,22},{7,23},{8,24},{9,... | collective-permute-start | bytes 589832 | tf_op jit(solution)/shard_map/ppermute | solution.py:1032
  221.0 2.6 collective-permute-done.30.refs_4_
  223.7 7.7 %collective-permute-start.28 = (f32[128,384]{1,0:T(8,128)}, f32[128,384]{1,0:T(8,128)S(1)}, u32[]{:S(2)}, u32[]{:S(2)}) collective-permute-start(f32[128,384]{1,0:T(8,128)} %add_parts.3.refs_1_), channel_id=1, source_target_pairs={{0,8},{1,9},{2,10},{3,11},{4,12},{5,13},{6,14},{7,15},{8,0},{9,1},... | collective-permute-start | bytes 589832 | tf_op jit(solution)/shard_map/ppermute | solution.py:1032
  231.4 3.6 %collective-permute-done.29.refs_3_ = f32[128,384]{1,0:T(8,128)S(1)} collective-permute-done((f32[128,384]{1,0:T(8,128)}, f32[128,384]{1,0:T(8,128)S(1)}, u32[]{:S(2)}, u32[]{:S(2)}) %collective-permute-start.29) | collective-permute-done | bytes 196640 | tf_op jit(solution)/shard_map/ppermute | solution.py:1032
  234.9 4.1 %collective-permute-done.28.refs_2_ = f32[128,384]{1,0:T(8,128)S(1)} collective-permute-done((f32[128,384]{1,0:T(8,128)}, f32[128,384]{1,0:T(8,128)S(1)}, u32[]{:S(2)}, u32[]{:S(2)}) %collective-permute-start.28) | collective-permute-done | bytes 196640 | tf_op jit(solution)/shard_map/ppermute | solution.py:1032
  239.7 2.2 hop_in.3
  243.0 1.1 collective-permute-done.31.refs_6_
  244.1 1.0 collective-permute-done.32.refs_7_
  245.1 1.0 collective-permute-done.33.refs_8_
  246.1 1.0 collective-permute-done.34.refs_9_
  247.1 0.9 copy-done.28
  248.0 1.3 collective-permute-start.37
  249.3 2.1 collective-permute-start.35
  251.5 6.3 %unpack_upper.1 = (f32[4,960,384]{2,1,0:T(8,128)}, f32[3,192,384]{2,1,0:T(8,128)}, f32[192,192]{1,0:T(8,128)}, f32[192,192]{1,0:T(8,128)}, f32[80,192]{1,0:T(8,1...) custom-call(s32[1]{0:T(128)} %bitcast.8.refs_10_.refs_0_.refs_24_, f32[8,128]{1,0:T(8,128)} %get-tuple-element.123.refs_1_.refs_5_, ...), custom_call_target="tpu_custom_call" | custom-call | flops 5750000128 | bytes 1048576 | tf_op jit(solution)/shard_map/unpack_upper/pallas_call | solution.py:102
  257.9 5.0 %frames.1 = (f32[4,80,1024]{2,1,0:T(8,128)}, f32[1,1]{1,0:T(1,128)}) custom-call(f32[4,80,1024]{2,1,0:T(8,128)} %bitcast.19, s32[4,256]{1,0:T(4,128)} %refs_1_.11, f32[4,512,256]{2,1,0:T(8,128)} %get-tuple-element.122.refs_2_, f32[8,128]{1,0:T(8,128)} %add.27.refs_4_.refs_3_, f32[8,128]{1,0:T(8,128)} %get-tuple-element.174.refs_4_, ...), custom_call_target="tpu_custom_call" | custom-call | flops 5750000128 | bytes 1048576 | tf_op jit(solution)/shard_map/frames/pallas_call | solution.py:102
  262.9 6.6 %collective-permute-done.37.refs_6_ = f32[512,384]{1,0:T(8,128)S(1)} collective-permute-done((f32[512,384]{1,0:T(8,128)}, f32[512,384]{1,0:T(8,128)S(1)}, u32[]{:S(2)}, u32[]{:S(2)}) %collective-permute-start.37) | collective-permute-done | bytes 786464 | tf_op jit(solution)/shard_map/ppermute | solution.py:1032
  269.5 16.0 %collective-permute-done.36.refs_5_ = f32[512,384]{1,0:T(8,128)S(1)} collective-permute-done((f32[512,384]{1,0:T(8,128)}, f32[512,384]{1,0:T(8,128)S(1)}, u32[]{:S(2)}, u32[]{:S(2)}) %collective-permute-start.36) | collective-permute-done | bytes 786464 | tf_op jit(solution)/shard_map/ppermute | solution.py:1032
  287.9 1.1 collective-permute-done.40.refs_9_
  289.0 1.1 collective-permute-done.41.refs_10_
  290.1 0.9 copy-done.17
  291.1 6.6 %unpack_lower.1 = (f32[4,960,384]{2,1,0:T(8,128)}, f32[3,192,384]{2,1,0:T(8,128)}, f32[576,768]{1,0:T(8,128)}, f32[192,2304]{1,0:T(8,128)}, f32[148,192]{1,0:T(8...) custom-call(s32[1]{0:T(128)} %bitcast.8.refs_10_.refs_0_.refs_24_, ...), custom_call_target="tpu_custom_call", output_to_operand_aliasing={{0}: (1, {}), {1}: (2, {})} | custom-call | flops 5750000128 | bytes 1048576 | tf_op jit(solution)/shard_map/unpack_lower/pallas_call | solution.py:102
  (123 shorter events, 13.6 us)
Async XLA Ops:
  3.0 3.9 %collective-permute-start.2 = (f32[8,128]{1,0:T(8,128)}, f32[8,128]{1,0:T(8,128)S(1)}, u32[]{:S(2)}, u32[]{:S(2)}) collective-permute-start(f32[8,128]{1,0:T(8,128)} %stats.1.refs_10_), channel_id=1, source_target_pairs={{0,3},{1,2},{2,1},{3,0},{4,7},{5,6},{6,5},{7,4},{8,11},{9,10},{10,... | collective-permute-start | bytes 12296 | tf_op jit(solution)/shard_map/ppermute | solution.py:1032
  5.4 3.8 %collective-permute-start.1 = (f32[8,128]{1,0:T(8,128)}, f32[8,128]{1,0:T(8,128)S(1)}, u32[]{:S(2)}, u32[]{:S(2)}) collective-permute-start(f32[8,128]{1,0:T(8,128)} %stats.1.refs_10_), channel_id=1, source_target_pairs={{0,2},{1,3},{2,0},{3,1},{4,6},{5,7},{6,4},{7,5},{8,10},{9,11},{10,... | collective-permute-start | bytes 12296 | tf_op jit(solution)/shard_map/ppermute | solution.py:1032
  6.0 3.2 %collective-permute-start = (f32[8,128]{1,0:T(8,128)}, f32[8,128]{1,0:T(8,128)S(1)}, u32[]{:S(2)}, u32[]{:S(2)}) collective-permute-start(f32[8,128]{1,0:T(8,128)} %stats.1.refs_10_), channel_id=1, source_target_pairs={{0,1},{1,0},{2,3},{3,2},{4,5},{5,4},{6,7},{7,6},{8,9},{9,8},{10,11... | collective-permute-start | bytes 12296 | tf_op jit(solution)/shard_map/ppermute | solution.py:1032
  9.9 6.9 %copy-start.1 = (f32[8,128]{1,0:T(8,128)}, f32[8,128]{1,0:T(8,128)S(1)}, u32[]{:S(2)}) copy-start(f32[8,128]{1,0:T(8,128)S(1)} %add_add_fusion.1.refs_14_) | copy-start | bytes 12292
  9.9 6.9 %collective-permute-start.5 = (f32[8,128]{1,0:T(8,128)S(1)}, f32[8,128]{1,0:T(8,128)S(1)}, u32[]{:S(2)}, u32[]{:S(2)}) collective-permute-start(f32[8,128]{1,0:T(8,128)S(1)} %add_add_fusion.1.refs_14_), channel_id=1, source_target_pairs={{0,12},{1,13},{2,14},{3,15},{4,8},{5,9},{6,10},{7,11},{8,4},{9,5},... | collective-permute-start | bytes 12296 | tf_op jit(solution)/shard_map/ppermute | solution.py:1032
  12.4 4.4 %collective-permute-start.4 = (f32[8,128]{1,0:T(8,128)S(1)}, f32[8,128]{1,0:T(8,128)S(1)}, u32[]{:S(2)}, u32[]{:S(2)}) collective-permute-start(f32[8,128]{1,0:T(8,128)S(1)} %add_add_fusion.1.refs_14_), channel_id=1, source_target_pairs={{0,8},{1,9},{2,10},{3,11},{4,12},{5,13},{6,14},{7,15},{8,0},{9,1},... | collective-permute-start | bytes 12296 | tf_op jit(solution)/shard_map/ppermute | solution.py:1032
  12.9 3.9 %collective-permute-start.3 = (f32[8,128]{1,0:T(8,128)S(1)}, f32[8,128]{1,0:T(8,128)S(1)}, u32[]{:S(2)}, u32[]{:S(2)}) collective-permute-start(f32[8,128]{1,0:T(8,128)S(1)} %add_add_fusion.1.refs_14_), channel_id=1, source_target_pairs={{0,4},{1,5},{2,6},{3,7},{4,0},{5,1},{6,2},{7,3},{8,12},{9,13},{10,... | collective-permute-start | bytes 12296 | tf_op jit(solution)/shard_map/ppermute | solution.py:1032
  16.9 19.0 %collective-permute-start.6 = (f32[8,128]{1,0:T(8,128)S(1)}, f32[8,128]{1,0:T(8,128)S(1)}, u32[]{:S(2)}, u32[]{:S(2)}) collective-permute-start(f32[8,128]{1,0:T(8,128)S(1)} %add_add_fusion), channel_id=1, source_target_pairs={{0,16},{1,17},{2,18},{3,19},{4,20},{5,21},{6,22},{7,23},{8,24},{9,... | collective-permute-start | bytes 12296 | tf_op jit(solution)/shard_map/ppermute | solution.py:1032
  96.7 5.4 %collective-permute-start.7 = (f32[1792,384]{1,0:T(8,128)}, f32[1792,384]{1,0:T(8,128)S(1)}, u32[]{:S(2)}, u32[]{:S(2)}) collective-permute-start(f32[1792,384]{1,0:T(8,128)} %get-tuple-element.125), channel_id=1, source_target_pairs={{0,1},{1,0},{2,3},{3,2},{4,5},{5,4},{6,7},{7,6},{8,9},{9,8},{10,11... | collective-permute-start | bytes 8257544 | tf_op jit(solution)/shard_map/ppermute | solution.py:1032
  108.1 32.1 %collective-permute-start.8 = (f32[448,384]{1,0:T(8,128)}, f32[448,384]{1,0:T(8,128)S(1)}, u32[]{:S(2)}, u32[]{:S(2)}) collective-permute-start(f32[448,384]{1,0:T(8,128)} %get-tuple-element.127), channel_id=1, source_target_pairs={{0,2},{1,3},{2,0},{3,1},{4,6},{5,7},{6,4},{7,5},{8,10},{9,11},{10,... | collective-permute-start | bytes 2064392 | tf_op jit(solution)/shard_map/ppermute | solution.py:1032
  108.7 31.5 %collective-permute-start.9 = (f32[448,384]{1,0:T(8,128)}, f32[448,384]{1,0:T(8,128)S(1)}, u32[]{:S(2)}, u32[]{:S(2)}) collective-permute-start(f32[448,384]{1,0:T(8,128)} %get-tuple-element.128), channel_id=1, source_target_pairs={{0,4},{1,5},{2,6},{3,7},{4,0},{5,1},{6,2},{7,3},{8,12},{9,13},{10,... | collective-permute-start | bytes 2064392 | tf_op jit(solution)/shard_map/ppermute | solution.py:1032
  110.2 31.3 %collective-permute-start.10 = (f32[448,384]{1,0:T(8,128)}, f32[448,384]{1,0:T(8,128)S(1)}, u32[]{:S(2)}, u32[]{:S(2)}) collective-permute-start(f32[448,384]{1,0:T(8,128)} %get-tuple-element.129), channel_id=1, source_target_pairs={{0,6},{1,7},{2,4},{3,5},{4,2},{5,3},{6,0},{7,1},{8,14},{9,15},{10,... | collective-permute-start | bytes 2064392 | tf_op jit(solution)/shard_map/ppermute | solution.py:1032
  111.6 29.9 %copy-start.5 = (f32[576,384]{1,0:T(8,128)S(1)}, f32[576,384]{1,0:T(8,128)}, u32[]{:S(2)}) copy-start(f32[576,384]{1,0:T(8,128)} %get-tuple-element.155) | copy-start | bytes 2654212
  141.5 7.9 %collective-permute-start.15 = (f32[1472,384]{1,0:T(8,128)}, f32[1472,384]{1,0:T(8,128)S(1)}, u32[]{:S(2)}, u32[]{:S(2)}) collective-permute-start(f32[1472,384]{1,0:T(8,128)} %get-tuple-element.156), channel_id=1, source_target_pairs={{0,1},{1,0},{2,3},{3,2},{4,5},{5,4},{6,7},{7,6},{8,9},{9,8},{10,11... | collective-permute-start | bytes 6782984 | tf_op jit(solution)/shard_map/ppermute | solution.py:1032
  141.5 7.9 %collective-permute-start.14 = (f32[576,384]{1,0:T(8,128)S(1)}, f32[576,384]{1,0:T(8,128)S(1)}, u32[]{:S(2)}, u32[]{:S(2)}) collective-permute-start(f32[576,384]{1,0:T(8,128)S(1)} %copy-done.5), channel_id=1, source_target_pairs={{0,1},{1,0},{2,3},{3,2},{4,5},{5,4},{6,7},{7,6},{8,9},{9,8},{10,11... | collective-permute-start | bytes 2654216 | tf_op jit(solution)/shard_map/ppermute | solution.py:1032
  145.0 13.4 %collective-permute-start.11 = (f32[112,384]{1,0:T(8,128)}, f32[112,384]{1,0:T(8,128)S(1)}, u32[]{:S(2)}, u32[]{:S(2)}) collective-permute-start(f32[112,384]{1,0:T(8,128)} %get-tuple-element.151), channel_id=1, source_target_pairs={{0,8},{1,9},{2,10},{3,11},{4,12},{5,13},{6,14},{7,15},{8,0},{9,1},... | collective-permute-start | bytes 516104 | tf_op jit(solution)/shard_map/ppermute | solution.py:1032
  146.6 15.1 %collective-permute-start.12 = (f32[112,384]{1,0:T(8,128)}, f32[112,384]{1,0:T(8,128)S(1)}, u32[]{:S(2)}, u32[]{:S(2)}) collective-permute-start(f32[112,384]{1,0:T(8,128)} %get-tuple-element.152), channel_id=1, source_target_pairs={{0,16},{1,17},{2,18},{3,19},{4,20},{5,21},{6,22},{7,23},{8,24},{9,... | collective-permute-start | bytes 516104 | tf_op jit(solution)/shard_map/ppermute | solution.py:1032
  146.9 14.7 %collective-permute-start.13 = (f32[112,384]{1,0:T(8,128)}, f32[112,384]{1,0:T(8,128)S(1)}, u32[]{:S(2)}, u32[]{:S(2)}) collective-permute-start(f32[112,384]{1,0:T(8,128)} %get-tuple-element.153), channel_id=1, source_target_pairs={{0,24},{1,25},{2,26},{3,27},{4,28},{5,29},{6,30},{7,31},{8,16},{9,... | collective-permute-start | bytes 516104 | tf_op jit(solution)/shard_map/ppermute | solution.py:1032
  155.9 32.6 %collective-permute-start.22 = (f32[512,384]{1,0:T(8,128)}, f32[512,384]{1,0:T(8,128)S(1)}, u32[]{:S(2)}, u32[]{:S(2)}) collective-permute-start(f32[512,384]{1,0:T(8,128)} %get-tuple-element.158), channel_id=1, source_target_pairs={{0,2},{1,3},{2,0},{3,1},{4,6},{5,7},{6,4},{7,5},{8,10},{9,11},{10,... | collective-permute-start | bytes 2359304 | tf_op jit(solution)/shard_map/ppermute | solution.py:1032
  156.9 35.0 %collective-permute-start.23 = (f32[512,384]{1,0:T(8,128)}, f32[512,384]{1,0:T(8,128)S(1)}, u32[]{:S(2)}, u32[]{:S(2)}) collective-permute-start(f32[512,384]{1,0:T(8,128)} %get-tuple-element.159), channel_id=1, source_target_pairs={{0,4},{1,5},{2,6},{3,7},{4,0},{5,1},{6,2},{7,3},{8,12},{9,13},{10,... | collective-permute-start | bytes 2359304 | tf_op jit(solution)/shard_map/ppermute | solution.py:1032
  158.4 3.2 %copy-start.35 = (f32[112,384]{1,0:T(8,128)}, f32[112,384]{1,0:T(8,128)S(1)}, u32[]{:S(2)}) copy-start(f32[112,384]{1,0:T(8,128)S(1)} %collective-permute-done.11.refs_2_) | copy-start | bytes 516100
  158.4 33.5 %collective-permute-start.24 = (f32[512,384]{1,0:T(8,128)}, f32[512,384]{1,0:T(8,128)S(1)}, u32[]{:S(2)}, u32[]{:S(2)}) collective-permute-start(f32[512,384]{1,0:T(8,128)} %get-tuple-element.160), channel_id=1, source_target_pairs={{0,6},{1,7},{2,4},{3,5},{4,2},{5,3},{6,0},{7,1},{8,14},{9,15},{10,... | collective-permute-start | bytes 2359304 | tf_op jit(solution)/shard_map/ppermute | solution.py:1032
  164.2 9.1 %collective-permute-start.18 = (f32[112,384]{1,0:T(8,128)}, f32[112,384]{1,0:T(8,128)S(1)}, u32[]{:S(2)}, u32[]{:S(2)}) collective-permute-start(f32[112,384]{1,0:T(8,128)} %add_parts.2.refs_1_.refs_5_), channel_id=1, source_target_pairs={{0,24},{1,25},{2,26},{3,27},{4,28},{5,29},{6,30},{7,31},{8,16},{9,... | collective-permute-start | bytes 516104 | tf_op jit(solution)/shard_map/ppermute | solution.py:1032
  165.0 17.1 %collective-permute-start.17 = (f32[112,384]{1,0:T(8,128)}, f32[112,384]{1,0:T(8,128)S(1)}, u32[]{:S(2)}, u32[]{:S(2)}) collective-permute-start(f32[112,384]{1,0:T(8,128)} %add_parts.2.refs_1_.refs_5_), channel_id=1, source_target_pairs={{0,16},{1,17},{2,18},{3,19},{4,20},{5,21},{6,22},{7,23},{8,24},{9,... | collective-permute-start | bytes 516104 | tf_op jit(solution)/shard_map/ppermute | solution.py:1032
  173.3 12.4 %copy-start.38 = (f32[112,384]{1,0:T(8,128)}, f32[112,384]{1,0:T(8,128)S(1)}, u32[]{:S(2)}) copy-start(f32[112,384]{1,0:T(8,128)S(1)} %collective-permute-done.18.refs_4_) | copy-start | bytes 516100
  173.3 12.4 %collective-permute-start.16 = (f32[112,384]{1,0:T(8,128)}, f32[112,384]{1,0:T(8,128)S(1)}, u32[]{:S(2)}, u32[]{:S(2)}) collective-permute-start(f32[112,384]{1,0:T(8,128)} %add_parts.2.refs_1_.refs_5_), channel_id=1, source_target_pairs={{0,8},{1,9},{2,10},{3,11},{4,12},{5,13},{6,14},{7,15},{8,0},{9,1},... | collective-permute-start | bytes 516104 | tf_op jit(solution)/shard_map/ppermute | solution.py:1032
  182.1 3.6 %copy-start.39 = (f32[112,384]{1,0:T(8,128)}, f32[112,384]{1,0:T(8,128)S(1)}, u32[]{:S(2)}) copy-start(f32[112,384]{1,0:T(8,128)S(1)} %collective-permute-done.17.refs_3_) | copy-start | bytes 516100
  188.4 12.4 %copy-start.18 = (f32[4,112,384]{2,1,0:T(8,128)S(1)}, f32[4,112,384]{2,1,0:T(8,128)}, u32[]{:S(2)}) copy-start(f32[4,112,384]{2,1,0:T(8,128)} %hop_in.2.refs_5_) | copy-start | bytes 2064388
  188.4 3.4 %copy-start.11 = (f32[512,384]{1,0:T(8,128)}, f32[512,384]{1,0:T(8,128)S(1)}, u32[]{:S(2)}) copy-start(f32[512,384]{1,0:T(8,128)S(1)} %collective-permute-done.22.refs_2_) | copy-start | bytes 2359300
  196.5 9.7 %collective-permute-start.25 = (f32[128,384]{1,0:T(8,128)}, f32[128,384]{1,0:T(8,128)S(1)}, u32[]{:S(2)}, u32[]{:S(2)}) collective-permute-start(f32[128,384]{1,0:T(8,128)} %get-tuple-element.162), channel_id=1, source_target_pairs={{0,8},{1,9},{2,10},{3,11},{4,12},{5,13},{6,14},{7,15},{8,0},{9,1},... | collective-permute-start | bytes 589832 | tf_op jit(solution)/shard_map/ppermute | solution.py:1032
  197.2 14.8 %collective-permute-start.26 = (f32[128,384]{1,0:T(8,128)}, f32[128,384]{1,0:T(8,128)S(1)}, u32[]{:S(2)}, u32[]{:S(2)}) collective-permute-start(f32[128,384]{1,0:T(8,128)} %get-tuple-element.163), channel_id=1, source_target_pairs={{0,16},{1,17},{2,18},{3,19},{4,20},{5,21},{6,22},{7,23},{8,24},{9,... | collective-permute-start | bytes 589832 | tf_op jit(solution)/shard_map/ppermute | solution.py:1032
  198.4 13.5 %collective-permute-start.27 = (f32[128,384]{1,0:T(8,128)}, f32[128,384]{1,0:T(8,128)S(1)}, u32[]{:S(2)}, u32[]{:S(2)}) collective-permute-start(f32[128,384]{1,0:T(8,128)} %get-tuple-element.164), channel_id=1, source_target_pairs={{0,24},{1,25},{2,26},{3,27},{4,28},{5,29},{6,30},{7,31},{8,16},{9,... | collective-permute-start | bytes 589832 | tf_op jit(solution)/shard_map/ppermute | solution.py:1032
  200.9 41.0 %collective-permute-start.21 = (f32[448,384]{1,0:T(8,128)S(1)}, f32[448,384]{1,0:T(8,128)S(1)}, u32[]{:S(2)}, u32[]{:S(2)}) collective-permute-start(f32[448,384]{1,0:T(8,128)S(1)} %bitcast.28), channel_id=1, source_target_pairs={{0,6},{1,7},{2,4},{3,5},{4,2},{5,3},{6,0},{7,1},{8,14},{9,15},{10,... | collective-permute-start | bytes 2064392 | tf_op jit(solution)/shard_map/ppermute | solution.py:1032
  202.4 39.5 %collective-permute-start.20 = (f32[448,384]{1,0:T(8,128)S(1)}, f32[448,384]{1,0:T(8,128)S(1)}, u32[]{:S(2)}, u32[]{:S(2)}) collective-permute-start(f32[448,384]{1,0:T(8,128)S(1)} %bitcast.29), channel_id=1, source_target_pairs={{0,4},{1,5},{2,6},{3,7},{4,0},{5,1},{6,2},{7,3},{8,12},{9,13},{10,... | collective-permute-start | bytes 2064392 | tf_op jit(solution)/shard_map/ppermute | solution.py:1032
  206.1 5.8 %copy-start.29 = (f32[128,384]{1,0:T(8,128)}, f32[128,384]{1,0:T(8,128)S(1)}, u32[]{:S(2)}) copy-start(f32[128,384]{1,0:T(8,128)S(1)} %collective-permute-done.25.refs_2_) | copy-start | bytes 589828
  206.1 35.8 %collective-permute-start.19 = (f32[448,384]{1,0:T(8,128)S(1)}, f32[448,384]{1,0:T(8,128)S(1)}, u32[]{:S(2)}, u32[]{:S(2)}) collective-permute-start(f32[448,384]{1,0:T(8,128)S(1)} %bitcast.30), channel_id=1, source_target_pairs={{0,2},{1,3},{2,0},{3,1},{4,6},{5,7},{6,4},{7,5},{8,10},{9,11},{10,... | collective-permute-start | bytes 2064392 | tf_op jit(solution)/shard_map/ppermute | solution.py:1032
  214.6 9.1 %collective-permute-start.30 = (f32[128,384]{1,0:T(8,128)}, f32[128,384]{1,0:T(8,128)S(1)}, u32[]{:S(2)}, u32[]{:S(2)}) collective-permute-start(f32[128,384]{1,0:T(8,128)} %add_parts.3.refs_1_), channel_id=1, source_target_pairs={{0,24},{1,25},{2,26},{3,27},{4,28},{5,29},{6,30},{7,31},{8,16},{9,... | collective-permute-start | bytes 589832 | tf_op jit(solution)/shard_map/ppermute | solution.py:1032
  216.2 18.7 %collective-permute-start.29 = (f32[128,384]{1,0:T(8,128)}, f32[128,384]{1,0:T(8,128)S(1)}, u32[]{:S(2)}, u32[]{:S(2)}) collective-permute-start(f32[128,384]{1,0:T(8,128)} %add_parts.3.refs_1_), channel_id=1, source_target_pairs={{0,16},{1,17},{2,18},{3,19},{4,20},{5,21},{6,22},{7,23},{8,24},{9,... | collective-permute-start | bytes 589832 | tf_op jit(solution)/shard_map/ppermute | solution.py:1032
  223.7 15.4 %copy-start.32 = (f32[128,384]{1,0:T(8,128)}, f32[128,384]{1,0:T(8,128)S(1)}, u32[]{:S(2)}) copy-start(f32[128,384]{1,0:T(8,128)S(1)} %collective-permute-done.30.refs_4_) | copy-start | bytes 589828
  223.7 15.4 %collective-permute-start.28 = (f32[128,384]{1,0:T(8,128)}, f32[128,384]{1,0:T(8,128)S(1)}, u32[]{:S(2)}, u32[]{:S(2)}) collective-permute-start(f32[128,384]{1,0:T(8,128)} %add_parts.3.refs_1_), channel_id=1, source_target_pairs={{0,8},{1,9},{2,10},{3,11},{4,12},{5,13},{6,14},{7,15},{8,0},{9,1},... | collective-permute-start | bytes 589832 | tf_op jit(solution)/shard_map/ppermute | solution.py:1032
  234.9 4.1 %copy-start.33 = (f32[128,384]{1,0:T(8,128)}, f32[128,384]{1,0:T(8,128)S(1)}, u32[]{:S(2)}) copy-start(f32[128,384]{1,0:T(8,128)S(1)} %collective-permute-done.29.refs_3_) | copy-start | bytes 589828
  241.9 9.6 %copy-start.19 = (f32[448,384]{1,0:T(8,128)}, f32[448,384]{1,0:T(8,128)S(1)}, u32[]{:S(2)}) copy-start(f32[448,384]{1,0:T(8,128)S(1)} %collective-permute-done.21.refs_5_) | copy-start | bytes 2064388
  241.9 9.6 %copy-start.20 = (f32[448,384]{1,0:T(8,128)}, f32[448,384]{1,0:T(8,128)S(1)}, u32[]{:S(2)}) copy-start(f32[448,384]{1,0:T(8,128)S(1)} %collective-permute-done.20.refs_4_) | copy-start | bytes 2064388
  241.9 9.6 %copy-start.21 = (f32[448,384]{1,0:T(8,128)}, f32[448,384]{1,0:T(8,128)S(1)}, u32[]{:S(2)}) copy-start(f32[448,384]{1,0:T(8,128)S(1)} %collective-permute-done.19.refs_3_) | copy-start | bytes 2064388
  241.9 2.2 collective-permute-start.31
  242.0 3.1 %collective-permute-start.32 = (f32[448,384]{1,0:T(8,128)S(1)}, f32[448,384]{1,0:T(8,128)S(1)}, u32[]{:S(2)}, u32[]{:S(2)}) collective-permute-start(f32[448,384]{1,0:T(8,128)S(1)} %collective-permute-done.19.refs_3_), channel_id=1, source_target_pairs={{0,1},{1,0},{2,3},{3,2},{4,5},{5,4},{6,7},{7,6},{8,9},{9,8},{10,11... | collective-permute-start | bytes 2064392 | tf_op jit(solution)/shard_map/ppermute | solution.py:1032
  242.5 3.6 %collective-permute-start.33 = (f32[448,384]{1,0:T(8,128)S(1)}, f32[448,384]{1,0:T(8,128)S(1)}, u32[]{:S(2)}, u32[]{:S(2)}) collective-permute-start(f32[448,384]{1,0:T(8,128)S(1)} %collective-permute-done.20.refs_4_), channel_id=1, source_target_pairs={{0,1},{1,0},{2,3},{3,2},{4,5},{5,4},{6,7},{7,6},{8,9},{9,8},{10,11... | collective-permute-start | bytes 2064392 | tf_op jit(solution)/shard_map/ppermute | solution.py:1032
  242.6 4.5 %collective-permute-start.34 = (f32[448,384]{1,0:T(8,128)S(1)}, f32[448,384]{1,0:T(8,128)S(1)}, u32[]{:S(2)}, u32[]{:S(2)}) collective-permute-start(f32[448,384]{1,0:T(8,128)S(1)} %collective-permute-done.21.refs_5_), channel_id=1, source_target_pairs={{0,1},{1,0},{2,3},{3,2},{4,5},{5,4},{6,7},{7,6},{8,9},{9,8},{10,11... | collective-permute-start | bytes 2064392 | tf_op jit(solution)/shard_map/ppermute | solution.py:1032
  244.1 7.4 %copy-start.25 = (f32[448,384]{1,0:T(8,128)}, f32[448,384]{1,0:T(8,128)S(1)}, u32[]{:S(2)}) copy-start(f32[448,384]{1,0:T(8,128)S(1)} %collective-permute-done.31.refs_6_) | copy-start | bytes 2064388
  248.0 21.5 %collective-permute-start.37 = (f32[512,384]{1,0:T(8,128)}, f32[512,384]{1,0:T(8,128)S(1)}, u32[]{:S(2)}, u32[]{:S(2)}) collective-permute-start(f32[512,384]{1,0:T(8,128)} %bitcast.22), channel_id=1, source_target_pairs={{0,6},{1,7},{2,4},{3,5},{4,2},{5,3},{6,0},{7,1},{8,14},{9,15},{10,... | collective-permute-start | bytes 2359304 | tf_op jit(solution)/shard_map/ppermute | solution.py:1032
  249.3 36.2 %collective-permute-start.36 = (f32[512,384]{1,0:T(8,128)}, f32[512,384]{1,0:T(8,128)S(1)}, u32[]{:S(2)}, u32[]{:S(2)}) collective-permute-start(f32[512,384]{1,0:T(8,128)} %bitcast.23), channel_id=1, source_target_pairs={{0,4},{1,5},{2,6},{3,7},{4,0},{5,1},{6,2},{7,3},{8,12},{9,13},{10,... | collective-permute-start | bytes 2359304 | tf_op jit(solution)/shard_map/ppermute | solution.py:1032
  249.3 36.2 %collective-permute-start.35 = (f32[512,384]{1,0:T(8,128)}, f32[512,384]{1,0:T(8,128)S(1)}, u32[]{:S(2)}, u32[]{:S(2)}) collective-permute-start(f32[512,384]{1,0:T(8,128)} %bitcast.24), channel_id=1, source_target_pairs={{0,2},{1,3},{2,0},{3,1},{4,6},{5,7},{6,4},{7,5},{8,10},{9,11},{10,... | collective-permute-start | bytes 2359304 | tf_op jit(solution)/shard_map/ppermute | solution.py:1032
  257.8 5.1 %copy-start.7 = (f32[4,128,384]{2,1,0:T(8,128)S(1)}, f32[4,128,384]{2,1,0:T(8,128)}, u32[]{:S(2)}) copy-start(f32[4,128,384]{2,1,0:T(8,128)} %hop_in.3) | copy-start | bytes 2359300
  257.8 28.4 %copy-start.2 = (f32[8,128]{1,0:T(8,128)S(1)}, f32[8,128]{1,0:T(8,128)}, u32[]{:S(2)}) copy-start(f32[8,128]{1,0:T(8,128)} %get-tuple-element.196) | copy-start | bytes 12292
  257.9 28.9 %copy-start = (f32[192,192]{1,0:T(8,128)S(1)}, f32[192,192]{1,0:T(8,128)}, u32[]{:S(2)}) copy-start(f32[192,192]{1,0:T(8,128)} %get-tuple-element.201) | copy-start | bytes 442372
  262.9 24.5 %collective-permute-start.38 = (f32[512,384]{1,0:T(8,128)S(1)}, f32[512,384]{1,0:T(8,128)S(1)}, u32[]{:S(2)}, u32[]{:S(2)}) collective-permute-start(f32[512,384]{1,0:T(8,128)S(1)} %bitcast.26), channel_id=1, source_target_pairs={{0,1},{1,0},{2,3},{3,2},{4,5},{5,4},{6,7},{7,6},{8,9},{9,8},{10,11... | collective-permute-start | bytes 2359304 | tf_op jit(solution)/shard_map/ppermute | solution.py:1032
  269.5 21.5 %copy-start.8 = (f32[512,384]{1,0:T(8,128)}, f32[512,384]{1,0:T(8,128)S(1)}, u32[]{:S(2)}) copy-start(f32[512,384]{1,0:T(8,128)S(1)} %collective-permute-done.37.refs_6_) | copy-start | bytes 2359300
  285.5 5.5 %copy-start.9 = (f32[512,384]{1,0:T(8,128)}, f32[512,384]{1,0:T(8,128)S(1)}, u32[]{:S(2)}) copy-start(f32[512,384]{1,0:T(8,128)S(1)} %collective-permute-done.36.refs_5_) | copy-start | bytes 2359300
  285.5 5.5 %copy-start.10 = (f32[512,384]{1,0:T(8,128)}, f32[512,384]{1,0:T(8,128)S(1)}, u32[]{:S(2)}) copy-start(f32[512,384]{1,0:T(8,128)S(1)} %collective-permute-done.35.refs_4_) | copy-start | bytes 2359300
  285.5 2.3 collective-permute-start.39
  285.6 3.4 %collective-permute-start.40 = (f32[512,384]{1,0:T(8,128)S(1)}, f32[512,384]{1,0:T(8,128)S(1)}, u32[]{:S(2)}, u32[]{:S(2)}) collective-permute-start(f32[512,384]{1,0:T(8,128)S(1)} %collective-permute-done.36.refs_5_), channel_id=1, source_target_pairs={{0,1},{1,0},{2,3},{3,2},{4,5},{5,4},{6,7},{7,6},{8,9},{9,8},{10,11... | collective-permute-start | bytes 2359304 | tf_op jit(solution)/shard_map/ppermute | solution.py:1032
  286.1 4.0 %collective-permute-start.41 = (f32[512,384]{1,0:T(8,128)S(1)}, f32[512,384]{1,0:T(8,128)S(1)}, u32[]{:S(2)}, u32[]{:S(2)}) collective-permute-start(f32[512,384]{1,0:T(8,128)S(1)} %collective-permute-done.37.refs_6_), channel_id=1, source_target_pairs={{0,1},{1,0},{2,3},{3,2},{4,5},{5,4},{6,7},{7,6},{8,9},{9,8},{10,11... | collective-permute-start | bytes 2359304 | tf_op jit(solution)/shard_map/ppermute | solution.py:1032
  287.5 3.6 %copy-start.14 = (f32[512,384]{1,0:T(8,128)}, f32[512,384]{1,0:T(8,128)S(1)}, u32[]{:S(2)}) copy-start(f32[512,384]{1,0:T(8,128)S(1)} %collective-permute-done.38.refs_7_) | copy-start | bytes 2359300
  287.9 3.1 %copy-start.15 = (f32[512,384]{1,0:T(8,128)}, f32[512,384]{1,0:T(8,128)S(1)}, u32[]{:S(2)}) copy-start(f32[512,384]{1,0:T(8,128)S(1)} %collective-permute-done.39.refs_8_) | copy-start | bytes 2359300
  (19 other events, 21.2 us)

commit v4 on v3

--- a/solution.py
+++ b/solution.py
@@ -474,8 +474,11 @@
 def align_of(durations_row, pairs):
     length = durations_row.shape[1]
     upper = jnp.where(iota((length, length), 0) <= iota((length, length), 1), 1.0, 0.0).astype(F32)
-    wide = jnp.broadcast_to(durations_row.astype(F32), (8, length))
-    ends = dot_nn(wide, upper, HIGH)[0:1].astype(jnp.int32)
+    high = (durations_row >> 5).astype(F32)
+    low = (durations_row & 31).astype(F32)
+    both = jnp.where(iota((8, length), 0) == 0, high, low).astype(BF16)
+    sums = dot_nn(both, upper.astype(BF16))
+    ends = (32.0 * sums[0:1] + sums[1:2]).astype(jnp.int32)
     starts = ends - durations_row
     frame = 2 * rows_of(pairs)
     even = (frame >= starts) & (frame < ends)
@@ -1108,7 +1111,7 @@
             for step in range(radix):
                 out_refs[at + step][...] = table[digit ^ step]
 
-    found = call_whole(body, place, ins, outs, scratch, after, 3, "hop_out")
+    found = call_whole(body, place, ins, outs, scratch, after, 25, "hop_out")
     return [found[at : at + radix] for _, at, _, radix in plans]
 
 
@@ -1128,7 +1131,7 @@
             for step in range(radix):
                 out[digit ^ step] = refs[first + step][...]
 
-    return call_whole(body, place, ins, outs, (), after, 2, "hop_in")
+    return call_whole(body, place, ins, outs, (), after, 25, "hop_in")
 
 
 def add_parts(jobs, place, after=()):
@@ -1145,7 +1148,7 @@
             out[...] = value
             at += len(parts)
 
-    return call_whole(body, place, ins, outs, (), after, 1, "add_parts")
+    return call_whole(body, place, ins, outs, (), after, 25, "add_parts")
 
 
 def send_parts(parts, shift, devices):
@@ -1165,17 +1168,140 @@
     return hop_in([(send_parts([part] * radix, shift, devices), shift)], place, after)[0]
 
 
-def last_level(part, devices):
-    shift, radix = digits(devices)[0]
-    return send_parts([part.reshape(-1, WIDE)] * radix, shift, devices)
-
-
-def table_parts(place_ref, shift, radix, mine_refs, other_refs, table):
-    digit = (place_ref[0] >> shift) & (radix - 1)
+def first_bits(place_ref):
+    return (place_ref[0] >> 1) & 1, (place_ref[0] >> 2) & 1
+
+
+def pair_send(pair, first_bit, second_bit, devices):
+    (kept, sent), (other_kept, other_sent) = pair
+    return [kept, swap(sent, first_bit, devices)], [other_kept, swap(other_sent, second_bit, devices)]
+
+
+def pair_out(units, place, devices, after=()):
+    ins = [array for unit in units for array in unit]
+    rows = [unit[0].shape[0] // 8 for unit in units]
+    total = sum(rows)
+
+    def body(place_ref, *refs):
+        low, high = first_bits(place_ref)
+        outs = refs[len(ins) :]
+        at = 0
+        begin = 0
+        for unit, row in zip(units, rows):
+            for out, half, mine in ((0, 0, low), (1, 0, 1 - low), (2, 1, high), (3, 1, 1 - high)):
+                for other in range(2):
+                    digit = mine + 2 * other if half == 0 else other + 2 * mine
+                    span = pl.ds(pl.multiple_of((2 * digit + half) * row, 8), row)
+                    value = refs[at][span, :]
+                    for extra in range(1, len(unit)):
+                        value = value + refs[at + extra][span, :]
+                    outs[out][other, begin : begin + row, :] = value
+            at += len(unit)
+            begin += row
+
+    outs = [shape_of((2, total, WIDE))] * 4
+    found = call_whole(body, place, ins, outs, (), after, 25, "pair_out")
+    return pair_send((found[:2], found[2:]), 2, 4, devices)
+
+
+def pair_next(pair, place, devices, after=()):
+    ins = [*pair[0], *pair[1]]
+
+    def body(place_ref, one, one_more, two, two_more, *outs):
+        low, high = first_bits(place_ref)
+        for first, more, mine, kept, sent in (
+            (one, one_more, high, outs[0], outs[1]),
+            (two, two_more, low, outs[2], outs[3]),
+        ):
+            kept[...] = first[mine] + more[mine]
+            sent[...] = first[1 - mine] + more[1 - mine]
+
+    outs = [shape_of(ins[0].shape[1:])] * 4
+    found = call_whole(body, place, ins, outs, (), after, 25, "pair_next")
+    return pair_send((found[:2], found[2:]), 4, 2, devices)
+
+
+def pair_level(pair, level, place, devices, after=()):
+    shift, radix = digits(devices)[level]
+    ins = [*pair[0], *pair[1]]
+    rows = ins[0].shape[0]
+    part = 2 * rows // radix
+
+    def body(place_ref, one, one_more, two, two_more, *refs):
+        table = refs[-1]
+        digit = (place_ref[0] >> shift) & (radix - 1)
+        for half, (first, more) in enumerate(((one, one_more), (two, two_more))):
+            value = first[...] + more[...]
+            for i in range(radix // 2):
+                table[half * (radix // 2) + i] = value[i * part : (i + 1) * part, :]
+        for step in range(radix):
+            refs[step][...] = table[digit ^ step]
+
+    outs = [shape_of((part, WIDE))] * radix
+    scratch = [pltpu.VMEM((radix, part, WIDE), F32)]
+    parts = call_whole(body, place, ins, outs, scratch, after, 25, "pair_level")
+    return send_parts(parts, shift, devices)
+
+
+def gather_pair(part, level, place, devices, after=()):
+    shift, radix = digits(devices)[level]
+    parts = send_parts([part.reshape(-1, WIDE)] * radix, shift, devices)
+    rows = parts[0].shape[0]
+
+    def body(place_ref, *refs):
+        table = refs[-1]
+        digit = (place_ref[0] >> shift) & (radix - 1)
+        for step in range(radix):
+            table[digit ^ step] = refs[step][...]
+        for half in range(2):
+            for i in range(radix // 2):
+                refs[radix + half][i * rows : (i + 1) * rows, :] = table[half * (radix // 2) + i]
+
+    outs = [shape_of((rows * radix // 2, WIDE))] * 2
+    scratch = [pltpu.VMEM((radix, rows, WIDE), F32)]
+    return call_whole(body, place, parts, outs, scratch, after, 25, "gather_pair")
+
+
+def pair_join(one, two, place, devices, after=()):
+    one_more = swap(one, 4, devices)
+    two_more = swap(two, 2, devices)
+
+    def body(place_ref, one_ref, one_more_ref, two_ref, two_more_ref, *outs):
+        low, high = first_bits(place_ref)
+        for first, more, mine, out in (
+            (one_ref, one_more_ref, high, outs[0]),
+            (two_ref, two_more_ref, low, outs[1]),
+        ):
+            out[mine] = first[...]
+            out[1 - mine] = more[...]
+
+    outs = [shape_of((2, *one.shape))] * 2
+    ins = [one, one_more, two, two_more]
+    one, two = call_whole(body, place, ins, outs, (), after, 25, "pair_join")
+    return [one, swap(one, 2, devices), two, swap(two, 4, devices)]
+
+
+def table_parts(place_ref, mine_refs, other_refs, table, sems):
+    low, high = first_bits(place_ref)
     core = place_ref[0] & 1
-    for step in range(radix):
-        table[core, digit ^ step] = mine_refs[step][...]
-        table[1 - core, digit ^ step] = other_refs[step][...]
+    copies = []
+    for side, refs in ((core, mine_refs), (1 - core, other_refs)):
+        for half, bit in ((0, low), (1, high)):
+            for step in range(2):
+                mine = bit ^ step
+                for other in range(2):
+                    digit = mine + 2 * other if half == 0 else other + 2 * mine
+                    copies.append(
+                        pltpu.make_async_copy(
+                            refs[2 * half + step].at[other],
+                            table.at[side, 2 * digit + half],
+                            sems.at[len(copies)],
+                        )
+                    )
+    for copy in copies:
+        copy.start()
+    for copy in copies:
+        copy.wait()
 
 
 def segments(begin, count, rows):
@@ -1189,16 +1315,10 @@
     return found
 
 
-def unpack_upper_body(
-    shift,
-    radix,
-    place_ref,
-    small_ref,
-    *refs,
-):
-    mine, other = refs[:radix], refs[radix : 2 * radix]
-    in_ref, res_ref, last_ref, end_ref, start_ref, mix_ref, sums_ref, table, tail, sems = refs[2 * radix :]
-    table_parts(place_ref, shift, radix, mine, other, table)
+def unpack_upper_body(place_ref, small_ref, *refs):
+    mine, other = refs[:4], refs[4:8]
+    in_ref, res_ref, last_ref, end_ref, start_ref, mix_ref, sums_ref, table, tail, sems, first_sems = refs[8:]
+    table_parts(place_ref, mine, other, table, first_sems)
     rows = table.shape[2]
     conv = WKER * HID
     half = UNIT // 2
@@ -1239,8 +1359,7 @@
         copy.wait()
 
 
-def unpack_upper(parts, other, place, small, devices, after):
-    shift, radix = digits(devices)[0]
+def unpack_upper(parts, other, place, small, after):
     vmem = pl.BlockSpec(memory_space=pltpu.VMEM)
     anywhere = pl.BlockSpec(memory_space=pl.ANY)
     outs = [
@@ -1253,16 +1372,17 @@
         shape_of((8, LANES)),
     ]
     return run(
-        functools.partial(unpack_upper_body, shift, radix),
+        unpack_upper_body,
         (),
         [place, small, *parts, *other],
-        [pl.BlockSpec(memory_space=pltpu.SMEM)] + [vmem] * (1 + 2 * radix),
+        [pl.BlockSpec(memory_space=pltpu.SMEM), vmem] + [anywhere] * 8,
         outs,
         [anywhere] * 2 + [vmem] * 5,
         [
-            pltpu.VMEM((2, radix, *parts[0].shape), F32),
+            pltpu.VMEM((2, 8, *parts[0].shape[1:]), F32),
             pltpu.VMEM((TAIL, WIDE), F32),
-            pltpu.SemaphoreType.DMA((40,)),
+            pltpu.SemaphoreType.DMA((64,)),
+            pltpu.SemaphoreType.DMA((16,)),
         ],
         micros=5,
         after=after,
@@ -1270,8 +1390,8 @@
     )
 
 
-def unpack_lower_body(shift, radix, place_ref, in_given, res_given, *refs):
-    mine, other = refs[:radix], refs[radix : 2 * radix]
+def unpack_lower_body(place_ref, in_given, res_given, *refs):
+    mine, other = refs[:4], refs[4:8]
     (
         in_ref,
         res_ref,
@@ -1287,33 +1407,34 @@
         table,
         rest,
         sems,
-    ) = refs[2 * radix :]
-    table_parts(place_ref, shift, radix, mine, other, table)
+        first_sems,
+    ) = refs[8:]
+    table_parts(place_ref, mine, other, table, first_sems)
     conv = WKER * HID
     half = UNIT // 2
-    quarter = half // radix
+    eighth = half // 8
     copies = []
     for core in range(2):
-        for digit in range(radix):
-            at = core * half + digit * quarter
-            pieces = [(0, max(0, min(quarter, conv - at)), in_ref, at)]
-            pieces.append((pieces[0][1], quarter - pieces[0][1], res_ref, at + pieces[0][1] - conv))
+        for block in range(8):
+            at = core * half + block * eighth
+            pieces = [(0, max(0, min(eighth, conv - at)), in_ref, at)]
+            pieces.append((pieces[0][1], eighth - pieces[0][1], res_ref, at + pieces[0][1] - conv))
             for row, size, target, to in pieces:
                 if size:
                     copies.append(
                         pltpu.make_async_copy(
-                            table.at[core, digit, pl.ds(row, size), :],
+                            table.at[core, block, pl.ds(row, size), :],
                             target.at[0, pl.ds(to, size), :],
                             sems.at[len(copies)],
                         )
                     )
     for copy in copies:
         copy.start()
-    rows = table.shape[2] - quarter
+    rows = table.shape[2] - eighth
 
     def read(core, begin, count):
         return [
-            (table[core, part, quarter + row : quarter + row + size, :], at)
+            (table[core, part, eighth + row : eighth + row + size, :], at)
             for part, row, size, at in segments(begin, count, rows)
         ]
 
@@ -1346,8 +1467,7 @@
         copy.wait()
 
 
-def unpack_lower(parts, other, place, in_grad, res_grad, devices):
-    shift, radix = digits(devices)[0]
+def unpack_lower(parts, other, place, in_grad, res_grad):
     vmem = pl.BlockSpec(memory_space=pltpu.VMEM)
     anywhere = pl.BlockSpec(memory_space=pl.ANY)
     reach = 2 * WINDOW + 1
@@ -1365,16 +1485,17 @@
         *[shape_of((D,))] * 4,
     ]
     return run(
-        functools.partial(unpack_lower_body, shift, radix),
+        unpack_lower_body,
         (),
         [place, in_grad, res_grad, *parts, *other],
-        [pl.BlockSpec(memory_space=pltpu.SMEM)] + [anywhere] * 2 + [vmem] * (2 * radix),
+        [pl.BlockSpec(memory_space=pltpu.SMEM)] + [anywhere] * 10,
         outs,
         [anywhere] * 2 + [vmem] * (len(outs) - 2),
         [
-            pltpu.VMEM((2, radix, *parts[0].shape), F32),
+            pltpu.VMEM((2, 8, *parts[0].shape[1:]), F32),
             pltpu.VMEM((REST, WIDE), F32),
-            pltpu.SemaphoreType.DMA((2 * radix + 2,)),
+            pltpu.SemaphoreType.DMA((32,)),
+            pltpu.SemaphoreType.DMA((16,)),
         ],
         micros=5,
         aliases={1: 0, 2: 1},
@@ -1651,22 +1772,25 @@
     for level in range(1, levels):
         upper = spread_level([upper], level, place, devices, (fed_kept,))
     units = [[last_kept, last_recv], [fed_kept, fed_recv]]
-    lower = spread_level(units, 0, place, devices, (upper[0],))
-    upper = add_parts([upper], place, (lower[0],))[0]
-    for level in reversed(range(1, levels)):
-        upper = gather_level(upper, level, place, devices, (upper,))
-    upper_parts = last_level(upper, devices)
-    for level in range(1, levels):
-        lower = spread_level([lower], level, place, devices, (upper,))
-    lower = add_parts([lower], place)[0]
-    for level in reversed(range(1, levels)):
+    lower = pair_out(units, place, devices, (upper[0],))
+    upper = add_parts([upper], place, (lower[0][0],))[0]
+    for level in reversed(range(2, levels)):
+        upper = gather_level(upper, level, place, devices)
+    lower = pair_next(lower, place, devices)
+    upper = gather_pair(upper, 1, place, devices, (lower[0][0],))
+    lower = pair_level(lower, 1, place, devices, (upper[0],))
+    upper_parts = pair_join(*upper, place, devices, (lower[0],))
+    for level in range(2, levels):
+        lower = spread_level([lower], level, place, devices)
+    lower = add_parts([lower], place, (upper_parts[0],))[0]
+    for level in reversed(range(2, levels)):
         lower = gather_level(lower, level, place, devices)
+    lower = gather_pair(lower, 1, place, devices)
     upper_parts, lower = lax.optimization_barrier((upper_parts, lower))
     upper_other = [swap(part, 1, devices) for part in upper_parts]
-    lower, upper_other = lax.optimization_barrier((lower, upper_other))
-    lower_parts = last_level(lower, devices)
+    lower_parts = pair_join(*lower, place, devices, (upper_other[0], upper_other[3]))
     in_grad, res_grad, last_grad, end_grad, start_grad, mix_grad, sums = unpack_upper(
-        upper_parts, upper_other, place, small, devices, ()
+        upper_parts, upper_other, place, small, ()
     )
     ins = [mel_frames, durations, normal_grad, stats, sums, small]
     kinds = [item_spec, full_spec, item_spec, full_spec, full_spec, full_spec]
@@ -1695,7 +1819,7 @@
         relv_grad,
         prior_grad,
         *norm_grads,
-    ) = unpack_lower(lower_parts, lower_other, place, in_grad, res_grad, devices)
+    ) = unpack_lower(lower_parts, lower_other, place, in_grad, res_grad)
 
     return (
         loss.reshape(()),

time: 298 us -> 282 us (0.946)
  waiting for transfers between devices: 74.6 us -> 58.9 us
  starting transfers between devices: 57.9 us -> 47.2 us
  Pallas kernels: 152 us -> 159 us
  local copies, waits for them, and re-layouts: 11.1 us -> 14.1 us
    ppermute x42 -> x45, waiting for transfers between devices: 74.6 us -> 58.9 us  [swap(): return lax.ppermute(values, 'dp', [(i, i ^ bit) for i in range(devices)])]
    ppermute x42 -> x45, starting transfers between devices: 57.9 us -> 47.2 us  [swap(): return lax.ppermute(values, 'dp', [(i, i ^ bit) for i in range(devices)])]
    pallas_call x16 -> x19, Pallas kernels: 152 us -> 159 us  [run(): pl.pallas_call(wrapped, grid=grid, in_specs=list(in_specs) + [pl.BlockSpe...]
    unnamed x82 -> x86, local copies, waits for them, and re-layouts: 9.88 us -> 12.8 us
  transfers between devices with their start and end apart: 42 -> 45, of which waited for: 23 -> 19; matrix products, arithmetic and copies ran while one was open for 0% -> 0% of each run, Pallas kernels for 25% -> 31%
where the time goes in v4:
time: 282 us
  Pallas kernels  159 us (56%)
  waiting for transfers between devices  58.9 us (21%)
  starting transfers between devices  47.2 us (17%)
  local copies, waits for them, and re-layouts  14.1 us (5%)
    pallas_call x19, Pallas kernels, run(): pl.pallas_call(wrapped, grid=grid, in_specs=list(in_specs) + [pl.BlockSpe...  159 us
    ppermute x45, waiting for transfers between devices, swap(): return lax.ppermute(values, 'dp', [(i, i ^ bit) for i in range(devices)])  58.9 us
    ppermute x45, starting transfers between devices, swap(): return lax.ppermute(values, 'dp', [(i, i ^ bit) for i in range(devices)])  47.2 us
    unnamed x86, local copies, waits for them, and re-layouts  12.8 us
  transfers between devices with their start and end apart: 45, of which 19 were waited for; matrix products, arithmetic and copies ran while one was open for 0% of the time, Pallas kernels for 31%

profile of v4, /device:TPU:0, one launch (start us, length us, event | category | flops | bytes accessed | tf_op | source)
XLA Modules:
  0.0 281.7 jit_solution(15325338226355815205)
XLA Ops:
  0.7 2.4 stats.1.refs_10_
  3.0 2.4 collective-permute-start.2
  6.1 0.9 collective-permute-done.2
  6.9 2.3 collective-permute-done.1
  9.2 0.7 add_add_fusion.1.refs_14_
  9.9 2.5 collective-permute-start.5
  13.4 3.4 %weights.1 = (f32[256,256]{1,0:T(8,128)}, f32[8,128]{1,0:T(8,128)}, bf16[192,768]{1,0:T(8,128)(2,1)}, bf16[128,128]{1,0:T(8,128)(2,1)}, bf16[128,128]{1,0:T(8,12...) custom-call(f32[4,4]{1,0:T(4,128)} %refs_0_.3, ...), custom_call_target="tpu_custom_call" | custom-call | flops 5750000128 | bytes 1048576 | tf_op jit(solution)/shard_map/weights/pallas_call | solution.py:102
  16.8 2.7 collective-permute-start.6
  19.5 16.4 %encoder.1 = (bf16[4,256,192]{2,1,0:T(8,128)(2,1)}, bf16[4,256,768]{2,1,0:T(8,128)(2,1)}, bf16[4,2,256,256]{3,2,1,0:T(8,128)(2,1)}, bf16[4,2,256,128]{3,2,1,0:T(...) custom-call(s32[4,256]{1,0:T(4,128)} %refs_0_.5, ...), custom_call_target="tpu_custom_call" | custom-call | flops 23000000512 | bytes 1048576 | tf_op jit(solution)/shard_map/encoder/pallas_call | solution.py:102
  36.5 59.9 %decoder.1 = (f32[1792,384]{1,0:T(8,128)}, f32[1792,384]{1,0:T(8,128)}, f32[576,384]{1,0:T(8,128)}, f32[576,384]{1,0:T(8,128)}, bf16[4,512,512]{2,1,0:T(8,128)(2,1)}, /*index=5*/f32[4,512,256]{2,1,0:T(8,128)}) custom-call(f32[4,80,1024]{2,1,0:T(8,128)} %bitcast.16, s32[4,256]{1,0:T(4,128)} %refs_1_.11, bf16[4,512,512]{2,1,0:T(8,128)(2,1)} %get-tuple-element.124.refs_2_, ...), custom_call_target="tpu_custom_call" | custom-call | flops 92000002048 | bytes 1048576 | tf_op jit(solution)/shard_map/decoder/pallas_call | solution.py:102
  97.0 4.8 %collective-permute-done.7.refs_2_ = f32[1792,384]{1,0:T(8,128)S(1)} collective-permute-done((f32[1792,384]{1,0:T(8,128)}, f32[1792,384]{1,0:T(8,128)S(1)}, u32[]{:S(2)}, u32[]{:S(2)}) %collective-permute-start.7) | collective-permute-done | bytes 2752544 | tf_op jit(solution)/shard_map/ppermute | solution.py:1035
  101.8 1.5 copy-done.3
  103.3 4.5 %hop_out.2 = (f32[448,384]{1,0:T(8,128)}, f32[448,384]{1,0:T(8,128)}, f32[448,384]{1,0:T(8,128)}, f32[448,384]{1,0:T(8,128)}) custom-call(s32[1]{0:T(128)} %bitcast.8.refs_10_.refs_0_.refs_24_, f32[1792,384]{1,0:T(8,128)} %get-tuple-element.132.refs_1_, f32[1792,384]{1,0:T(8,128)} %copy-done.3), custom_call_target="tpu_custom_call" | custom-call | flops 28750000128 | bytes 1048576 | tf_op jit(solution)/shard_map/hop_out/pallas_call | solution.py:102
  108.4 1.5 collective-permute-start.9
  109.9 1.4 collective-permute-start.10
  111.3 27.9 %encoder_back.1 = (f32[1472,384]{1,0:T(8,128)}, f32[1472,384]{1,0:T(8,128)}) custom-call(s32[4,256]{1,0:T(4,128)} %refs_0_.5, s32[4,256]{1,0:T(4,128)} %refs_1_.11, bf16[4,512,512]{2,1,0:T(8,128)(2,1)} %get-tuple-element.138.refs_2_, bf16[4,256,192]{2,1,0:T(8,128)(2,1)} %get-tuple-element.139.refs_3_, f32[4,256,192]{2,1,0:T(8,128)} %get-tuple-element.140.refs_4_, ...), custom_call_target="tpu_custom_call" | custom-call | flops 34500001792 | bytes 1048576 | tf_op jit(solution)/shard_map/encoder_back/pallas_call | solution.py:102
  139.7 1.5 collective-permute-done.10.refs_4_
  141.2 0.8 copy-done.24
  142.0 2.7 hop_out.3
  144.7 1.6 collective-permute-start.11
  146.6 2.5 collective-permute-start.13
  149.1 0.9 copy-done.5
  150.0 0.7 copy-done.4
  150.7 4.8 %pair_out.1 = (f32[2,256,384]{2,1,0:T(8,128)}, f32[2,256,384]{2,1,0:T(8,128)}, f32[2,256,384]{2,1,0:T(8,128)}, f32[2,256,384]{2,1,0:T(8,128)}) custom-call(s32[1]{0:T(128)} %bitcast.8.refs_10_.refs_0_.refs_24_, f32[576,384]{1,0:T(8,128)} %get-tuple-element.162.refs_1_, f32[576,384]{1,0:T(8,128)} %copy-done.5, ...), custom_call_target="tpu_custom_call" | custom-call | flops 28750000128 | bytes 1048576 | tf_op jit(solution)/shard_map/pair_out/pallas_call | solution.py:102
  155.6 1.0 collective-permute-start.19
  156.6 1.5 collective-permute-start.20
  158.1 3.1 %collective-permute-done.12.refs_3_ = f32[112,384]{1,0:T(8,128)S(1)} collective-permute-done((f32[112,384]{1,0:T(8,128)}, f32[112,384]{1,0:T(8,128)S(1)}, u32[]{:S(2)}, u32[]{:S(2)}) %collective-permute-start.12) | collective-permute-done | bytes 172064 | tf_op jit(solution)/shard_map/ppermute | solution.py:1035
  162.0 1.9 add_parts.2.refs_1_
  163.8 0.8 collective-permute-start.18
  164.6 4.0 %collective-permute-start.17 = (f32[112,384]{1,0:T(8,128)}, f32[112,384]{1,0:T(8,128)S(1)}, u32[]{:S(2)}, u32[]{:S(2)}) collective-permute-start(f32[112,384]{1,0:T(8,128)} %add_parts.2.refs_1_), channel_id=1, source_target_pairs={{0,16},{1,17},{2,18},{3,19},{4,20},{5,21},{6,22},{7,23},{8,24},{9,... | collective-permute-start | bytes 516104 | tf_op jit(solution)/shard_map/ppermute | solution.py:1035
  168.6 5.4 %collective-permute-done.19.refs_2_ = f32[2,256,384]{2,1,0:T(8,128)S(1)} collective-permute-done((f32[2,256,384]{2,1,0:T(8,128)}, f32[2,256,384]{2,1,0:T(8,128)S(1)}, u32[]{:S(2)}, u32[]{:S(2)}) %collective-permute-start.19) | collective-permute-done | bytes 786464 | tf_op jit(solution)/shard_map/ppermute | solution.py:1035
  175.5 3.1 %pair_next.1 = (f32[256,384]{1,0:T(8,128)}, f32[256,384]{1,0:T(8,128)}, f32[256,384]{1,0:T(8,128)}, f32[256,384]{1,0:T(8,128)}) custom-call(s32[1]{0:T(128)} %bitcast.8.refs_10_.refs_0_.refs_24_, f32[2,256,384]{2,1,0:T(8,128)} %get-tuple-element.165.refs_5_.refs_1_, f32[2,256,384]{2,1,0:T(8,128)} %copy-done.12, f32[2,256,384]{2,1,0:T(8,128)} %get-tuple-element.167.refs_3_, ...), custom_call_target="tpu_custom_call" | custom-call | flops 28750000128 | bytes 1048576 | tf_op jit(solution)/shard_map/pair_next/pallas_call | solution.py:102
  178.7 1.5 collective-permute-start.23
  180.8 0.8 collective-permute-done.17.refs_3_
  182.3 2.1 gather_pair.2
  184.4 0.7 collective-permute-start.22
  185.1 1.5 collective-permute-start.21
  186.7 1.5 collective-permute-done.23.refs_2_
  188.2 2.5 collective-permute-done.24.refs_4_
  190.7 0.7 copy-done.26
  191.5 2.3 pair_level.1
  193.8 2.2 collective-permute-start.27
  196.1 2.4 collective-permute-start.29
  198.4 0.7 copy-done.29
  199.3 2.4 pair_join.2
  201.7 10.7 %collective-permute-done.28.refs_3_ = f32[128,384]{1,0:T(8,128)S(1)} collective-permute-done((f32[128,384]{1,0:T(8,128)}, f32[128,384]{1,0:T(8,128)S(1)}, u32[]{:S(2)}, u32[]{:S(2)}) %collective-permute-start.28) | collective-permute-done | bytes 196640 | tf_op jit(solution)/shard_map/ppermute | solution.py:1035
  213.1 2.0 add_parts.3.refs_1_
  215.2 0.9 collective-permute-start.32
  216.1 5.3 %collective-permute-start.31 = (f32[128,384]{1,0:T(8,128)}, f32[128,384]{1,0:T(8,128)S(1)}, u32[]{:S(2)}, u32[]{:S(2)}) collective-permute-start(f32[128,384]{1,0:T(8,128)} %add_parts.3.refs_1_), channel_id=1, source_target_pairs={{0,16},{1,17},{2,18},{3,19},{4,20},{5,21},{6,22},{7,23},{8,24},{9,... | collective-permute-start | bytes 589832 | tf_op jit(solution)/shard_map/ppermute | solution.py:1035
  222.0 0.8 collective-permute-done.32.refs_4_
  222.9 6.6 %collective-permute-done.31.refs_3_ = f32[128,384]{1,0:T(8,128)S(1)} collective-permute-done((f32[128,384]{1,0:T(8,128)}, f32[128,384]{1,0:T(8,128)S(1)}, u32[]{:S(2)}, u32[]{:S(2)}) %collective-permute-start.31) | collective-permute-done | bytes 196640 | tf_op jit(solution)/shard_map/ppermute | solution.py:1035
  230.8 2.2 gather_pair.3
  234.1 1.4 collective-permute-start.38
  235.5 9.4 %collective-permute-done.37.refs_2_ = f32[256,384]{1,0:T(8,128)S(1)} collective-permute-done((f32[256,384]{1,0:T(8,128)}, f32[256,384]{1,0:T(8,128)S(1)}, u32[]{:S(2)}, u32[]{:S(2)}) %collective-permute-start.37) | collective-permute-done | bytes 393248 | tf_op jit(solution)/shard_map/ppermute | solution.py:1035
  246.2 0.9 copy-done.21
  247.1 2.6 pair_join.3
  249.7 1.4 collective-permute-start.39
  251.0 1.5 collective-permute-start.40
  252.5 6.9 %unpack_upper.1 = (f32[4,960,384]{2,1,0:T(8,128)}, f32[3,192,384]{2,1,0:T(8,128)}, f32[192,192]{1,0:T(8,128)}, f32[192,192]{1,0:T(8,128)}, f32[80,192]{1,0:T(8,1...) custom-call(s32[1]{0:T(128)} %bitcast.8.refs_10_.refs_0_.refs_24_, f32[8,128]{1,0:T(8,128)} %get-tuple-element.131.refs_1_.refs_5_, ...), custom_call_target="tpu_custom_call" | custom-call | flops 5750000128 | bytes 1048576 | tf_op jit(solution)/shard_map/unpack_upper/pallas_call | solution.py:102
  259.5 5.1 %frames.1 = (f32[4,80,1024]{2,1,0:T(8,128)}, f32[1,1]{1,0:T(1,128)}) custom-call(f32[4,80,1024]{2,1,0:T(8,128)} %bitcast.17, s32[4,256]{1,0:T(4,128)} %refs_1_.11, f32[4,512,256]{2,1,0:T(8,128)} %get-tuple-element.130.refs_2_, f32[8,128]{1,0:T(8,128)} %add.27.refs_4_.refs_3_, f32[8,128]{1,0:T(8,128)} %get-tuple-element.187.refs_4_, ...), custom_call_target="tpu_custom_call" | custom-call | flops 5750000128 | bytes 1048576 | tf_op jit(solution)/shard_map/frames/pallas_call | solution.py:102
  265.1 5.5 %collective-permute-done.40.refs_6_ = f32[2,256,384]{2,1,0:T(8,128)S(1)} collective-permute-done((f32[2,256,384]{2,1,0:T(8,128)}, f32[2,256,384]{2,1,0:T(8,128)S(1)}, u32[]{:S(2)}, u32[]{:S(2)}) %collective-permute-start.40) | collective-permute-done | bytes 786464 | tf_op jit(solution)/shard_map/ppermute | solution.py:1035
  273.0 1.1 collective-permute-done.44.refs_10_
  274.1 0.9 copy-done.15
  275.0 6.5 %unpack_lower.1 = (f32[4,960,384]{2,1,0:T(8,128)}, f32[3,192,384]{2,1,0:T(8,128)}, f32[576,768]{1,0:T(8,128)}, f32[192,2304]{1,0:T(8,128)}, f32[148,192]{1,0:T(8...) custom-call(s32[1]{0:T(128)} %bitcast.8.refs_10_.refs_0_.refs_24_, ...), custom_call_target="tpu_custom_call", output_to_operand_aliasing={{0}: (1, {}), {1}: (2, {})} | custom-call | flops 5750000128 | bytes 1048576 | tf_op jit(solution)/shard_map/unpack_lower/pallas_call | solution.py:102
  (136 shorter events, 16.0 us)
Async XLA Ops:
  3.0 3.9 %collective-permute-start.2 = (f32[8,128]{1,0:T(8,128)}, f32[8,128]{1,0:T(8,128)S(1)}, u32[]{:S(2)}, u32[]{:S(2)}) collective-permute-start(f32[8,128]{1,0:T(8,128)} %stats.1.refs_10_), channel_id=1, source_target_pairs={{0,3},{1,2},{2,1},{3,0},{4,7},{5,6},{6,5},{7,4},{8,11},{9,10},{10,... | collective-permute-start | bytes 12296 | tf_op jit(solution)/shard_map/ppermute | solution.py:1035
  5.4 3.8 %collective-permute-start.1 = (f32[8,128]{1,0:T(8,128)}, f32[8,128]{1,0:T(8,128)S(1)}, u32[]{:S(2)}, u32[]{:S(2)}) collective-permute-start(f32[8,128]{1,0:T(8,128)} %stats.1.refs_10_), channel_id=1, source_target_pairs={{0,2},{1,3},{2,0},{3,1},{4,6},{5,7},{6,4},{7,5},{8,10},{9,11},{10,... | collective-permute-start | bytes 12296 | tf_op jit(solution)/shard_map/ppermute | solution.py:1035
  6.0 3.2 %collective-permute-start = (f32[8,128]{1,0:T(8,128)}, f32[8,128]{1,0:T(8,128)S(1)}, u32[]{:S(2)}, u32[]{:S(2)}) collective-permute-start(f32[8,128]{1,0:T(8,128)} %stats.1.refs_10_), channel_id=1, source_target_pairs={{0,1},{1,0},{2,3},{3,2},{4,5},{5,4},{6,7},{7,6},{8,9},{9,8},{10,11... | collective-permute-start | bytes 12296 | tf_op jit(solution)/shard_map/ppermute | solution.py:1035
  9.9 6.9 %copy-start.1 = (f32[8,128]{1,0:T(8,128)}, f32[8,128]{1,0:T(8,128)S(1)}, u32[]{:S(2)}) copy-start(f32[8,128]{1,0:T(8,128)S(1)} %add_add_fusion.1.refs_14_) | copy-start | bytes 12292
  9.9 6.9 %collective-permute-start.5 = (f32[8,128]{1,0:T(8,128)S(1)}, f32[8,128]{1,0:T(8,128)S(1)}, u32[]{:S(2)}, u32[]{:S(2)}) collective-permute-start(f32[8,128]{1,0:T(8,128)S(1)} %add_add_fusion.1.refs_14_), channel_id=1, source_target_pairs={{0,12},{1,13},{2,14},{3,15},{4,8},{5,9},{6,10},{7,11},{8,4},{9,5},... | collective-permute-start | bytes 12296 | tf_op jit(solution)/shard_map/ppermute | solution.py:1035
  12.4 4.3 %collective-permute-start.4 = (f32[8,128]{1,0:T(8,128)S(1)}, f32[8,128]{1,0:T(8,128)S(1)}, u32[]{:S(2)}, u32[]{:S(2)}) collective-permute-start(f32[8,128]{1,0:T(8,128)S(1)} %add_add_fusion.1.refs_14_), channel_id=1, source_target_pairs={{0,8},{1,9},{2,10},{3,11},{4,12},{5,13},{6,14},{7,15},{8,0},{9,1},... | collective-permute-start | bytes 12296 | tf_op jit(solution)/shard_map/ppermute | solution.py:1035
  12.9 3.9 %collective-permute-start.3 = (f32[8,128]{1,0:T(8,128)S(1)}, f32[8,128]{1,0:T(8,128)S(1)}, u32[]{:S(2)}, u32[]{:S(2)}) collective-permute-start(f32[8,128]{1,0:T(8,128)S(1)} %add_add_fusion.1.refs_14_), channel_id=1, source_target_pairs={{0,4},{1,5},{2,6},{3,7},{4,0},{5,1},{6,2},{7,3},{8,12},{9,13},{10,... | collective-permute-start | bytes 12296 | tf_op jit(solution)/shard_map/ppermute | solution.py:1035
  16.8 19.0 %collective-permute-start.6 = (f32[8,128]{1,0:T(8,128)S(1)}, f32[8,128]{1,0:T(8,128)S(1)}, u32[]{:S(2)}, u32[]{:S(2)}) collective-permute-start(f32[8,128]{1,0:T(8,128)S(1)} %add_add_fusion), channel_id=1, source_target_pairs={{0,16},{1,17},{2,18},{3,19},{4,20},{5,21},{6,22},{7,23},{8,24},{9,... | collective-permute-start | bytes 12296 | tf_op jit(solution)/shard_map/ppermute | solution.py:1035
  96.4 5.4 %collective-permute-start.7 = (f32[1792,384]{1,0:T(8,128)}, f32[1792,384]{1,0:T(8,128)S(1)}, u32[]{:S(2)}, u32[]{:S(2)}) collective-permute-start(f32[1792,384]{1,0:T(8,128)} %get-tuple-element.133), channel_id=1, source_target_pairs={{0,1},{1,0},{2,3},{3,2},{4,5},{5,4},{6,7},{7,6},{8,9},{9,8},{10,11... | collective-permute-start | bytes 8257544 | tf_op jit(solution)/shard_map/ppermute | solution.py:1035
  96.5 52.6 %collective-permute-start.14 = (f32[576,384]{1,0:T(8,128)}, f32[576,384]{1,0:T(8,128)S(1)}, u32[]{:S(2)}, u32[]{:S(2)}) collective-permute-start(f32[576,384]{1,0:T(8,128)} %get-tuple-element.163), channel_id=1, source_target_pairs={{0,1},{1,0},{2,3},{3,2},{4,5},{5,4},{6,7},{7,6},{8,9},{9,8},{10,11... | collective-permute-start | bytes 2654216 | tf_op jit(solution)/shard_map/ppermute | solution.py:1035
  107.8 31.4 %collective-permute-start.8 = (f32[448,384]{1,0:T(8,128)}, f32[448,384]{1,0:T(8,128)S(1)}, u32[]{:S(2)}, u32[]{:S(2)}) collective-permute-start(f32[448,384]{1,0:T(8,128)} %get-tuple-element.135), channel_id=1, source_target_pairs={{0,2},{1,3},{2,0},{3,1},{4,6},{5,7},{6,4},{7,5},{8,10},{9,11},{10,... | collective-permute-start | bytes 2064392 | tf_op jit(solution)/shard_map/ppermute | solution.py:1035
  108.4 31.3 %collective-permute-start.9 = (f32[448,384]{1,0:T(8,128)}, f32[448,384]{1,0:T(8,128)S(1)}, u32[]{:S(2)}, u32[]{:S(2)}) collective-permute-start(f32[448,384]{1,0:T(8,128)} %get-tuple-element.136), channel_id=1, source_target_pairs={{0,4},{1,5},{2,6},{3,7},{4,0},{5,1},{6,2},{7,3},{8,12},{9,13},{10,... | collective-permute-start | bytes 2064392 | tf_op jit(solution)/shard_map/ppermute | solution.py:1035
  109.9 31.3 %collective-permute-start.10 = (f32[448,384]{1,0:T(8,128)}, f32[448,384]{1,0:T(8,128)S(1)}, u32[]{:S(2)}, u32[]{:S(2)}) collective-permute-start(f32[448,384]{1,0:T(8,128)} %get-tuple-element.137), channel_id=1, source_target_pairs={{0,6},{1,7},{2,4},{3,5},{4,2},{5,3},{6,0},{7,1},{8,14},{9,15},{10,... | collective-permute-start | bytes 2064392 | tf_op jit(solution)/shard_map/ppermute | solution.py:1035
  139.1 2.0 copy-start.22
  141.2 7.9 %collective-permute-start.15 = (f32[1472,384]{1,0:T(8,128)}, f32[1472,384]{1,0:T(8,128)S(1)}, u32[]{:S(2)}, u32[]{:S(2)}) collective-permute-start(f32[1472,384]{1,0:T(8,128)} %get-tuple-element.164), channel_id=1, source_target_pairs={{0,1},{1,0},{2,3},{3,2},{4,5},{5,4},{6,7},{7,6},{8,9},{9,8},{10,11... | collective-permute-start | bytes 6782984 | tf_op jit(solution)/shard_map/ppermute | solution.py:1035
  144.7 13.4 %collective-permute-start.11 = (f32[112,384]{1,0:T(8,128)}, f32[112,384]{1,0:T(8,128)S(1)}, u32[]{:S(2)}, u32[]{:S(2)}) collective-permute-start(f32[112,384]{1,0:T(8,128)} %get-tuple-element.159), channel_id=1, source_target_pairs={{0,8},{1,9},{2,10},{3,11},{4,12},{5,13},{6,14},{7,15},{8,0},{9,1},... | collective-permute-start | bytes 516104 | tf_op jit(solution)/shard_map/ppermute | solution.py:1035
  146.3 15.0 %collective-permute-start.12 = (f32[112,384]{1,0:T(8,128)}, f32[112,384]{1,0:T(8,128)S(1)}, u32[]{:S(2)}, u32[]{:S(2)}) collective-permute-start(f32[112,384]{1,0:T(8,128)} %get-tuple-element.160), channel_id=1, source_target_pairs={{0,16},{1,17},{2,18},{3,19},{4,20},{5,21},{6,22},{7,23},{8,24},{9,... | collective-permute-start | bytes 516104 | tf_op jit(solution)/shard_map/ppermute | solution.py:1035
  146.6 14.6 %collective-permute-start.13 = (f32[112,384]{1,0:T(8,128)}, f32[112,384]{1,0:T(8,128)S(1)}, u32[]{:S(2)}, u32[]{:S(2)}) collective-permute-start(f32[112,384]{1,0:T(8,128)} %get-tuple-element.161), channel_id=1, source_target_pairs={{0,24},{1,25},{2,26},{3,27},{4,28},{5,29},{6,30},{7,31},{8,16},{9,... | collective-permute-start | bytes 516104 | tf_op jit(solution)/shard_map/ppermute | solution.py:1035
  155.6 18.5 %collective-permute-start.19 = (f32[2,256,384]{2,1,0:T(8,128)}, f32[2,256,384]{2,1,0:T(8,128)S(1)}, u32[]{:S(2)}, u32[]{:S(2)}) collective-permute-start(f32[2,256,384]{2,1,0:T(8,128)} %get-tuple-element.166), channel_id=1, source_target_pairs={{0,2},{1,3},{2,0},{3,1},{4,6},{5,7},{6,4},{7,5},{8,10},{9,11},{10,... | collective-permute-start | bytes 2359304 | tf_op jit(solution)/shard_map/ppermute | solution.py:1035
  156.6 18.1 %collective-permute-start.20 = (f32[2,256,384]{2,1,0:T(8,128)}, f32[2,256,384]{2,1,0:T(8,128)S(1)}, u32[]{:S(2)}, u32[]{:S(2)}) collective-permute-start(f32[2,256,384]{2,1,0:T(8,128)} %get-tuple-element.168), channel_id=1, source_target_pairs={{0,4},{1,5},{2,6},{3,7},{4,0},{5,1},{6,2},{7,3},{8,12},{9,13},{10,... | collective-permute-start | bytes 2359304 | tf_op jit(solution)/shard_map/ppermute | solution.py:1035
  158.1 3.1 %copy-start.37 = (f32[112,384]{1,0:T(8,128)}, f32[112,384]{1,0:T(8,128)S(1)}, u32[]{:S(2)}) copy-start(f32[112,384]{1,0:T(8,128)S(1)} %collective-permute-done.11.refs_2_) | copy-start | bytes 516100
  163.8 17.0 %collective-permute-start.18 = (f32[112,384]{1,0:T(8,128)}, f32[112,384]{1,0:T(8,128)S(1)}, u32[]{:S(2)}, u32[]{:S(2)}) collective-permute-start(f32[112,384]{1,0:T(8,128)} %add_parts.2.refs_1_), channel_id=1, source_target_pairs={{0,24},{1,25},{2,26},{3,27},{4,28},{5,29},{6,30},{7,31},{8,16},{9,... | collective-permute-start | bytes 516104 | tf_op jit(solution)/shard_map/ppermute | solution.py:1035
  164.6 17.0 %collective-permute-start.17 = (f32[112,384]{1,0:T(8,128)}, f32[112,384]{1,0:T(8,128)S(1)}, u32[]{:S(2)}, u32[]{:S(2)}) collective-permute-start(f32[112,384]{1,0:T(8,128)} %add_parts.2.refs_1_), channel_id=1, source_target_pairs={{0,16},{1,17},{2,18},{3,19},{4,20},{5,21},{6,22},{7,23},{8,24},{9,... | collective-permute-start | bytes 516104 | tf_op jit(solution)/shard_map/ppermute | solution.py:1035
  168.6 13.0 %collective-permute-start.16 = (f32[112,384]{1,0:T(8,128)}, f32[112,384]{1,0:T(8,128)S(1)}, u32[]{:S(2)}, u32[]{:S(2)}) collective-permute-start(f32[112,384]{1,0:T(8,128)} %add_parts.2.refs_1_), channel_id=1, source_target_pairs={{0,8},{1,9},{2,10},{3,11},{4,12},{5,13},{6,14},{7,15},{8,0},{9,1},... | collective-permute-start | bytes 516104 | tf_op jit(solution)/shard_map/ppermute | solution.py:1035
  178.7 9.5 %collective-permute-start.23 = (f32[256,384]{1,0:T(8,128)}, f32[256,384]{1,0:T(8,128)S(1)}, u32[]{:S(2)}, u32[]{:S(2)}) collective-permute-start(f32[256,384]{1,0:T(8,128)} %get-tuple-element.172), channel_id=1, source_target_pairs={{0,4},{1,5},{2,6},{3,7},{4,0},{5,1},{6,2},{7,3},{8,12},{9,13},{10,... | collective-permute-start | bytes 1179656 | tf_op jit(solution)/shard_map/ppermute | solution.py:1035
  180.2 10.5 %collective-permute-start.24 = (f32[256,384]{1,0:T(8,128)}, f32[256,384]{1,0:T(8,128)S(1)}, u32[]{:S(2)}, u32[]{:S(2)}) collective-permute-start(f32[256,384]{1,0:T(8,128)} %get-tuple-element.174), channel_id=1, source_target_pairs={{0,2},{1,3},{2,0},{3,1},{4,6},{5,7},{6,4},{7,5},{8,10},{9,11},{10,... | collective-permute-start | bytes 1179656 | tf_op jit(solution)/shard_map/ppermute | solution.py:1035
  184.4 14.0 %collective-permute-start.22 = (f32[224,384]{1,0:T(8,128)}, f32[224,384]{1,0:T(8,128)S(1)}, u32[]{:S(2)}, u32[]{:S(2)}) collective-permute-start(f32[224,384]{1,0:T(8,128)} %get-tuple-element.171.refs_3_), channel_id=1, source_target_pairs={{0,2},{1,3},{2,0},{3,1},{4,6},{5,7},{6,4},{7,5},{8,10},{9,11},{10,... | collective-permute-start | bytes 1032200 | tf_op jit(solution)/shard_map/ppermute | solution.py:1035
  185.1 13.3 %collective-permute-start.21 = (f32[224,384]{1,0:T(8,128)}, f32[224,384]{1,0:T(8,128)S(1)}, u32[]{:S(2)}, u32[]{:S(2)}) collective-permute-start(f32[224,384]{1,0:T(8,128)} %get-tuple-element.170.refs_5_.refs_1_), channel_id=1, source_target_pairs={{0,4},{1,5},{2,6},{3,7},{4,0},{5,1},{6,2},{7,3},{8,12},{9,13},{10,... | collective-permute-start | bytes 1032200 | tf_op jit(solution)/shard_map/ppermute | solution.py:1035
  188.2 2.5 copy-start.25
  193.8 7.9 %collective-permute-start.27 = (f32[128,384]{1,0:T(8,128)}, f32[128,384]{1,0:T(8,128)S(1)}, u32[]{:S(2)}, u32[]{:S(2)}) collective-permute-start(f32[128,384]{1,0:T(8,128)} %get-tuple-element.178), channel_id=1, source_target_pairs={{0,8},{1,9},{2,10},{3,11},{4,12},{5,13},{6,14},{7,15},{8,0},{9,1},... | collective-permute-start | bytes 589832 | tf_op jit(solution)/shard_map/ppermute | solution.py:1035
  196.0 16.4 %collective-permute-start.28 = (f32[128,384]{1,0:T(8,128)}, f32[128,384]{1,0:T(8,128)S(1)}, u32[]{:S(2)}, u32[]{:S(2)}) collective-permute-start(f32[128,384]{1,0:T(8,128)} %get-tuple-element.179), channel_id=1, source_target_pairs={{0,16},{1,17},{2,18},{3,19},{4,20},{5,21},{6,22},{7,23},{8,24},{9,... | collective-permute-start | bytes 589832 | tf_op jit(solution)/shard_map/ppermute | solution.py:1035
  196.1 16.4 %collective-permute-start.29 = (f32[128,384]{1,0:T(8,128)}, f32[128,384]{1,0:T(8,128)S(1)}, u32[]{:S(2)}, u32[]{:S(2)}) collective-permute-start(f32[128,384]{1,0:T(8,128)} %get-tuple-element.180), channel_id=1, source_target_pairs={{0,24},{1,25},{2,26},{3,27},{4,28},{5,29},{6,30},{7,31},{8,16},{9,... | collective-permute-start | bytes 589832 | tf_op jit(solution)/shard_map/ppermute | solution.py:1035
  201.7 10.7 %copy-start.31 = (f32[128,384]{1,0:T(8,128)}, f32[128,384]{1,0:T(8,128)S(1)}, u32[]{:S(2)}) copy-start(f32[128,384]{1,0:T(8,128)S(1)} %collective-permute-done.27.refs_2_) | copy-start | bytes 589828
  213.1 8.2 %copy-start.16 = (f32[2,224,384]{2,1,0:T(8,128)S(1)}, f32[2,224,384]{2,1,0:T(8,128)}, u32[]{:S(2)}) copy-start(f32[2,224,384]{2,1,0:T(8,128)} %get-tuple-element.183.refs_5_.refs_2_) | copy-start | bytes 2064388
  213.1 8.9 %copy-start.17 = (f32[2,224,384]{2,1,0:T(8,128)S(1)}, f32[2,224,384]{2,1,0:T(8,128)}, u32[]{:S(2)}) copy-start(f32[2,224,384]{2,1,0:T(8,128)} %get-tuple-element.185.refs_4_) | copy-start | bytes 2064388
  215.2 7.7 %collective-permute-start.32 = (f32[128,384]{1,0:T(8,128)}, f32[128,384]{1,0:T(8,128)S(1)}, u32[]{:S(2)}, u32[]{:S(2)}) collective-permute-start(f32[128,384]{1,0:T(8,128)} %add_parts.3.refs_1_), channel_id=1, source_target_pairs={{0,24},{1,25},{2,26},{3,27},{4,28},{5,29},{6,30},{7,31},{8,16},{9,... | collective-permute-start | bytes 589832 | tf_op jit(solution)/shard_map/ppermute | solution.py:1035
  216.1 13.4 %collective-permute-start.31 = (f32[128,384]{1,0:T(8,128)}, f32[128,384]{1,0:T(8,128)S(1)}, u32[]{:S(2)}, u32[]{:S(2)}) collective-permute-start(f32[128,384]{1,0:T(8,128)} %add_parts.3.refs_1_), channel_id=1, source_target_pairs={{0,16},{1,17},{2,18},{3,19},{4,20},{5,21},{6,22},{7,23},{8,24},{9,... | collective-permute-start | bytes 589832 | tf_op jit(solution)/shard_map/ppermute | solution.py:1035
  221.4 8.1 %collective-permute-start.30 = (f32[128,384]{1,0:T(8,128)}, f32[128,384]{1,0:T(8,128)S(1)}, u32[]{:S(2)}, u32[]{:S(2)}) collective-permute-start(f32[128,384]{1,0:T(8,128)} %add_parts.3.refs_1_), channel_id=1, source_target_pairs={{0,8},{1,9},{2,10},{3,11},{4,12},{5,13},{6,14},{7,15},{8,0},{9,1},... | collective-permute-start | bytes 589832 | tf_op jit(solution)/shard_map/ppermute | solution.py:1035
  221.4 11.6 %collective-permute-start.25 = (f32[2,224,384]{2,1,0:T(8,128)S(1)}, f32[2,224,384]{2,1,0:T(8,128)S(1)}, u32[]{:S(2)}, u32[]{:S(2)}) collective-permute-start(f32[2,224,384]{2,1,0:T(8,128)S(1)} %copy-done.16), channel_id=1, source_target_pairs={{0,2},{1,3},{2,0},{3,1},{4,6},{5,7},{6,4},{7,5},{8,10},{9,11},{10,... | collective-permute-start | bytes 2064392 | tf_op jit(solution)/shard_map/ppermute | solution.py:1035
  222.0 10.9 %collective-permute-start.26 = (f32[2,224,384]{2,1,0:T(8,128)S(1)}, f32[2,224,384]{2,1,0:T(8,128)S(1)}, u32[]{:S(2)}, u32[]{:S(2)}) collective-permute-start(f32[2,224,384]{2,1,0:T(8,128)S(1)} %copy-done.17), channel_id=1, source_target_pairs={{0,4},{1,5},{2,6},{3,7},{4,0},{5,1},{6,2},{7,3},{8,12},{9,13},{10,... | collective-permute-start | bytes 2064392 | tf_op jit(solution)/shard_map/ppermute | solution.py:1035
  222.9 6.6 %copy-start.34 = (f32[128,384]{1,0:T(8,128)}, f32[128,384]{1,0:T(8,128)S(1)}, u32[]{:S(2)}) copy-start(f32[128,384]{1,0:T(8,128)S(1)} %collective-permute-done.32.refs_4_) | copy-start | bytes 589828
  233.0 16.7 %copy-start.19 = (f32[2,224,384]{2,1,0:T(8,128)}, f32[2,224,384]{2,1,0:T(8,128)S(1)}, u32[]{:S(2)}) copy-start(f32[2,224,384]{2,1,0:T(8,128)S(1)} %collective-permute-done.26.refs_5_) | copy-start | bytes 2064388
  233.0 16.7 %copy-start.18 = (f32[2,224,384]{2,1,0:T(8,128)}, f32[2,224,384]{2,1,0:T(8,128)S(1)}, u32[]{:S(2)}) copy-start(f32[2,224,384]{2,1,0:T(8,128)S(1)} %collective-permute-done.25.refs_3_) | copy-start | bytes 2064388
  233.0 12.2 %collective-permute-start.33 = (f32[2,224,384]{2,1,0:T(8,128)S(1)}, f32[2,224,384]{2,1,0:T(8,128)S(1)}, u32[]{:S(2)}, u32[]{:S(2)}) collective-permute-start(f32[2,224,384]{2,1,0:T(8,128)S(1)} %copy-done.16), channel_id=1, source_target_pairs={{0,1},{1,0},{2,3},{3,2},{4,5},{5,4},{6,7},{7,6},{8,9},{9,8},{10,11... | collective-permute-start | bytes 2064392 | tf_op jit(solution)/shard_map/ppermute | solution.py:1035
  233.1 12.1 %collective-permute-start.36 = (f32[2,224,384]{2,1,0:T(8,128)S(1)}, f32[2,224,384]{2,1,0:T(8,128)S(1)}, u32[]{:S(2)}, u32[]{:S(2)}) collective-permute-start(f32[2,224,384]{2,1,0:T(8,128)S(1)} %collective-permute-done.26.refs_5_), channel_id=1, source_target_pairs={{0,1},{1,0},{2,3},{3,2},{4,5},{5,4},{6,7},{7,6},{8,9},{9,8},{10,11... | collective-permute-start | bytes 2064392 | tf_op jit(solution)/shard_map/ppermute | solution.py:1035
  233.5 11.3 %collective-permute-start.37 = (f32[256,384]{1,0:T(8,128)}, f32[256,384]{1,0:T(8,128)S(1)}, u32[]{:S(2)}, u32[]{:S(2)}) collective-permute-start(f32[256,384]{1,0:T(8,128)} %get-tuple-element.192.refs_1_), channel_id=1, source_target_pairs={{0,4},{1,5},{2,6},{3,7},{4,0},{5,1},{6,2},{7,3},{8,12},{9,13},{10,... | collective-permute-start | bytes 1179656 | tf_op jit(solution)/shard_map/ppermute | solution.py:1035
  234.1 11.0 %collective-permute-start.38 = (f32[256,384]{1,0:T(8,128)}, f32[256,384]{1,0:T(8,128)S(1)}, u32[]{:S(2)}, u32[]{:S(2)}) collective-permute-start(f32[256,384]{1,0:T(8,128)} %get-tuple-element.193.refs_3_), channel_id=1, source_target_pairs={{0,2},{1,3},{2,0},{3,1},{4,6},{5,7},{6,4},{7,5},{8,10},{9,11},{10,... | collective-permute-start | bytes 1179656 | tf_op jit(solution)/shard_map/ppermute | solution.py:1035
  235.5 17.0 %collective-permute-start.34 = (f32[2,224,384]{2,1,0:T(8,128)S(1)}, f32[2,224,384]{2,1,0:T(8,128)}, u32[]{:S(2)}, u32[]{:S(2)}) collective-permute-start(f32[2,224,384]{2,1,0:T(8,128)S(1)} %collective-permute-done.25.refs_3_), channel_id=1, source_target_pairs={{0,1},{1,0},{2,3},{3,2},{4,5},{5,4},{6,7},{7,6},{8,9},{9,8},{10,11... | collective-permute-start | bytes 2064392 | tf_op jit(solution)/shard_map/ppermute | solution.py:1035
  244.9 7.6 %collective-permute-start.35 = (f32[2,224,384]{2,1,0:T(8,128)S(1)}, f32[2,224,384]{2,1,0:T(8,128)}, u32[]{:S(2)}, u32[]{:S(2)}) collective-permute-start(f32[2,224,384]{2,1,0:T(8,128)S(1)} %copy-done.17), channel_id=1, source_target_pairs={{0,1},{1,0},{2,3},{3,2},{4,5},{5,4},{6,7},{7,6},{8,9},{9,8},{10,11... | collective-permute-start | bytes 2064392 | tf_op jit(solution)/shard_map/ppermute | solution.py:1035
  249.7 21.0 %collective-permute-start.39 = (f32[2,256,384]{2,1,0:T(8,128)}, f32[2,256,384]{2,1,0:T(8,128)S(1)}, u32[]{:S(2)}, u32[]{:S(2)}) collective-permute-start(f32[2,256,384]{2,1,0:T(8,128)} %get-tuple-element.195.refs_3_), channel_id=1, source_target_pairs={{0,2},{1,3},{2,0},{3,1},{4,6},{5,7},{6,4},{7,5},{8,10},{9,11},{10,... | collective-permute-start | bytes 2359304 | tf_op jit(solution)/shard_map/ppermute | solution.py:1035
  251.0 19.6 %collective-permute-start.40 = (f32[2,256,384]{2,1,0:T(8,128)}, f32[2,256,384]{2,1,0:T(8,128)S(1)}, u32[]{:S(2)}, u32[]{:S(2)}) collective-permute-start(f32[2,256,384]{2,1,0:T(8,128)} %get-tuple-element.198.refs_5_), channel_id=1, source_target_pairs={{0,4},{1,5},{2,6},{3,7},{4,0},{5,1},{6,2},{7,3},{8,12},{9,13},{10,... | collective-permute-start | bytes 2359304 | tf_op jit(solution)/shard_map/ppermute | solution.py:1035
  259.5 5.1 %copy-start.6 = (f32[2,256,384]{2,1,0:T(8,128)S(1)}, f32[2,256,384]{2,1,0:T(8,128)}, u32[]{:S(2)}) copy-start(f32[2,256,384]{2,1,0:T(8,128)} %get-tuple-element.195.refs_3_) | copy-start | bytes 2359300
  259.5 5.1 %copy-start.7 = (f32[2,256,384]{2,1,0:T(8,128)S(1)}, f32[2,256,384]{2,1,0:T(8,128)}, u32[]{:S(2)}) copy-start(f32[2,256,384]{2,1,0:T(8,128)} %get-tuple-element.198.refs_5_) | copy-start | bytes 2359300
  259.5 11.8 %copy-start.2 = (f32[8,128]{1,0:T(8,128)S(1)}, f32[8,128]{1,0:T(8,128)}, u32[]{:S(2)}) copy-start(f32[8,128]{1,0:T(8,128)} %get-tuple-element.212) | copy-start | bytes 12292
  259.5 12.3 %copy-start = (f32[192,192]{1,0:T(8,128)S(1)}, f32[192,192]{1,0:T(8,128)}, u32[]{:S(2)}) copy-start(f32[192,192]{1,0:T(8,128)} %get-tuple-element.217) | copy-start | bytes 442372
  264.6 7.9 %collective-permute-start.41 = (f32[2,256,384]{2,1,0:T(8,128)S(1)}, f32[2,256,384]{2,1,0:T(8,128)S(1)}, u32[]{:S(2)}, u32[]{:S(2)}) collective-permute-start(f32[2,256,384]{2,1,0:T(8,128)S(1)} %copy-done.6), channel_id=1, source_target_pairs={{0,1},{1,0},{2,3},{3,2},{4,5},{5,4},{6,7},{7,6},{8,9},{9,8},{10,11... | collective-permute-start | bytes 2359304 | tf_op jit(solution)/shard_map/ppermute | solution.py:1035
  264.6 7.9 %collective-permute-start.43 = (f32[2,256,384]{2,1,0:T(8,128)S(1)}, f32[2,256,384]{2,1,0:T(8,128)S(1)}, u32[]{:S(2)}, u32[]{:S(2)}) collective-permute-start(f32[2,256,384]{2,1,0:T(8,128)S(1)} %copy-done.7), channel_id=1, source_target_pairs={{0,1},{1,0},{2,3},{3,2},{4,5},{5,4},{6,7},{7,6},{8,9},{9,8},{10,11... | collective-permute-start | bytes 2359304 | tf_op jit(solution)/shard_map/ppermute | solution.py:1035
  270.6 4.4 %copy-start.9 = (f32[2,256,384]{2,1,0:T(8,128)}, f32[2,256,384]{2,1,0:T(8,128)S(1)}, u32[]{:S(2)}) copy-start(f32[2,256,384]{2,1,0:T(8,128)S(1)} %collective-permute-done.40.refs_6_) | copy-start | bytes 2359300
  270.6 4.4 %copy-start.8 = (f32[2,256,384]{2,1,0:T(8,128)}, f32[2,256,384]{2,1,0:T(8,128)S(1)}, u32[]{:S(2)}) copy-start(f32[2,256,384]{2,1,0:T(8,128)S(1)} %collective-permute-done.39.refs_4_) | copy-start | bytes 2359300
  270.6 2.3 collective-permute-start.42
  270.7 3.4 %collective-permute-start.44 = (f32[2,256,384]{2,1,0:T(8,128)S(1)}, f32[2,256,384]{2,1,0:T(8,128)S(1)}, u32[]{:S(2)}, u32[]{:S(2)}) collective-permute-start(f32[2,256,384]{2,1,0:T(8,128)S(1)} %collective-permute-done.40.refs_6_), channel_id=1, source_target_pairs={{0,1},{1,0},{2,3},{3,2},{4,5},{5,4},{6,7},{7,6},{8,9},{9,8},{10,11... | collective-permute-start | bytes 2359304 | tf_op jit(solution)/shard_map/ppermute | solution.py:1035
  272.5 2.5 copy-start.10
  272.5 2.5 copy-start.11
  273.0 2.0 copy-start.14
  (24 other events, 21.1 us)

commit v5 on v4

--- a/solution.py
+++ b/solution.py
@@ -26,6 +26,7 @@
 BF16 = jnp.bfloat16
 HIGH = lax.Precision.HIGHEST
 VMEM_BYTES = 58 * 1024 * 1024
+VMEM_WHOLE = 64 * 1024 * 1024
 WIDE = 384
 UNIT = 1152
 REST = 640
@@ -93,7 +94,7 @@
     return jax.ShapeDtypeStruct(shape, dtype)
 
 
-def run(body, grid, ins, in_specs, outs, out_specs, scratch=(), micros=5, after=(), aliases=None, name=None):
+def run(body, grid, ins, in_specs, outs, out_specs, scratch=(), micros=5, after=(), aliases=None, name=None, vmem=VMEM_BYTES):
     count, extra = len(ins), len(after)
 
     def wrapped(*refs):
@@ -106,7 +107,7 @@
         out_specs=out_specs,
         out_shape=outs,
         scratch_shapes=list(scratch),
-        compiler_params=pltpu.CompilerParams(vmem_limit_bytes=VMEM_BYTES),
+        compiler_params=pltpu.CompilerParams(vmem_limit_bytes=vmem),
         cost_estimate=pl.CostEstimate(
             flops=int(micros * COST), bytes_accessed=1 << 20, transcendentals=0
         ),
@@ -773,6 +774,7 @@
         pltpu.make_async_copy(expand_low_ref, low, sems.at[1]),
     ]
     write = pltpu.make_async_copy(flow, flow_ref, sems.at[2])
+    ngrad_write = pltpu.make_async_copy(normal, ngrad_ref, sems.at[5 + 2 * WLAYERS])
     mine = place_ref[0] & 1
 
     def deal(source, rows_each, targets, begin, first_sem):
@@ -975,7 +977,7 @@
             )
             normal_grad = dot_three(turned_grad, mixm_ref[...], back=True)
             normal_grad = jnp.where(inside_item(item), normal_grad, 0.0)
-            ngrad_ref[item] = normal_grad
+            normal[item] = normal_grad
             one_sum = jnp.sum(normal_grad, axis=0, keepdims=True)
             two_sum = jnp.sum(normal_grad * normalized, axis=0, keepdims=True)
             for at, found in ((0, one_sum), (2, two_sum)):
@@ -983,6 +985,7 @@
                 sums[at + 1 : at + 2, :] = sums[at + 1 : at + 2, :] + found[:, LANES:]
 
         each(one)
+        ngrad_write.start()
         tail[...] = jnp.zeros_like(tail)
         cut = MEL // 2
         tail[:cut, :] = jnp.concatenate([start_acc[:cut, :], start_acc[cut:MEL, :]], axis=1)
@@ -1000,7 +1003,7 @@
         tail[cut : cut + 8, LANES : 2 * LANES] = sums[...]
         for copy in last_deal:
             copy.start()
-        for copy in (*last_deal, *deals[0], *deals[1], write):
+        for copy in (*last_deal, *deals[0], *deals[1], write, ngrad_write):
             copy.wait()
 
 
@@ -1054,21 +1057,108 @@
 
 
 def call_whole(body, place, ins, outs, scratch, after, micros, name):
+    count, given = len(ins), len(outs)
+
+    def wrapped(place_ref, *refs):
+        sources, targets = refs[:count], refs[count : count + given]
+        held, sems = refs[count + given : 2 * count + given], refs[-1]
+        copies = [
+            pltpu.make_async_copy(source, target, sems.at[i])
+            for i, (source, target) in enumerate(zip(sources, held))
+        ]
+        for copy in copies:
+            copy.start()
+        for copy in copies:
+            copy.wait()
+        body(place_ref, *held, *targets, *refs[2 * count + given : -1])
+
+    return run(
+        wrapped,
+        (),
+        [place, *ins],
+        [pl.BlockSpec(memory_space=pltpu.SMEM)] + [pl.BlockSpec(memory_space=pl.ANY)] * count,
+        outs,
+        whole_vmem(given),
+        [pltpu.VMEM(array.shape, array.dtype) for array in ins]
+        + list(scratch)
+        + [pltpu.SemaphoreType.DMA((count,))],
+        micros=micros,
+        after=after,
+        name=name,
+        vmem=VMEM_WHOLE,
+    )
+
+
+def call_parts(plan, place, ins, outs, after, name):
+    count, given = len(ins), len(outs)
+    layers = 1 + max(
+        layer for _, pieces in plan(None) for layer in (piece[4] for piece in pieces)
+    )
+    pieces_all = sum(len(pieces) for _, pieces in plan(None))
+
+    def body(place_ref, *refs):
+        sources, targets = refs[:count], refs[count : count + given]
+        held = refs[count + given : count + 2 * given]
+        in_sems, out_sems = refs[-2:]
+        todo = []
+        at = 0
+        for out, pieces in plan(place_ref):
+            copies = []
+            for source, begin, rows, spot, layer in pieces:
+                copies.append(
+                    pltpu.make_async_copy(
+                        sources[source].at[pl.ds(pl.multiple_of(begin, 8), rows), :],
+                        held[out].at[(layer, *spot[:-1], pl.ds(spot[-1], rows))],
+                        in_sems.at[at],
+                    )
+                )
+                copies[-1].start()
+                at += 1
+            todo.append((out, copies))
+        writes = []
+        for out, copies in todo:
+            for copy in copies:
+                copy.wait()
+            value = held[out][0]
+            for layer in range(1, layers):
+                value = value + held[out][layer]
+            held[out][0] = value
+            writes.append(pltpu.make_async_copy(held[out].at[0], targets[out], out_sems.at[out]))
+            writes[-1].start()
+        for write in writes:
+            write.wait()
+
+    anywhere = pl.BlockSpec(memory_space=pl.ANY)
     return run(
         body,
         (),
         [place, *ins],
-        [pl.BlockSpec(memory_space=pltpu.SMEM)] + whole_vmem(len(ins)),
+        [pl.BlockSpec(memory_space=pltpu.SMEM)] + [anywhere] * count,
         outs,
-        whole_vmem(len(outs)),
-        scratch,
-        micros=micros,
+        [anywhere] * given,
+        [pltpu.VMEM((layers, *out.shape), F32) for out in outs]
+        + [pltpu.SemaphoreType.DMA((pieces_all,)), pltpu.SemaphoreType.DMA((given,))],
+        micros=25,
         after=after,
         name=name,
+        vmem=VMEM_WHOLE,
     )
 
 
 def hop_out(jobs, place, after=()):
+    units, shift, radix = jobs[0]
+    row = units[0][0].shape[0] // radix
+    if len(jobs) == 1 and len(units) == 1 and row % 8 == 0:
+        arrays = units[0]
+
+        def by_parts(place_ref):
+            digit = 0 if place_ref is None else (place_ref[0] >> shift) & (radix - 1)
+            return [
+                (step, [(k, (digit ^ step) * row, row, (0,), k) for k in range(len(arrays))])
+                for step in (*range(1, radix), 0)
+            ]
+
+        return [call_parts(by_parts, place, arrays, [shape_of((row, WIDE))] * radix, after, "hop_out")]
     ins = []
     outs = []
     scratch = []
@@ -1182,25 +1272,27 @@
     rows = [unit[0].shape[0] // 8 for unit in units]
     total = sum(rows)
 
-    def body(place_ref, *refs):
-        low, high = first_bits(place_ref)
-        outs = refs[len(ins) :]
-        at = 0
-        begin = 0
-        for unit, row in zip(units, rows):
-            for out, half, mine in ((0, 0, low), (1, 0, 1 - low), (2, 1, high), (3, 1, 1 - high)):
-                for other in range(2):
-                    digit = mine + 2 * other if half == 0 else other + 2 * mine
-                    span = pl.ds(pl.multiple_of((2 * digit + half) * row, 8), row)
-                    value = refs[at][span, :]
-                    for extra in range(1, len(unit)):
-                        value = value + refs[at + extra][span, :]
-                    outs[out][other, begin : begin + row, :] = value
-            at += len(unit)
-            begin += row
+    def by_parts(place_ref):
+        low, high = (0, 0) if place_ref is None else first_bits(place_ref)
+        found = []
+        for out, half, mine in ((1, 0, 1 - low), (3, 1, 1 - high), (0, 0, low), (2, 1, high)):
+            pieces = []
+            for other in range(2):
+                digit = mine + 2 * other if half == 0 else other + 2 * mine
+                at = 0
+                begin = 0
+                for unit, row in zip(units, rows):
+                    for layer in range(len(unit)):
+                        pieces.append(
+                            (at + layer, (2 * digit + half) * row, row, (other, begin), layer)
+                        )
+                    at += len(unit)
+                    begin += row
+            found.append((out, pieces))
+        return found
 
     outs = [shape_of((2, total, WIDE))] * 4
-    found = call_whole(body, place, ins, outs, (), after, 25, "pair_out")
+    found = call_parts(by_parts, place, ins, outs, after, "pair_out")
     return pair_send((found[:2], found[2:]), 2, 4, devices)
 
 
@@ -1387,6 +1479,7 @@
         micros=5,
         after=after,
         name="unpack_upper",
+        vmem=VMEM_WHOLE,
     )
 
 
@@ -1500,6 +1593,7 @@
         micros=5,
         aliases={1: 0, 2: 1},
         name="unpack_lower",
+        vmem=VMEM_WHOLE,
     )
 
 
@@ -1671,7 +1765,7 @@
         shape_of((items, pairs, 4 * LANES), BF16),
         shape_of((items, pairs, 2 * LANES)),
     ]
-    out_specs = [pl.BlockSpec(memory_space=pl.ANY)] * 5 + [full_spec(outs[5])]
+    out_specs = [pl.BlockSpec(memory_space=pl.ANY)] * 6
     count = items * pairs
     kept, sent, last_kept, last_sent, flow, normal_grad = run(
         decoder_body,
@@ -1704,7 +1798,7 @@
             pltpu.VMEM(expand.shape, BF16),
             pltpu.VMEM((items, pairs, 4 * LANES), BF16),
             pltpu.VMEM((8, LANES), F32),
-            pltpu.SemaphoreType.DMA((5 + 2 * WLAYERS,)),
+            pltpu.SemaphoreType.DMA((6 + 2 * WLAYERS,)),
         ],
         micros=80,
         name="decoder",

time: 282 us -> 276 us (0.979)
  local copies, waits for them, and re-layouts: 14.1 us -> 4.88 us
  waiting for transfers between devices: 58.9 us -> 63.9 us
    unnamed x86 -> x18, local copies, waits for them, and re-layouts: 12.8 us -> 3.62 us
    ppermute x45, waiting for transfers between devices: 58.9 us -> 63.9 us  [swap(): return lax.ppermute(values, 'dp', [(i, i ^ bit) for i in range(devices)])]
  transfers between devices with their start and end apart: 45 -> 45, of which waited for: 19 -> 18; matrix products, arithmetic and copies ran while one was open for 0% -> 0% of each run, Pallas kernels for 31% -> 32%
where the time goes in v5:
time: 276 us
  Pallas kernels  158 us (57%)
  waiting for transfers between devices  63.9 us (23%)
  starting transfers between devices  46.4 us (17%)
  local copies, waits for them, and re-layouts  4.88 us (2%)
    pallas_call x19, Pallas kernels, run(): pl.pallas_call(wrapped, grid=grid, in_specs=list(in_specs) + [pl.BlockSpe...  158 us
    ppermute x45, waiting for transfers between devices, swap(): return lax.ppermute(values, 'dp', [(i, i ^ bit) for i in range(devices)])  63.9 us
    ppermute x45, starting transfers between devices, swap(): return lax.ppermute(values, 'dp', [(i, i ^ bit) for i in range(devices)])  46.4 us
  transfers between devices with their start and end apart: 45, of which 18 were waited for; matrix products, arithmetic and copies ran while one was open for 0% of the time, Pallas kernels for 32%

profile of v5, /device:TPU:0, one launch (start us, length us, event | category | flops | bytes accessed | tf_op | source)
XLA Modules:
  0.0 275.6 jit_solution(10690820609114821079)
XLA Ops:
  0.7 2.4 stats.1.refs_10_
  3.0 2.4 collective-permute-start.2
  6.1 0.9 collective-permute-done.2
  6.9 2.3 collective-permute-done.1
  9.2 0.7 add_add_fusion.1.refs_14_
  9.9 2.5 collective-permute-start.5
  13.4 3.4 %weights.1 = (f32[256,256]{1,0:T(8,128)}, f32[8,128]{1,0:T(8,128)}, bf16[192,768]{1,0:T(8,128)(2,1)}, bf16[128,128]{1,0:T(8,128)(2,1)}, bf16[128,128]{1,0:T(8,12...) custom-call(f32[4,4]{1,0:T(4,128)} %refs_0_.3, ...), custom_call_target="tpu_custom_call" | custom-call | flops 5750000128 | bytes 1048576 | tf_op jit(solution)/shard_map/weights/pallas_call | solution.py:103
  16.8 2.7 collective-permute-start.6
  19.5 16.4 %encoder.1 = (bf16[4,256,192]{2,1,0:T(8,128)(2,1)}, bf16[4,256,768]{2,1,0:T(8,128)(2,1)}, bf16[4,2,256,256]{3,2,1,0:T(8,128)(2,1)}, bf16[4,2,256,128]{3,2,1,0:T(...) custom-call(s32[4,256]{1,0:T(4,128)} %refs_0_.5, ...), custom_call_target="tpu_custom_call" | custom-call | flops 23000000512 | bytes 1048576 | tf_op jit(solution)/shard_map/encoder/pallas_call | solution.py:103
  36.4 59.0 %decoder.1 = (f32[1792,384]{1,0:T(8,128)}, f32[1792,384]{1,0:T(8,128)}, f32[576,384]{1,0:T(8,128)}, f32[576,384]{1,0:T(8,128)}, bf16[4,512,512]{2,1,0:T(8,128)(2,1)}, /*index=5*/f32[4,512,256]{2,1,0:T(8,128)}) custom-call(f32[4,80,1024]{2,1,0:T(8,128)} %bitcast.16, s32[4,256]{1,0:T(4,128)} %refs_1_.11, bf16[4,512,512]{2,1,0:T(8,128)(2,1)} %get-tuple-element.124.refs_2_, ...), custom_call_target="tpu_custom_call" | custom-call | flops 92000002048 | bytes 1048576 | tf_op jit(solution)/shard_map/decoder/pallas_call | solution.py:103
  96.1 4.9 %collective-permute-done.7.refs_2_ = f32[1792,384]{1,0:T(8,128)} collective-permute-done((f32[1792,384]{1,0:T(8,128)}, f32[1792,384]{1,0:T(8,128)}, u32[]{:S(2)}, u32[]{:S(2)}) %collective-permute-start.7) | collective-permute-done | bytes 2752544 | tf_op jit(solution)/shard_map/ppermute | solution.py:1038
  101.0 4.1 %hop_out.2 = (f32[448,384]{1,0:T(8,128)}, f32[448,384]{1,0:T(8,128)}, f32[448,384]{1,0:T(8,128)}, f32[448,384]{1,0:T(8,128)}) custom-call(s32[1]{0:T(128)} %bitcast.8.refs_10_.refs_0_.refs_24_, f32[1792,384]{1,0:T(8,128)} %get-tuple-element.132.refs_1_, f32[1792,384]{1,0:T(8,128)} %collective-permute-done.7.refs_2_), custom_call_target="tpu_custom_call" | custom-call | flops 28750000128 | bytes 1048576 | tf_op jit(solution)/shard_map/hop_out/pallas_call | solution.py:103
  105.1 0.7 collective-permute-start.8
  105.7 1.5 collective-permute-start.9
  107.3 1.4 collective-permute-start.10
  108.6 27.9 %encoder_back.1 = (f32[1472,384]{1,0:T(8,128)}, f32[1472,384]{1,0:T(8,128)}) custom-call(s32[4,256]{1,0:T(4,128)} %refs_0_.5, s32[4,256]{1,0:T(4,128)} %refs_1_.11, bf16[4,512,512]{2,1,0:T(8,128)(2,1)} %get-tuple-element.138.refs_2_, bf16[4,256,192]{2,1,0:T(8,128)(2,1)} %get-tuple-element.139.refs_3_, f32[4,256,192]{2,1,0:T(8,128)} %get-tuple-element.140.refs_4_, ...), custom_call_target="tpu_custom_call" | custom-call | flops 34500001792 | bytes 1048576 | tf_op jit(solution)/shard_map/encoder_back/pallas_call | solution.py:103
  137.1 1.6 collective-permute-done.10.refs_4_
  138.6 2.7 hop_out.3
  141.4 1.6 collective-permute-start.11
  143.3 2.5 collective-permute-start.13
  145.8 4.8 %pair_out.1 = (f32[2,256,384]{2,1,0:T(8,128)}, f32[2,256,384]{2,1,0:T(8,128)}, f32[2,256,384]{2,1,0:T(8,128)}, f32[2,256,384]{2,1,0:T(8,128)}) custom-call(s32[1]{0:T(128)} %bitcast.8.refs_10_.refs_0_.refs_24_, f32[576,384]{1,0:T(8,128)} %get-tuple-element.162.refs_1_, f32[576,384]{1,0:T(8,128)} %collective-permute-done.14.refs_2_, ...), custom_call_target="tpu_custom_call" | custom-call | flops 28750000128 | bytes 1048576 | tf_op jit(solution)/shard_map/pair_out/pallas_call | solution.py:103
  150.6 0.8 collective-permute-start.19
  151.4 1.5 collective-permute-start.20
  153.0 5.8 %collective-permute-done.12.refs_3_ = f32[112,384]{1,0:T(8,128)} collective-permute-done((f32[112,384]{1,0:T(8,128)}, f32[112,384]{1,0:T(8,128)}, u32[]{:S(2)}, u32[]{:S(2)}) %collective-permute-start.12) | collective-permute-done | bytes 172064 | tf_op jit(solution)/shard_map/ppermute | solution.py:1038
  158.8 1.9 add_parts.2.refs_1_
  160.7 0.6 collective-permute-start.18
  161.3 4.4 %collective-permute-start.17 = (f32[112,384]{1,0:T(8,128)}, f32[112,384]{1,0:T(8,128)}, u32[]{:S(2)}, u32[]{:S(2)}) collective-permute-start(f32[112,384]{1,0:T(8,128)} %add_parts.2.refs_1_), channel_id=1, source_target_pairs={{0,16},{1,17},{2,18},{3,19},{4,20},{5,21},{6,22},{7,23},{8,24},{9,... | collective-permute-start | bytes 516104 | tf_op jit(solution)/shard_map/ppermute | solution.py:1038
  165.8 4.3 %collective-permute-done.19.refs_2_ = f32[2,256,384]{2,1,0:T(8,128)} collective-permute-done((f32[2,256,384]{2,1,0:T(8,128)}, f32[2,256,384]{2,1,0:T(8,128)}, u32[]{:S(2)}, u32[]{:S(2)}) %collective-permute-start.19) | collective-permute-done | bytes 786464 | tf_op jit(solution)/shard_map/ppermute | solution.py:1038
  170.6 3.2 %pair_next.1 = (f32[256,384]{1,0:T(8,128)}, f32[256,384]{1,0:T(8,128)}, f32[256,384]{1,0:T(8,128)}, f32[256,384]{1,0:T(8,128)}) custom-call(s32[1]{0:T(128)} %bitcast.8.refs_10_.refs_0_.refs_24_, f32[2,256,384]{2,1,0:T(8,128)} %get-tuple-element.165.refs_5_.refs_1_, f32[2,256,384]{2,1,0:T(8,128)} %collective-permute-done.19.refs_2_, ...), custom_call_target="tpu_custom_call" | custom-call | flops 28750000128 | bytes 1048576 | tf_op jit(solution)/shard_map/pair_next/pallas_call | solution.py:103
  173.8 1.6 collective-permute-start.23
  176.0 3.0 %collective-permute-done.17.refs_3_ = f32[112,384]{1,0:T(8,128)} collective-permute-done((f32[112,384]{1,0:T(8,128)}, f32[112,384]{1,0:T(8,128)}, u32[]{:S(2)}, u32[]{:S(2)}) %collective-permute-start.17) | collective-permute-done | bytes 172064 | tf_op jit(solution)/shard_map/ppermute | solution.py:1038
  179.0 2.1 gather_pair.2
  181.1 0.9 collective-permute-start.22
  182.0 1.5 collective-permute-start.21
  183.6 2.4 collective-permute-done.24.refs_4_
  186.1 2.4 pair_level.1
  188.4 2.3 collective-permute-start.27
  190.7 2.4 collective-permute-start.29
  193.2 2.5 pair_join.2
  195.6 2.2 collective-permute-done.27.refs_2_
  197.8 7.9 %collective-permute-done.28.refs_3_ = f32[128,384]{1,0:T(8,128)} collective-permute-done((f32[128,384]{1,0:T(8,128)}, f32[128,384]{1,0:T(8,128)}, u32[]{:S(2)}, u32[]{:S(2)}) %collective-permute-start.28) | collective-permute-done | bytes 196640 | tf_op jit(solution)/shard_map/ppermute | solution.py:1038
  205.8 2.0 add_parts.3.refs_1_
  207.7 1.5 collective-permute-start.32
  209.2 2.7 collective-permute-start.31
  212.8 1.1 collective-permute-start.26
  213.9 3.7 %collective-permute-done.32.refs_4_ = f32[128,384]{1,0:T(8,128)} collective-permute-done((f32[128,384]{1,0:T(8,128)}, f32[128,384]{1,0:T(8,128)}, u32[]{:S(2)}, u32[]{:S(2)}) %collective-permute-start.32) | collective-permute-done | bytes 196640 | tf_op jit(solution)/shard_map/ppermute | solution.py:1038
  217.6 7.7 %collective-permute-done.31.refs_3_ = f32[128,384]{1,0:T(8,128)} collective-permute-done((f32[128,384]{1,0:T(8,128)}, f32[128,384]{1,0:T(8,128)}, u32[]{:S(2)}, u32[]{:S(2)}) %collective-permute-start.31) | collective-permute-done | bytes 196640 | tf_op jit(solution)/shard_map/ppermute | solution.py:1038
  225.4 2.2 gather_pair.3
  228.2 1.1 collective-permute-start.37
  229.3 0.8 collective-permute-start.38
  230.1 9.5 %collective-permute-done.37.refs_2_ = f32[256,384]{1,0:T(8,128)} collective-permute-done((f32[256,384]{1,0:T(8,128)}, f32[256,384]{1,0:T(8,128)}, u32[]{:S(2)}, u32[]{:S(2)}) %collective-permute-start.37) | collective-permute-done | bytes 393248 | tf_op jit(solution)/shard_map/ppermute | solution.py:1038
  239.6 0.7 collective-permute-done.38.refs_4_
  240.3 2.6 pair_join.3
  243.0 1.0 collective-permute-start.39
  243.9 1.3 collective-permute-start.40
  245.2 7.0 %unpack_upper.1 = (f32[4,960,384]{2,1,0:T(8,128)}, f32[3,192,384]{2,1,0:T(8,128)}, f32[192,192]{1,0:T(8,128)}, f32[192,192]{1,0:T(8,128)}, f32[80,192]{1,0:T(8,1...) custom-call(s32[1]{0:T(128)} %bitcast.8.refs_10_.refs_0_.refs_24_, f32[8,128]{1,0:T(8,128)} %get-tuple-element.131.refs_1_.refs_5_, ...), custom_call_target="tpu_custom_call" | custom-call | flops 5750000128 | bytes 1048576 | tf_op jit(solution)/shard_map/unpack_upper/pallas_call | solution.py:103
  252.3 5.1 %frames.1 = (f32[4,80,1024]{2,1,0:T(8,128)}, f32[1,1]{1,0:T(1,128)}) custom-call(f32[4,80,1024]{2,1,0:T(8,128)} %bitcast.17, s32[4,256]{1,0:T(4,128)} %refs_1_.11, f32[4,512,256]{2,1,0:T(8,128)} %get-tuple-element.130.refs_2_, f32[8,128]{1,0:T(8,128)} %add.27.refs_4_.refs_3_, f32[8,128]{1,0:T(8,128)} %get-tuple-element.187.refs_4_, ...), custom_call_target="tpu_custom_call" | custom-call | flops 5750000128 | bytes 1048576 | tf_op jit(solution)/shard_map/frames/pallas_call | solution.py:103
  257.9 5.6 %collective-permute-done.40.refs_6_ = f32[2,256,384]{2,1,0:T(8,128)} collective-permute-done((f32[2,256,384]{2,1,0:T(8,128)}, f32[2,256,384]{2,1,0:T(8,128)}, u32[]{:S(2)}, u32[]{:S(2)}) %collective-permute-start.40) | collective-permute-done | bytes 786464 | tf_op jit(solution)/shard_map/ppermute | solution.py:1038
  264.5 0.7 slice_bitcast_fusion
  265.2 0.9 copy-done.5
  266.1 0.9 copy-done.6
  267.1 0.9 copy-done.7
  267.9 0.9 copy-done.8
  268.9 6.5 %unpack_lower.1 = (f32[4,960,384]{2,1,0:T(8,128)}, f32[3,192,384]{2,1,0:T(8,128)}, f32[576,768]{1,0:T(8,128)}, f32[192,2304]{1,0:T(8,128)}, f32[148,192]{1,0:T(8...) custom-call(s32[1]{0:T(128)} %bitcast.8.refs_10_.refs_0_.refs_24_, ...), custom_call_target="tpu_custom_call", output_to_operand_aliasing={{0}: (1, {}), {1}: (2, {})} | custom-call | flops 5750000128 | bytes 1048576 | tf_op jit(solution)/shard_map/unpack_lower/pallas_call | solution.py:103
  (68 shorter events, 8.1 us)
Async XLA Ops:
  3.0 3.9 %collective-permute-start.2 = (f32[8,128]{1,0:T(8,128)}, f32[8,128]{1,0:T(8,128)S(1)}, u32[]{:S(2)}, u32[]{:S(2)}) collective-permute-start(f32[8,128]{1,0:T(8,128)} %stats.1.refs_10_), channel_id=1, source_target_pairs={{0,3},{1,2},{2,1},{3,0},{4,7},{5,6},{6,5},{7,4},{8,11},{9,10},{10,... | collective-permute-start | bytes 12296 | tf_op jit(solution)/shard_map/ppermute | solution.py:1038
  5.4 3.8 %collective-permute-start.1 = (f32[8,128]{1,0:T(8,128)}, f32[8,128]{1,0:T(8,128)S(1)}, u32[]{:S(2)}, u32[]{:S(2)}) collective-permute-start(f32[8,128]{1,0:T(8,128)} %stats.1.refs_10_), channel_id=1, source_target_pairs={{0,2},{1,3},{2,0},{3,1},{4,6},{5,7},{6,4},{7,5},{8,10},{9,11},{10,... | collective-permute-start | bytes 12296 | tf_op jit(solution)/shard_map/ppermute | solution.py:1038
  6.0 3.2 %collective-permute-start = (f32[8,128]{1,0:T(8,128)}, f32[8,128]{1,0:T(8,128)S(1)}, u32[]{:S(2)}, u32[]{:S(2)}) collective-permute-start(f32[8,128]{1,0:T(8,128)} %stats.1.refs_10_), channel_id=1, source_target_pairs={{0,1},{1,0},{2,3},{3,2},{4,5},{5,4},{6,7},{7,6},{8,9},{9,8},{10,11... | collective-permute-start | bytes 12296 | tf_op jit(solution)/shard_map/ppermute | solution.py:1038
  9.9 6.9 %copy-start.1 = (f32[8,128]{1,0:T(8,128)}, f32[8,128]{1,0:T(8,128)S(1)}, u32[]{:S(2)}) copy-start(f32[8,128]{1,0:T(8,128)S(1)} %add_add_fusion.1.refs_14_) | copy-start | bytes 12292
  9.9 6.9 %collective-permute-start.5 = (f32[8,128]{1,0:T(8,128)S(1)}, f32[8,128]{1,0:T(8,128)S(1)}, u32[]{:S(2)}, u32[]{:S(2)}) collective-permute-start(f32[8,128]{1,0:T(8,128)S(1)} %add_add_fusion.1.refs_14_), channel_id=1, source_target_pairs={{0,12},{1,13},{2,14},{3,15},{4,8},{5,9},{6,10},{7,11},{8,4},{9,5},... | collective-permute-start | bytes 12296 | tf_op jit(solution)/shard_map/ppermute | solution.py:1038
  12.4 4.3 %collective-permute-start.4 = (f32[8,128]{1,0:T(8,128)S(1)}, f32[8,128]{1,0:T(8,128)S(1)}, u32[]{:S(2)}, u32[]{:S(2)}) collective-permute-start(f32[8,128]{1,0:T(8,128)S(1)} %add_add_fusion.1.refs_14_), channel_id=1, source_target_pairs={{0,8},{1,9},{2,10},{3,11},{4,12},{5,13},{6,14},{7,15},{8,0},{9,1},... | collective-permute-start | bytes 12296 | tf_op jit(solution)/shard_map/ppermute | solution.py:1038
  12.9 3.9 %collective-permute-start.3 = (f32[8,128]{1,0:T(8,128)S(1)}, f32[8,128]{1,0:T(8,128)S(1)}, u32[]{:S(2)}, u32[]{:S(2)}) collective-permute-start(f32[8,128]{1,0:T(8,128)S(1)} %add_add_fusion.1.refs_14_), channel_id=1, source_target_pairs={{0,4},{1,5},{2,6},{3,7},{4,0},{5,1},{6,2},{7,3},{8,12},{9,13},{10,... | collective-permute-start | bytes 12296 | tf_op jit(solution)/shard_map/ppermute | solution.py:1038
  16.8 19.0 %collective-permute-start.6 = (f32[8,128]{1,0:T(8,128)S(1)}, f32[8,128]{1,0:T(8,128)S(1)}, u32[]{:S(2)}, u32[]{:S(2)}) collective-permute-start(f32[8,128]{1,0:T(8,128)S(1)} %add_add_fusion), channel_id=1, source_target_pairs={{0,16},{1,17},{2,18},{3,19},{4,20},{5,21},{6,22},{7,23},{8,24},{9,... | collective-permute-start | bytes 12296 | tf_op jit(solution)/shard_map/ppermute | solution.py:1038
  95.5 5.5 %collective-permute-start.7 = (f32[1792,384]{1,0:T(8,128)}, f32[1792,384]{1,0:T(8,128)}, u32[]{:S(2)}, u32[]{:S(2)}) collective-permute-start(f32[1792,384]{1,0:T(8,128)} %get-tuple-element.133), channel_id=1, source_target_pairs={{0,1},{1,0},{2,3},{3,2},{4,5},{5,4},{6,7},{7,6},{8,9},{9,8},{10,11... | collective-permute-start | bytes 8257544 | tf_op jit(solution)/shard_map/ppermute | solution.py:1038
  95.6 50.3 %collective-permute-start.14 = (f32[576,384]{1,0:T(8,128)}, f32[576,384]{1,0:T(8,128)}, u32[]{:S(2)}, u32[]{:S(2)}) collective-permute-start(f32[576,384]{1,0:T(8,128)} %get-tuple-element.163), channel_id=1, source_target_pairs={{0,1},{1,0},{2,3},{3,2},{4,5},{5,4},{6,7},{7,6},{8,9},{9,8},{10,11... | collective-permute-start | bytes 2654216 | tf_op jit(solution)/shard_map/ppermute | solution.py:1038
  105.1 31.4 %collective-permute-start.8 = (f32[448,384]{1,0:T(8,128)}, f32[448,384]{1,0:T(8,128)}, u32[]{:S(2)}, u32[]{:S(2)}) collective-permute-start(f32[448,384]{1,0:T(8,128)} %get-tuple-element.135), channel_id=1, source_target_pairs={{0,2},{1,3},{2,0},{3,1},{4,6},{5,7},{6,4},{7,5},{8,10},{9,11},{10,... | collective-permute-start | bytes 2064392 | tf_op jit(solution)/shard_map/ppermute | solution.py:1038
  105.7 31.3 %collective-permute-start.9 = (f32[448,384]{1,0:T(8,128)}, f32[448,384]{1,0:T(8,128)}, u32[]{:S(2)}, u32[]{:S(2)}) collective-permute-start(f32[448,384]{1,0:T(8,128)} %get-tuple-element.136), channel_id=1, source_target_pairs={{0,4},{1,5},{2,6},{3,7},{4,0},{5,1},{6,2},{7,3},{8,12},{9,13},{10,... | collective-permute-start | bytes 2064392 | tf_op jit(solution)/shard_map/ppermute | solution.py:1038
  107.3 31.4 %collective-permute-start.10 = (f32[448,384]{1,0:T(8,128)}, f32[448,384]{1,0:T(8,128)}, u32[]{:S(2)}, u32[]{:S(2)}) collective-permute-start(f32[448,384]{1,0:T(8,128)} %get-tuple-element.137), channel_id=1, source_target_pairs={{0,6},{1,7},{2,4},{3,5},{4,2},{5,3},{6,0},{7,1},{8,14},{9,15},{10,... | collective-permute-start | bytes 2064392 | tf_op jit(solution)/shard_map/ppermute | solution.py:1038
  138.6 7.2 %collective-permute-start.15 = (f32[1472,384]{1,0:T(8,128)}, f32[1472,384]{1,0:T(8,128)}, u32[]{:S(2)}, u32[]{:S(2)}) collective-permute-start(f32[1472,384]{1,0:T(8,128)} %get-tuple-element.164), channel_id=1, source_target_pairs={{0,1},{1,0},{2,3},{3,2},{4,5},{5,4},{6,7},{7,6},{8,9},{9,8},{10,11... | collective-permute-start | bytes 6782984 | tf_op jit(solution)/shard_map/ppermute | solution.py:1038
  141.4 11.6 %collective-permute-start.11 = (f32[112,384]{1,0:T(8,128)}, f32[112,384]{1,0:T(8,128)}, u32[]{:S(2)}, u32[]{:S(2)}) collective-permute-start(f32[112,384]{1,0:T(8,128)} %get-tuple-element.159), channel_id=1, source_target_pairs={{0,8},{1,9},{2,10},{3,11},{4,12},{5,13},{6,14},{7,15},{8,0},{9,1},... | collective-permute-start | bytes 516104 | tf_op jit(solution)/shard_map/ppermute | solution.py:1038
  143.0 15.8 %collective-permute-start.12 = (f32[112,384]{1,0:T(8,128)}, f32[112,384]{1,0:T(8,128)}, u32[]{:S(2)}, u32[]{:S(2)}) collective-permute-start(f32[112,384]{1,0:T(8,128)} %get-tuple-element.160), channel_id=1, source_target_pairs={{0,16},{1,17},{2,18},{3,19},{4,20},{5,21},{6,22},{7,23},{8,24},{9,... | collective-permute-start | bytes 516104 | tf_op jit(solution)/shard_map/ppermute | solution.py:1038
  143.3 15.5 %collective-permute-start.13 = (f32[112,384]{1,0:T(8,128)}, f32[112,384]{1,0:T(8,128)}, u32[]{:S(2)}, u32[]{:S(2)}) collective-permute-start(f32[112,384]{1,0:T(8,128)} %get-tuple-element.161), channel_id=1, source_target_pairs={{0,24},{1,25},{2,26},{3,27},{4,28},{5,29},{6,30},{7,31},{8,16},{9,... | collective-permute-start | bytes 516104 | tf_op jit(solution)/shard_map/ppermute | solution.py:1038
  150.6 19.5 %collective-permute-start.19 = (f32[2,256,384]{2,1,0:T(8,128)}, f32[2,256,384]{2,1,0:T(8,128)}, u32[]{:S(2)}, u32[]{:S(2)}) collective-permute-start(f32[2,256,384]{2,1,0:T(8,128)} %get-tuple-element.166), channel_id=1, source_target_pairs={{0,2},{1,3},{2,0},{3,1},{4,6},{5,7},{6,4},{7,5},{8,10},{9,11},{10,... | collective-permute-start | bytes 2359304 | tf_op jit(solution)/shard_map/ppermute | solution.py:1038
  151.4 19.1 %collective-permute-start.20 = (f32[2,256,384]{2,1,0:T(8,128)}, f32[2,256,384]{2,1,0:T(8,128)}, u32[]{:S(2)}, u32[]{:S(2)}) collective-permute-start(f32[2,256,384]{2,1,0:T(8,128)} %get-tuple-element.168), channel_id=1, source_target_pairs={{0,4},{1,5},{2,6},{3,7},{4,0},{5,1},{6,2},{7,3},{8,12},{9,13},{10,... | collective-permute-start | bytes 2359304 | tf_op jit(solution)/shard_map/ppermute | solution.py:1038
  160.7 15.3 %collective-permute-start.18 = (f32[112,384]{1,0:T(8,128)}, f32[112,384]{1,0:T(8,128)}, u32[]{:S(2)}, u32[]{:S(2)}) collective-permute-start(f32[112,384]{1,0:T(8,128)} %add_parts.2.refs_1_), channel_id=1, source_target_pairs={{0,24},{1,25},{2,26},{3,27},{4,28},{5,29},{6,30},{7,31},{8,16},{9,... | collective-permute-start | bytes 516104 | tf_op jit(solution)/shard_map/ppermute | solution.py:1038
  161.3 17.6 %collective-permute-start.17 = (f32[112,384]{1,0:T(8,128)}, f32[112,384]{1,0:T(8,128)}, u32[]{:S(2)}, u32[]{:S(2)}) collective-permute-start(f32[112,384]{1,0:T(8,128)} %add_parts.2.refs_1_), channel_id=1, source_target_pairs={{0,16},{1,17},{2,18},{3,19},{4,20},{5,21},{6,22},{7,23},{8,24},{9,... | collective-permute-start | bytes 516104 | tf_op jit(solution)/shard_map/ppermute | solution.py:1038
  165.8 13.2 %collective-permute-start.16 = (f32[112,384]{1,0:T(8,128)}, f32[112,384]{1,0:T(8,128)}, u32[]{:S(2)}, u32[]{:S(2)}) collective-permute-start(f32[112,384]{1,0:T(8,128)} %add_parts.2.refs_1_), channel_id=1, source_target_pairs={{0,8},{1,9},{2,10},{3,11},{4,12},{5,13},{6,14},{7,15},{8,0},{9,1},... | collective-permute-start | bytes 516104 | tf_op jit(solution)/shard_map/ppermute | solution.py:1038
  173.8 9.9 %collective-permute-start.23 = (f32[256,384]{1,0:T(8,128)}, f32[256,384]{1,0:T(8,128)}, u32[]{:S(2)}, u32[]{:S(2)}) collective-permute-start(f32[256,384]{1,0:T(8,128)} %get-tuple-element.172), channel_id=1, source_target_pairs={{0,4},{1,5},{2,6},{3,7},{4,0},{5,1},{6,2},{7,3},{8,12},{9,13},{10,... | collective-permute-start | bytes 1179656 | tf_op jit(solution)/shard_map/ppermute | solution.py:1038
  175.4 10.7 %collective-permute-start.24 = (f32[256,384]{1,0:T(8,128)}, f32[256,384]{1,0:T(8,128)}, u32[]{:S(2)}, u32[]{:S(2)}) collective-permute-start(f32[256,384]{1,0:T(8,128)} %get-tuple-element.174), channel_id=1, source_target_pairs={{0,2},{1,3},{2,0},{3,1},{4,6},{5,7},{6,4},{7,5},{8,10},{9,11},{10,... | collective-permute-start | bytes 1179656 | tf_op jit(solution)/shard_map/ppermute | solution.py:1038
  181.1 12.1 %collective-permute-start.22 = (f32[224,384]{1,0:T(8,128)}, f32[224,384]{1,0:T(8,128)}, u32[]{:S(2)}, u32[]{:S(2)}) collective-permute-start(f32[224,384]{1,0:T(8,128)} %get-tuple-element.171.refs_3_), channel_id=1, source_target_pairs={{0,2},{1,3},{2,0},{3,1},{4,6},{5,7},{6,4},{7,5},{8,10},{9,11},{10,... | collective-permute-start | bytes 1032200 | tf_op jit(solution)/shard_map/ppermute | solution.py:1038
  182.0 11.2 %collective-permute-start.21 = (f32[224,384]{1,0:T(8,128)}, f32[224,384]{1,0:T(8,128)}, u32[]{:S(2)}, u32[]{:S(2)}) collective-permute-start(f32[224,384]{1,0:T(8,128)} %get-tuple-element.170.refs_5_.refs_1_), channel_id=1, source_target_pairs={{0,4},{1,5},{2,6},{3,7},{4,0},{5,1},{6,2},{7,3},{8,12},{9,13},{10,... | collective-permute-start | bytes 1032200 | tf_op jit(solution)/shard_map/ppermute | solution.py:1038
  188.4 9.4 %collective-permute-start.27 = (f32[128,384]{1,0:T(8,128)}, f32[128,384]{1,0:T(8,128)}, u32[]{:S(2)}, u32[]{:S(2)}) collective-permute-start(f32[128,384]{1,0:T(8,128)} %get-tuple-element.178), channel_id=1, source_target_pairs={{0,8},{1,9},{2,10},{3,11},{4,12},{5,13},{6,14},{7,15},{8,0},{9,1},... | collective-permute-start | bytes 589832 | tf_op jit(solution)/shard_map/ppermute | solution.py:1038
  190.7 15.0 %collective-permute-start.28 = (f32[128,384]{1,0:T(8,128)}, f32[128,384]{1,0:T(8,128)}, u32[]{:S(2)}, u32[]{:S(2)}) collective-permute-start(f32[128,384]{1,0:T(8,128)} %get-tuple-element.179), channel_id=1, source_target_pairs={{0,16},{1,17},{2,18},{3,19},{4,20},{5,21},{6,22},{7,23},{8,24},{9,... | collective-permute-start | bytes 589832 | tf_op jit(solution)/shard_map/ppermute | solution.py:1038
  190.7 15.0 %collective-permute-start.29 = (f32[128,384]{1,0:T(8,128)}, f32[128,384]{1,0:T(8,128)}, u32[]{:S(2)}, u32[]{:S(2)}) collective-permute-start(f32[128,384]{1,0:T(8,128)} %get-tuple-element.180), channel_id=1, source_target_pairs={{0,24},{1,25},{2,26},{3,27},{4,28},{5,29},{6,30},{7,31},{8,16},{9,... | collective-permute-start | bytes 589832 | tf_op jit(solution)/shard_map/ppermute | solution.py:1038
  207.7 9.9 %collective-permute-start.32 = (f32[128,384]{1,0:T(8,128)}, f32[128,384]{1,0:T(8,128)}, u32[]{:S(2)}, u32[]{:S(2)}) collective-permute-start(f32[128,384]{1,0:T(8,128)} %add_parts.3.refs_1_), channel_id=1, source_target_pairs={{0,24},{1,25},{2,26},{3,27},{4,28},{5,29},{6,30},{7,31},{8,16},{9,... | collective-permute-start | bytes 589832 | tf_op jit(solution)/shard_map/ppermute | solution.py:1038
  209.2 16.2 %collective-permute-start.31 = (f32[128,384]{1,0:T(8,128)}, f32[128,384]{1,0:T(8,128)}, u32[]{:S(2)}, u32[]{:S(2)}) collective-permute-start(f32[128,384]{1,0:T(8,128)} %add_parts.3.refs_1_), channel_id=1, source_target_pairs={{0,16},{1,17},{2,18},{3,19},{4,20},{5,21},{6,22},{7,23},{8,24},{9,... | collective-permute-start | bytes 589832 | tf_op jit(solution)/shard_map/ppermute | solution.py:1038
  211.9 13.5 %collective-permute-start.30 = (f32[128,384]{1,0:T(8,128)}, f32[128,384]{1,0:T(8,128)}, u32[]{:S(2)}, u32[]{:S(2)}) collective-permute-start(f32[128,384]{1,0:T(8,128)} %add_parts.3.refs_1_), channel_id=1, source_target_pairs={{0,8},{1,9},{2,10},{3,11},{4,12},{5,13},{6,14},{7,15},{8,0},{9,1},... | collective-permute-start | bytes 589832 | tf_op jit(solution)/shard_map/ppermute | solution.py:1038
  212.2 15.4 %collective-permute-start.25 = (f32[2,224,384]{2,1,0:T(8,128)}, f32[2,224,384]{2,1,0:T(8,128)}, u32[]{:S(2)}, u32[]{:S(2)}) collective-permute-start(f32[2,224,384]{2,1,0:T(8,128)} %get-tuple-element.183.refs_5_.refs_2_), channel_id=1, source_target_pairs={{0,2},{1,3},{2,0},{3,1},{4,6},{5,7},{6,4},{7,5},{8,10},{9,11},{10,... | collective-permute-start | bytes 2064392 | tf_op jit(solution)/shard_map/ppermute | solution.py:1038
  212.8 14.8 %collective-permute-start.26 = (f32[2,224,384]{2,1,0:T(8,128)}, f32[2,224,384]{2,1,0:T(8,128)}, u32[]{:S(2)}, u32[]{:S(2)}) collective-permute-start(f32[2,224,384]{2,1,0:T(8,128)} %get-tuple-element.185.refs_4_), channel_id=1, source_target_pairs={{0,4},{1,5},{2,6},{3,7},{4,0},{5,1},{6,2},{7,3},{8,12},{9,13},{10,... | collective-permute-start | bytes 2064392 | tf_op jit(solution)/shard_map/ppermute | solution.py:1038
  227.6 12.7 %collective-permute-start.33 = (f32[2,224,384]{2,1,0:T(8,128)}, f32[2,224,384]{2,1,0:T(8,128)}, u32[]{:S(2)}, u32[]{:S(2)}) collective-permute-start(f32[2,224,384]{2,1,0:T(8,128)} %get-tuple-element.183.refs_5_.refs_2_), channel_id=1, source_target_pairs={{0,1},{1,0},{2,3},{3,2},{4,5},{5,4},{6,7},{7,6},{8,9},{9,8},{10,11... | collective-permute-start | bytes 2064392 | tf_op jit(solution)/shard_map/ppermute | solution.py:1038
  227.7 12.6 %collective-permute-start.36 = (f32[2,224,384]{2,1,0:T(8,128)}, f32[2,224,384]{2,1,0:T(8,128)}, u32[]{:S(2)}, u32[]{:S(2)}) collective-permute-start(f32[2,224,384]{2,1,0:T(8,128)} %collective-permute-done.26.refs_5_), channel_id=1, source_target_pairs={{0,1},{1,0},{2,3},{3,2},{4,5},{5,4},{6,7},{7,6},{8,9},{9,8},{10,11... | collective-permute-start | bytes 2064392 | tf_op jit(solution)/shard_map/ppermute | solution.py:1038
  228.2 11.4 %collective-permute-start.37 = (f32[256,384]{1,0:T(8,128)}, f32[256,384]{1,0:T(8,128)}, u32[]{:S(2)}, u32[]{:S(2)}) collective-permute-start(f32[256,384]{1,0:T(8,128)} %get-tuple-element.192.refs_1_), channel_id=1, source_target_pairs={{0,4},{1,5},{2,6},{3,7},{4,0},{5,1},{6,2},{7,3},{8,12},{9,13},{10,... | collective-permute-start | bytes 1179656 | tf_op jit(solution)/shard_map/ppermute | solution.py:1038
  229.3 11.1 %collective-permute-start.38 = (f32[256,384]{1,0:T(8,128)}, f32[256,384]{1,0:T(8,128)}, u32[]{:S(2)}, u32[]{:S(2)}) collective-permute-start(f32[256,384]{1,0:T(8,128)} %get-tuple-element.193.refs_3_), channel_id=1, source_target_pairs={{0,2},{1,3},{2,0},{3,1},{4,6},{5,7},{6,4},{7,5},{8,10},{9,11},{10,... | collective-permute-start | bytes 1179656 | tf_op jit(solution)/shard_map/ppermute | solution.py:1038
  230.1 15.1 %collective-permute-start.34 = (f32[2,224,384]{2,1,0:T(8,128)}, f32[2,224,384]{2,1,0:T(8,128)}, u32[]{:S(2)}, u32[]{:S(2)}) collective-permute-start(f32[2,224,384]{2,1,0:T(8,128)} %collective-permute-done.25.refs_3_), channel_id=1, source_target_pairs={{0,1},{1,0},{2,3},{3,2},{4,5},{5,4},{6,7},{7,6},{8,9},{9,8},{10,11... | collective-permute-start | bytes 2064392 | tf_op jit(solution)/shard_map/ppermute | solution.py:1038
  239.6 5.6 %collective-permute-start.35 = (f32[2,224,384]{2,1,0:T(8,128)}, f32[2,224,384]{2,1,0:T(8,128)}, u32[]{:S(2)}, u32[]{:S(2)}) collective-permute-start(f32[2,224,384]{2,1,0:T(8,128)} %get-tuple-element.185.refs_4_), channel_id=1, source_target_pairs={{0,1},{1,0},{2,3},{3,2},{4,5},{5,4},{6,7},{7,6},{8,9},{9,8},{10,11... | collective-permute-start | bytes 2064392 | tf_op jit(solution)/shard_map/ppermute | solution.py:1038
  243.0 20.5 %collective-permute-start.39 = (f32[2,256,384]{2,1,0:T(8,128)}, f32[2,256,384]{2,1,0:T(8,128)}, u32[]{:S(2)}, u32[]{:S(2)}) collective-permute-start(f32[2,256,384]{2,1,0:T(8,128)} %get-tuple-element.195.refs_3_), channel_id=1, source_target_pairs={{0,2},{1,3},{2,0},{3,1},{4,6},{5,7},{6,4},{7,5},{8,10},{9,11},{10,... | collective-permute-start | bytes 2359304 | tf_op jit(solution)/shard_map/ppermute | solution.py:1038
  243.9 19.5 %collective-permute-start.40 = (f32[2,256,384]{2,1,0:T(8,128)}, f32[2,256,384]{2,1,0:T(8,128)}, u32[]{:S(2)}, u32[]{:S(2)}) collective-permute-start(f32[2,256,384]{2,1,0:T(8,128)} %get-tuple-element.198.refs_5_), channel_id=1, source_target_pairs={{0,4},{1,5},{2,6},{3,7},{4,0},{5,1},{6,2},{7,3},{8,12},{9,13},{10,... | collective-permute-start | bytes 2359304 | tf_op jit(solution)/shard_map/ppermute | solution.py:1038
  252.2 5.1 %copy-start.3 = (f32[2,256,384]{2,1,0:T(8,128)S(1)}, f32[2,256,384]{2,1,0:T(8,128)}, u32[]{:S(2)}) copy-start(f32[2,256,384]{2,1,0:T(8,128)} %get-tuple-element.195.refs_3_) | copy-start | bytes 2359300
  252.2 5.1 %copy-start.4 = (f32[2,256,384]{2,1,0:T(8,128)S(1)}, f32[2,256,384]{2,1,0:T(8,128)}, u32[]{:S(2)}) copy-start(f32[2,256,384]{2,1,0:T(8,128)} %get-tuple-element.198.refs_5_) | copy-start | bytes 2359300
  252.2 11.7 %copy-start.2 = (f32[8,128]{1,0:T(8,128)S(1)}, f32[8,128]{1,0:T(8,128)}, u32[]{:S(2)}) copy-start(f32[8,128]{1,0:T(8,128)} %get-tuple-element.212) | copy-start | bytes 12292
  252.2 12.3 %copy-start = (f32[192,192]{1,0:T(8,128)S(1)}, f32[192,192]{1,0:T(8,128)}, u32[]{:S(2)}) copy-start(f32[192,192]{1,0:T(8,128)} %get-tuple-element.217) | copy-start | bytes 442372
  257.4 7.9 %collective-permute-start.41 = (f32[2,256,384]{2,1,0:T(8,128)S(1)}, f32[2,256,384]{2,1,0:T(8,128)S(1)}, u32[]{:S(2)}, u32[]{:S(2)}) collective-permute-start(f32[2,256,384]{2,1,0:T(8,128)S(1)} %copy-done.3), channel_id=1, source_target_pairs={{0,1},{1,0},{2,3},{3,2},{4,5},{5,4},{6,7},{7,6},{8,9},{9,8},{10,11... | collective-permute-start | bytes 2359304 | tf_op jit(solution)/shard_map/ppermute | solution.py:1038
  257.4 7.9 %collective-permute-start.43 = (f32[2,256,384]{2,1,0:T(8,128)S(1)}, f32[2,256,384]{2,1,0:T(8,128)S(1)}, u32[]{:S(2)}, u32[]{:S(2)}) collective-permute-start(f32[2,256,384]{2,1,0:T(8,128)S(1)} %copy-done.4), channel_id=1, source_target_pairs={{0,1},{1,0},{2,3},{3,2},{4,5},{5,4},{6,7},{7,6},{8,9},{9,8},{10,11... | collective-permute-start | bytes 2359304 | tf_op jit(solution)/shard_map/ppermute | solution.py:1038
  263.4 2.7 collective-permute-start.42
  263.5 3.6 %collective-permute-start.44 = (f32[2,256,384]{2,1,0:T(8,128)}, f32[2,256,384]{2,1,0:T(8,128)S(1)}, u32[]{:S(2)}, u32[]{:S(2)}) collective-permute-start(f32[2,256,384]{2,1,0:T(8,128)} %collective-permute-done.40.refs_6_), channel_id=1, source_target_pairs={{0,1},{1,0},{2,3},{3,2},{4,5},{5,4},{6,7},{7,6},{8,9},{9,8},{10,11... | collective-permute-start | bytes 2359304 | tf_op jit(solution)/shard_map/ppermute | solution.py:1038
  265.2 0.9 copy-start.5
  266.1 0.9 copy-start.6
  267.0 0.9 copy-start.7
  267.9 0.9 copy-start.8
